TPU v7x, 32 devices: a whole 2x2x4 slice. The times are simulated.
32 devices in a mesh: row: 8 (over z, x), col: 4 (over y, core).
Axes of the slice: x: 2, y: 2, z: 4, core: 2. Of those that a mesh axis runs over, the one named last changes fastest.
Arguments:
- stem_map: bfloat16 [384, 128, 128], P('row', 'col'), may hold values from -6 to 6
- layout: int32 [5, 192, 64], P(None, 'row', 'col'), may hold values from 0 to 192, as said below
- labels: int32 [52], replicated, may hold values from 0 to 999
- live: int32 [52], replicated, may hold values 0 or 1
- conv_weight: float32 [1152, 256], P(None, 'row'), may hold values from -0.1875 to 0.1875
- input_proj: float32 [2, 256, 768], P(None, 'row'), may hold values from -0.375 to 0.375
- output_proj: float32 [2, 256, 256], P(None, 'row'), may hold values from -2.5 to 2.5
- expand_weight: float32 [2, 256, 768], P(None, 'row'), may hold values from -0.375 to 0.375
- reduce_weight: float32 [2, 768, 256], P(None, 'row'), may hold values from -0.21875 to 0.21875
- head_weight: float32 [256, 1000], P('row'), may hold values from -0.375 to 0.375
- small_params: float32 [8312], replicated
- first_conv: float32 [1152, 256], P(None, 'row'), may hold values from -0.0007324219 to 0.0007324219
- first_input: float32 [2, 256, 768], P(None, 'row'), may hold values from -0.0007324219 to 0.0007324219
- first_output: float32 [2, 256, 256], P(None, 'row'), may hold values from -0.0007324219 to 0.0007324219
- first_expand: float32 [2, 256, 768], P(None, 'row'), may hold values from -0.0007324219 to 0.0007324219
- first_reduce: float32 [2, 768, 256], P(None, 'row'), may hold values from -0.0007324219 to 0.0007324219
- first_head: float32 [256, 1000], P('row'), may hold values from -0.0007324219 to 0.0007324219
- first_small: float32 [8312], replicated, may hold values from -0.005859375 to 0.005859375
- second_conv: float32 [1152, 256], P(None, 'row'), may hold values from 6.3476563e-10 to 1.0172526e-08
- second_input: float32 [2, 256, 768], P(None, 'row'), may hold values from 6.3476563e-10 to 1.0172526e-08
- second_output: float32 [2, 256, 256], P(None, 'row'), may hold values from 6.3476563e-10 to 1.0172526e-08
- second_expand: float32 [2, 256, 768], P(None, 'row'), may hold values from 6.3476563e-10 to 1.0172526e-08
- second_reduce: float32 [2, 768, 256], P(None, 'row'), may hold values from 6.3476563e-10 to 1.0172526e-08
- second_head: float32 [256, 1000], P('row'), may hold values from 6.3476563e-10 to 1.0172526e-08
- second_small: float32 [8312], replicated, may hold values from 4.0690104e-08 to 6.5104166e-07
Outputs:
- loss: float32 [], replicated
- conv_first_new: float32 [1152, 256], P(None, 'row')
- conv_second_new: float32 [1152, 256], P(None, 'row')
- conv_weight_new: float32 [1152, 256], P(None, 'row')
- input_first_new: float32 [2, 256, 768], P(None, 'row')
- input_second_new: float32 [2, 256, 768], P(None, 'row')
- input_weight_new: float32 [2, 256, 768], P(None, 'row')
- output_first_new: float32 [2, 256, 256], P(None, 'row')
- output_second_new: float32 [2, 256, 256], P(None, 'row')
- output_weight_new: float32 [2, 256, 256], P(None, 'row')
- expand_first_new: float32 [2, 256, 768], P(None, 'row')
- expand_second_new: float32 [2, 256, 768], P(None, 'row')
- expand_weight_new: float32 [2, 256, 768], P(None, 'row')
- reduce_first_new: float32 [2, 768, 256], P(None, 'row')
- reduce_second_new: float32 [2, 768, 256], P(None, 'row')
- reduce_weight_new: float32 [2, 768, 256], P(None, 'row')
- head_first_new: float32 [256, 1000], P('row')
- head_second_new: float32 [256, 1000], P('row')
- head_weight_new: float32 [256, 1000], P('row')
- small_first_new: float32 [8312], replicated
- small_second_new: float32 [8312], replicated
- small_params_new: float32 [8312], replicated
Inputs may be any that keep to these rules, and one draw needn't show every extreme that they name: The canvas is cut into bands of rows; most bands are 14, 18 or 24 rows high, the last one 14 to 37 and ending at row 192. Each band is cut into images as wide as the band's bucket side, the last one in a band taking the remaining columns up to 64; every image is 14 or more positions high and wide. layout gives each position its image's top row, bottom row (exclusive), left column, right column (exclusive) and slot; slots are unique to an image and numbered in order of bands and columns, the canvas's last image having slot 51; the lowest slots hold no positions. Images cross tile borders.
All inputs are finite; a program needn't handle non-finite values.
Results may differ from a plain program's by a relative error of at most 0.019.
Values may be sent and summed in bfloat16 or wider, within the bound.
No kernel may reach another device: no remote copies, remote signals or barrier semaphores. Data moves between devices by JAX's collectives and lax.ppermute only.
A program may use at most 448 MiB of HBM per device.

v0:
```python
import jax
import jax.numpy as jnp
from jax import lax
from jax.sharding import PartitionSpec as P

D = 256
HEADS = 8
FF = 768
CLASSES = 1000
LAYERS = 2
STEP = 5


eps_norm = 1e-05
beta_one = 0.9
beta_two = 0.999
learn_rate = 0.2
decay_rate = 0.05
eps_adam = 1e-08


def with_halo(block, sides, width):
    for axis, dim in sides:
        count = lax.axis_size(axis)
        forward = [(i, i + 1) for i in range(count - 1)]
        backward = [(target, source) for source, target in forward]
        low = lax.ppermute(
            lax.slice_in_dim(block, block.shape[dim] - width, None, axis=dim), axis, forward
        )
        high = lax.ppermute(lax.slice_in_dim(block, 0, width, axis=dim), axis, backward)
        block = jnp.concatenate([low, block, high], axis=dim)
    return block


def passed_along(value, axis, steps):
    count = lax.axis_size(axis)
    leading, last = (max(0, -steps), min(count, count - steps))
    return lax.ppermute(value, axis, [(source, source + steps) for source in range(leading, last)])


def layer_norm(values, gain, bias):
    centre = values - jnp.mean(values, -1, keepdims=True)
    spread = jnp.mean(centre * centre, -1, keepdims=True)
    return centre * lax.rsqrt(spread + eps_norm) * gain + bias


def unpack(small):
    count_norm = (2 + 2 * LAYERS) * 2 * D
    norms = small[:count_norm].reshape(2 + 2 * LAYERS, 2, D)
    exp_bias = small[count_norm : count_norm + LAYERS * FF].reshape(LAYERS, FF)
    start = count_norm + LAYERS * FF
    head_bias = small[start : start + CLASSES]
    pos_bias = small[start + CLASSES :].reshape(LAYERS, HEADS, 169)
    return (norms, exp_bias, head_bias, pos_bias)


def make_patches(framed, layout, row_first, col_first):
    rows, cols = (layout.shape[1], layout.shape[2])
    row_pos = row_first + jnp.arange(rows, dtype=jnp.int32)[:, None]
    col_pos = col_first + jnp.arange(cols, dtype=jnp.int32)[None, :]
    first_row = (row_pos == layout[0])[..., None]
    first_col = (col_pos == layout[2])[..., None]
    taps = []
    for a in range(3):
        for b in range(3):
            tap = framed[a : a + 2 * rows : 2, b : b + 2 * cols : 2]
            if a == 0:
                tap = jnp.where(first_row, jnp.zeros_like(tap), tap)
            if b == 0:
                tap = jnp.where(first_col, jnp.zeros_like(tap), tap)
            taps.append(tap)
    return jnp.concatenate(taps, -1).reshape(rows * cols, -1)


def offsets(layout, dilation, row_first, col_first):
    rows, cols = (layout.shape[1], layout.shape[2])
    row_pos = (
        row_first + jnp.arange(rows, dtype=jnp.int32)[:, None] + jnp.zeros((rows, cols), jnp.int32)
    )
    col_pos = (
        col_first + jnp.arange(cols, dtype=jnp.int32)[None, :] + jnp.zeros((rows, cols), jnp.int32)
    )

    def begin(place, first, extent):
        local = place - first
        group = local % dilation
        index = local // dilation
        length = (extent - group + dilation - 1) // dilation
        return jnp.clip(index - 3, 0, length - 7) - index

    return (
        begin(row_pos, layout[0], layout[1] - layout[0]),
        begin(col_pos, layout[2], layout[3] - layout[2]),
    )


def window_index(lo_row, lo_col, dilation, reach, pad_cols):
    rows, cols = lo_row.shape
    steps = jnp.arange(7, dtype=jnp.int32)
    row_key = (
        jnp.arange(rows, dtype=jnp.int32)[:, None, None, None]
        + reach
        + dilation * (lo_row[:, :, None, None] + steps[:, None])
    )
    col_key = (
        jnp.arange(cols, dtype=jnp.int32)[None, :, None, None]
        + reach
        + dilation * (lo_col[:, :, None, None] + steps[None, :])
    )
    keys = (row_key * pad_cols + col_key).reshape(rows * cols, 49)
    table = (
        (lo_row[:, :, None, None] + steps[:, None] + 6) * 13
        + lo_col[:, :, None, None]
        + steps[None, :]
        + 6
    ).reshape(rows * cols, 49)
    return (keys, table)


def adamw(weight, grad, first, second):
    first = beta_one * first + (1.0 - beta_one) * grad
    second = beta_two * second + (1.0 - beta_two) * grad * grad
    fix_one = 1.0 - beta_one**STEP
    fix_two = 1.0 - beta_two**STEP
    new = weight - learn_rate * (
        first / fix_one / (jnp.sqrt(second / fix_two) + eps_adam) + decay_rate * weight
    )
    return (first, second, new)


def product(left, right):
    return jnp.dot(left, right, preferred_element_type=jnp.float32)


def window_scores(query, flat, keys, table, bias):
    near = jnp.take(flat, keys, axis=0)
    count = query.shape[0]
    query4 = query.reshape(count, HEADS, -1)
    size = query4.shape[-1]
    key4 = near[..., :D].reshape(count, 49, HEADS, size)
    value4 = near[..., D:].reshape(count, 49, HEADS, size)
    score = jnp.einsum(
        "nhc,nkhc->nhk", query4, key4, preferred_element_type=jnp.float32
    ) * size ** (-0.5)
    return (score + jnp.take(bias, table, axis=1).transpose(1, 0, 2), query4, key4, value4)


def attend_tile(query, flat, keys, table, bias):
    count = query.shape[0]

    def one_block(pieces):
        score, query4, key4, value4 = window_scores(pieces[0], flat, pieces[1], pieces[2], bias)
        top = jnp.max(score, -1, keepdims=True)
        logsum = top + jnp.log(jnp.sum(jnp.exp(score - top), -1, keepdims=True))
        probs = jnp.exp(score - logsum).astype(jnp.bfloat16)
        result = jnp.einsum("nhk,nkhc->nhc", probs, value4, preferred_element_type=jnp.float32)
        return (result.reshape(result.shape[0], -1), logsum[..., 0])

    result, logsum = lax.map(
        one_block,
        (query.reshape(-1, count, D), keys.reshape(-1, count, 49), table.reshape(-1, count, 49)),
    )
    return (result.reshape(count, D), logsum.reshape(count, -1))


def attend_back(query, flat, keys, table, bias, logsum, dout):
    count = query.shape[0]

    def one_block(dflat, pieces):
        query_b, keys_b, table_b, logsum_b, dout_b = pieces
        score, query4, key4, value4 = window_scores(query_b, flat, keys_b, table_b, bias)
        probs = jnp.exp(score - logsum_b[..., None])
        scale = query4.shape[-1] ** (-0.5)
        dout4 = dout_b.reshape(query4.shape)
        dvalue = jnp.einsum("nhk,nhc->nkhc", probs.astype(jnp.bfloat16).astype(jnp.float32), dout4)
        dprob = jnp.einsum("nhc,nkhc->nhk", dout4, value4.astype(jnp.float32))
        dscore = probs * (dprob - jnp.sum(probs * dprob, -1, keepdims=True))
        dquery = jnp.einsum("nhk,nkhc->nhc", dscore, key4.astype(jnp.float32)) * scale
        dkey = jnp.einsum("nhk,nhc->nkhc", dscore, query4.astype(jnp.float32)) * scale
        dnear = jnp.concatenate([dkey, dvalue], 2)
        dflat = dflat.at[keys_b.reshape(-1)].add(dnear.reshape(-1, 2 * D))
        dbias = jax.ops.segment_sum(
            dscore.transpose(0, 2, 1).reshape(-1, dscore.shape[1]), table_b.reshape(-1), 169
        ).T
        return (dflat, (dquery.reshape(dquery.shape[0], -1), dbias))

    pieces = (
        query.reshape(-1, count, D),
        keys.reshape(-1, count, 49),
        table.reshape(-1, count, 49),
        logsum.reshape(-1, count, logsum.shape[1]),
        dout.reshape(-1, count, D),
    )
    dflat, (dquery, dbias) = lax.scan(one_block, jnp.zeros(flat.shape, jnp.float32), pieces)
    return (dquery.reshape(count, D), dflat, jnp.sum(dbias, 0))


def halo_keys(keyval, reach):
    return with_halo(keyval, (("row", 0), ("col", 1)), reach)


def give_back(padded, reach):
    top_rim = padded[:reach]
    bottom_rim = padded[-reach:]
    middle = padded[reach:-reach]
    from_below = passed_along(top_rim.astype(jnp.bfloat16), "row", -1).astype(top_rim.dtype)
    from_above = passed_along(bottom_rim.astype(jnp.bfloat16), "row", 1).astype(bottom_rim.dtype)
    middle = middle.at[:reach].add(from_above)
    middle = middle.at[-reach:].add(from_below)
    left_rim = middle[:, :reach]
    right_rim = middle[:, -reach:]
    inner = middle[:, reach:-reach]
    from_right = passed_along(left_rim.astype(jnp.bfloat16), "col", -1).astype(left_rim.dtype)
    from_left = passed_along(right_rim.astype(jnp.bfloat16), "col", 1).astype(right_rim.dtype)
    inner = inner.at[:, :reach].add(from_left)
    inner = inner.at[:, -reach:].add(from_right)
    return inner


def on_device(
    stem_map,
    layout,
    labels,
    live,
    conv_weight,
    input_proj,
    output_proj,
    expand_weight,
    reduce_weight,
    head_weight,
    small_params,
    first_conv,
    first_input,
    first_output,
    first_expand,
    first_reduce,
    first_head,
    first_small,
    second_conv,
    second_input,
    second_output,
    second_expand,
    second_reduce,
    second_head,
    second_small,
):
    wconv, wqkv, wproj, wexp, wred, whead = (
        lax.all_gather(conv_weight.astype(jnp.bfloat16), "row", axis=1, tiled=True),
        lax.all_gather(input_proj.astype(jnp.bfloat16), "row", axis=1, tiled=True),
        lax.all_gather(output_proj.astype(jnp.bfloat16), "row", axis=1, tiled=True),
        lax.all_gather(expand_weight.astype(jnp.bfloat16), "row", axis=1, tiled=True),
        lax.all_gather(reduce_weight.astype(jnp.bfloat16), "row", axis=1, tiled=True),
        lax.all_gather(head_weight.astype(jnp.bfloat16), "row", axis=0, tiled=True),
    )
    norms, exp_bias, head_bias, pos_bias = unpack(small_params)
    rows = stem_map.shape[0] // 2
    cols = stem_map.shape[1] // 2
    tokens = rows * cols
    images = labels.shape[0]
    row_first = lax.axis_index("row") * rows
    col_first = lax.axis_index("col") * cols
    above = passed_along(stem_map[-1:], "row", 1)
    taller = jnp.concatenate([above, stem_map], 0)
    leftmost = passed_along(taller[:, -1:], "col", 1)
    framed = jnp.concatenate([leftmost, taller], 1)
    patches = make_patches(framed, layout, row_first, col_first)
    conv_out = product(patches, wconv)
    hidden = layer_norm(conv_out, norms[0, 0], norms[0, 1])
    indices = []
    for layer in range(LAYERS):
        dilation = layer + 1
        lo_row, lo_col = offsets(layout, dilation, row_first, col_first)
        indices.append(window_index(lo_row, lo_col, dilation, 6 * dilation, cols + 12 * dilation))
    saved = []
    for layer in range(LAYERS):
        reach = 6 * (layer + 1)
        res_in = hidden
        normed = layer_norm(hidden, norms[1 + 2 * layer, 0], norms[1 + 2 * layer, 1]).astype(
            jnp.bfloat16
        )
        mixed = product(normed, wqkv[layer])
        query = mixed[:, :D].astype(jnp.bfloat16)
        keyval = mixed[:, D:].astype(jnp.bfloat16).reshape(rows, cols, 2 * D)
        flat = halo_keys(keyval, reach).reshape(-1, 2 * D)
        att, logsum = attend_tile(
            query, flat, indices[layer][0], indices[layer][1], pos_bias[layer]
        )
        att_low = att.astype(jnp.bfloat16)
        hidden = hidden + product(att_low, wproj[layer])
        res_mid = hidden
        normed2 = layer_norm(hidden, norms[2 + 2 * layer, 0], norms[2 + 2 * layer, 1]).astype(
            jnp.bfloat16
        )
        upper = product(normed2, wexp[layer]) + exp_bias[layer]
        gelu_low = jax.nn.gelu(upper, approximate=False).astype(jnp.bfloat16)
        hidden = hidden + product(gelu_low, wred[layer])
        saved.append(
            (
                res_in,
                normed,
                query,
                keyval,
                flat,
                logsum,
                att_low,
                res_mid,
                normed2,
                upper,
                gelu_low,
            )
        )
    final = layer_norm(hidden, norms[-1, 0], norms[-1, 1])
    slot = layout[4].reshape(tokens)
    part_sums = jax.ops.segment_sum(final, slot, images)
    part_area = jax.ops.segment_sum(jnp.ones((tokens,), jnp.float32), slot, images)
    sums, area = lax.psum((part_sums, part_area), ("row", "col"))
    spread_area = jnp.maximum(area, 1.0)
    pooled_low = (sums / spread_area[:, None]).astype(jnp.bfloat16)
    logits = product(pooled_low, whead) + head_bias
    weight_item = live.astype(jnp.float32) * (area > 0.5).astype(jnp.float32)
    count = jnp.maximum(jnp.sum(weight_item), 1.0)
    onehot = (labels[:, None] == jnp.arange(whead.shape[1], dtype=jnp.int32)[None, :]).astype(
        jnp.float32
    )
    top = jnp.max(logits, -1, keepdims=True)
    logsum_cls = jnp.log(jnp.sum(jnp.exp(logits - top), -1, keepdims=True)) + top
    cross = logsum_cls[:, 0] - jnp.sum(onehot * logits, -1)
    loss = jnp.sum(weight_item * cross) / count
    dlogit_low = ((weight_item / count)[:, None] * (jnp.exp(logits - logsum_cls) - onehot)).astype(
        jnp.bfloat16
    )
    parts = lax.axis_size("row")
    owner = lax.axis_index("row")
    share = whead.shape[0] // parts
    own_pooled = lax.dynamic_slice_in_dim(pooled_low, owner * share, share, 1)
    grad_head = product(own_pooled.T, dlogit_low)
    grad_hbias = jnp.sum(dlogit_low.astype(jnp.float32), 0)
    dpooled = product(dlogit_low, whead.T)
    dfinal = jnp.take(dpooled / spread_area[:, None], slot, axis=0)
    norm_grads = [None] * (2 + 2 * LAYERS)
    dhid, gain_grad, bias_grad = jax.vjp(layer_norm, hidden, norms[-1, 0], norms[-1, 1])[1](dfinal)
    norm_grads[-1] = jnp.stack([gain_grad, bias_grad])
    grads_qkv, grads_proj, grads_exp, grads_red, grads_ebias, grads_pos = ([], [], [], [], [], [])
    for layer in reversed(range(LAYERS)):
        reach = 6 * (layer + 1)
        res_in, normed, query, keyval, flat, logsum, att_low, res_mid, normed2, upper, gelu_low = (
            saved[layer]
        )
        dz_low = dhid.astype(jnp.bfloat16)
        grads_red.append(product(gelu_low.T, dz_low))
        dgelu = product(dz_low, wred[layer].T)
        dupper = jax.vjp(lambda values: jax.nn.gelu(values, approximate=False), upper)[1](dgelu)[0]
        dup_low = dupper.astype(jnp.bfloat16)
        grads_ebias.append(jnp.sum(dup_low.astype(jnp.float32), 0))
        grads_exp.append(product(normed2.T, dup_low))
        dnormed2 = product(dup_low, wexp[layer].T)
        dres, gain_grad, bias_grad = jax.vjp(
            layer_norm, res_mid, norms[2 + 2 * layer, 0], norms[2 + 2 * layer, 1]
        )[1](dnormed2)
        norm_grads[2 + 2 * layer] = jnp.stack([gain_grad, bias_grad])
        dhid = dhid + dres
        dy_low = dhid.astype(jnp.bfloat16)
        grads_proj.append(product(att_low.T, dy_low))
        datt = product(dy_low, wproj[layer].T)
        dquery, dflat, dpos = attend_back(
            query, flat, indices[layer][0], indices[layer][1], pos_bias[layer], logsum, datt
        )
        grads_pos.append(dpos)
        dkeyval = give_back(dflat.reshape(rows + 2 * reach, cols + 2 * reach, 2 * D), reach)
        dmixed = jnp.concatenate([dquery, dkeyval.reshape(tokens, 2 * D)], 1).astype(jnp.bfloat16)
        grads_qkv.append(product(normed.T, dmixed))
        dnormed = product(dmixed, wqkv[layer].T)
        dres, gain_grad, bias_grad = jax.vjp(
            layer_norm, res_in, norms[1 + 2 * layer, 0], norms[1 + 2 * layer, 1]
        )[1](dnormed)
        norm_grads[1 + 2 * layer] = jnp.stack([gain_grad, bias_grad])
        dhid = dhid + dres
    dconv, gain_grad, bias_grad = jax.vjp(layer_norm, conv_out, norms[0, 0], norms[0, 1])[1](dhid)
    norm_grads[0] = jnp.stack([gain_grad, bias_grad])
    grad_conv = product(patches.T, dconv.astype(jnp.bfloat16))
    grad_qkv = jnp.stack(grads_qkv[::-1])
    grad_proj = jnp.stack(grads_proj[::-1])
    grad_exp = jnp.stack(grads_exp[::-1])
    grad_red = jnp.stack(grads_red[::-1])
    front = jnp.concatenate(
        [jnp.stack(norm_grads).reshape(-1), jnp.stack(grads_ebias[::-1]).reshape(-1)]
    )
    summed_front, summed_pos = lax.psum(
        (front, jnp.stack(grads_pos[::-1]).reshape(-1)), ("row", "col")
    )
    grad_small = jnp.concatenate([summed_front, grad_hbias, summed_pos])
    summed = lax.psum((grad_conv, grad_qkv, grad_proj, grad_exp, grad_red), ("row", "col"))
    shares = []
    for grad in summed:
        width = grad.shape[1] // parts
        shares.append(lax.dynamic_slice_in_dim(grad, owner * width, width, 1))
    params = (
        conv_weight,
        input_proj,
        output_proj,
        expand_weight,
        reduce_weight,
        head_weight,
        small_params,
    )
    grads = (shares[0], shares[1], shares[2], shares[3], shares[4], grad_head, grad_small)
    firsts = (
        first_conv,
        first_input,
        first_output,
        first_expand,
        first_reduce,
        first_head,
        first_small,
    )
    seconds = (
        second_conv,
        second_input,
        second_output,
        second_expand,
        second_reduce,
        second_head,
        second_small,
    )
    res = [adamw(w, g, m, v) for w, g, m, v in zip(params, grads, firsts, seconds)]
    return (
        loss,
        res[0][0],
        res[0][1],
        res[0][2],
        res[1][0],
        res[1][1],
        res[1][2],
        res[2][0],
        res[2][1],
        res[2][2],
        res[3][0],
        res[3][1],
        res[3][2],
        res[4][0],
        res[4][1],
        res[4][2],
        res[5][0],
        res[5][1],
        res[5][2],
        res[6][0],
        res[6][1],
        res[6][2],
    )


def solution(mesh):
    return jax.shard_map(
        on_device,
        mesh=mesh,
        in_specs=(
            P("row", "col", None),
            P(None, "row", "col"),
            P(),
            P(),
            P(None, "row"),
            P(None, "row", None),
            P(None, "row", None),
            P(None, "row", None),
            P(None, "row", None),
            P("row", None),
            P(),
            P(None, "row"),
            P(None, "row", None),
            P(None, "row", None),
            P(None, "row", None),
            P(None, "row", None),
            P("row", None),
            P(),
            P(None, "row"),
            P(None, "row", None),
            P(None, "row", None),
            P(None, "row", None),
            P(None, "row", None),
            P("row", None),
            P(),
        ),
        out_specs=(
            P(),
            P(None, "row"),
            P(None, "row"),
            P(None, "row"),
            P(None, "row", None),
            P(None, "row", None),
            P(None, "row", None),
            P(None, "row", None),
            P(None, "row", None),
            P(None, "row", None),
            P(None, "row", None),
            P(None, "row", None),
            P(None, "row", None),
            P(None, "row", None),
            P(None, "row", None),
            P(None, "row", None),
            P("row", None),
            P("row", None),
            P("row", None),
            P(),
            P(),
            P(),
        ),
        check_vma=False,
    )
```

profile of v0, /device:TPU:0, one launch (start us, length us, event | category | flops | bytes accessed | tf_op | source)
XLA Modules:
  0.0 1977.4 jit_solution(8950890407580159290)
XLA Ops:
  32.1 30.8 %all_gather.20 = bf16[2,256,256]{2,1,0:T(8,128)(2,1)S(1)} all-gather(bf16[2,32,256]{2,1,0:T(8,128)(2,1)S(1)} %convert_element_type.178), channel_id=1, replica_groups=mesh['row'=8,'col'=4] {'row'}, dimensions={1}, use_global_device_ids=true | all-gather | bytes 294912 | tf_op jit(solution)/shard_map/all_gather | solution.py:250
  63.7 33.4 %all_gather.18 = bf16[1152,256]{0,1:T(8,128)(2,1)} all-gather(bf16[1152,32]{0,1:T(8,128)(2,1)S(1)} %convert_element_type.172), channel_id=1, replica_groups=mesh['row'=8,'col'=4] {'row'}, dimensions={1}, use_global_device_ids=true | all-gather | bytes 663552 | tf_op jit(solution)/shard_map/all_gather | solution.py:248
  97.2 34.4 %all_gather.22 = bf16[2,768,256]{2,1,0:T(8,128)(2,1)} all-gather(bf16[2,96,256]{2,1,0:T(8,128)(2,1)S(1)} %convert_element_type.182), channel_id=1, replica_groups=mesh['row'=8,'col'=4] {'row'}, dimensions={1}, use_global_device_ids=true | all-gather | bytes 884736 | tf_op jit(solution)/shard_map/all_gather | solution.py:252
  131.5 34.2 %all_gather.21 = bf16[2,256,768]{2,1,0:T(8,128)(2,1)} all-gather(bf16[2,32,768]{2,1,0:T(8,128)(2,1)S(1)} %convert_element_type.180), channel_id=1, replica_groups=mesh['row'=8,'col'=4] {'row'}, dimensions={1}, use_global_device_ids=true | all-gather | bytes 884736 | tf_op jit(solution)/shard_map/all_gather | solution.py:251
  165.8 33.6 %all_gather.19 = bf16[2,256,768]{2,1,0:T(8,128)(2,1)} all-gather(bf16[2,32,768]{2,1,0:T(8,128)(2,1)S(1)} %convert_element_type.174), channel_id=1, replica_groups=mesh['row'=8,'col'=4] {'row'}, dimensions={1}, use_global_device_ids=true | all-gather | bytes 884736 | tf_op jit(solution)/shard_map/all_gather | solution.py:249
  222.6 35.4 %gather_fusion.2 = f32[18816,8]{1,0:T(8,128)} fusion(f32[8,169]{0,1:T(8,128)S(1)} %copy.172, s32[19456]{0:T(1024)S(1)} %pad_clamp_fusion.2), kind=kCustom, calls=%fused_computation.1.clone | custom fusion | bytes 1279488 | tf_op jit(solution)/shard_map/while/body/eval_jaxpr/jit(_take)/gather | solution.py:145
  310.1 53.0 %gather_fusion.1 = bf16[18816,512]{1,0:T(8,128)(2,1)} fusion(bf16[1008,512]{1,0:T(8,128)(2,1)S(1)} %reshape.1244, s32[19456]{0:T(1024)S(1)} %pad_clamp_fusion.3), kind=kCustom, calls=%fused_computation.clone | custom fusion | bytes 38610432 | tf_op jit(solution)/shard_map/while/body/eval_jaxpr/jit(_take)/gather | solution.py:136
  363.1 24.7 %reshape.1380 = bf16[384,49,512]{2,1,0:T(8,128)(2,1)} reshape(bf16[18816,512]{1,0:T(8,128)(2,1)} %gather_fusion.1) | data formatting | bytes 38535168 | tf_op jit(solution)/shard_map/while/body/eval_jaxpr/jit(_take)/gather | solution.py:136
  470.7 35.1 %all_gather.23 = bf16[256,1000]{1,0:T(8,128)(2,1)S(1)} all-gather(bf16[32,1000]{1,0:T(8,128)(2,1)S(1)} %copy-done.101), channel_id=1, replica_groups=mesh['row'=8,'col'=4] {'row'}, dimensions={0}, use_global_device_ids=true | all-gather | bytes 576000 | tf_op jit(solution)/shard_map/all_gather | solution.py:253
  513.1 35.4 %gather_fusion.4 = f32[18816,8]{1,0:T(8,128)} fusion(f32[8,169]{0,1:T(8,128)S(1)} %copy.189, s32[19456]{0:T(1024)S(1)} %copy-done.70), kind=kCustom, calls=%fused_computation.3.clone | custom fusion | bytes 1279488 | tf_op jit(solution)/shard_map/while/body/eval_jaxpr/jit(_take)/gather | solution.py:145
  566.4 53.0 %gather_fusion.3 = bf16[18816,512]{1,0:T(8,128)(2,1)} fusion(bf16[1920,512]{1,0:T(8,128)(2,1)S(1)} %bitcast.302, s32[19456]{0:T(1024)S(1)} %copy-done.71), kind=kCustom, calls=%fused_computation.2.clone | custom fusion | bytes 38610432 | tf_op jit(solution)/shard_map/while/body/eval_jaxpr/jit(_take)/gather | solution.py:136
  619.4 24.7 %reshape.1388 = bf16[384,49,512]{2,1,0:T(8,128)(2,1)} reshape(bf16[18816,512]{1,0:T(8,128)(2,1)} %gather_fusion.3) | data formatting | bytes 38535168 | tf_op jit(solution)/shard_map/while/body/eval_jaxpr/jit(_take)/gather | solution.py:136
  728.7 42.2 %all-reduce.1 = (f32[52]{0:T(128)S(1)}, f32[52,256]{1,0:T(8,128)S(1)}) all-reduce(f32[52]{0:T(128)S(1)} %copy-done.220, f32[52,256]{1,0:T(8,128)S(1)} %scatter_custom_fusion.1), channel_id=1, replica_groups=mesh['row'=8,'col'=4] {'row','col'}, use_global_device_ids=true, to_apply=%region_1.2 | all-reduce | flops 13364 | bytes 106912 | tf_op jit(solution)/shard_map/psum | solution.py:316
  814.0 28.2 %pad_maximum_fusion = f32[384,49,16,32]{0,3,2,1:T(8,128)} fusion(f32[384,49,8,32]{0,3,2,1:T(8,128)} %get-tuple-element.327, f32[384,49,8,32]{0,3,2,1:T(8,128)} %multiply_bitcast_fusion.3), kind=kLoop, calls=%fused_computation.11 | loop fusion | flops 9633792 | bytes 77070336 | tf_op jit(solution)/shard_map/while/body/eval_jaxpr/concatenate | solution.py:180
  842.2 115.4 %copy.284 = f32[384,49,16,32]{3,2,1,0:T(8,128)} copy(f32[384,49,16,32]{0,3,2,1:T(8,128)} %pad_maximum_fusion) | data formatting | bytes 77070336 | tf_op jit(solution)/shard_map/while/body/eval_jaxpr/reshape | solution.py:181
  957.6 109.8 %reshape.1415 = f32[18816,512]{1,0:T(8,128)} reshape(f32[384,49,16,32]{3,2,1,0:T(8,128)} %copy.284) | data formatting | bytes 77070336 | tf_op jit(solution)/shard_map/while/body/eval_jaxpr/reshape | solution.py:181
  1067.4 114.1 %scatter_custom_fusion.2 = f32[1920,512]{1,0:T(8,128)} fusion(s32[18816]{0:T(1024)} %fusion.48, f32[18816,512]{1,0:T(8,128)} %reshape.1415, f32[]{:T(128)} %constant.605.clone.1), kind=kCustom, calls=%fused_computation.28 | custom fusion | flops 9633792 | bytes 3932672 | tf_op jit(solution)/shard_map/while/body/eval_jaxpr/scatter-add | solution.py:181
  1270.6 28.2 %pad_maximum_fusion.1 = f32[384,49,16,32]{0,3,2,1:T(8,128)} fusion(f32[384,49,8,32]{0,3,2,1:T(8,128)} %get-tuple-element.325, f32[384,49,8,32]{0,3,2,1:T(8,128)} %multiply_bitcast_fusion.1), kind=kLoop, calls=%fused_computation.12 | loop fusion | flops 9633792 | bytes 77070336 | tf_op jit(solution)/shard_map/while/body/eval_jaxpr/concatenate | solution.py:180
  1298.8 115.4 %copy.288 = f32[384,49,16,32]{3,2,1,0:T(8,128)} copy(f32[384,49,16,32]{0,3,2,1:T(8,128)} %pad_maximum_fusion.1) | data formatting | bytes 77070336 | tf_op jit(solution)/shard_map/while/body/eval_jaxpr/reshape | solution.py:181
  1414.2 109.7 %reshape.1416 = f32[18816,512]{1,0:T(8,128)} reshape(f32[384,49,16,32]{3,2,1,0:T(8,128)} %copy.288) | data formatting | bytes 77070336 | tf_op jit(solution)/shard_map/while/body/eval_jaxpr/reshape | solution.py:181
  1523.9 112.5 %scatter_custom_fusion.3 = f32[1008,512]{1,0:T(8,128)S(1)} fusion(s32[18816]{0:T(1024)} %fusion.49, f32[18816,512]{1,0:T(8,128)} %reshape.1416, f32[]{:T(128)} %constant.605.clone.1), kind=kCustom, calls=%fused_computation.110 | custom fusion | flops 9633792 | bytes 2064896 | tf_op jit(solution)/shard_map/while/body/eval_jaxpr/scatter-add | solution.py:181
  1696.2 101.8 %scatter_custom_fusion.5 = f32[169,8]{1,0:T(8,128)S(1)} fusion(s32[18816]{0:T(1024)} %reshape.1359, f32[18816,8]{1,0:T(8,128)} %copy.216, f32[]{:T(128)} %constant.605.clone.1), kind=kCustom, calls=%fused_computation.254 | custom fusion | flops 150528 | bytes 5920 | tf_op jit(solution)/shard_map/while/body/eval_jaxpr/scatter-add | solution.py:182
  1813.5 101.6 %scatter_custom_fusion.4 = f32[169,8]{1,0:T(8,128)S(1)} fusion(s32[18816]{0:T(1024)} %reshape.1351, f32[18816,8]{1,0:T(8,128)} %copy.215, f32[]{:T(128)} %constant.605.clone.1), kind=kCustom, calls=%fused_computation.256 | custom fusion | flops 150528 | bytes 5920 | tf_op jit(solution)/shard_map/while/body/eval_jaxpr/scatter-add | solution.py:182
  1915.5 43.9 %all-reduce = (f32[4608]{0:T(1024)S(1)}, f32[2704]{0:T(1024)S(1)}) all-reduce(f32[4608]{0:T(1024)S(1)} %pad_maximum_fusion.17, f32[2704]{0:T(1024)S(1)} %reshape.1276), channel_id=1, replica_groups=mesh['row'=8,'col'=4] {'row','col'}, use_global_device_ids=true, to_apply=%region_60.64 | all-reduce | flops 7312 | bytes 58496 | tf_op jit(solution)/shard_map/psum | solution.py:388
  (827 shorter events, 506.3 us)
Async XLA Ops:
  7.2 1953.0 %all-reduce.5.cloned.1.call-start = ((), (), s32[]{:S(2)}) async-start(), calls=%async_computation | async-start | bytes 12845056 | tf_op jit(solution)/shard_map/psum | solution.py:392
  8.5 197.7 %collective-permute-start = (bf16[1,32,128]{2,1,0:T(8,128)(2,1)}, bf16[1,32,128]{2,1,0:T(8,128)(2,1)}, u32[]{:S(2)}, u32[]{:S(2)}) collective-permute-start(bf16[1,32,128]{2,1,0:T(8,128)(2,1)} %slice.505), channel_id=1, source_target_pairs={{0,4},{4,8},{8,12},{12,16},{16,20},{20,24},{24,28},{1,5},{5,9},{9,... | collective-permute-start | bytes 24584 | tf_op jit(solution)/shard_map/ppermute | solution.py:38
  32.0 425.8 %copy-start.133 = (f32[1,1,256]{2,1,0:T(1,128)}, f32[1,1,256]{2,1,0:T(1,128)S(1)}, u32[]{:S(2)}) copy-start(f32[1,1,256]{2,1,0:T(1,128)S(1)} %get-tuple-element.353) | copy-start | bytes 3076
  32.0 425.8 %copy-start.148 = (f32[1,1,256]{2,1,0:T(1,128)}, f32[1,1,256]{2,1,0:T(1,128)S(1)}, u32[]{:S(2)}) copy-start(f32[1,1,256]{2,1,0:T(1,128)S(1)} %get-tuple-element.352) | copy-start | bytes 3076
  32.0 426.8 %copy-start.160 = (f32[1,1,256]{2,1,0:T(1,128)}, f32[1,1,256]{2,1,0:T(1,128)S(1)}, u32[]{:S(2)}) copy-start(f32[1,1,256]{2,1,0:T(1,128)S(1)} %get-tuple-element.349) | copy-start | bytes 3076
  32.0 431.6 %copy-start.166 = (f32[1,1,256]{2,1,0:T(1,128)}, f32[1,1,256]{2,1,0:T(1,128)S(1)}, u32[]{:S(2)}) copy-start(f32[1,1,256]{2,1,0:T(1,128)S(1)} %get-tuple-element.347) | copy-start | bytes 3076
  207.0 73.7 %collective-permute-start.1 = (bf16[49,1,128]{2,1,0:T(2,128)(2,1)S(1)}, bf16[49,1,128]{2,1,0:T(2,128)(2,1)}, u32[]{:S(2)}, u32[]{:S(2)}) collective-permute-start(bf16[49,1,128]{2,1,0:T(2,128)(2,1)S(1)} %slice.598), channel_id=1, source_target_pairs={{0,1},{1,2},{2,3},{4,5},{5,6},{6,7},{8,9},{9,10},{10,11},{12,13},{... | collective-permute-start | bytes 37640 | tf_op jit(solution)/shard_map/ppermute | solution.py:38
  291.1 7.4 collective-permute-start.3
  292.4 7.7 collective-permute-start.2
  300.2 3.9 collective-permute-start.4
  302.6 3.5 collective-permute-start.5
  463.5 252.9 %copy-start.11 = (f32[384,256]{0,1:T(8,128)}, f32[384,256]{0,1:T(8,128)S(1)}, u32[]{:S(2)}) copy-start(f32[384,256]{0,1:T(8,128)S(1)} %get-tuple-element.368) | copy-start | bytes 1179652
  465.2 40.9 %collective-permute-start.6 = (bf16[12,16,512]{2,0,1:T(8,128)(2,1)S(1)}, bf16[12,16,512]{2,0,1:T(8,128)(2,1)S(1)}, u32[]{:S(2)}, u32[]{:S(2)}) collective-permute-start(bf16[12,16,512]{2,0,1:T(8,128)(2,1)S(1)} %copy.180), channel_id=1, source_target_pairs={{0,4},{4,8},{8,12},{12,16},{16,20},{20,24},{24,28},{1,5},{5,9},{9,... | collective-permute-start | bytes 589832 | tf_op jit(solution)/shard_map/ppermute | solution.py:27
  469.4 36.6 %collective-permute-start.7 = (bf16[12,16,512]{2,0,1:T(8,128)(2,1)S(1)}, bf16[12,16,512]{2,0,1:T(8,128)(2,1)S(1)}, u32[]{:S(2)}, u32[]{:S(2)}) collective-permute-start(bf16[12,16,512]{2,0,1:T(8,128)(2,1)S(1)} %copy.181), channel_id=1, source_target_pairs={{4,0},{8,4},{12,8},{16,12},{20,16},{24,20},{28,24},{5,1},{9,5},{13... | collective-permute-start | bytes 589832 | tf_op jit(solution)/shard_map/ppermute | solution.py:30
  507.6 56.1 %collective-permute-start.8 = (bf16[48,12,512]{2,0,1:T(8,128)(2,1)}, bf16[48,12,512]{2,0,1:T(8,128)(2,1)}, u32[]{:S(2)}, u32[]{:S(2)}) collective-permute-start(bf16[48,12,512]{2,0,1:T(8,128)(2,1)} %get-tuple-element.316), channel_id=1, source_target_pairs={{0,1},{1,2},{2,3},{4,5},{5,6},{6,7},{8,9},{9,10},{10,11},{12,13},{... | collective-permute-start | bytes 1769480 | tf_op jit(solution)/shard_map/ppermute | solution.py:27
  509.7 54.0 %collective-permute-start.9 = (bf16[48,12,512]{2,0,1:T(8,128)(2,1)}, bf16[48,12,512]{2,0,1:T(8,128)(2,1)}, u32[]{:S(2)}, u32[]{:S(2)}) collective-permute-start(bf16[48,12,512]{2,0,1:T(8,128)(2,1)} %get-tuple-element.317), channel_id=1, source_target_pairs={{1,0},{2,1},{3,2},{5,4},{6,5},{7,6},{9,8},{10,9},{11,10},{13,12},{... | collective-permute-start | bytes 1769480 | tf_op jit(solution)/shard_map/ppermute | solution.py:30
  1184.0 13.1 collective-permute-start.10
  1194.0 13.6 collective-permute-start.11
  1208.9 6.8 collective-permute-start.12
  1212.3 9.9 collective-permute-start.13
  1637.9 13.6 collective-permute-start.14
  1648.6 9.0 collective-permute-start.15
  1657.8 5.5 collective-permute-start.16
  1662.0 5.3 collective-permute-start.17
  (227 other events, 6739.1 us)
Sparse Core Ops, SparseCore 0:
  1676.7 162.8 all-reduce.4
where the time goes:
time: 1990 us; the launch traced here: 1980 us
  local copies, waits for them, and re-layouts  888 us (45%)
  other arithmetic  679 us (34%)
  blocking collectives  288 us (14%)
  starting transfers between devices  46.5 us (2%)
  matrix products  33.9 us (2%)
  waiting for transfers between devices  21.7 us (1%)
  between operations  20.5 us (1%)
    reshape x4, local copies, waits for them, and re-layouts, one_block(): dflat = dflat.at[keys_b.reshape(-1)].add(dnear.reshape(-1, 2 * D))  450 us
    scatter-add x2, other arithmetic, one_block(): dflat = dflat.at[keys_b.reshape(-1)].add(dnear.reshape(-1, 2 * D))  227 us
    scatter-add x2, other arithmetic, one_block(): jax.ops.segment_sum(dscore.transpose(0, 2, 1).reshape(-1, dscore.shape[1]...  203 us
    gather x4, local copies, waits for them, and re-layouts, window_scores(): near = jnp.take(flat, keys, axis=0)  155 us
    gather x6, local copies, waits for them, and re-layouts, window_scores(): jnp.take(bias, table, axis=1).transpose(1, 0, 2)  88.2 us
    unnamed x467, local copies, waits for them, and re-layouts  78.7 us
    concatenate x2, other arithmetic, one_block(): dnear = jnp.concatenate([dkey, dvalue], 2)  56.4 us
    unnamed x19, other arithmetic  46.1 us
  transfers between devices with their start and end apart: 19, of which 5 were waited for; matrix products, arithmetic and copies ran while one was open for 21% of the time, Pallas kernels for 0%

commit v1 on v0

v1 whole, which is shorter than its diff:
```python
import functools

import jax
import jax.numpy as jnp
from jax import lax
from jax.experimental import pallas as pl
from jax.experimental.pallas import tpu as pltpu
from jax.sharding import PartitionSpec as P

D = 256
HEADS = 8
FF = 768
CLASSES = 1000
LAYERS = 2
STEP = 5
WIN = 176

eps_norm = 1e-05
beta_one = 0.9
beta_two = 0.999
learn_rate = 0.2
decay_rate = 0.05
eps_adam = 1e-08
scale = (D // HEADS) ** -0.5

bf16 = jnp.bfloat16
f32 = jnp.float32
i32 = jnp.int32
MASKED = -1e30
VMEM = 56 * 1024 * 1024


def nn(a, b):
    return lax.dot_general(a, b, (((1,), (0,)), ((), ())), preferred_element_type=f32)


def nt(a, b):
    return lax.dot_general(a, b, (((1,), (1,)), ((), ())), preferred_element_type=f32)


def tn(a, b):
    return lax.dot_general(a, b, (((0,), (0,)), ((), ())), preferred_element_type=f32)


def two_parts(x):
    high = x.astype(bf16)
    return high, (x - high.astype(f32)).astype(bf16)


def norm_parts(x):
    centre = x - jnp.mean(x, -1, keepdims=True)
    rstd = lax.rsqrt(jnp.mean(centre * centre, -1, keepdims=True) + eps_norm)
    return centre * rstd, rstd


def norm(x, gain_bias):
    return norm_parts(x)[0] * gain_bias[0:1] + gain_bias[1:2]


def norm_back(x, gain_bias, dy):
    xhat, rstd = norm_parts(x)
    dxhat = dy * gain_bias[0:1]
    dx = rstd * (
        dxhat
        - jnp.mean(dxhat, -1, keepdims=True)
        - xhat * jnp.mean(dxhat * xhat, -1, keepdims=True)
    )
    return dx, jnp.sum(dy * xhat, 0, keepdims=True), jnp.sum(dy, 0, keepdims=True)


def normal_cdf(u):
    return 0.5 * (1.0 + lax.erf(u * 0.7071067811865476))


def join(ref, first, count):
    rows = ref.shape[1] // 3
    wide = [
        ref[:, k * rows : (k + 1) * rows, :].reshape(D, ref.shape[2])
        for k in range(first, first + count)
    ]
    return wide[0] if count == 1 else jnp.concatenate(wide, 1)


class One:
    dilation, queries, across, pieces, steps = 1, 64, 16, 4, 6
    keys = pieces * 128

    @staticmethod
    def key_col(piece, c8):
        two = 2 * (c8 & 3) + (c8 >> 2)
        return jnp.where(
            piece == 0,
            2 * c8,
            jnp.where(piece == 1, 2 * c8 + 1, jnp.where(piece == 2, two - 8, two + 16)),
        )

    @staticmethod
    def query_col(index):
        return 2 * (index & 7) + (index >> 3)


class Two:
    dilation, queries, across, pieces, steps = 2, 32, 8, 3, 12
    keys = pieces * 128

    @staticmethod
    def key_col(piece, c8):
        return jnp.where(piece == 0, c8, jnp.where(piece == 1, c8 - 8, c8 + 8))

    @staticmethod
    def query_col(index):
        return index


def key_place(geo):
    lane = lax.broadcasted_iota(i32, (1, geo.keys), 1)
    return (lane >> 3) & 15, geo.key_col(lane >> 7, lane & 7)


def window_mask(geo, lay, step, row_first, col_first):
    token = lax.broadcasted_iota(i32, (geo.queries, 1), 0)
    if geo.dilation == 1:
        block = step
        row = block * 4 + (token >> 4)
        col = geo.query_col(token & 15)
        row_pos, col_pos = row_first + row, col_first + col
    else:
        group = step // 3
        block = step - 3 * group
        row = block * 4 + (token >> 3)
        col = token & 7
        row_pos = row_first + 2 * row + (group >> 1)
        col_pos = col_first + 2 * col + (group & 1)

    def begin(place, first, end):
        local = place - first
        extent = end - first
        if geo.dilation == 1:
            index, length = local, extent
        else:
            index, length = local >> 1, (extent - (local & 1) + 1) >> 1
        return jnp.minimum(jnp.maximum(index - 3, 0), length - 7) - index

    row_start = row + begin(row_pos, lay[:, 0:1], lay[:, 1:2])
    col_start = col + begin(col_pos, lay[:, 2:3], lay[:, 3:4])
    key_row, key_col = key_place(geo)
    down = key_row + (block * 4 - 6) - row_start
    right = key_col - col_start
    inside = (down >= 0) & (down <= 6) & (right >= 0) & (right <= 6)
    return jnp.where(inside, 0.0, MASKED).astype(f32)


def position_onehot(geo, across):
    key_row, key_col = key_place(geo)
    right = key_col - geo.query_col(across) + 6
    index = jnp.where((right >= 0) & (right <= 12) & (key_row <= 12), key_row * 13 + right, -1)
    entry = lax.broadcasted_iota(i32, (WIN, geo.keys), 0)
    return jnp.where(entry == index, 1.0, 0.0).astype(bf16)


def position_table(geo, bias, first_ref):
    high = bias.astype(bf16)
    rest = bias - high.astype(f32)
    mid = rest.astype(bf16)
    low = (rest - mid.astype(f32)).astype(bf16)
    for across in range(geo.across):
        onehot = position_onehot(geo, across)
        row = nn(high, onehot) + nn(mid, onehot) + nn(low, onehot)
        for piece in range(geo.pieces):
            lanes = slice(piece * 128, piece * 128 + 128)
            first_ref[piece, pl.ds(across, HEADS, stride=geo.across), :] = row[:, lanes]


def spread_table(geo, first_ref, table_ref):
    for head in range(HEADS):
        for row in range(4):
            for piece in range(geo.pieces):
                lanes = slice(piece * 128, piece * 128 + 128)
                value = first_ref[piece, head * geo.across : (head + 1) * geo.across, :]
                if row:
                    value = pltpu.roll(value, 8 * row, 1)
                begin = head * geo.queries + row * geo.across
                table_ref[begin : begin + geo.across, lanes] = value


def gather_table(geo, table_ref, first_ref):
    for head in range(HEADS):
        for piece in range(geo.pieces):
            lanes = slice(piece * 128, piece * 128 + 128)
            total = None
            for row in range(4):
                begin = head * geo.queries + row * geo.across
                value = table_ref[begin : begin + geo.across, lanes]
                if row:
                    value = pltpu.roll(value, 128 - 8 * row, 1)
                total = value if total is None else total + value
            first_ref[piece, head * geo.across : (head + 1) * geo.across, :] = total
    grad = jnp.zeros((HEADS, WIN), f32)
    for across in range(geo.across):
        onehot = position_onehot(geo, across)
        rows = pl.ds(across, HEADS, stride=geo.across)
        first = [first_ref[piece, rows, :] for piece in range(geo.pieces)]
        high, low = two_parts(jnp.concatenate(first, 1))
        grad = grad + nt(high, onehot) + nt(low, onehot)
    return grad


def head_lanes(head):
    lane = lax.broadcasted_iota(i32, (1, D), 1)
    return jnp.where((lane >> 5) == head, 1.0, 0.0)


def by_head(x):
    return jnp.concatenate([x * head_lanes(h).astype(x.dtype) for h in range(HEADS)], 0)


def from_heads(x):
    count = x.shape[0] // HEADS
    total = None
    for h in range(HEADS):
        part = x[h * count : (h + 1) * count] * head_lanes(h)
        total = part if total is None else total + part
    return total


def key_rows(geo, step):
    if geo.dilation == 1:
        return None, pl.multiple_of(step * 32, 32)
    group = step // 3
    return group, pl.multiple_of((step - 3 * group) * 32, 32)


def load_keys(geo, pieces, step, lanes):
    group, first = key_rows(geo, step)
    if geo.dilation == 1:
        parts = [pieces[p, pl.ds(first, 128), lanes] for p in range(4)]
    else:
        parts = [pieces[p, group, pl.ds(first, 128), lanes] for p in range(3)]
    return jnp.concatenate(parts, 0)


def add_keys(geo, pieces, step, lanes, value):
    group, first = key_rows(geo, step)
    for p in range(geo.pieces):
        part = value[p * 128 : (p + 1) * 128]
        if geo.dilation == 1:
            pieces[p, pl.ds(first, 128), lanes] += part
        else:
            pieces[p, group, pl.ds(first, 128), lanes] += part


KEY = slice(0, D)
VALUE = slice(D, 2 * D)


def softmax_rows(score, table, mask):
    score = score * scale + (table + mask)
    top = jnp.max(score, -1, keepdims=True)
    weight = jnp.exp(score - top)
    return weight * (1.0 / jnp.sum(weight, -1, keepdims=True))


def attend(geo, place, lay_ref, query_ref, pieces, table_ref, out_ref, score_ref, prob_ref):
    count = geo.queries

    def step_of(step, carry):
        rows = pl.ds(pl.multiple_of(step * count, count), count)
        mask = window_mask(geo, lay_ref[rows, :], step, place[0], place[1])
        wide = by_head(query_ref[rows, :])
        score_ref[...] = nt(wide, load_keys(geo, pieces, step, KEY))
        for h in range(HEADS):
            span = slice(h * count, (h + 1) * count)
            prob = softmax_rows(score_ref[span, :], table_ref[span, :], mask)
            prob_ref[span, :] = prob.astype(bf16)
        out = nn(prob_ref[...], load_keys(geo, pieces, step, VALUE))
        out_ref[rows, :] = from_heads(out).astype(out_ref.dtype)
        return carry

    lax.fori_loop(0, geo.steps, step_of, 0)


def attend_back(
    geo, place, lay_ref, query_ref, dout_ref, pieces, table_ref, dquery_ref, dpieces, dtable_ref,
    score_ref, dprob_ref, prob_ref, dscore_ref,
):
    count = geo.queries
    dtable_ref[...] = jnp.zeros_like(dtable_ref)
    dpieces[...] = jnp.zeros_like(dpieces)

    def step_of(step, carry):
        rows = pl.ds(pl.multiple_of(step * count, count), count)
        mask = window_mask(geo, lay_ref[rows, :], step, place[0], place[1])
        wide = by_head(query_ref[rows, :])
        dwide = by_head(dout_ref[rows, :])
        keys = load_keys(geo, pieces, step, KEY)
        score_ref[...] = nt(wide, keys)
        dprob_ref[...] = nt(dwide, load_keys(geo, pieces, step, VALUE))
        for h in range(HEADS):
            span = slice(h * count, (h + 1) * count)
            prob = softmax_rows(score_ref[span, :], table_ref[span, :], mask)
            prob_ref[span, :] = prob.astype(bf16)
            dprob = dprob_ref[span, :]
            dscore = prob * (dprob - jnp.sum(prob * dprob, -1, keepdims=True))
            dtable_ref[span, :] += dscore
            dscore_ref[span, :] = dscore.astype(bf16)
        dscore = dscore_ref[...]
        add_keys(geo, dpieces, step, VALUE, tn(prob_ref[...], dwide))
        add_keys(geo, dpieces, step, KEY, tn(dscore, wide) * scale)
        dquery_ref[rows, :] = from_heads(nn(dscore, keys)) * scale
        return carry

    lax.fori_loop(0, geo.steps, step_of, 0)


def grouped(x):
    parts = x.reshape(12, 2, 2, 8, x.shape[-1])
    return [parts[:, g >> 1, g & 1].reshape(96, x.shape[-1]) for g in range(4)]


def run(kernel, outs, ins, scratch=(), specs=None, flops=0):
    in_specs = [pl.BlockSpec(memory_space=pltpu.VMEM)] * len(ins)
    for index, spec in (specs or {}).items():
        in_specs[index] = spec
    return pl.pallas_call(
        kernel,
        out_shape=outs,
        in_specs=in_specs,
        out_specs=[pl.BlockSpec(memory_space=pltpu.VMEM)] * len(outs),
        scratch_shapes=list(scratch),
        compiler_params=pltpu.CompilerParams(vmem_limit_bytes=VMEM),
        cost_estimate=pl.CostEstimate(flops=flops, bytes_accessed=4 << 20, transcendentals=0),
    )(*ins)


SMEM = pl.BlockSpec(memory_space=pltpu.SMEM)


def out(shape, dtype=f32):
    return jax.ShapeDtypeStruct(shape, dtype)


def pack_kernel(conv, qkv, proj, exp, red, head, early, late):
    sh = qkv.shape[1]
    for tap in range(9):
        early[tap * sh : (tap + 1) * sh, :] = conv[tap * 128 : (tap + 1) * 128, :].T.astype(bf16)
    for k in range(6):
        begin = (9 + k) * sh
        early[begin : begin + sh, :] = qkv[0, :, k * 128 : (k + 1) * 128].astype(bf16)

    def put(slot, value):
        late[slot * sh : slot * sh + value.shape[0], :] = value.astype(bf16)

    for k in range(3):
        cols = slice(k * D, (k + 1) * D)
        put(k, qkv[1, :, cols])
        put(3 + k, exp[0, :, cols])
        put(6 + k, exp[1, :, cols])
    put(9, red[0])
    put(12, red[1])
    put(15, proj[0])
    put(16, proj[1])
    for k in range(3):
        put(17 + k, head[:, k * D : (k + 1) * D])
    tail = head[:, 3 * D :]
    put(20, jnp.concatenate([tail, jnp.zeros((sh, 4 * D - CLASSES), f32)], 1))


def table_kernel(bias, first_one, first_two):
    position_table(One, bias[0:8, :], first_one)
    position_table(Two, bias[8:16, :], first_two)


def front_kernel(
    place, stem, above, left, lay, early, norms,
    patches, conv_out, hidden, query, keyval, edges,
    stem_f, above_f,
):
    nr, sh = early.shape[0], early.shape[1] // 15
    stem_f[...] = stem[...].astype(f32)
    above_f[...] = above[...].astype(f32)
    left_f = left[...].astype(f32)
    tiles = left_f[:384].reshape(24, 2, 8, 128)
    left_odd = tiles[:, 0]
    beside = [left_odd, tiles[:, 1], jnp.concatenate([left_odd[1:], left_f[384:392][None]], 0)]
    phases = []
    for m in range(4):
        part = stem_f[pl.ds(m, 384, stride=4), :].reshape(24, 2, 8, 128)
        even, odd = part[:, 0], part[:, 1]
        top = above_f[pl.ds(m, 8, stride=4), :]
        phases.append([jnp.concatenate([top[None], odd[:-1]], 0), even, odd])
    token = lax.broadcasted_iota(i32, (384, 1), 0)
    row_pos = place[0] + (token >> 4)
    col_pos = place[1] + One.query_col(token & 15)
    inner_row = jnp.where(row_pos == lay[:, 0:1], 0.0, 1.0)
    inner_col = jnp.where(col_pos == lay[:, 2:3], 0.0, 1.0)
    half = lax.broadcasted_iota(i32, (24, 8, 128), 1)
    for a in range(3):
        last = phases[3][a].reshape(192, 128)
        shifted = pltpu.roll(last.reshape(24, 8, 128), 1, 1)
        shifted = jnp.where(half == 0, beside[a], shifted)
        taps = (
            (shifted, phases[1][a]),
            (phases[0][a], phases[2][a]),
            (phases[1][a], phases[3][a]),
        )
        for b in range(3):
            value = jnp.stack(taps[b], 1).reshape(384, 128)
            if a == 0:
                value = value * inner_row
            if b == 0:
                value = value * inner_col
            lanes = slice((3 * a + b) * 128, (3 * a + b + 1) * 128)
            patches[:, lanes] = value.astype(bf16)
    wide = [early[:, k * sh : (k + 1) * sh, :].reshape(D, 128) for k in range(15)]
    conv = nt(patches[...], jnp.concatenate(wide[:9], 1))
    conv_out[...] = conv
    h = norm(conv, norms[0:2, :])
    hidden[...] = h
    low = norm(h, norms[2:4, :]).astype(bf16)
    mixed = nn(low, jnp.concatenate(wide[9:], 1))
    query[...] = mixed[:, :D].astype(bf16)
    both = mixed[:, D:].reshape(24, 2, 8, 2 * D)
    zero, one = both[:, 0], both[:, 1]
    keyval[0] = zero.reshape(192, 2 * D).astype(bf16)
    keyval[1] = one.reshape(192, 2 * D).astype(bf16)
    sub = lax.broadcasted_iota(i32, zero.shape, 1)
    edge_left = jnp.where(sub < 4, zero, pltpu.roll(one, 4, 1))
    edge_right = jnp.where(sub < 4, pltpu.roll(zero, 4, 1), one)
    edges[0] = edge_left.reshape(192, 2 * D).astype(bf16)
    edges[1] = edge_right.reshape(192, 2 * D).astype(bf16)


def gather_keys_one(keyval, left, right, above, below, pieces):
    for p in range(4):
        own = keyval[p] if p < 2 else (left, right)[p - 2][...]
        pieces[p, 0:48, :] = above[p]
        pieces[p, 48:240, :] = own
        pieces[p, 240:288, :] = below[p]


def feed_forward(hidden, norms, w_exp, w_red, bias):
    low = norm(hidden, norms).astype(bf16)
    upper = nn(low, w_exp) + bias
    gelu = upper * normal_cdf(upper)
    return hidden + nn(gelu.astype(bf16), w_red)


def fetch(late, slots, buffers, sems):
    rows = buffers.shape[2]
    takers = []
    for n, slot in enumerate(slots):
        copy = pltpu.make_async_copy(
            late.at[:, pl.ds(slot * rows, rows), :], buffers.at[n], sems.at[n]
        )
        copy.start()

        def take(copy=copy, n=n):
            copy.wait()
            return buffers.at[n]

        takers.append(take)
    return takers


QKV_TWO, EXP_ONE, EXP_TWO, RED_ONE, RED_TWO, PROJ, HEAD = range(7)


def first_block_kernel(
    place, lay, hidden, query, keyval, left, right, above, below, first_table, late, norms, ebias,
    att, middle, last, query2, keyval2,
    pieces, table, score, prob, buffers, sems,
):
    w_proj, w_exp, w_red, w_qkv = fetch(late, (PROJ, EXP_ONE, RED_ONE, QKV_TWO), buffers, sems)
    gather_keys_one(keyval, left, right, above, below, pieces)
    spread_table(One, first_table, table)
    attend(One, place, lay, query, pieces, table, att, score, prob)
    mid = hidden[...] + nn(att[...], join(w_proj(), 0, 1))
    middle[...] = mid
    end = feed_forward(mid, norms[4:6, :], join(w_exp(), 0, 3), red_of(w_red()), ebias[0:1, :])
    last[...] = end
    low = norm(end, norms[6:8, :]).astype(bf16)
    mixed = nn(low, join(w_qkv(), 0, 3))
    for g, part in enumerate(grouped(mixed)):
        query2[g * 96 : (g + 1) * 96, :] = part[:, :D].astype(bf16)
        keyval2[g] = part[:, D:].astype(bf16)


def red_of(ref):
    return ref[...].reshape(FF, D)


def slot_onehot(slots, images):
    entry = lax.broadcasted_iota(i32, (384, images), 1)
    return jnp.where(slots[:, 4:5] == entry, 1.0, 0.0).astype(bf16)


def ungroup(value, ref):
    for g in range(4):
        ref[:, g >> 1, g & 1] = value[g * 96 : (g + 1) * 96].reshape(12, 8, value.shape[-1])


def second_block_kernel(
    place, lay, slots, hidden, query, own, left, right, first_table, late, norms, ebias,
    att, middle, last, sums,
    pieces, table, score, prob, att_group, att_token, buffers, sems,
):
    w_proj, w_exp, w_red = fetch(late, (PROJ, EXP_TWO, RED_TWO), buffers, sems)
    pieces[0] = own[...]
    pieces[1] = left[...]
    pieces[2] = right[...]
    spread_table(Two, first_table, table)
    attend(Two, place, lay, query, pieces, table, att_group, score, prob)
    ungroup(att_group[...], att_token)
    low = att_token[...].reshape(384, D).astype(bf16)
    att[...] = low
    mid = hidden[...] + nn(low, join(w_proj(), 1, 1))
    middle[...] = mid
    end = feed_forward(mid, norms[8:10, :], join(w_exp(), 0, 3), red_of(w_red()), ebias[1:2, :])
    last[...] = end
    final = norm(end, norms[10:12, :])
    where = slot_onehot(slots, sums.shape[0])
    high, low = two_parts(final)
    sums[:, :D] = tn(where, high) + tn(where, low)
    sums[:, D:] = tn(where, jnp.ones((384, 128), bf16))


def feed_forward_back(dhid, mid, gain_bias, w_exp, w_red, bias):
    low = norm(mid, gain_bias).astype(bf16)
    upper = nn(low, w_exp) + bias
    cdf = normal_cdf(upper)
    dz = dhid.astype(bf16)
    grad_red = tn((upper * cdf).astype(bf16), dz)
    slope = cdf + upper * (jnp.exp(-0.5 * upper * upper) * 0.3989422804014327)
    dupper = (nt(dz, w_red) * slope).astype(bf16)
    grad_bias = jnp.sum(dupper.astype(f32), 0, keepdims=True)
    grad_exp = tn(low, dupper)
    dx, dgain, dbias = norm_back(mid, gain_bias, nt(dupper, w_exp))
    return dhid + dx, grad_red, grad_exp, grad_bias, dgain, dbias


def put_cols(grads, first, value):
    devices, width = grads.shape[0], grads.shape[2]
    share = D // devices
    for k in range(value.shape[1] // width):
        part = value[:, k * width : (k + 1) * width].reshape(devices, share, width)
        grads[:, (first + k) * share : (first + k + 1) * share, :] = part.astype(bf16)


def put_red(grads, first, value):
    devices = grads.shape[0]
    share = D // devices
    part = value.reshape(devices, 3 * share, D)
    grads[:, first * share : (first + 3) * share, :] = part.astype(bf16)


def second_back_kernel(
    place, lay, slots, sums, labels, live, hbias, hidden, middle, att, query, own, left, right,
    first_table, late, norms, ebias,
    loss, grad_head, grad_hbias, dhidden, grads, dnorms, debias, dpos, dquery, down, dleft, dright,
    pieces, table, dtable, score, dscore_f, prob, dscore, dpieces, datt, dq_group, dfirst, dq_token, buffers, sems,
):
    w_p, w_h, w_red, w_exp = fetch(late, (PROJ, HEAD, RED_TWO, EXP_TWO), buffers, sems)
    pieces[0] = own[...]
    pieces[1] = left[...]
    pieces[2] = right[...]
    spread_table(Two, first_table, table)
    total, area = sums[:, :D], sums[:, D : D + 1]
    spread_area = jnp.maximum(area, 1.0)
    pooled = (total / spread_area).astype(bf16)
    proj_ref, head_ref = w_p(), w_h()
    w_head = jnp.concatenate([join(proj_ref, 2, 1), join(head_ref, 0, 3)], 1)
    logits = nn(pooled, w_head) + hbias[...]
    weight = live[...] * jnp.where(area > 0.5, 1.0, 0.0)
    count = jnp.maximum(jnp.sum(weight, 0, keepdims=True), 1.0)
    cls = lax.broadcasted_iota(i32, logits.shape, 1)
    onehot = jnp.where(cls == labels[...], 1.0, 0.0)
    top = jnp.max(logits, -1, keepdims=True)
    logsum = jnp.log(jnp.sum(jnp.exp(logits - top), -1, keepdims=True)) + top
    cross = logsum - jnp.sum(onehot * logits, -1, keepdims=True)
    loss[...] = jnp.broadcast_to(jnp.sum(weight * cross, 0, keepdims=True) / count, loss.shape)
    dlogit = ((weight / count) * (jnp.exp(logits - logsum) - onehot)).astype(bf16)
    grad_hbias[...] = jnp.sum(dlogit.astype(f32), 0, keepdims=True)
    share = grad_head.shape[0]
    channel = lax.broadcasted_iota(i32, (D, share), 0)
    mine = lax.broadcasted_iota(i32, (D, share), 1) + place[2]
    own_pooled = nn(pooled, jnp.where(channel == mine, 1.0, 0.0).astype(bf16)).astype(bf16)
    grad_head[...] = tn(own_pooled, dlogit)
    high, low = two_parts(nt(dlogit, w_head) / spread_area)
    where = slot_onehot(slots, sums.shape[0])
    dfinal = nn(where, high) + nn(where, low)
    dhid, dgain, dbias = norm_back(hidden[...], norms[10:12, :], dfinal)
    dnorms[2:3, :] = dgain
    dnorms[3:4, :] = dbias
    dhid, grad_red, grad_exp, grad_bias, dgain, dbias = feed_forward_back(
        dhid, middle[...], norms[8:10, :], join(w_exp(), 0, 3), red_of(w_red()), ebias[1:2, :]
    )
    put_cols(grads, 0, grad_exp)
    put_red(grads, 3, grad_red)
    debias[...] = grad_bias
    dnorms[0:1, :] = dgain
    dnorms[1:2, :] = dbias
    dhidden[...] = dhid
    dy = dhid.astype(bf16)
    put_cols(grads, 6, tn(att[...], dy))
    back = nt(dy, join(proj_ref, 1, 1))
    for g, part in enumerate(grouped(back)):
        datt[g * 96 : (g + 1) * 96, :] = part.astype(bf16)
    attend_back(
        Two, place, lay, query, datt, pieces, table, dq_group, dpieces, dtable,
        score, dscore_f, prob, dscore,
    )
    ungroup(dq_group[...], dq_token)
    dquery[...] = dq_token[...].reshape(384, D).astype(bf16)
    down[...] = dpieces[0]
    dleft[...] = dpieces[1].astype(bf16)
    dright[...] = dpieces[2].astype(bf16)
    dpos[...] = gather_table(Two, dtable, dfirst)


def first_back_kernel(
    place, lay, dhid_in, dquery2, dkv, from_above, from_below, hidden, middle, att, query, keyval,
    left, right, above, below, first_table, late, norms, ebias,
    dhidden, grads, dnorms, debias, dpos, dquery, inner, up, down,
    pieces, table, dtable, score, dscore_f, prob, dscore, dpieces, datt, dq, dfirst, dkv_token, buffers, sems,
):
    w_qkv, w_red, w_exp, w_proj = fetch(late, (QKV_TWO, RED_ONE, EXP_ONE, PROJ), buffers, sems)
    gather_keys_one(keyval, left, right, above, below, pieces)
    spread_table(One, first_table, table)
    for g in range(4):
        top = dkv[g, 0:48, :] + from_above[g].astype(f32)
        bottom = dkv[g, 48:96, :] + from_below[g].astype(f32)
        dkv_token[:, g >> 1, g & 1] = jnp.concatenate([top, bottom], 0).reshape(12, 8, 2 * D)
    dmixed = jnp.concatenate(
        [dquery2[...], dkv_token[...].reshape(384, 2 * D).astype(bf16)], 1
    )
    low = norm(hidden[...], norms[6:8, :]).astype(bf16)
    put_cols(grads, 0, tn(low, dmixed))
    dx, dgain, dbias = norm_back(
        hidden[...], norms[6:8, :], nt(dmixed, join(w_qkv(), 0, 3))
    )
    dnorms[2:3, :] = dgain
    dnorms[3:4, :] = dbias
    dhid, grad_red, grad_exp, grad_bias, dgain, dbias = feed_forward_back(
        dhid_in[...] + dx, middle[...], norms[4:6, :], join(w_exp(), 0, 3), red_of(w_red()), ebias[0:1, :]
    )
    put_cols(grads, 3, grad_exp)
    put_red(grads, 6, grad_red)
    debias[...] = grad_bias
    dnorms[0:1, :] = dgain
    dnorms[1:2, :] = dbias
    dhidden[...] = dhid
    dy = dhid.astype(bf16)
    put_cols(grads, 9, tn(att[...], dy))
    datt[...] = nt(dy, join(w_proj(), 0, 1)).astype(bf16)
    attend_back(
        One, place, lay, query, datt, pieces, table, dq, dpieces, dtable,
        score, dscore_f, prob, dscore,
    )
    dquery[...] = dq[...].astype(bf16)
    up[...] = dpieces[:, 0:48, :].astype(bf16)
    inner[...] = dpieces[:, 48:240, :]
    down[...] = dpieces[:, 240:288, :].astype(bf16)
    dpos[...] = gather_table(One, dtable, dfirst)


def front_back_kernel(
    dhid_in, dquery, inner, from_above, from_below, edge_left, edge_right, hidden, conv, patches,
    early, norms,
    grads, dnorms,
):
    sh = early.shape[1] // 15
    left = edge_left[...].astype(f32).reshape(24, 8, 2 * D)
    right = edge_right[...].astype(f32).reshape(24, 8, 2 * D)
    sub = lax.broadcasted_iota(i32, left.shape, 1)

    def whole(p):
        top = inner[p, 0:48, :] + from_above[p].astype(f32)
        bottom = inner[p, 144:192, :] + from_below[p].astype(f32)
        return jnp.concatenate([top, inner[p, 48:144, :], bottom], 0).reshape(24, 8, 2 * D)

    zero = whole(0) + jnp.where(sub < 4, left, pltpu.roll(right, 4, 1))
    one = whole(1) + jnp.where(sub < 4, pltpu.roll(left, 4, 1), right)
    dkv = jnp.stack([zero, one], 1).reshape(384, 2 * D).astype(bf16)
    dmixed = jnp.concatenate([dquery[...], dkv], 1)
    h = hidden[...]
    low = norm(h, norms[2:4, :]).astype(bf16)
    put_cols(grads, 9, tn(low, dmixed))
    w_qkv = jnp.concatenate(
        [early[:, k * sh : (k + 1) * sh, :].reshape(D, 128) for k in range(9, 15)], 1
    )
    dx, dgain, dbias = norm_back(h, norms[2:4, :], nt(dmixed, w_qkv))
    dnorms[2:3, :] = dgain
    dnorms[3:4, :] = dbias
    dconv, dgain, dbias = norm_back(conv[...], norms[0:2, :], dhid_in[...] + dx)
    dnorms[0:1, :] = dgain
    dnorms[1:2, :] = dbias
    put_cols(grads, 0, tn(dconv.astype(bf16), patches[...]))


def passed_along(value, axis, steps):
    count = lax.axis_size(axis)
    leading, last = (max(0, -steps), min(count, count - steps))
    return lax.ppermute(value, axis, [(source, source + steps) for source in range(leading, last)])


def sum_all(value):
    for axis in ("col", "row"):
        count = lax.axis_size(axis)
        step = 1
        while step < count:
            value = value + lax.ppermute(value, axis, [(i, i ^ step) for i in range(count)])
            step *= 2
    return value


def split_small(value):
    high = lax.reduce_precision(value, 8, 7)
    return jnp.concatenate([high.astype(bf16), (value - high).astype(bf16)], 0)


def join_small(parts):
    rows = parts.shape[-2] // 2
    return parts[..., :rows, :] + parts[..., rows:, :]


def reduce_big(grads):
    part = lax.psum_scatter(grads, "row", scatter_dimension=0, tiled=False)
    return lax.psum(part, "col").astype(f32)


def reduce_last(grads, small):
    devices, count, lanes = grads.shape
    cols = lax.axis_size("col")
    part = count // cols
    extra = small.shape[0] * 2
    value = grads.reshape(devices, cols, part, lanes).transpose(1, 0, 2, 3)
    value = value.reshape(cols, devices * part, lanes)
    value = jnp.concatenate([value, jnp.broadcast_to(split_small(small), (cols, extra, lanes))], 1)
    value = lax.all_to_all(value, "col", 0, 0, tiled=True).astype(f32)
    total = jnp.sum(value, 0)
    small = join_small(total[devices * part :])
    value = total[: devices * part].astype(bf16).reshape(devices, part, lanes)
    value = jnp.concatenate(
        [value, jnp.broadcast_to(split_small(small), (devices, extra, lanes))], 1
    )
    value = lax.all_to_all(value, "row", 0, 0, tiled=True).astype(f32)
    total = jnp.sum(value, 0)
    small = join_small(total[part:])
    main = lax.all_gather(total[:part].astype(bf16), "col", axis=0, tiled=True)
    return main.astype(f32), small


def adamw(weight, grad, first, second):
    first = beta_one * first + (1.0 - beta_one) * grad
    second = beta_two * second + (1.0 - beta_two) * grad * grad
    fix_one = 1.0 - beta_one**STEP
    fix_two = 1.0 - beta_two**STEP
    new = weight - learn_rate * (
        first / fix_one / (jnp.sqrt(second / fix_two) + eps_adam) + decay_rate * weight
    )
    return (first, second, new)


def on_device(
    stem_map, layout, labels, live,
    conv_weight, input_proj, output_proj, expand_weight, reduce_weight, head_weight, small_params,
    first_conv, first_input, first_output, first_expand, first_reduce, first_head, first_small,
    second_conv, second_input, second_output, second_expand, second_reduce, second_head, second_small,
):
    nr = lax.axis_size("row")
    sh = D // nr
    images = labels.shape[0]
    padded = -(-images // 16) * 16
    early, late = run(
        pack_kernel,
        [out((15 * sh, 128), bf16), out((21 * sh, D), bf16)],
        [conv_weight, input_proj, output_proj, expand_weight, reduce_weight, head_weight],
    )
    early = lax.all_gather(early, "row", axis=0)
    late = lax.all_gather(late, "row", axis=0)
    norms = small_params[: 12 * D].reshape(12, D)
    start = 12 * D
    ebias = small_params[start : start + LAYERS * FF].reshape(LAYERS, FF)
    start += LAYERS * FF
    hbias = jnp.pad(small_params[start : start + CLASSES], (0, 24), constant_values=MASKED)[None]
    start += CLASSES
    pos_bias = small_params[start:].reshape(LAYERS * HEADS, 169)
    first_one, first_two = run(
        table_kernel,
        [out((geo.pieces, HEADS * geo.across, 128)) for geo in (One, Two)],
        [jnp.pad(pos_bias, ((0, 0), (0, WIN - 169)))],
    )
    row_first = lax.axis_index("row") * 24
    col_first = lax.axis_index("col") * 16
    place = jnp.stack([row_first, col_first, lax.axis_index("row") * sh]).astype(i32)
    lay_one = layout.reshape(5, 24, 8, 2).transpose(1, 3, 2, 0).reshape(384, 5)
    lay_two = layout.reshape(5, 12, 2, 8, 2).transpose(2, 4, 1, 3, 0).reshape(384, 5)
    above = passed_along(stem_map[-1:], "row", 1)
    rim = jnp.concatenate([above[:, -1:], stem_map[:, -1:]], 0)
    rim = jnp.broadcast_to(passed_along(rim, "col", 1), (49, 8, 128))
    patches, conv_out, hidden0, query1, keyval1, edges1 = run(
        front_kernel,
        [
            out((384, 1152), bf16), out((384, D)), out((384, D)), out((384, D), bf16),
            out((2, 192, 2 * D), bf16), out((2, 192, 2 * D), bf16),
        ],
        [place, stem_map.reshape(1536, 128), above.reshape(32, 128), rim.reshape(392, 128), lay_one, early, norms],
        [pltpu.VMEM((1536, 128), f32), pltpu.VMEM((32, 128), f32)],
        {0: SMEM},
    )
    left1 = passed_along(edges1[1], "col", 1)
    right1 = passed_along(edges1[0], "col", -1)
    ring = lambda rows: jnp.concatenate([keyval1[:, rows], left1[None, rows], right1[None, rows]], 0)
    below1 = passed_along(ring(slice(0, 48)), "row", -1)
    above1 = passed_along(ring(slice(144, 192)), "row", 1)
    anywhere = pl.BlockSpec(memory_space=pl.ANY)
    block = lambda count: [pltpu.VMEM((count, nr, 3 * sh, D), bf16), pltpu.SemaphoreType.DMA((count,))]

    def tiles(geo, back):
        rows, keys = HEADS * geo.queries, geo.keys
        shape = (4, 288, 2 * D) if geo is One else (3, 4, 192, 2 * D)
        square = (rows, keys)
        if not back:
            return [pltpu.VMEM(shape, bf16), pltpu.VMEM(square, f32), pltpu.VMEM(square, f32), pltpu.VMEM(square, bf16)]
        return [
            pltpu.VMEM(shape, bf16), pltpu.VMEM(square, f32), pltpu.VMEM(square, f32), pltpu.VMEM(square, f32),
            pltpu.VMEM(square, f32), pltpu.VMEM(square, bf16), pltpu.VMEM(square, bf16), pltpu.VMEM(shape, f32),
            pltpu.VMEM((384, D), bf16), pltpu.VMEM((384, D), f32),
            pltpu.VMEM((geo.pieces, HEADS * geo.across, 128), f32),
        ]

    near1 = [keyval1, left1, right1, above1, below1, first_one]
    att1, middle1, last1, query2, keyval2 = run(
        first_block_kernel,
        [
            out((384, D), bf16), out((384, D)), out((384, D)), out((384, D), bf16),
            out((4, 96, 2 * D), bf16),
        ],
        [place, lay_one, hidden0, query1, *near1, late, norms, ebias],
        tiles(One, False) + block(4),
        {0: SMEM, 10: anywhere},
    )
    below2 = passed_along(keyval2[:, :48], "row", -1)
    above2 = passed_along(keyval2[:, 48:], "row", 1)
    own2 = jnp.concatenate([above2, keyval2, below2], 1)
    left2 = passed_along(own2, "col", 1)
    right2 = passed_along(own2, "col", -1)
    token5 = lambda width: pltpu.VMEM((12, 2, 2, 8, width), f32)
    near2 = [own2, left2, right2, first_two]
    att2, middle2, last2, sums = run(
        second_block_kernel,
        [out((384, D), bf16), out((384, D)), out((384, D)), out((padded, D + 128))],
        [place, lay_two, lay_one, last1, query2, *near2, late, norms, ebias],
        tiles(Two, False) + [pltpu.VMEM((384, D), f32), token5(D)] + block(3),
        {0: SMEM, 9: anywhere},
    )
    sums = sum_all(sums)
    pad_images = lambda x: jnp.pad(x, (0, padded - images))[:, None]
    (
        loss, grad_head, grad_hbias, dhid, grads2, dnorms2, debias2, dpos2, dquery2, down2, dleft2, dright2,
    ) = run(
        second_back_kernel,
        [
            out((8, 128)), out((sh, 1024)), out((1, 1024)), out((384, D)), out((nr, 7 * sh, D), bf16),
            out((4, D)), out((1, FF)), out((HEADS, WIN)), out((384, D), bf16),
            out((4, 192, 2 * D)), out((4, 192, 2 * D), bf16), out((4, 192, 2 * D), bf16),
        ],
        [
            place, lay_two, lay_one, sums, pad_images(labels), pad_images(live.astype(f32)), hbias,
            last2, middle2, att2, query2, *near2, late, norms, ebias,
        ],
        tiles(Two, True) + [token5(D)] + block(4),
        {0: SMEM, 15: anywhere},
    )
    from_right = passed_along(dleft2, "col", -1)
    from_left = passed_along(dright2, "col", 1)
    whole2 = down2 + from_right.astype(f32) + from_left.astype(f32)
    lower2 = passed_along(whole2[:, :48].astype(bf16), "row", -1)
    upper2 = passed_along(whole2[:, 144:].astype(bf16), "row", 1)
    big2 = reduce_big(grads2)
    dhid, grads1, dnorms1, debias1, dpos1, dquery1, inner1, up1, down1 = run(
        first_back_kernel,
        [
            out((384, D)), out((nr, 10 * sh, D), bf16), out((4, D)), out((1, FF)), out((HEADS, WIN)),
            out((384, D), bf16), out((4, 192, 2 * D)), out((4, 48, 2 * D), bf16), out((4, 48, 2 * D), bf16),
        ],
        [
            place, lay_one, dhid, dquery2, whole2[:, 48:144], upper2, lower2, last1, middle1, att1, query1,
            *near1, late, norms, ebias,
        ],
        tiles(One, True) + [token5(2 * D)] + block(4),
        {0: SMEM, 17: anywhere},
    )
    big1 = reduce_big(grads1)
    lower1 = passed_along(up1, "row", -1)
    upper1 = passed_along(down1, "row", 1)
    sides = inner1[2:] + jnp.concatenate(
        [upper1[2:].astype(f32), jnp.zeros((2, 96, 2 * D), f32), lower1[2:].astype(f32)], 1
    )
    sides = sides.astype(bf16)
    edge_right = passed_along(sides[0], "col", -1)
    edge_left = passed_along(sides[1], "col", 1)
    grads0, dnorms0 = run(
        front_back_kernel,
        [out((nr, 15 * sh, 128), bf16), out((4, D))],
        [
            dhid, dquery1, inner1, upper1, lower1, edge_left, edge_right, hidden0, conv_out, patches,
            early, norms,
        ],
    )
    small = jnp.concatenate(
        [
            dnorms0.reshape(-1), dnorms1.reshape(-1), dnorms2.reshape(-1), debias1[0], debias2[0],
            dpos1[:, :169].reshape(-1), dpos2[:, :169].reshape(-1),
        ]
    )
    width = small.shape[0]
    small = jnp.pad(small, (0, 8192 - width)).reshape(64, 128)
    main, small = reduce_last(grads0, small)
    small = small.reshape(-1)[:width]
    front = 12 * D + LAYERS * FF
    grad_small = jnp.concatenate([small[:front], grad_hbias[0, :CLASSES], small[front:]])
    cols = lambda x, first, count: jnp.concatenate(
        [x[k * sh : (k + 1) * sh] for k in range(first, first + count)], 1
    )
    grads = (
        cols(main, 0, 9).T,
        jnp.stack([cols(main, 9, 6), cols(big1, 0, 3)]),
        jnp.stack([big1[9 * sh :], big2[6 * sh :]]),
        jnp.stack([cols(big1, 3, 3), cols(big2, 0, 3)]),
        jnp.stack([big1[6 * sh : 9 * sh], big2[3 * sh : 6 * sh]]),
        grad_head[:, :CLASSES],
        grad_small,
    )
    params = (
        conv_weight, input_proj, output_proj, expand_weight, reduce_weight, head_weight, small_params,
    )
    firsts = (first_conv, first_input, first_output, first_expand, first_reduce, first_head, first_small)
    seconds = (
        second_conv, second_input, second_output, second_expand, second_reduce, second_head, second_small,
    )
    res = [adamw(w, g, m, v) for w, g, m, v in zip(params, grads, firsts, seconds)]
    return (loss[0, 0], *[entry for triple in res for entry in triple])


def solution(mesh):
    return jax.shard_map(
        on_device,
        mesh=mesh,
        in_specs=(
            P("row", "col", None),
            P(None, "row", "col"),
            P(),
            P(),
            P(None, "row"),
            P(None, "row", None),
            P(None, "row", None),
            P(None, "row", None),
            P(None, "row", None),
            P("row", None),
            P(),
            P(None, "row"),
            P(None, "row", None),
            P(None, "row", None),
            P(None, "row", None),
            P(None, "row", None),
            P("row", None),
            P(),
            P(None, "row"),
            P(None, "row", None),
            P(None, "row", None),
            P(None, "row", None),
            P(None, "row", None),
            P("row", None),
            P(),
        ),
        out_specs=(
            P(),
            P(None, "row"),
            P(None, "row"),
            P(None, "row"),
            P(None, "row", None),
            P(None, "row", None),
            P(None, "row", None),
            P(None, "row", None),
            P(None, "row", None),
            P(None, "row", None),
            P(None, "row", None),
            P(None, "row", None),
            P(None, "row", None),
            P(None, "row", None),
            P(None, "row", None),
            P(None, "row", None),
            P("row", None),
            P("row", None),
            P("row", None),
            P(),
            P(),
            P(),
        ),
        check_vma=False,
    )
```

time: 1990 us -> 450 us (0.23)
  local copies, waits for them, and re-layouts: 888 us -> 22.3 us
  other arithmetic: 679 us -> 15.2 us
  blocking collectives: 288 us -> 42.6 us
  waiting for transfers between devices: 21.7 us -> 202 us
  Pallas kernels: 0 us -> 77.3 us
  matrix products: 33.9 us -> 0 us
  starting transfers between devices: 46.5 us -> 74.1 us
    reshape x15 -> x8, local copies, waits for them, and re-layouts: 470 us -> 4.27 us  [the longest x1 1.3 us: reduce_last(): value = grads.reshape(devices, cols, part, lanes).transpose(1, 0, 2, 3)]
    scatter-add x10 -> x0, other arithmetic: 440 us -> none  [the longest x2 227 us: one_block(): dflat = dflat.at[keys_b.reshape(-1)].add(dnear.reshape(-1, 2 * D))]
    gather x12 -> x0, local copies, waits for them, and re-layouts: 245 us -> none  [the longest x4 155 us: window_scores(): near = jnp.take(flat, keys, axis=0)]
    all_gather x6 -> x2, blocking collectives: 202 us -> 42.6 us  [the longest x1 37.2 us: on_device(): early = lax.all_gather(early, 'row', axis=0)]
    reduce_scatter x0 -> x2, waiting for transfers between devices: none -> 93.4 us  [reduce_big(): part = lax.psum_scatter(grads, 'row', scatter_dimension=0, tiled=False)]
    psum x2 -> x0, blocking collectives: 86.1 us -> none  [the longest x1 43.9 us: on_device(): lax.psum((front, jnp.stack(grads_pos[::-1]).reshape(-1)), ('row', 'col'))]
    pallas_call x0 -> x8, Pallas kernels: none -> 77.3 us  [run(): pl.pallas_call(kernel, out_shape=outs, in_specs=in_specs, out_specs=[pl.B...]
    unnamed x467 -> x110, local copies, waits for them, and re-layouts: 78.7 us -> 6.34 us
  transfers between devices with their start and end apart: 19 -> 29, of which waited for: 5 -> 20; matrix products, arithmetic and copies ran while one was open for 21% -> 4% of each run, Pallas kernels for 0% -> 2%
where the time goes in v1:
time: 450 us; the launch traced here: 449 us
  waiting for transfers between devices  202 us (45%)
  Pallas kernels  77.3 us (17%)
  starting transfers between devices  74.1 us (16%)
  blocking collectives  42.6 us (9%)
  local copies, waits for them, and re-layouts  22.3 us (5%)
  other arithmetic  15.2 us (3%)
  between operations  14.8 us (3%)
    reduce_scatter x2, waiting for transfers between devices, reduce_big(): part = lax.psum_scatter(grads, 'row', scatter_dimension=0, tiled=False)  93.4 us
    pallas_call x8, Pallas kernels, run(): pl.pallas_call(kernel, out_shape=outs, in_specs=in_specs, out_specs=[pl.B...  77.3 us
    ppermute x18, starting transfers between devices, passed_along(): lax.ppermute(value, axis, [(source, source + steps) for source in range(l...  50.1 us
    all_gather x1, blocking collectives, on_device(): early = lax.all_gather(early, 'row', axis=0)  37.2 us
    psum x1, waiting for transfers between devices, reduce_big(): return lax.psum(part, 'col').astype(f32)  32.6 us
    ppermute x18, waiting for transfers between devices, passed_along(): lax.ppermute(value, axis, [(source, source + steps) for source in range(l...  28.7 us
    ppermute x5, waiting for transfers between devices, sum_all(): lax.ppermute(value, axis, [(i, i ^ step) for i in range(count)])  16.8 us
    all_to_all x1, waiting for transfers between devices, reduce_last(): value = lax.all_to_all(value, 'row', 0, 0, tiled=True).astype(f32)  15.6 us
  transfers between devices with their start and end apart: 29, of which 20 were waited for; matrix products, arithmetic and copies ran while one was open for 4% of the time, Pallas kernels for 2%

profile of v1, /device:TPU:0, one launch (start us, length us, event | category | flops | bytes accessed | tf_op | source)
XLA Modules:
  0.0 448.6 jit_solution(9206793665470947062)
XLA Ops:
  12.2 4.8 %collective-permute-start = (bf16[1,32,128]{2,1,0:T(8,128)(2,1)S(1)}, bf16[1,32,128]{2,1,0:T(8,128)(2,1)S(1)}, u32[]{:S(2)}, u32[]{:S(2)}) collective-permute-start(bf16[1,32,128]{2,1,0:T(8,128)(2,1)S(1)} %slice.214), channel_id=1, source_target_pairs={{0,4},{4,8},{8,12},{12,16},{16,20},{20,24},{24,28},{1,5},{5,9},{9,... | collective-permute-start | bytes 24584 | tf_op jit(solution)/shard_map/ppermute | solution.py:703
  17.0 37.2 %all-gather = bf16[3840,128]{1,0:T(8,128)(2,1)} all-gather(bf16[480,128]{1,0:T(8,128)(2,1)} %get-tuple-element.64), channel_id=2, replica_groups=mesh['row'=8,'col'=4] {'row'}, dimensions={0}, use_global_device_ids=true | all-gather | bytes 1105920 | tf_op jit(solution)/shard_map/all_gather | solution.py:779
  73.4 4.6 %collective-permute-start.4 = (bf16[4,48,512]{2,1,0:T(8,128)(2,1)S(1)}, bf16[4,48,512]{2,1,0:T(8,128)(2,1)S(1)}, u32[]{:S(2)}, u32[]{:S(2)}) collective-permute-start(bf16[4,48,512]{2,1,0:T(8,128)(2,1)S(1)} %pad_maximum_fusion.2), channel_id=1, source_target_pairs={{0,4},{4,8},{8,12},{12,16},{16,20},{20,24},{24,28},{1,5},{5,9},{9,... | collective-permute-start | bytes 589832 | tf_op jit(solution)/shard_map/ppermute | solution.py:703
  84.4 10.5 %shard_map.411 = (bf16[384,256]{1,0:T(8,128)(2,1)}, f32[384,256]{1,0:T(8,128)}, f32[384,256]{1,0:T(8,128)}, bf16[384,256]{1,0:T(8,128)(2,1)}, bf16[4,96,512]{2,1,0:T(8,128)(2,1)}) custom-call(s32[3]{0:T(128)} %pad_add_fusion.place, s32[384,5]{1,0:T(8,128)} %bitcast.95, f32[384,256]{1,0:T(8,128)} %get-tuple-element.65.hidden, ...), custom_call_target="tpu_custom_call" | custom-call | bytes 4194304 | tf_op jit(solution)/shard_map/pallas_call | solution.py:324
  101.6 7.9 %collective-permute-done.6 = bf16[4,48,512]{2,1,0:T(8,128)(2,1)S(1)} collective-permute-done((bf16[4,48,512]{2,1,0:T(8,128)(2,1)S(1)}, bf16[4,48,512]{2,1,0:T(8,128)(2,1)S(1)}, u32[]{:S(2)}, u32[]{:S(2)}) %collective-permute-start.6) | collective-permute-done | bytes 196640 | tf_op jit(solution)/shard_map/ppermute | solution.py:703
  118.0 12.7 %shard_map.412 = (bf16[384,256]{1,0:T(8,128)(2,1)}, f32[384,256]{1,0:T(8,128)}, f32[384,256]{1,0:T(8,128)}, f32[64,384]{1,0:T(8,128)}) custom-call(s32[3]{0:T(128)} %pad_add_fusion.place, s32[384,5]{1,0:T(8,128)} %bitcast.100, s32[384,5]{1,0:T(8,128)} %bitcast.96, f32[384,256]{1,0:T(8,128)} %get-tuple-element.71.hidden, ...), custom_call_target="tpu_custom_call" | custom-call | bytes 4194304 | tf_op jit(solution)/shard_map/pallas_call | solution.py:324
  130.7 9.2 %collective-permute-start.10 = (f32[64,384]{1,0:T(8,128)}, f32[64,384]{1,0:T(8,128)S(1)}, u32[]{:S(2)}, u32[]{:S(2)}) collective-permute-start(f32[64,384]{1,0:T(8,128)} %get-tuple-element.75), channel_id=1, source_target_pairs={{0,1},{1,0},{2,3},{3,2},{4,5},{5,4},{6,7},{7,6},{8,9},{9,8},{10,11... | collective-permute-start | bytes 294920 | tf_op jit(solution)/shard_map/ppermute | solution.py:711
  142.1 5.0 %collective-permute-done.11 = f32[64,384]{1,0:T(8,128)S(1)} collective-permute-done((f32[64,384]{1,0:T(8,128)S(1)}, f32[64,384]{1,0:T(8,128)S(1)}, u32[]{:S(2)}, u32[]{:S(2)}) %collective-permute-start.11) | collective-permute-done | bytes 98336 | tf_op jit(solution)/shard_map/ppermute | solution.py:711
  158.4 4.9 %collective-permute-done.14 = f32[64,384]{1,0:T(8,128)S(1)} collective-permute-done((f32[64,384]{1,0:T(8,128)S(1)}, f32[64,384]{1,0:T(8,128)S(1)}, u32[]{:S(2)}, u32[]{:S(2)}) %collective-permute-start.14) | collective-permute-done | bytes 98336 | tf_op jit(solution)/shard_map/ppermute | solution.py:711
  163.9 21.0 %shard_map.413 = (f32[8,128]{1,0:T(8,128)}, f32[32,1024]{1,0:T(8,128)}, f32[1,1024]{1,0:T(1,128)}, f32[384,256]{1,0:T(8,128)}, bf16[8,224,256]{2,1,0:T(8,128)(2,...) custom-call(s32[3]{0:T(128)} %pad_add_fusion.place, ...), custom_call_target="tpu_custom_call" | custom-call | bytes 4194304 | tf_op jit(solution)/shard_map/pallas_call | solution.py:324
  199.7 4.4 collective-permute-done.18.from_below
  204.8 18.5 %shard_map.414 = (f32[384,256]{1,0:T(8,128)}, bf16[8,320,256]{2,1,0:T(8,128)(2,1)}, f32[4,256]{1,0:T(4,128)}, f32[1,768]{1,0:T(1,128)}, f32[8,176]{1,0:T(8,128)}...) custom-call(s32[3]{0:T(128)} %pad_add_fusion.place, ...), custom_call_target="tpu_custom_call" | custom-call | bytes 4194304 | tf_op jit(solution)/shard_map/pallas_call | solution.py:324
  224.9 4.5 %collective-permute-start.19 = (bf16[4,48,512]{2,1,0:T(8,128)(2,1)}, bf16[4,48,512]{2,1,0:T(8,128)(2,1)S(1)}, u32[]{:S(2)}, u32[]{:S(2)}) collective-permute-start(bf16[4,48,512]{2,1,0:T(8,128)(2,1)} %get-tuple-element.90), channel_id=1, source_target_pairs={{0,4},{4,8},{8,12},{12,16},{16,20},{20,24},{24,28},{1,5},{5,9},{9,... | collective-permute-start | bytes 589832 | tf_op jit(solution)/shard_map/ppermute | solution.py:703
  234.3 6.9 %collective-permute-start.21 = (bf16[192,512]{1,0:T(8,128)(2,1)S(1)}, bf16[192,512]{1,0:T(8,128)(2,1)S(1)}, u32[]{:S(2)}, u32[]{:S(2)}) collective-permute-start(bf16[192,512]{1,0:T(8,128)(2,1)S(1)} %get-tuple-element.136), channel_id=1, source_target_pairs={{0,1},{1,2},{2,3},{4,5},{5,6},{6,7},{8,9},{9,10},{10,11},{12,13},{... | collective-permute-start | bytes 589832 | tf_op jit(solution)/shard_map/ppermute | solution.py:703
  242.9 5.7 %collective-permute-done.22.edge_right = bf16[192,512]{1,0:T(8,128)(2,1)S(1)} collective-permute-done((bf16[192,512]{1,0:T(8,128)(2,1)S(1)}, bf16[192,512]{1,0:T(8,128)(2,1)S(1)}, u32[]{:S(2)}, u32[]{:S(2)}) %collective-permute-start.22) | collective-permute-done | bytes 196640 | tf_op jit(solution)/shard_map/ppermute | solution.py:703
  249.3 5.3 %shard_map.415 = (bf16[8,480,128]{2,1,0:T(8,128)(2,1)}, f32[4,256]{1,0:T(4,128)}) custom-call(f32[384,256]{1,0:T(8,128)} %get-tuple-element.87.dhid_in, bf16[384,256]{1,0:T(8,128)(2,1)} %get-tuple-element.88.dquery, f32[4,192,512]{2,1,0:T(8,128)} %get-tuple-element.89.inner, bf16[4,48,512]{2,1,0:T(8,128)(2,1)} %copy-done.13, bf16[4,48,512]{2,1,0:T(8,128)(2,1)} %copy-done.12, ...), custom_call_target="tpu_custom_call" | custom-call | bytes 4194304 | tf_op jit(solution)/shard_map/pallas_call | solution.py:324
  257.1 5.4 %all-to-all-start = ((bf16[4,1088,128]{2,1,0:T(8,128)(2,1)}), bf16[4,1088,128]{2,1,0:T(8,128)(2,1)S(1)}, u32[]{:S(2)}, u32[]{:S(2)}) async-start(bf16[4,1088,128]{2,1,0:T(8,128)(2,1)} %pad_maximum_fusion), calls=%async_computation | async-start | bytes 2228224 | tf_op jit(solution)/shard_map/all_to_all | solution.py:739
  263.3 14.4 %all-to-all-done = bf16[4,1088,128]{2,1,0:T(8,128)(2,1)S(1)} async-done(((bf16[4,1088,128]{2,1,0:T(8,128)(2,1)}), bf16[4,1088,128]{2,1,0:T(8,128)(2,1)S(1)}, u32[]{:S(2)}, u32[]{:S(2)}) %all-to-all-start) | async-done | bytes 1114144 | tf_op jit(solution)/shard_map/all_to_all | solution.py:739
  278.9 5.7 %all-to-all-start.1 = ((bf16[8,248,128]{2,1,0:T(8,128)(2,1)}), bf16[8,248,128]{2,1,0:T(8,128)(2,1)S(1)}, u32[]{:S(2)}, u32[]{:S(2)}) async-start(bf16[8,248,128]{2,1,0:T(8,128)(2,1)} %pad_maximum_fusion.1), calls=%async_computation.1 | async-start | bytes 1015808 | tf_op jit(solution)/shard_map/all_to_all | solution.py:746
  286.7 15.6 %all-to-all-done.1 = bf16[8,248,128]{2,1,0:T(8,128)(2,1)S(1)} async-done(((bf16[8,248,128]{2,1,0:T(8,128)(2,1)}), bf16[8,248,128]{2,1,0:T(8,128)(2,1)S(1)}, u32[]{:S(2)}, u32[]{:S(2)}) %all-to-all-start.1) | async-done | bytes 507936 | tf_op jit(solution)/shard_map/all_to_all | solution.py:746
  302.5 5.4 %all_gather.19 = bf16[480,128]{1,0:T(8,128)(2,1)S(1)} all-gather(bf16[120,128]{1,0:T(8,128)(2,1)S(1)} %slice.378), channel_id=1, replica_groups=mesh['row'=8,'col'=4] {'col'}, dimensions={0}, use_global_device_ids=true | all-gather | bytes 153600 | tf_op jit(solution)/shard_map/all_gather | solution.py:749
  308.9 26.2 %reduce-scatter.5.cloned.1.call-done = bf16[1,224,256]{2,1,0:T(8,128)(2,1)} async-done(((bf16[8,224,256]{2,1,0:T(8,128)(2,1)}), bf16[1,224,256]{2,1,0:T(8,128)(2,1)}) %reduce-scatter.5.cloned.1.call-update) | async-done | bytes 114704 | tf_op jit(solution)/shard_map/reduce_scatter | solution.py:727
  335.1 67.2 %reduce-scatter.3.cloned.1.call-done = bf16[1,320,256]{2,1,0:T(8,128)(2,1)} async-done(((bf16[8,320,256]{2,1,0:T(8,128)(2,1)}), bf16[1,320,256]{2,1,0:T(8,128)(2,1)}) %reduce-scatter.3.cloned.1.call-update) | async-done | bytes 163856 | tf_op jit(solution)/shard_map/reduce_scatter | solution.py:727
  403.0 32.6 %all-reduce.8.cloned.1.call-done = (bf16[320,256]{1,0:T(8,128)(2,1)}, bf16[224,256]{1,0:T(8,128)(2,1)}) async-done(((bf16[320,256]{1,0:T(8,128)(2,1)}, bf16[224,256]{1,0:T(8,128)(2,1)}), (bf16[320,256]{1,0:T(8,128)(2,1)}, bf16[224,256]{1,0:T(8,128)(2,1)})) %all-reduce.8.cloned.1.call-update) | async-done | bytes 278544 | tf_op jit(solution)/shard_map/psum | solution.py:728
  (245 shorter events, 98.2 us)
Async XLA Ops:
  7.2 76.5 %all-gather.4.cloned.1.call-start = ((), (), s32[]{:S(2)}) async-start(), calls=%async_computation.6 | async-start | bytes 3096576 | tf_op jit(solution)/shard_map/all_gather | solution.py:780
  12.2 42.9 %collective-permute-start = (bf16[1,32,128]{2,1,0:T(8,128)(2,1)S(1)}, bf16[1,32,128]{2,1,0:T(8,128)(2,1)S(1)}, u32[]{:S(2)}, u32[]{:S(2)}) collective-permute-start(bf16[1,32,128]{2,1,0:T(8,128)(2,1)S(1)} %slice.214), channel_id=1, source_target_pairs={{0,4},{4,8},{8,12},{12,16},{16,20},{20,24},{24,28},{1,5},{5,9},{9,... | collective-permute-start | bytes 24584 | tf_op jit(solution)/shard_map/ppermute | solution.py:703
  64.3 6.1 %collective-permute-start.2 = (bf16[192,512]{1,0:T(8,128)(2,1)S(1)}, bf16[192,512]{1,0:T(8,128)(2,1)S(1)}, u32[]{:S(2)}, u32[]{:S(2)}) collective-permute-start(bf16[192,512]{1,0:T(8,128)(2,1)S(1)} %get-tuple-element.142), channel_id=1, source_target_pairs={{0,1},{1,2},{2,3},{4,5},{5,6},{6,7},{8,9},{9,10},{10,11},{12,13},{... | collective-permute-start | bytes 589832 | tf_op jit(solution)/shard_map/ppermute | solution.py:703
  72.0 10.5 %collective-permute-start.5 = (bf16[4,48,512]{2,1,0:T(8,128)(2,1)S(1)}, bf16[4,48,512]{2,1,0:T(8,128)(2,1)S(1)}, u32[]{:S(2)}, u32[]{:S(2)}) collective-permute-start(bf16[4,48,512]{2,1,0:T(8,128)(2,1)S(1)} %pad_maximum_fusion.3), channel_id=1, source_target_pairs={{4,0},{8,4},{12,8},{16,12},{20,16},{24,20},{28,24},{5,1},{9,5},{13... | collective-permute-start | bytes 589832 | tf_op jit(solution)/shard_map/ppermute | solution.py:703
  73.4 10.3 %collective-permute-start.4 = (bf16[4,48,512]{2,1,0:T(8,128)(2,1)S(1)}, bf16[4,48,512]{2,1,0:T(8,128)(2,1)S(1)}, u32[]{:S(2)}, u32[]{:S(2)}) collective-permute-start(bf16[4,48,512]{2,1,0:T(8,128)(2,1)S(1)} %pad_maximum_fusion.2), channel_id=1, source_target_pairs={{0,4},{4,8},{8,12},{12,16},{16,20},{20,24},{24,28},{1,5},{5,9},{9,... | collective-permute-start | bytes 589832 | tf_op jit(solution)/shard_map/ppermute | solution.py:703
  95.9 13.6 %collective-permute-start.6 = (bf16[4,48,512]{2,1,0:T(8,128)(2,1)S(1)}, bf16[4,48,512]{2,1,0:T(8,128)(2,1)S(1)}, u32[]{:S(2)}, u32[]{:S(2)}) collective-permute-start(bf16[4,48,512]{2,1,0:T(8,128)(2,1)S(1)} %get-tuple-element.138), channel_id=1, source_target_pairs={{0,4},{4,8},{8,12},{12,16},{16,20},{20,24},{24,28},{1,5},{5,9},{9,... | collective-permute-start | bytes 589832 | tf_op jit(solution)/shard_map/ppermute | solution.py:703
  100.3 10.2 %collective-permute-start.7 = (bf16[4,48,512]{2,1,0:T(8,128)(2,1)S(1)}, bf16[4,48,512]{2,1,0:T(8,128)(2,1)S(1)}, u32[]{:S(2)}, u32[]{:S(2)}) collective-permute-start(bf16[4,48,512]{2,1,0:T(8,128)(2,1)S(1)} %get-tuple-element.137), channel_id=1, source_target_pairs={{4,0},{8,4},{12,8},{16,12},{20,16},{24,20},{28,24},{5,1},{9,5},{13... | collective-permute-start | bytes 589832 | tf_op jit(solution)/shard_map/ppermute | solution.py:703
  110.6 4.7 %collective-permute-start.8 = (bf16[4,192,512]{2,1,0:T(8,128)(2,1)S(1)}, bf16[4,192,512]{2,1,0:T(8,128)(2,1)S(1)}, u32[]{:S(2)}, u32[]{:S(2)}) collective-permute-start(bf16[4,192,512]{2,1,0:T(8,128)(2,1)S(1)} %constant_dynamic-update-slice_fusion.own), channel_id=1, source_target_pairs={{0,1},{1,2},{2,3},{4,5},{5,6},{6,7},{8,9},{9,10},{10,11},{12,13},{... | collective-permute-start | bytes 2359304 | tf_op jit(solution)/shard_map/ppermute | solution.py:703
  130.7 10.3 %collective-permute-start.10 = (f32[64,384]{1,0:T(8,128)}, f32[64,384]{1,0:T(8,128)S(1)}, u32[]{:S(2)}, u32[]{:S(2)}) collective-permute-start(f32[64,384]{1,0:T(8,128)} %get-tuple-element.75), channel_id=1, source_target_pairs={{0,1},{1,0},{2,3},{3,2},{4,5},{5,4},{6,7},{7,6},{8,9},{9,8},{10,11... | collective-permute-start | bytes 294920 | tf_op jit(solution)/shard_map/ppermute | solution.py:711
  141.9 5.1 %collective-permute-start.11 = (f32[64,384]{1,0:T(8,128)S(1)}, f32[64,384]{1,0:T(8,128)S(1)}, u32[]{:S(2)}, u32[]{:S(2)}) collective-permute-start(f32[64,384]{1,0:T(8,128)S(1)} %add.147), channel_id=1, source_target_pairs={{0,2},{1,3},{2,0},{3,1},{4,6},{5,7},{6,4},{7,5},{8,10},{9,11},{10,... | collective-permute-start | bytes 294920 | tf_op jit(solution)/shard_map/ppermute | solution.py:711
  147.1 4.8 %collective-permute-start.12 = (f32[64,384]{1,0:T(8,128)S(1)}, f32[64,384]{1,0:T(8,128)S(1)}, u32[]{:S(2)}, u32[]{:S(2)}) collective-permute-start(f32[64,384]{1,0:T(8,128)S(1)} %add.148), channel_id=1, source_target_pairs={{0,4},{4,0},{8,12},{12,8},{16,20},{20,16},{24,28},{28,24},{1,5},{5... | collective-permute-start | bytes 294920 | tf_op jit(solution)/shard_map/ppermute | solution.py:711
  156.6 6.6 %collective-permute-start.14 = (f32[64,384]{1,0:T(8,128)S(1)}, f32[64,384]{1,0:T(8,128)S(1)}, u32[]{:S(2)}, u32[]{:S(2)}) collective-permute-start(f32[64,384]{1,0:T(8,128)S(1)} %add.150), channel_id=1, source_target_pairs={{0,16},{4,20},{8,24},{12,28},{16,0},{20,4},{24,8},{28,12},{1,17},{... | collective-permute-start | bytes 294920 | tf_op jit(solution)/shard_map/ppermute | solution.py:711
  186.2 5.1 %collective-permute-start.16 = (bf16[4,192,512]{2,1,0:T(8,128)(2,1)}, bf16[4,192,512]{2,1,0:T(8,128)(2,1)S(1)}, u32[]{:S(2)}, u32[]{:S(2)}) collective-permute-start(bf16[4,192,512]{2,1,0:T(8,128)(2,1)} %get-tuple-element.84), channel_id=1, source_target_pairs={{0,1},{1,2},{2,3},{4,5},{5,6},{6,7},{8,9},{9,10},{10,11},{12,13},{... | collective-permute-start | bytes 2359304 | tf_op jit(solution)/shard_map/ppermute | solution.py:703
  193.2 6.5 %collective-permute-start.17 = (bf16[4,48,512]{2,1,0:T(8,128)(2,1)S(1)}, bf16[4,48,512]{2,1,0:T(8,128)(2,1)S(1)}, u32[]{:S(2)}, u32[]{:S(2)}) collective-permute-start(bf16[4,48,512]{2,1,0:T(8,128)(2,1)S(1)} %get-tuple-element.132), channel_id=1, source_target_pairs={{0,4},{4,8},{8,12},{12,16},{16,20},{20,24},{24,28},{1,5},{5,9},{9,... | collective-permute-start | bytes 589832 | tf_op jit(solution)/shard_map/ppermute | solution.py:703
  196.6 7.6 %collective-permute-start.18 = (bf16[4,48,512]{2,1,0:T(8,128)(2,1)S(1)}, bf16[4,48,512]{2,1,0:T(8,128)(2,1)S(1)}, u32[]{:S(2)}, u32[]{:S(2)}) collective-permute-start(bf16[4,48,512]{2,1,0:T(8,128)(2,1)S(1)} %get-tuple-element.131), channel_id=1, source_target_pairs={{4,0},{8,4},{12,8},{16,12},{20,16},{24,20},{28,24},{5,1},{9,5},{13... | collective-permute-start | bytes 589832 | tf_op jit(solution)/shard_map/ppermute | solution.py:703
  223.4 7.9 %collective-permute-start.20 = (bf16[4,48,512]{2,1,0:T(8,128)(2,1)}, bf16[4,48,512]{2,1,0:T(8,128)(2,1)S(1)}, u32[]{:S(2)}, u32[]{:S(2)}) collective-permute-start(bf16[4,48,512]{2,1,0:T(8,128)(2,1)} %get-tuple-element.91), channel_id=1, source_target_pairs={{4,0},{8,4},{12,8},{16,12},{20,16},{24,20},{28,24},{5,1},{9,5},{13... | collective-permute-start | bytes 589832 | tf_op jit(solution)/shard_map/ppermute | solution.py:703
  224.9 8.0 %collective-permute-start.19 = (bf16[4,48,512]{2,1,0:T(8,128)(2,1)}, bf16[4,48,512]{2,1,0:T(8,128)(2,1)S(1)}, u32[]{:S(2)}, u32[]{:S(2)}) collective-permute-start(bf16[4,48,512]{2,1,0:T(8,128)(2,1)} %get-tuple-element.90), channel_id=1, source_target_pairs={{0,4},{4,8},{8,12},{12,16},{16,20},{20,24},{24,28},{1,5},{5,9},{9,... | collective-permute-start | bytes 589832 | tf_op jit(solution)/shard_map/ppermute | solution.py:703
  234.3 8.6 %collective-permute-start.21 = (bf16[192,512]{1,0:T(8,128)(2,1)S(1)}, bf16[192,512]{1,0:T(8,128)(2,1)S(1)}, u32[]{:S(2)}, u32[]{:S(2)}) collective-permute-start(bf16[192,512]{1,0:T(8,128)(2,1)S(1)} %get-tuple-element.136), channel_id=1, source_target_pairs={{0,1},{1,2},{2,3},{4,5},{5,6},{6,7},{8,9},{9,10},{10,11},{12,13},{... | collective-permute-start | bytes 589832 | tf_op jit(solution)/shard_map/ppermute | solution.py:703
  241.3 7.3 %collective-permute-start.22 = (bf16[192,512]{1,0:T(8,128)(2,1)S(1)}, bf16[192,512]{1,0:T(8,128)(2,1)S(1)}, u32[]{:S(2)}, u32[]{:S(2)}) collective-permute-start(bf16[192,512]{1,0:T(8,128)(2,1)S(1)} %get-tuple-element.135), channel_id=1, source_target_pairs={{1,0},{2,1},{3,2},{5,4},{6,5},{7,6},{9,8},{10,9},{11,10},{13,12},{... | collective-permute-start | bytes 589832 | tf_op jit(solution)/shard_map/ppermute | solution.py:703
  257.1 20.6 %all-to-all-start = ((bf16[4,1088,128]{2,1,0:T(8,128)(2,1)}), bf16[4,1088,128]{2,1,0:T(8,128)(2,1)S(1)}, u32[]{:S(2)}, u32[]{:S(2)}) async-start(bf16[4,1088,128]{2,1,0:T(8,128)(2,1)} %pad_maximum_fusion), calls=%async_computation | async-start | bytes 2228224 | tf_op jit(solution)/shard_map/all_to_all | solution.py:739
  262.6 72.6 %reduce-scatter.5.cloned.1.call-start = ((), (), s32[]{:S(2)}) async-start(), calls=%async_computation.5 | async-start | bytes 1032192 | tf_op jit(solution)/shard_map/reduce_scatter | solution.py:727
  278.9 23.5 %all-to-all-start.1 = ((bf16[8,248,128]{2,1,0:T(8,128)(2,1)}), bf16[8,248,128]{2,1,0:T(8,128)(2,1)S(1)}, u32[]{:S(2)}, u32[]{:S(2)}) async-start(bf16[8,248,128]{2,1,0:T(8,128)(2,1)} %pad_maximum_fusion.1), calls=%async_computation.1 | async-start | bytes 1015808 | tf_op jit(solution)/shard_map/all_to_all | solution.py:746
  284.5 117.8 %reduce-scatter.3.cloned.1.call-start = ((), (), s32[]{:S(2)}) async-start(), calls=%async_computation.4 | async-start | bytes 1474560 | tf_op jit(solution)/shard_map/reduce_scatter | solution.py:727
  286.7 149.0 %all-reduce.8.cloned.1.call-start = ((), (), s32[]{:S(2)}) async-start(), calls=%async_computation.7 | async-start | bytes 557056 | tf_op jit(solution)/shard_map/psum | solution.py:728
  (54 other events, 1176.1 us)
Sparse Core Ops, SparseCore 0:
  11.6 65.5 all-gather.3
  266.7 68.3 reduce-scatter.4
  338.9 63.3 reduce-scatter.2
  404.7 30.8 all-reduce.7

commit v2 on v1

--- a/solution.py
+++ b/solution.py
@@ -70,15 +70,6 @@
 
 def normal_cdf(u):
     return 0.5 * (1.0 + lax.erf(u * 0.7071067811865476))
-
-
-def join(ref, first, count):
-    rows = ref.shape[1] // 3
-    wide = [
-        ref[:, k * rows : (k + 1) * rows, :].reshape(D, ref.shape[2])
-        for k in range(first, first + count)
-    ]
-    return wide[0] if count == 1 else jnp.concatenate(wide, 1)
 
 
 class One:
@@ -339,30 +330,48 @@
     return jax.ShapeDtypeStruct(shape, dtype)
 
 
-def pack_kernel(conv, qkv, proj, exp, red, head, early, late):
+def pack_kernel(col, conv, qkv, proj, exp, red, head, *refs):
     sh = qkv.shape[1]
-    for tap in range(9):
-        early[tap * sh : (tap + 1) * sh, :] = conv[tap * 128 : (tap + 1) * 128, :].T.astype(bf16)
-    for k in range(6):
-        begin = (9 + k) * sh
-        early[begin : begin + sh, :] = qkv[0, :, k * 128 : (k + 1) * 128].astype(bf16)
-
-    def put(slot, value):
-        late[slot * sh : slot * sh + value.shape[0], :] = value.astype(bf16)
-
-    for k in range(3):
-        cols = slice(k * D, (k + 1) * D)
-        put(k, qkv[1, :, cols])
-        put(3 + k, exp[0, :, cols])
-        put(6 + k, exp[1, :, cols])
-    put(9, red[0])
-    put(12, red[1])
-    put(15, proj[0])
-    put(16, proj[1])
-    for k in range(3):
-        put(17 + k, head[:, k * D : (k + 1) * D])
-    tail = head[:, 3 * D :]
-    put(20, jnp.concatenate([tail, jnp.zeros((sh, 4 * D - CLASSES), f32)], 1))
+    outs, groups = refs[:3], refs[3:]
+
+    def cols(x):
+        return [x[:, k * 128 : (k + 1) * 128] for k in range(x.shape[1] // 128)]
+
+    def reds(x):
+        return [part for k in range(3) for part in cols(x[k * sh : (k + 1) * sh, :])]
+
+    tail = jnp.concatenate([head[:, 896:], jnp.zeros((sh, 1024 - CLASSES), f32)], 1)
+    blocks = (
+        cols(conv[...]) + cols(qkv[0]),
+        cols(proj[0]) + cols(exp[0]) + reds(red[0]) + cols(qkv[1]),
+        cols(proj[1]) + cols(exp[1]) + reds(red[1]) + cols(head[:, :896]) + [tail],
+    )
+    for result, group, values in zip(outs, groups, blocks):
+        for k, value in enumerate(values):
+            group[k * sh : (k + 1) * sh, :] = value.astype(bf16)
+        empty = group.shape[0] - len(values) * sh
+        if empty:
+            group[len(values) * sh :, :] = jnp.zeros((empty, 128), bf16)
+        part = result.shape[1]
+        mine = group[pl.ds(pl.multiple_of(col[0] * part, 16), part), :]
+        for row in range(result.shape[0]):
+            result[row] = mine
+
+
+def weight_of(blocks, first, count):
+    sh = D // blocks.shape[1]
+    per = blocks.shape[2] // sh
+    parts = [
+        blocks[k // per, :, (k % per) * sh : (k % per + 1) * sh, :].reshape(D, 128)
+        for k in range(first, first + count)
+    ]
+    return jnp.concatenate(parts, 1)
+
+
+def weight_red(blocks, first):
+    rows = blocks.shape[1]
+    parts = [weight_of(blocks, first + 2 * k, 2).reshape(rows, 1, D // rows, D) for k in range(3)]
+    return jnp.concatenate(parts, 1).reshape(FF, D)
 
 
 def table_kernel(bias, first_one, first_two):
@@ -370,12 +379,7 @@
     position_table(Two, bias[8:16, :], first_two)
 
 
-def front_kernel(
-    place, stem, above, left, lay, early, norms,
-    patches, conv_out, hidden, query, keyval, edges,
-    stem_f, above_f,
-):
-    nr, sh = early.shape[0], early.shape[1] // 15
+def patch_kernel(place, stem, above, left, lay, patches, stem_f, above_f):
     stem_f[...] = stem[...].astype(f32)
     above_f[...] = above[...].astype(f32)
     left_f = left[...].astype(f32)
@@ -395,9 +399,7 @@
     inner_col = jnp.where(col_pos == lay[:, 2:3], 0.0, 1.0)
     half = lax.broadcasted_iota(i32, (24, 8, 128), 1)
     for a in range(3):
-        last = phases[3][a].reshape(192, 128)
-        shifted = pltpu.roll(last.reshape(24, 8, 128), 1, 1)
-        shifted = jnp.where(half == 0, beside[a], shifted)
+        shifted = jnp.where(half == 0, beside[a], pltpu.roll(phases[3][a], 1, 1))
         taps = (
             (shifted, phases[1][a]),
             (phases[0][a], phases[2][a]),
@@ -411,23 +413,25 @@
                 value = value * inner_col
             lanes = slice((3 * a + b) * 128, (3 * a + b + 1) * 128)
             patches[:, lanes] = value.astype(bf16)
-    wide = [early[:, k * sh : (k + 1) * sh, :].reshape(D, 128) for k in range(15)]
-    conv = nt(patches[...], jnp.concatenate(wide[:9], 1))
+
+
+def front_kernel(patches, early, norms, conv_out, hidden, query, keyval, edge_left, edge_right):
+    conv = nt(patches[...], weight_of(early, 0, 9))
     conv_out[...] = conv
     h = norm(conv, norms[0:2, :])
     hidden[...] = h
     low = norm(h, norms[2:4, :]).astype(bf16)
-    mixed = nn(low, jnp.concatenate(wide[9:], 1))
+    mixed = nn(low, weight_of(early, 9, 6))
     query[...] = mixed[:, :D].astype(bf16)
     both = mixed[:, D:].reshape(24, 2, 8, 2 * D)
     zero, one = both[:, 0], both[:, 1]
     keyval[0] = zero.reshape(192, 2 * D).astype(bf16)
     keyval[1] = one.reshape(192, 2 * D).astype(bf16)
     sub = lax.broadcasted_iota(i32, zero.shape, 1)
-    edge_left = jnp.where(sub < 4, zero, pltpu.roll(one, 4, 1))
-    edge_right = jnp.where(sub < 4, pltpu.roll(zero, 4, 1), one)
-    edges[0] = edge_left.reshape(192, 2 * D).astype(bf16)
-    edges[1] = edge_right.reshape(192, 2 * D).astype(bf16)
+    left = jnp.where(sub < 4, zero, pltpu.roll(one, 4, 1))
+    right = jnp.where(sub < 4, pltpu.roll(zero, 4, 1), one)
+    edge_left[...] = left.reshape(192, 2 * D).astype(bf16)
+    edge_right[...] = right.reshape(192, 2 * D).astype(bf16)
 
 
 def gather_keys_one(keyval, left, right, above, below, pieces):
@@ -445,48 +449,37 @@
     return hidden + nn(gelu.astype(bf16), w_red)
 
 
-def fetch(late, slots, buffers, sems):
-    rows = buffers.shape[2]
-    takers = []
-    for n, slot in enumerate(slots):
-        copy = pltpu.make_async_copy(
-            late.at[:, pl.ds(slot * rows, rows), :], buffers.at[n], sems.at[n]
-        )
-        copy.start()
-
-        def take(copy=copy, n=n):
-            copy.wait()
-            return buffers.at[n]
-
-        takers.append(take)
-    return takers
-
-
-QKV_TWO, EXP_ONE, EXP_TWO, RED_ONE, RED_TWO, PROJ, HEAD = range(7)
+PROJ, EXP, RED, QKV, HEAD = 0, 2, 8, 14, 14
+
+
+def fetch(source, buffer, sem):
+    copy = pltpu.make_async_copy(source, buffer, sem.at[0])
+    copy.start()
+    return copy.wait
 
 
 def first_block_kernel(
     place, lay, hidden, query, keyval, left, right, above, below, first_table, late, norms, ebias,
-    att, middle, last, query2, keyval2,
-    pieces, table, score, prob, buffers, sems,
+    att, middle, last, query2, keyval2, up, down,
+    pieces, table, score, prob, group, sem,
 ):
-    w_proj, w_exp, w_red, w_qkv = fetch(late, (PROJ, EXP_ONE, RED_ONE, QKV_TWO), buffers, sems)
+    arrived = fetch(late, group, sem)
     gather_keys_one(keyval, left, right, above, below, pieces)
     spread_table(One, first_table, table)
     attend(One, place, lay, query, pieces, table, att, score, prob)
-    mid = hidden[...] + nn(att[...], join(w_proj(), 0, 1))
+    arrived()
+    mid = hidden[...] + nn(att[...], weight_of(group, PROJ, 2))
     middle[...] = mid
-    end = feed_forward(mid, norms[4:6, :], join(w_exp(), 0, 3), red_of(w_red()), ebias[0:1, :])
+    end = feed_forward(mid, norms[4:6, :], weight_of(group, EXP, 6), weight_red(group, RED), ebias[0:1, :])
     last[...] = end
     low = norm(end, norms[6:8, :]).astype(bf16)
-    mixed = nn(low, join(w_qkv(), 0, 3))
+    mixed = nn(low, weight_of(group, QKV, 6))
     for g, part in enumerate(grouped(mixed)):
         query2[g * 96 : (g + 1) * 96, :] = part[:, :D].astype(bf16)
-        keyval2[g] = part[:, D:].astype(bf16)
-
-
-def red_of(ref):
-    return ref[...].reshape(FF, D)
+        low = part[:, D:].astype(bf16)
+        keyval2[g] = low
+        up[g] = low[:48]
+        down[g] = low[48:]
 
 
 def slot_onehot(slots, images):
@@ -502,9 +495,9 @@
 def second_block_kernel(
     place, lay, slots, hidden, query, own, left, right, first_table, late, norms, ebias,
     att, middle, last, sums,
-    pieces, table, score, prob, att_group, att_token, buffers, sems,
+    pieces, table, score, prob, att_group, att_token, group, sem,
 ):
-    w_proj, w_exp, w_red = fetch(late, (PROJ, EXP_TWO, RED_TWO), buffers, sems)
+    arrived = fetch(late, group, sem)
     pieces[0] = own[...]
     pieces[1] = left[...]
     pieces[2] = right[...]
@@ -513,15 +506,18 @@
     ungroup(att_group[...], att_token)
     low = att_token[...].reshape(384, D).astype(bf16)
     att[...] = low
-    mid = hidden[...] + nn(low, join(w_proj(), 1, 1))
+    arrived()
+    mid = hidden[...] + nn(low, weight_of(group, PROJ, 2))
     middle[...] = mid
-    end = feed_forward(mid, norms[8:10, :], join(w_exp(), 0, 3), red_of(w_red()), ebias[1:2, :])
+    end = feed_forward(mid, norms[8:10, :], weight_of(group, EXP, 6), weight_red(group, RED), ebias[1:2, :])
     last[...] = end
     final = norm(end, norms[10:12, :])
-    where = slot_onehot(slots, sums.shape[0])
+    images = sums.shape[0] - 8
+    where = slot_onehot(slots, images)
     high, low = two_parts(final)
-    sums[:, :D] = tn(where, high) + tn(where, low)
-    sums[:, D:] = tn(where, jnp.ones((384, 128), bf16))
+    sums[...] = jnp.zeros_like(sums)
+    sums[:images, :D] = tn(where, high) + tn(where, low)
+    sums[images:, :images] = tn(jnp.ones((384, 8), bf16), where)
 
 
 def feed_forward_back(dhid, mid, gain_bias, w_exp, w_red, bias):
@@ -538,37 +534,49 @@
     return dhid + dx, grad_red, grad_exp, grad_bias, dgain, dbias
 
 
+def put_block(grads, k, value):
+    per = grads.shape[1] // D
+    grads[k // per, (k % per) * D : (k % per + 1) * D, :] = value.astype(bf16)
+
+
 def put_cols(grads, first, value):
-    devices, width = grads.shape[0], grads.shape[2]
-    share = D // devices
-    for k in range(value.shape[1] // width):
-        part = value[:, k * width : (k + 1) * width].reshape(devices, share, width)
-        grads[:, (first + k) * share : (first + k + 1) * share, :] = part.astype(bf16)
-
-
-def put_red(grads, first, value):
-    devices = grads.shape[0]
-    share = D // devices
-    part = value.reshape(devices, 3 * share, D)
-    grads[:, first * share : (first + 3) * share, :] = part.astype(bf16)
+    for k in range(value.shape[1] // 128):
+        put_block(grads, first + k, value[:, k * 128 : (k + 1) * 128])
+
+
+def put_red(grads, first, value, share):
+    parts = value.reshape(D // share, 3, share, D)
+    for k in range(3):
+        put_cols(grads, first + 2 * k, parts[:, k].reshape(D, D))
+
+
+def put_zeros(grads, first):
+    per = grads.shape[1] // D
+    for k in range(first, per * grads.shape[0]):
+        put_block(grads, k, jnp.zeros((D, 128), f32))
 
 
 def second_back_kernel(
     place, lay, slots, sums, labels, live, hbias, hidden, middle, att, query, own, left, right,
     first_table, late, norms, ebias,
     loss, grad_head, grad_hbias, dhidden, grads, dnorms, debias, dpos, dquery, down, dleft, dright,
-    pieces, table, dtable, score, dscore_f, prob, dscore, dpieces, datt, dq_group, dfirst, dq_token, buffers, sems,
+    pieces, table, dtable, score, dscore_f, prob, dscore, dpieces, datt, dq_group, dfirst, dq_token, group, sem,
 ):
-    w_p, w_h, w_red, w_exp = fetch(late, (PROJ, HEAD, RED_TWO, EXP_TWO), buffers, sems)
+    arrived = fetch(late, group, sem)
     pieces[0] = own[...]
     pieces[1] = left[...]
     pieces[2] = right[...]
     spread_table(Two, first_table, table)
-    total, area = sums[:, :D], sums[:, D : D + 1]
+    images = sums.shape[0] - 8
+    total = sums[:images, :D]
+    diagonal = lax.broadcasted_iota(i32, (images, images), 0)
+    diagonal = diagonal == lax.broadcasted_iota(i32, (images, images), 1)
+    area = jnp.where(diagonal, sums[images : images + 1, :images], 0.0)
+    area = jnp.sum(area, -1, keepdims=True)
     spread_area = jnp.maximum(area, 1.0)
     pooled = (total / spread_area).astype(bf16)
-    proj_ref, head_ref = w_p(), w_h()
-    w_head = jnp.concatenate([join(proj_ref, 2, 1), join(head_ref, 0, 3)], 1)
+    arrived()
+    w_head = weight_of(group, HEAD, 8)
     logits = nn(pooled, w_head) + hbias[...]
     weight = live[...] * jnp.where(area > 0.5, 1.0, 0.0)
     count = jnp.maximum(jnp.sum(weight, 0, keepdims=True), 1.0)
@@ -586,23 +594,24 @@
     own_pooled = nn(pooled, jnp.where(channel == mine, 1.0, 0.0).astype(bf16)).astype(bf16)
     grad_head[...] = tn(own_pooled, dlogit)
     high, low = two_parts(nt(dlogit, w_head) / spread_area)
-    where = slot_onehot(slots, sums.shape[0])
+    where = slot_onehot(slots, images)
     dfinal = nn(where, high) + nn(where, low)
     dhid, dgain, dbias = norm_back(hidden[...], norms[10:12, :], dfinal)
     dnorms[2:3, :] = dgain
     dnorms[3:4, :] = dbias
     dhid, grad_red, grad_exp, grad_bias, dgain, dbias = feed_forward_back(
-        dhid, middle[...], norms[8:10, :], join(w_exp(), 0, 3), red_of(w_red()), ebias[1:2, :]
+        dhid, middle[...], norms[8:10, :], weight_of(group, EXP, 6), weight_red(group, RED), ebias[1:2, :]
     )
     put_cols(grads, 0, grad_exp)
-    put_red(grads, 3, grad_red)
+    put_red(grads, 6, grad_red, share)
     debias[...] = grad_bias
     dnorms[0:1, :] = dgain
     dnorms[1:2, :] = dbias
     dhidden[...] = dhid
     dy = dhid.astype(bf16)
-    put_cols(grads, 6, tn(att[...], dy))
-    back = nt(dy, join(proj_ref, 1, 1))
+    put_cols(grads, 12, tn(att[...], dy))
+    put_zeros(grads, 14)
+    back = nt(dy, weight_of(group, PROJ, 2))
     for g, part in enumerate(grouped(back)):
         datt[g * 96 : (g + 1) * 96, :] = part.astype(bf16)
     attend_back(
@@ -618,40 +627,43 @@
 
 
 def first_back_kernel(
-    place, lay, dhid_in, dquery2, dkv, from_above, from_below, hidden, middle, att, query, keyval,
+    place, lay, dhid_in, dquery2, dkv, from_left, from_right, from_above, from_below, hidden, middle, att, query, keyval,
     left, right, above, below, first_table, late, norms, ebias,
     dhidden, grads, dnorms, debias, dpos, dquery, inner, up, down,
-    pieces, table, dtable, score, dscore_f, prob, dscore, dpieces, datt, dq, dfirst, dkv_token, buffers, sems,
+    pieces, table, dtable, score, dscore_f, prob, dscore, dpieces, datt, dq, dfirst, dkv_token, group, sem,
 ):
-    w_qkv, w_red, w_exp, w_proj = fetch(late, (QKV_TWO, RED_ONE, EXP_ONE, PROJ), buffers, sems)
+    arrived = fetch(late, group, sem)
     gather_keys_one(keyval, left, right, above, below, pieces)
     spread_table(One, first_table, table)
     for g in range(4):
-        top = dkv[g, 0:48, :] + from_above[g].astype(f32)
-        bottom = dkv[g, 48:96, :] + from_below[g].astype(f32)
-        dkv_token[:, g >> 1, g & 1] = jnp.concatenate([top, bottom], 0).reshape(12, 8, 2 * D)
+        rows = slice(48, 144)
+        total = dkv[g, rows, :] + from_left[g, rows, :].astype(f32) + from_right[g, rows, :].astype(f32)
+        total += jnp.concatenate([from_above[g], from_below[g]], 0).astype(f32)
+        dkv_token[:, g >> 1, g & 1] = total.reshape(12, 8, 2 * D)
     dmixed = jnp.concatenate(
         [dquery2[...], dkv_token[...].reshape(384, 2 * D).astype(bf16)], 1
     )
     low = norm(hidden[...], norms[6:8, :]).astype(bf16)
     put_cols(grads, 0, tn(low, dmixed))
+    arrived()
     dx, dgain, dbias = norm_back(
-        hidden[...], norms[6:8, :], nt(dmixed, join(w_qkv(), 0, 3))
+        hidden[...], norms[6:8, :], nt(dmixed, weight_of(group, QKV, 6))
     )
     dnorms[2:3, :] = dgain
     dnorms[3:4, :] = dbias
     dhid, grad_red, grad_exp, grad_bias, dgain, dbias = feed_forward_back(
-        dhid_in[...] + dx, middle[...], norms[4:6, :], join(w_exp(), 0, 3), red_of(w_red()), ebias[0:1, :]
-    )
-    put_cols(grads, 3, grad_exp)
-    put_red(grads, 6, grad_red)
+        dhid_in[...] + dx, middle[...], norms[4:6, :], weight_of(group, EXP, 6), weight_red(group, RED), ebias[0:1, :]
+    )
+    put_cols(grads, 6, grad_exp)
+    put_red(grads, 12, grad_red, D // late.shape[1])
     debias[...] = grad_bias
     dnorms[0:1, :] = dgain
     dnorms[1:2, :] = dbias
     dhidden[...] = dhid
     dy = dhid.astype(bf16)
-    put_cols(grads, 9, tn(att[...], dy))
-    datt[...] = nt(dy, join(w_proj(), 0, 1)).astype(bf16)
+    put_cols(grads, 18, tn(att[...], dy))
+    put_zeros(grads, 20)
+    datt[...] = nt(dy, weight_of(group, PROJ, 2)).astype(bf16)
     attend_back(
         One, place, lay, query, datt, pieces, table, dq, dpieces, dtable,
         score, dscore_f, prob, dscore,
@@ -663,12 +675,14 @@
     dpos[...] = gather_table(One, dtable, dfirst)
 
 
+SMALL_ROWS = 80
+
+
 def front_back_kernel(
     dhid_in, dquery, inner, from_above, from_below, edge_left, edge_right, hidden, conv, patches,
-    early, norms,
-    grads, dnorms,
+    early, norms, dnorms1, dnorms2, debias1, debias2, dpos1, dpos2,
+    grads, small,
 ):
-    sh = early.shape[1] // 15
     left = edge_left[...].astype(f32).reshape(24, 8, 2 * D)
     right = edge_right[...].astype(f32).reshape(24, 8, 2 * D)
     sub = lax.broadcasted_iota(i32, left.shape, 1)
@@ -685,16 +699,115 @@
     h = hidden[...]
     low = norm(h, norms[2:4, :]).astype(bf16)
     put_cols(grads, 9, tn(low, dmixed))
-    w_qkv = jnp.concatenate(
-        [early[:, k * sh : (k + 1) * sh, :].reshape(D, 128) for k in range(9, 15)], 1
-    )
-    dx, dgain, dbias = norm_back(h, norms[2:4, :], nt(dmixed, w_qkv))
-    dnorms[2:3, :] = dgain
-    dnorms[3:4, :] = dbias
-    dconv, dgain, dbias = norm_back(conv[...], norms[0:2, :], dhid_in[...] + dx)
-    dnorms[0:1, :] = dgain
-    dnorms[1:2, :] = dbias
+    w_qkv = weight_of(early, 9, 6)
+    dx, dgain1, dbias1 = norm_back(h, norms[2:4, :], nt(dmixed, w_qkv))
+    dconv, dgain0, dbias0 = norm_back(conv[...], norms[0:2, :], dhid_in[...] + dx)
     put_cols(grads, 0, tn(dconv.astype(bf16), patches[...]))
+    put_zeros(grads, 15)
+
+    def place_row(first, value):
+        for k in range(value.shape[1] // 128):
+            small[first + k : first + k + 1, :] = value[:, k * 128 : (k + 1) * 128]
+
+    small[...] = jnp.zeros_like(small)
+    for k, value in enumerate((dgain0, dbias0, dgain1, dbias1)):
+        place_row(2 * k, value)
+    for k in range(4):
+        place_row(8 + 2 * k, dnorms1[k : k + 1, :])
+        place_row(16 + 2 * k, dnorms2[k : k + 1, :])
+    place_row(24, debias1[...])
+    place_row(30, debias2[...])
+    for first, value in ((40, dpos1), (56, dpos2)):
+        small[first : first + 8, :] = value[:, :128]
+        small[first + 8 : first + 16, : WIN - 128] = value[:, 128:]
+    high, low = two_parts(small[...])
+    begin = grads.shape[1] - 2 * SMALL_ROWS
+    for col in range(grads.shape[0]):
+        grads[col, begin : begin + SMALL_ROWS, :] = high
+        grads[col, begin + SMALL_ROWS :, :] = low
+
+
+def small_of(parts, index, begin):
+    high = parts[index, begin : begin + SMALL_ROWS, :].astype(f32)
+    return high + parts[index, begin + SMALL_ROWS : begin + 2 * SMALL_ROWS, :].astype(f32)
+
+
+def add_up(parts, rows):
+    total = parts[0, rows, :].astype(f32)
+    for index in range(1, parts.shape[0]):
+        total += parts[index, rows, :].astype(f32)
+    return total
+
+
+def between_kernel(second, first, parts, result):
+    rows = result.shape[0]
+    sh = D // rows
+    begin = 0
+    for group in (second, first):
+        for k in range(group.shape[0] // D):
+            result[:, begin : begin + sh, :] = group[k * D : (k + 1) * D, :].reshape(rows, sh, 128)
+            begin += sh
+    for k in range(parts.shape[1] // D):
+        total = add_up(parts, slice(k * D, (k + 1) * D)).astype(bf16)
+        result[:, begin : begin + sh, :] = total.reshape(rows, sh, 128)
+        begin += sh
+    low_rows = parts.shape[1] - 2 * SMALL_ROWS
+    total = small_of(parts, 0, low_rows)
+    for col in range(1, parts.shape[0]):
+        total += small_of(parts, col, low_rows)
+    high, low = two_parts(total)
+    for row in range(rows):
+        result[row, begin : begin + SMALL_ROWS, :] = high
+        result[row, begin + SMALL_ROWS :, :] = low
+
+
+def last_sum_kernel(parts, result, small):
+    count = result.shape[0]
+    result[...] = add_up(parts, slice(0, count)).astype(bf16)
+    total = small_of(parts, 0, count)
+    for row in range(1, parts.shape[0]):
+        total += small_of(parts, row, count)
+    small[...] = total
+
+
+def adamw(weight, grad, first, second):
+    first = beta_one * first + (1.0 - beta_one) * grad
+    second = beta_two * second + (1.0 - beta_two) * grad * grad
+    fix_one = 1.0 - beta_one**STEP
+    fix_two = 1.0 - beta_two**STEP
+    new = weight - learn_rate * (
+        first / fix_one / (jnp.sqrt(second / fix_two) + eps_adam) + decay_rate * weight
+    )
+    return (first, second, new)
+
+
+def adamw_kernel(grads, *refs, sh, per):
+    ins = [refs[3 * n : 3 * n + 3] for n in range(5)]
+    outs = [refs[15 + 3 * n : 18 + 3 * n] for n in range(5)]
+
+    def update(n, group, k, *where):
+        begin = (sum(per[:group]) + k % per[group]) * sh
+        grad = grads[k // per[group], begin : begin + sh, :].astype(f32)
+        weight, first, second = (ref[where] for ref in ins[n])
+        for ref, value in zip(outs[n], adamw(weight, grad, first, second)):
+            ref[where] = value
+
+    every = slice(None)
+    for k in range(9):
+        update(0, 2, k, every, slice(k * 128, (k + 1) * 128))
+    for k in range(6):
+        lanes = slice(k * 128, (k + 1) * 128)
+        update(1, 2, 9 + k, 0, every, lanes)
+        update(1, 1, k, 1, every, lanes)
+        update(3, 1, 6 + k, 0, every, lanes)
+        update(3, 0, k, 1, every, lanes)
+        rows, half = slice((k // 2) * sh, (k // 2 + 1) * sh), slice((k % 2) * 128, (k % 2 + 1) * 128)
+        update(4, 1, 12 + k, 0, rows, half)
+        update(4, 0, 6 + k, 1, rows, half)
+    for k in range(2):
+        lanes = slice(k * 128, (k + 1) * 128)
+        update(2, 1, 18 + k, 0, every, lanes)
+        update(2, 0, 12 + k, 1, every, lanes)
 
 
 def passed_along(value, axis, steps):
@@ -713,71 +826,32 @@
     return value
 
 
-def split_small(value):
-    high = lax.reduce_precision(value, 8, 7)
-    return jnp.concatenate([high.astype(bf16), (value - high).astype(bf16)], 0)
-
-
-def join_small(parts):
-    rows = parts.shape[-2] // 2
-    return parts[..., :rows, :] + parts[..., rows:, :]
-
-
-def reduce_big(grads):
-    part = lax.psum_scatter(grads, "row", scatter_dimension=0, tiled=False)
-    return lax.psum(part, "col").astype(f32)
-
-
-def reduce_last(grads, small):
-    devices, count, lanes = grads.shape
-    cols = lax.axis_size("col")
-    part = count // cols
-    extra = small.shape[0] * 2
-    value = grads.reshape(devices, cols, part, lanes).transpose(1, 0, 2, 3)
-    value = value.reshape(cols, devices * part, lanes)
-    value = jnp.concatenate([value, jnp.broadcast_to(split_small(small), (cols, extra, lanes))], 1)
-    value = lax.all_to_all(value, "col", 0, 0, tiled=True).astype(f32)
-    total = jnp.sum(value, 0)
-    small = join_small(total[devices * part :])
-    value = total[: devices * part].astype(bf16).reshape(devices, part, lanes)
-    value = jnp.concatenate(
-        [value, jnp.broadcast_to(split_small(small), (devices, extra, lanes))], 1
-    )
-    value = lax.all_to_all(value, "row", 0, 0, tiled=True).astype(f32)
-    total = jnp.sum(value, 0)
-    small = join_small(total[part:])
-    main = lax.all_gather(total[:part].astype(bf16), "col", axis=0, tiled=True)
-    return main.astype(f32), small
-
-
-def adamw(weight, grad, first, second):
-    first = beta_one * first + (1.0 - beta_one) * grad
-    second = beta_two * second + (1.0 - beta_two) * grad * grad
-    fix_one = 1.0 - beta_one**STEP
-    fix_two = 1.0 - beta_two**STEP
-    new = weight - learn_rate * (
-        first / fix_one / (jnp.sqrt(second / fix_two) + eps_adam) + decay_rate * weight
-    )
-    return (first, second, new)
-
-
 def on_device(
     stem_map, layout, labels, live,
     conv_weight, input_proj, output_proj, expand_weight, reduce_weight, head_weight, small_params,
     first_conv, first_input, first_output, first_expand, first_reduce, first_head, first_small,
     second_conv, second_input, second_output, second_expand, second_reduce, second_head, second_small,
 ):
-    nr = lax.axis_size("row")
+    nr, nc = lax.axis_size("row"), lax.axis_size("col")
     sh = D // nr
     images = labels.shape[0]
-    padded = -(-images // 16) * 16
-    early, late = run(
+    padded = -(-images // 8) * 8
+    per = [-(-count // nc) for count in (14, 20, 15)]
+    row_index, col_index = lax.axis_index("row"), lax.axis_index("col")
+    parts = [-(-count // nc) * sh for count in (15, 20, 22)]
+    early, late1, late2 = run(
         pack_kernel,
-        [out((15 * sh, 128), bf16), out((21 * sh, D), bf16)],
-        [conv_weight, input_proj, output_proj, expand_weight, reduce_weight, head_weight],
-    )
-    early = lax.all_gather(early, "row", axis=0)
-    late = lax.all_gather(late, "row", axis=0)
+        [out((nr, part, 128), bf16) for part in parts],
+        [
+            col_index.astype(i32)[None], conv_weight.T, input_proj, output_proj, expand_weight, reduce_weight,
+            head_weight,
+        ],
+        [pltpu.VMEM((part * nc, 128), bf16) for part in parts],
+        {0: SMEM},
+    )
+    early = lax.all_to_all(early, "row", 0, 0, tiled=True)
+    early, late = lax.optimization_barrier((early, jnp.concatenate([late1, late2], 1)))
+    late = lax.all_to_all(late, "row", 0, 0, tiled=True)
     norms = small_params[: 12 * D].reshape(12, D)
     start = 12 * D
     ebias = small_params[start : start + LAYERS * FF].reshape(LAYERS, FF)
@@ -790,68 +864,73 @@
         [out((geo.pieces, HEADS * geo.across, 128)) for geo in (One, Two)],
         [jnp.pad(pos_bias, ((0, 0), (0, WIN - 169)))],
     )
-    row_first = lax.axis_index("row") * 24
-    col_first = lax.axis_index("col") * 16
-    place = jnp.stack([row_first, col_first, lax.axis_index("row") * sh]).astype(i32)
+    place = jnp.stack([row_index * 24, col_index * 16, row_index * sh]).astype(i32)
     lay_one = layout.reshape(5, 24, 8, 2).transpose(1, 3, 2, 0).reshape(384, 5)
     lay_two = layout.reshape(5, 12, 2, 8, 2).transpose(2, 4, 1, 3, 0).reshape(384, 5)
     above = passed_along(stem_map[-1:], "row", 1)
     rim = jnp.concatenate([above[:, -1:], stem_map[:, -1:]], 0)
     rim = jnp.broadcast_to(passed_along(rim, "col", 1), (49, 8, 128))
-    patches, conv_out, hidden0, query1, keyval1, edges1 = run(
+    patches = run(
+        patch_kernel,
+        [out((384, 1152), bf16)],
+        [place, stem_map.reshape(1536, 128), above.reshape(32, 128), rim.reshape(392, 128), lay_one],
+        [pltpu.VMEM((1536, 128), f32), pltpu.VMEM((32, 128), f32)],
+        {0: SMEM},
+    )[0]
+    early = lax.all_gather(early, "col", axis=0)
+    late, patches = lax.optimization_barrier((late, patches))
+    late1 = lax.all_gather(late[:, : parts[1]], "col", axis=0)
+    late2 = lax.all_gather(late[:, parts[1] :], "col", axis=0)
+    conv_out, hidden0, query1, keyval1, edge_left, edge_right = run(
         front_kernel,
         [
-            out((384, 1152), bf16), out((384, D)), out((384, D)), out((384, D), bf16),
-            out((2, 192, 2 * D), bf16), out((2, 192, 2 * D), bf16),
+            out((384, D)), out((384, D)), out((384, D), bf16), out((2, 192, 2 * D), bf16),
+            out((192, 2 * D), bf16), out((192, 2 * D), bf16),
         ],
-        [place, stem_map.reshape(1536, 128), above.reshape(32, 128), rim.reshape(392, 128), lay_one, early, norms],
-        [pltpu.VMEM((1536, 128), f32), pltpu.VMEM((32, 128), f32)],
-        {0: SMEM},
-    )
-    left1 = passed_along(edges1[1], "col", 1)
-    right1 = passed_along(edges1[0], "col", -1)
+        [patches, early, norms],
+    )
+    left1 = passed_along(edge_right, "col", 1)
+    right1 = passed_along(edge_left, "col", -1)
     ring = lambda rows: jnp.concatenate([keyval1[:, rows], left1[None, rows], right1[None, rows]], 0)
     below1 = passed_along(ring(slice(0, 48)), "row", -1)
     above1 = passed_along(ring(slice(144, 192)), "row", 1)
     anywhere = pl.BlockSpec(memory_space=pl.ANY)
-    block = lambda count: [pltpu.VMEM((count, nr, 3 * sh, D), bf16), pltpu.SemaphoreType.DMA((count,))]
+    block = lambda group: [pltpu.VMEM(group.shape, bf16), pltpu.SemaphoreType.DMA((1,))]
 
     def tiles(geo, back):
-        rows, keys = HEADS * geo.queries, geo.keys
+        square = (HEADS * geo.queries, geo.keys)
         shape = (4, 288, 2 * D) if geo is One else (3, 4, 192, 2 * D)
-        square = (rows, keys)
+        wide, narrow = pltpu.VMEM(square, f32), pltpu.VMEM(square, bf16)
         if not back:
-            return [pltpu.VMEM(shape, bf16), pltpu.VMEM(square, f32), pltpu.VMEM(square, f32), pltpu.VMEM(square, bf16)]
+            return [pltpu.VMEM(shape, bf16), wide, wide, narrow]
         return [
-            pltpu.VMEM(shape, bf16), pltpu.VMEM(square, f32), pltpu.VMEM(square, f32), pltpu.VMEM(square, f32),
-            pltpu.VMEM(square, f32), pltpu.VMEM(square, bf16), pltpu.VMEM(square, bf16), pltpu.VMEM(shape, f32),
+            pltpu.VMEM(shape, bf16), wide, wide, wide, wide, narrow, narrow, pltpu.VMEM(shape, f32),
             pltpu.VMEM((384, D), bf16), pltpu.VMEM((384, D), f32),
             pltpu.VMEM((geo.pieces, HEADS * geo.across, 128), f32),
         ]
 
+    token5 = lambda width: pltpu.VMEM((12, 2, 2, 8, width), f32)
+    tokens, rows48, ext = out((384, D)), out((4, 48, 2 * D), bf16), out((4, 192, 2 * D), bf16)
+    tokens_low = out((384, D), bf16)
     near1 = [keyval1, left1, right1, above1, below1, first_one]
-    att1, middle1, last1, query2, keyval2 = run(
+    att1, middle1, last1, query2, keyval2, up2, down2 = run(
         first_block_kernel,
-        [
-            out((384, D), bf16), out((384, D)), out((384, D)), out((384, D), bf16),
-            out((4, 96, 2 * D), bf16),
-        ],
-        [place, lay_one, hidden0, query1, *near1, late, norms, ebias],
-        tiles(One, False) + block(4),
+        [tokens_low, tokens, tokens, tokens_low, out((4, 96, 2 * D), bf16), rows48, rows48],
+        [place, lay_one, hidden0, query1, *near1, late1, norms, ebias],
+        tiles(One, False) + block(late1),
         {0: SMEM, 10: anywhere},
     )
-    below2 = passed_along(keyval2[:, :48], "row", -1)
-    above2 = passed_along(keyval2[:, 48:], "row", 1)
+    below2 = passed_along(up2, "row", -1)
+    above2 = passed_along(down2, "row", 1)
     own2 = jnp.concatenate([above2, keyval2, below2], 1)
     left2 = passed_along(own2, "col", 1)
     right2 = passed_along(own2, "col", -1)
-    token5 = lambda width: pltpu.VMEM((12, 2, 2, 8, width), f32)
     near2 = [own2, left2, right2, first_two]
     att2, middle2, last2, sums = run(
         second_block_kernel,
-        [out((384, D), bf16), out((384, D)), out((384, D)), out((padded, D + 128))],
-        [place, lay_two, lay_one, last1, query2, *near2, late, norms, ebias],
-        tiles(Two, False) + [pltpu.VMEM((384, D), f32), token5(D)] + block(3),
+        [tokens_low, tokens, tokens, out((padded + 8, max(D, -(-padded // 128) * 128)))],
+        [place, lay_two, lay_one, last1, query2, *near2, late2, norms, ebias],
+        tiles(Two, False) + [pltpu.VMEM((384, D), f32), token5(D)] + block(late2),
         {0: SMEM, 9: anywhere},
     )
     sums = sum_all(sums)
@@ -861,86 +940,84 @@
     ) = run(
         second_back_kernel,
         [
-            out((8, 128)), out((sh, 1024)), out((1, 1024)), out((384, D)), out((nr, 7 * sh, D), bf16),
-            out((4, D)), out((1, FF)), out((HEADS, WIN)), out((384, D), bf16),
-            out((4, 192, 2 * D)), out((4, 192, 2 * D), bf16), out((4, 192, 2 * D), bf16),
+            out((8, 128)), out((sh, 1024)), out((1, 1024)), tokens, out((nc, per[0] * D, 128), bf16),
+            out((4, D)), out((1, FF)), out((HEADS, WIN)), tokens_low,
+            out((4, 192, 2 * D)), ext, ext,
         ],
         [
             place, lay_two, lay_one, sums, pad_images(labels), pad_images(live.astype(f32)), hbias,
-            last2, middle2, att2, query2, *near2, late, norms, ebias,
+            last2, middle2, att2, query2, *near2, late2, norms, ebias,
         ],
-        tiles(Two, True) + [token5(D)] + block(4),
+        tiles(Two, True) + [token5(D)] + block(late2),
         {0: SMEM, 15: anywhere},
     )
     from_right = passed_along(dleft2, "col", -1)
     from_left = passed_along(dright2, "col", 1)
-    whole2 = down2 + from_right.astype(f32) + from_left.astype(f32)
-    lower2 = passed_along(whole2[:, :48].astype(bf16), "row", -1)
-    upper2 = passed_along(whole2[:, 144:].astype(bf16), "row", 1)
-    big2 = reduce_big(grads2)
+    rim2 = lambda rows: (
+        down2[:, rows] + from_left[:, rows].astype(f32) + from_right[:, rows].astype(f32)
+    ).astype(bf16)
+    lower2 = passed_along(rim2(slice(0, 48)), "row", -1)
+    upper2 = passed_along(rim2(slice(144, 192)), "row", 1)
+    grads2 = lax.psum_scatter(grads2, "col", scatter_dimension=0, tiled=False)
     dhid, grads1, dnorms1, debias1, dpos1, dquery1, inner1, up1, down1 = run(
         first_back_kernel,
         [
-            out((384, D)), out((nr, 10 * sh, D), bf16), out((4, D)), out((1, FF)), out((HEADS, WIN)),
-            out((384, D), bf16), out((4, 192, 2 * D)), out((4, 48, 2 * D), bf16), out((4, 48, 2 * D), bf16),
+            tokens, out((nc, per[1] * D, 128), bf16), out((4, D)), out((1, FF)), out((HEADS, WIN)),
+            tokens_low, out((4, 192, 2 * D)), rows48, rows48,
         ],
         [
-            place, lay_one, dhid, dquery2, whole2[:, 48:144], upper2, lower2, last1, middle1, att1, query1,
-            *near1, late, norms, ebias,
+            place, lay_one, dhid, dquery2, down2, from_left, from_right, upper2, lower2, last1, middle1, att1, query1,
+            *near1, late1, norms, ebias,
         ],
-        tiles(One, True) + [token5(2 * D)] + block(4),
-        {0: SMEM, 17: anywhere},
-    )
-    big1 = reduce_big(grads1)
+        tiles(One, True) + [token5(2 * D)] + block(late1),
+        {0: SMEM, 19: anywhere},
+    )
     lower1 = passed_along(up1, "row", -1)
     upper1 = passed_along(down1, "row", 1)
+    grads1 = lax.psum_scatter(grads1, "col", scatter_dimension=0, tiled=False)
     sides = inner1[2:] + jnp.concatenate(
         [upper1[2:].astype(f32), jnp.zeros((2, 96, 2 * D), f32), lower1[2:].astype(f32)], 1
     )
     sides = sides.astype(bf16)
     edge_right = passed_along(sides[0], "col", -1)
     edge_left = passed_along(sides[1], "col", 1)
-    grads0, dnorms0 = run(
+    grads0, _ = run(
         front_back_kernel,
-        [out((nr, 15 * sh, 128), bf16), out((4, D))],
+        [out((nc, per[2] * D + 2 * SMALL_ROWS, 128), bf16), out((SMALL_ROWS, 128))],
         [
             dhid, dquery1, inner1, upper1, lower1, edge_left, edge_right, hidden0, conv_out, patches,
-            early, norms,
+            early, norms, dnorms1, dnorms2, debias1, debias2, dpos1, dpos2,
         ],
     )
-    small = jnp.concatenate(
-        [
-            dnorms0.reshape(-1), dnorms1.reshape(-1), dnorms2.reshape(-1), debias1[0], debias2[0],
-            dpos1[:, :169].reshape(-1), dpos2[:, :169].reshape(-1),
-        ]
-    )
-    width = small.shape[0]
-    small = jnp.pad(small, (0, 8192 - width)).reshape(64, 128)
-    main, small = reduce_last(grads0, small)
-    small = small.reshape(-1)[:width]
-    front = 12 * D + LAYERS * FF
-    grad_small = jnp.concatenate([small[:front], grad_hbias[0, :CLASSES], small[front:]])
-    cols = lambda x, first, count: jnp.concatenate(
-        [x[k * sh : (k + 1) * sh] for k in range(first, first + count)], 1
-    )
-    grads = (
-        cols(main, 0, 9).T,
-        jnp.stack([cols(main, 9, 6), cols(big1, 0, 3)]),
-        jnp.stack([big1[9 * sh :], big2[6 * sh :]]),
-        jnp.stack([cols(big1, 3, 3), cols(big2, 0, 3)]),
-        jnp.stack([big1[6 * sh : 9 * sh], big2[3 * sh : 6 * sh]]),
-        grad_head[:, :CLASSES],
-        grad_small,
-    )
-    params = (
-        conv_weight, input_proj, output_proj, expand_weight, reduce_weight, head_weight, small_params,
-    )
-    firsts = (first_conv, first_input, first_output, first_expand, first_reduce, first_head, first_small)
-    seconds = (
-        second_conv, second_input, second_output, second_expand, second_reduce, second_head, second_small,
-    )
-    res = [adamw(w, g, m, v) for w, g, m, v in zip(params, grads, firsts, seconds)]
-    return (loss[0, 0], *[entry for triple in res for entry in triple])
+    grads0 = lax.all_to_all(grads0, "col", 0, 0, tiled=True)
+    grads0 = run(
+        between_kernel,
+        [out((nr, sum(per) * sh + 2 * SMALL_ROWS, 128), bf16)],
+        [grads2, grads1, grads0],
+    )[0]
+    grads0 = lax.all_to_all(grads0, "row", 0, 0, tiled=True)
+    mine, small = run(
+        last_sum_kernel,
+        [out((sum(per) * sh, 128), bf16), out((SMALL_ROWS, 128))],
+        [grads0],
+    )
+    grads = lax.all_gather(mine, "col", axis=0)
+    wide = [
+        conv_weight.T, first_conv.T, second_conv.T, input_proj, first_input, second_input,
+        output_proj, first_output, second_output, expand_weight, first_expand, second_expand,
+        reduce_weight, first_reduce, second_reduce,
+    ]
+    new = run(
+        functools.partial(adamw_kernel, sh=sh, per=per), [out(x.shape) for x in wide], [grads, *wide]
+    )
+    new = [x.T for x in new[:3]] + list(new[3:])
+    pos = [
+        jnp.concatenate([small[k : k + 8], small[k + 8 : k + 16, : 169 - 128]], 1).reshape(-1)
+        for k in (40, 56)
+    ]
+    grad_small = jnp.concatenate([small[:36].reshape(-1), grad_hbias[0, :CLASSES], *pos])
+    head = adamw(head_weight, grad_head[:, :CLASSES], first_head, second_head)
+    return (loss[0, 0], *new, *head, *adamw(small_params, grad_small, first_small, second_small))
 
 
 def solution(mesh):

time: 450 us -> 338 us (0.75)
  waiting for transfers between devices: 202 us -> 98 us
  blocking collectives: 42.6 us -> 7.22 us
  starting transfers between devices: 74.1 us -> 101 us
  Pallas kernels: 77.3 us -> 88.1 us
  other arithmetic: 15.2 us -> 7.42 us
    reduce_scatter x2, waiting for transfers between devices: 93.4 us -> 0.01 us  [the longest x1 0.01 us: on_device(): grads2 = lax.psum_scatter(grads2, 'col', scatter_dimension=0, tiled=False)]
    all_gather x2 -> x1, blocking collectives: 42.6 us -> 7.22 us  [on_device(): grads = lax.all_gather(mine, 'col', axis=0)]
    psum x1 -> x0, waiting for transfers between devices: 32.6 us -> none  [reduce_big(): return lax.psum(part, 'col').astype(f32)]
    all_to_all x2 -> x4, waiting for transfers between devices: 30.1 us -> 56 us  [the longest x1 26.3 us: on_device(): grads0 = lax.all_to_all(grads0, 'row', 0, 0, tiled=True)]
    all_to_all x2 -> x4, starting transfers between devices: 11.1 us -> 26.1 us  [the longest x1 9.83 us: on_device(): grads0 = lax.all_to_all(grads0, 'col', 0, 0, tiled=True)]
    pallas_call x8 -> x12, Pallas kernels: 77.3 us -> 88.1 us  [run(): pl.pallas_call(kernel, out_shape=outs, in_specs=in_specs, out_specs=[pl.B...]
    ppermute x18, starting transfers between devices: 50.1 us -> 56.4 us  [passed_along(): lax.ppermute(value, axis, [(source, source + steps) for source in range(l...]
    ppermute x5, waiting for transfers between devices: 16.8 us -> 10.8 us  [sum_all(): lax.ppermute(value, axis, [(i, i ^ step) for i in range(count)])]
  transfers between devices with their start and end apart: 29 -> 32, of which waited for: 20 -> 23; matrix products, arithmetic and copies ran while one was open for 4% -> 5% of each run, Pallas kernels for 2% -> 13%
where the time goes in v2:
time: 338 us; the launch traced here: 337 us
  starting transfers between devices  101 us (30%)
  waiting for transfers between devices  98 us (29%)
  Pallas kernels  88.1 us (26%)
  local copies, waits for them, and re-layouts  20.5 us (6%)
  between operations  14.3 us (4%)
  other arithmetic  7.42 us (2%)
  blocking collectives  7.22 us (2%)
    pallas_call x12, Pallas kernels, run(): pl.pallas_call(kernel, out_shape=outs, in_specs=in_specs, out_specs=[pl.B...  88.1 us
    ppermute x18, starting transfers between devices, passed_along(): lax.ppermute(value, axis, [(source, source + steps) for source in range(l...  56.4 us
    ppermute x18, waiting for transfers between devices, passed_along(): lax.ppermute(value, axis, [(source, source + steps) for source in range(l...  30.2 us
    all_to_all x1, waiting for transfers between devices, on_device(): grads0 = lax.all_to_all(grads0, 'row', 0, 0, tiled=True)  26.3 us
    ppermute x5, starting transfers between devices, sum_all(): lax.ppermute(value, axis, [(i, i ^ step) for i in range(count)])  18.2 us
    all_to_all x1, waiting for transfers between devices, on_device(): grads0 = lax.all_to_all(grads0, 'col', 0, 0, tiled=True)  16.2 us
    ppermute x5, waiting for transfers between devices, sum_all(): lax.ppermute(value, axis, [(i, i ^ step) for i in range(count)])  10.8 us
    all_to_all x1, starting transfers between devices, on_device(): grads0 = lax.all_to_all(grads0, 'col', 0, 0, tiled=True)  9.83 us
  transfers between devices with their start and end apart: 32, of which 23 were waited for; matrix products, arithmetic and copies ran while one was open for 5% of the time, Pallas kernels for 13%

profile of v2, /device:TPU:0, one launch (start us, length us, event | category | flops | bytes accessed | tf_op | source)
XLA Modules:
  0.0 336.5 jit_solution(3554611123311628371)
XLA Ops:
  9.4 7.3 %all-to-all-start = ((bf16[8,128,128]{2,1,0:T(8,128)(2,1)}), bf16[8,128,128]{2,1,0:T(8,128)(2,1)S(1)}, u32[]{:S(2)}, u32[]{:S(2)}) async-start(bf16[8,128,128]{2,1,0:T(8,128)(2,1)} %get-tuple-element.87), calls=%async_computation | async-start | bytes 524288 | tf_op jit(solution)/shard_map/all_to_all | solution.py:852
  18.8 6.8 %all-to-all-done = bf16[8,128,128]{2,1,0:T(8,128)(2,1)S(1)} async-done(((bf16[8,128,128]{2,1,0:T(8,128)(2,1)}), bf16[8,128,128]{2,1,0:T(8,128)(2,1)S(1)}, u32[]{:S(2)}, u32[]{:S(2)}) %all-to-all-start) | async-done | bytes 262176 | tf_op jit(solution)/shard_map/all_to_all | solution.py:852
  30.7 3.9 %collective-permute-start = (bf16[1,32,128]{2,1,0:T(8,128)(2,1)S(1)}, bf16[1,32,128]{2,1,0:T(8,128)(2,1)S(1)}, u32[]{:S(2)}, u32[]{:S(2)}) collective-permute-start(bf16[1,32,128]{2,1,0:T(8,128)(2,1)S(1)} %slice.102), channel_id=1, source_target_pairs={{0,4},{4,8},{8,12},{12,16},{16,20},{20,24},{24,28},{1,5},{5,9},{9,... | collective-permute-start | bytes 24584 | tf_op jit(solution)/shard_map/ppermute | solution.py:816
  41.8 6.6 %all-to-all-done.1 = bf16[8,352,128]{2,1,0:T(8,128)(2,1)S(1)} async-done(((bf16[8,352,128]{2,1,0:T(8,128)(2,1)}), bf16[8,352,128]{2,1,0:T(8,128)(2,1)S(1)}, u32[]{:S(2)}, u32[]{:S(2)}) %all-to-all-start.1) | async-done | bytes 720928 | tf_op jit(solution)/shard_map/all_to_all | solution.py:854
  62.4 5.6 %collective-permute-start.4 = (bf16[4,48,512]{2,1,0:T(8,128)(2,1)S(1)}, bf16[4,48,512]{2,1,0:T(8,128)(2,1)S(1)}, u32[]{:S(2)}, u32[]{:S(2)}) collective-permute-start(bf16[4,48,512]{2,1,0:T(8,128)(2,1)S(1)} %pad_maximum_fusion.1), channel_id=1, source_target_pairs={{0,4},{4,8},{8,12},{12,16},{16,20},{20,24},{24,28},{1,5},{5,9},{9,... | collective-permute-start | bytes 589832 | tf_op jit(solution)/shard_map/ppermute | solution.py:816
  73.9 10.4 %shard_map.412 = (bf16[384,256]{1,0:T(8,128)(2,1)}, f32[384,256]{1,0:T(8,128)}, f32[384,256]{1,0:T(8,128)}, bf16[384,256]{1,0:T(8,128)(2,1)}, bf16[4,96,512]{2,1...) custom-call(s32[3]{0:T(128)} %pad_add_fusion.place, s32[384,5]{1,0:T(8,128)} %bitcast.54, ...), custom_call_target="tpu_custom_call" | custom-call | bytes 4194304 | tf_op jit(solution)/shard_map/pallas_call | solution.py:315
  84.3 5.0 %collective-permute-start.6 = (bf16[4,48,512]{2,1,0:T(8,128)(2,1)}, bf16[4,48,512]{2,1,0:T(8,128)(2,1)S(1)}, u32[]{:S(2)}, u32[]{:S(2)}) collective-permute-start(bf16[4,48,512]{2,1,0:T(8,128)(2,1)} %get-tuple-element.102), channel_id=1, source_target_pairs={{0,4},{4,8},{8,12},{12,16},{16,20},{20,24},{24,28},{1,5},{5,9},{9,... | collective-permute-start | bytes 589832 | tf_op jit(solution)/shard_map/ppermute | solution.py:816
  93.8 4.3 %collective-permute-done.7 = bf16[4,48,512]{2,1,0:T(8,128)(2,1)S(1)} collective-permute-done((bf16[4,48,512]{2,1,0:T(8,128)(2,1)}, bf16[4,48,512]{2,1,0:T(8,128)(2,1)S(1)}, u32[]{:S(2)}, u32[]{:S(2)}) %collective-permute-start.7) | collective-permute-done | bytes 196640 | tf_op jit(solution)/shard_map/ppermute | solution.py:816
  98.1 8.9 %collective-permute-start.8 = (bf16[4,192,512]{2,1,0:T(8,128)(2,1)S(1)}, bf16[4,192,512]{2,1,0:T(8,128)(2,1)S(1)}, u32[]{:S(2)}, u32[]{:S(2)}) collective-permute-start(bf16[4,192,512]{2,1,0:T(8,128)(2,1)S(1)} %constant_dynamic-update-slice_fusion.own), channel_id=1, source_target_pairs={{0,1},{1,2},{2,3},{4,5},{5,6},{6,7},{8,9},{9,10},{10,11},{12,13},{... | collective-permute-start | bytes 2359304 | tf_op jit(solution)/shard_map/ppermute | solution.py:816
  112.8 12.5 %shard_map.413 = (bf16[384,256]{1,0:T(8,128)(2,1)}, f32[384,256]{1,0:T(8,128)}, f32[384,256]{1,0:T(8,128)}, f32[64,256]{1,0:T(8,128)}) custom-call(s32[3]{0:T(128)} %pad_add_fusion.place, s32[384,5]{1,0:T(8,128)} %bitcast.64, s32[384,5]{1,0:T(8,128)} %bitcast.55, f32[384,256]{1,0:T(8,128)} %get-tuple-element.100.hidden, ...), custom_call_target="tpu_custom_call" | custom-call | bytes 4194304 | tf_op jit(solution)/shard_map/pallas_call | solution.py:315
  125.3 9.7 %collective-permute-start.10 = (f32[64,256]{1,0:T(8,128)}, f32[64,256]{1,0:T(8,128)S(1)}, u32[]{:S(2)}, u32[]{:S(2)}) collective-permute-start(f32[64,256]{1,0:T(8,128)} %get-tuple-element.106), channel_id=1, source_target_pairs={{0,1},{1,0},{2,3},{3,2},{4,5},{5,4},{6,7},{7,6},{8,9},{9,8},{10,11... | collective-permute-start | bytes 196616 | tf_op jit(solution)/shard_map/ppermute | solution.py:824
  137.1 4.3 %collective-permute-done.11 = f32[64,256]{1,0:T(8,128)S(1)} collective-permute-done((f32[64,256]{1,0:T(8,128)S(1)}, f32[64,256]{1,0:T(8,128)S(1)}, u32[]{:S(2)}, u32[]{:S(2)}) %collective-permute-start.11) | collective-permute-done | bytes 65568 | tf_op jit(solution)/shard_map/ppermute | solution.py:824
  157.9 20.9 %shard_map.414 = (f32[8,128]{1,0:T(8,128)}, f32[32,1024]{1,0:T(8,128)}, f32[1,1024]{1,0:T(1,128)}, f32[384,256]{1,0:T(8,128)}, bf16[4,1024,128]{2,1,0:T(8,128)(2...) custom-call(s32[3]{0:T(128)} %pad_add_fusion.place, ...), custom_call_target="tpu_custom_call" | custom-call | bytes 4194304 | tf_op jit(solution)/shard_map/pallas_call | solution.py:315
  186.6 4.0 %collective-permute-start.17 = (bf16[4,48,512]{2,1,0:T(8,128)(2,1)S(1)}, bf16[4,48,512]{2,1,0:T(8,128)(2,1)S(1)}, u32[]{:S(2)}, u32[]{:S(2)}) collective-permute-start(bf16[4,48,512]{2,1,0:T(8,128)(2,1)S(1)} %get-tuple-element.159), channel_id=1, source_target_pairs={{0,4},{4,8},{8,12},{12,16},{16,20},{20,24},{24,28},{1,5},{5,9},{9,... | collective-permute-start | bytes 589832 | tf_op jit(solution)/shard_map/ppermute | solution.py:816
  193.8 4.4 %collective-permute-done.18.from_below = bf16[4,48,512]{2,1,0:T(8,128)(2,1)S(1)} collective-permute-done((bf16[4,48,512]{2,1,0:T(8,128)(2,1)S(1)}, bf16[4,48,512]{2,1,0:T(8,128)(2,1)S(1)}, u32[]{:S(2)}, u32[]{:S(2)}) %collective-permute-start.18) | collective-permute-done | bytes 196640 | tf_op jit(solution)/shard_map/ppermute | solution.py:816
  198.9 19.0 %shard_map.415 = (f32[384,256]{1,0:T(8,128)}, bf16[4,1280,128]{2,1,0:T(8,128)(2,1)}, f32[4,256]{1,0:T(4,128)}, f32[1,768]{1,0:T(1,128)}, f32[8,176]{1,0:T(8,128)...) custom-call(s32[3]{0:T(128)} %pad_add_fusion.place, ...), custom_call_target="tpu_custom_call" | custom-call | bytes 4194304 | tf_op jit(solution)/shard_map/pallas_call | solution.py:315
  219.5 4.7 %collective-permute-start.19 = (bf16[4,48,512]{2,1,0:T(8,128)(2,1)}, bf16[4,48,512]{2,1,0:T(8,128)(2,1)S(1)}, u32[]{:S(2)}, u32[]{:S(2)}) collective-permute-start(bf16[4,48,512]{2,1,0:T(8,128)(2,1)} %get-tuple-element.123), channel_id=1, source_target_pairs={{0,4},{4,8},{8,12},{12,16},{16,20},{20,24},{24,28},{1,5},{5,9},{9,... | collective-permute-start | bytes 589832 | tf_op jit(solution)/shard_map/ppermute | solution.py:816
  228.9 9.5 %collective-permute-start.21 = (bf16[192,512]{1,0:T(8,128)(2,1)S(1)}, bf16[192,512]{1,0:T(8,128)(2,1)S(1)}, u32[]{:S(2)}, u32[]{:S(2)}) collective-permute-start(bf16[192,512]{1,0:T(8,128)(2,1)S(1)} %get-tuple-element.161), channel_id=1, source_target_pairs={{0,1},{1,2},{2,3},{4,5},{5,6},{6,7},{8,9},{9,10},{10,11},{12,13},{... | collective-permute-start | bytes 589832 | tf_op jit(solution)/shard_map/ppermute | solution.py:816
  243.9 5.5 %shard_map.416 = (bf16[4,1184,128]{2,1,0:T(8,128)(2,1)}, f32[80,128]{1,0:T(8,128)}) custom-call(f32[384,256]{1,0:T(8,128)} %get-tuple-element.120.dhid_in, bf16[384,256]{1,0:T(8,128)(2,1)} %get-tuple-element.121.dquery, f32[4,192,512]{2,1,0:T(8,128)} %get-tuple-element.122.inner, bf16[4,48,512]{2,1,0:T(8,128)(2,1)} %copy-done.15, ...), custom_call_target="tpu_custom_call" | custom-call | bytes 4194304 | tf_op jit(solution)/shard_map/pallas_call | solution.py:315
  249.3 9.8 %all-to-all-start.2 = ((bf16[4,1184,128]{2,1,0:T(8,128)(2,1)}), bf16[4,1184,128]{2,1,0:T(8,128)(2,1)S(1)}, u32[]{:S(2)}, u32[]{:S(2)}) async-start(bf16[4,1184,128]{2,1,0:T(8,128)(2,1)} %get-tuple-element.132), calls=%async_computation.4 | async-start | bytes 2424832 | tf_op jit(solution)/shard_map/all_to_all | solution.py:992
  259.2 16.2 %all-to-all-done.2.parts = bf16[4,1184,128]{2,1,0:T(8,128)(2,1)S(1)} async-done(((bf16[4,1184,128]{2,1,0:T(8,128)(2,1)}), bf16[4,1184,128]{2,1,0:T(8,128)(2,1)S(1)}, u32[]{:S(2)}, u32[]{:S(2)}) %all-to-all-start.2) | async-done | bytes 1212448 | tf_op jit(solution)/shard_map/all_to_all | solution.py:992
  279.2 5.4 %all-to-all-start.3 = ((bf16[8,576,128]{2,1,0:T(8,128)(2,1)}), bf16[8,576,128]{2,1,0:T(8,128)(2,1)S(1)}, u32[]{:S(2)}, u32[]{:S(2)}) async-start(bf16[8,576,128]{2,1,0:T(8,128)(2,1)} %shard_map.417), calls=%async_computation.5 | async-start | bytes 2359296 | tf_op jit(solution)/shard_map/all_to_all | solution.py:998
  286.7 26.3 %all-to-all-done.3.parts = bf16[8,576,128]{2,1,0:T(8,128)(2,1)S(1)} async-done(((bf16[8,576,128]{2,1,0:T(8,128)(2,1)}), bf16[8,576,128]{2,1,0:T(8,128)(2,1)S(1)}, u32[]{:S(2)}, u32[]{:S(2)}) %all-to-all-start.3) | async-done | bytes 1179680 | tf_op jit(solution)/shard_map/all_to_all | solution.py:998
  318.4 7.2 %all-gather.3 = bf16[1664,128]{1,0:T(8,128)(2,1)} all-gather(bf16[416,128]{1,0:T(8,128)(2,1)} %get-tuple-element.133), channel_id=5, replica_groups=mesh['row'=8,'col'=4] {'col'}, dimensions={0}, use_global_device_ids=true | all-gather | bytes 532480 | tf_op jit(solution)/shard_map/all_gather | solution.py:1004
  (179 shorter events, 104.0 us)
Async XLA Ops:
  9.4 16.2 %all-to-all-start = ((bf16[8,128,128]{2,1,0:T(8,128)(2,1)}), bf16[8,128,128]{2,1,0:T(8,128)(2,1)S(1)}, u32[]{:S(2)}, u32[]{:S(2)}) async-start(bf16[8,128,128]{2,1,0:T(8,128)(2,1)} %get-tuple-element.87), calls=%async_computation | async-start | bytes 524288 | tf_op jit(solution)/shard_map/all_to_all | solution.py:852
  16.7 34.0 %all-gather.8.cloned.1.call-start = ((), (), s32[]{:S(2)}) async-start(), calls=%async_computation.8 | async-start | bytes 1310720 | tf_op jit(solution)/shard_map/all_gather | solution.py:880
  26.4 22.0 %all-to-all-start.1 = ((bf16[8,352,128]{2,1,0:T(8,128)(2,1)}), bf16[8,352,128]{2,1,0:T(8,128)(2,1)S(1)}, u32[]{:S(2)}, u32[]{:S(2)}) async-start(bf16[8,352,128]{2,1,0:T(8,128)(2,1)} %pad_maximum_fusion), calls=%async_computation.1 | async-start | bytes 1441792 | tf_op jit(solution)/shard_map/all_to_all | solution.py:854
  30.0 43.9 %all-gather.10.cloned.1.call-start = ((), (), s32[]{:S(2)}) async-start(), calls=%async_computation.9 | async-start | bytes 1638400 | tf_op jit(solution)/shard_map/all_gather | solution.py:882
  30.7 5.2 %collective-permute-start = (bf16[1,32,128]{2,1,0:T(8,128)(2,1)S(1)}, bf16[1,32,128]{2,1,0:T(8,128)(2,1)S(1)}, u32[]{:S(2)}, u32[]{:S(2)}) collective-permute-start(bf16[1,32,128]{2,1,0:T(8,128)(2,1)S(1)} %slice.102), channel_id=1, source_target_pairs={{0,4},{4,8},{8,12},{12,16},{16,20},{20,24},{24,28},{1,5},{5,9},{9,... | collective-permute-start | bytes 24584 | tf_op jit(solution)/shard_map/ppermute | solution.py:816
  49.1 60.2 %all-gather.12.cloned.1.call-start = ((), (), s32[]{:S(2)}) async-start(), calls=%async_computation.10 | async-start | bytes 1966080 | tf_op jit(solution)/shard_map/all_gather | solution.py:883
  50.6 208.6 %reduce-scatter.3.cloned.1.call-start = ((), (), s32[]{:S(2)}) async-start(), calls=%async_computation.6 | async-start | bytes 1310720 | tf_op jit(solution)/shard_map/reduce_scatter | solution.py:961
  55.7 5.3 %collective-permute-start.3 = (bf16[192,512]{1,0:T(8,128)(2,1)}, bf16[192,512]{1,0:T(8,128)(2,1)S(1)}, u32[]{:S(2)}, u32[]{:S(2)}) collective-permute-start(bf16[192,512]{1,0:T(8,128)(2,1)} %get-tuple-element.97), channel_id=1, source_target_pairs={{1,0},{2,1},{3,2},{5,4},{6,5},{7,6},{9,8},{10,9},{11,10},{13,12},{... | collective-permute-start | bytes 589832 | tf_op jit(solution)/shard_map/ppermute | solution.py:816
  61.0 11.6 %collective-permute-start.5 = (bf16[4,48,512]{2,1,0:T(8,128)(2,1)S(1)}, bf16[4,48,512]{2,1,0:T(8,128)(2,1)S(1)}, u32[]{:S(2)}, u32[]{:S(2)}) collective-permute-start(bf16[4,48,512]{2,1,0:T(8,128)(2,1)S(1)} %pad_maximum_fusion.2), channel_id=1, source_target_pairs={{4,0},{8,4},{12,8},{16,12},{20,16},{24,20},{28,24},{5,1},{9,5},{13... | collective-permute-start | bytes 589832 | tf_op jit(solution)/shard_map/ppermute | solution.py:816
  62.4 10.6 %collective-permute-start.4 = (bf16[4,48,512]{2,1,0:T(8,128)(2,1)S(1)}, bf16[4,48,512]{2,1,0:T(8,128)(2,1)S(1)}, u32[]{:S(2)}, u32[]{:S(2)}) collective-permute-start(bf16[4,48,512]{2,1,0:T(8,128)(2,1)S(1)} %pad_maximum_fusion.1), channel_id=1, source_target_pairs={{0,4},{4,8},{8,12},{12,16},{16,20},{20,24},{24,28},{1,5},{5,9},{9,... | collective-permute-start | bytes 589832 | tf_op jit(solution)/shard_map/ppermute | solution.py:816
  84.3 8.5 %collective-permute-start.6 = (bf16[4,48,512]{2,1,0:T(8,128)(2,1)}, bf16[4,48,512]{2,1,0:T(8,128)(2,1)S(1)}, u32[]{:S(2)}, u32[]{:S(2)}) collective-permute-start(bf16[4,48,512]{2,1,0:T(8,128)(2,1)} %get-tuple-element.102), channel_id=1, source_target_pairs={{0,4},{4,8},{8,12},{12,16},{16,20},{20,24},{24,28},{1,5},{5,9},{9,... | collective-permute-start | bytes 589832 | tf_op jit(solution)/shard_map/ppermute | solution.py:816
  89.3 8.8 %collective-permute-start.7 = (bf16[4,48,512]{2,1,0:T(8,128)(2,1)}, bf16[4,48,512]{2,1,0:T(8,128)(2,1)S(1)}, u32[]{:S(2)}, u32[]{:S(2)}) collective-permute-start(bf16[4,48,512]{2,1,0:T(8,128)(2,1)} %get-tuple-element.104), channel_id=1, source_target_pairs={{4,0},{8,4},{12,8},{16,12},{20,16},{24,20},{28,24},{5,1},{9,5},{13... | collective-permute-start | bytes 589832 | tf_op jit(solution)/shard_map/ppermute | solution.py:816
  98.1 11.2 %collective-permute-start.8 = (bf16[4,192,512]{2,1,0:T(8,128)(2,1)S(1)}, bf16[4,192,512]{2,1,0:T(8,128)(2,1)S(1)}, u32[]{:S(2)}, u32[]{:S(2)}) collective-permute-start(bf16[4,192,512]{2,1,0:T(8,128)(2,1)S(1)} %constant_dynamic-update-slice_fusion.own), channel_id=1, source_target_pairs={{0,1},{1,2},{2,3},{4,5},{5,6},{6,7},{8,9},{9,10},{10,11},{12,13},{... | collective-permute-start | bytes 2359304 | tf_op jit(solution)/shard_map/ppermute | solution.py:816
  125.3 10.8 %collective-permute-start.10 = (f32[64,256]{1,0:T(8,128)}, f32[64,256]{1,0:T(8,128)S(1)}, u32[]{:S(2)}, u32[]{:S(2)}) collective-permute-start(f32[64,256]{1,0:T(8,128)} %get-tuple-element.106), channel_id=1, source_target_pairs={{0,1},{1,0},{2,3},{3,2},{4,5},{5,4},{6,7},{7,6},{8,9},{9,8},{10,11... | collective-permute-start | bytes 196616 | tf_op jit(solution)/shard_map/ppermute | solution.py:824
  146.6 5.4 %collective-permute-start.13 = (f32[64,256]{1,0:T(8,128)S(1)}, f32[64,256]{1,0:T(8,128)S(1)}, u32[]{:S(2)}, u32[]{:S(2)}) collective-permute-start(f32[64,256]{1,0:T(8,128)S(1)} %add.74), channel_id=1, source_target_pairs={{0,8},{4,12},{8,0},{12,4},{16,24},{20,28},{24,16},{28,20},{1,9},{5... | collective-permute-start | bytes 196616 | tf_op jit(solution)/shard_map/ppermute | solution.py:824
  152.0 5.2 %collective-permute-start.14 = (f32[64,256]{1,0:T(8,128)S(1)}, f32[64,256]{1,0:T(8,128)S(1)}, u32[]{:S(2)}, u32[]{:S(2)}) collective-permute-start(f32[64,256]{1,0:T(8,128)S(1)} %add.75), channel_id=1, source_target_pairs={{0,16},{4,20},{8,24},{12,28},{16,0},{20,4},{24,8},{28,12},{1,17},{... | collective-permute-start | bytes 196616 | tf_op jit(solution)/shard_map/ppermute | solution.py:824
  178.8 96.6 %reduce-scatter.5.cloned.1.call-start = ((), (), s32[]{:S(2)}) async-start(), calls=%async_computation.7 | async-start | bytes 1638400 | tf_op jit(solution)/shard_map/reduce_scatter | solution.py:977
  186.6 7.2 %collective-permute-start.17 = (bf16[4,48,512]{2,1,0:T(8,128)(2,1)S(1)}, bf16[4,48,512]{2,1,0:T(8,128)(2,1)S(1)}, u32[]{:S(2)}, u32[]{:S(2)}) collective-permute-start(bf16[4,48,512]{2,1,0:T(8,128)(2,1)S(1)} %get-tuple-element.159), channel_id=1, source_target_pairs={{0,4},{4,8},{8,12},{12,16},{16,20},{20,24},{24,28},{1,5},{5,9},{9,... | collective-permute-start | bytes 589832 | tf_op jit(solution)/shard_map/ppermute | solution.py:816
  190.7 7.6 %collective-permute-start.18 = (bf16[4,48,512]{2,1,0:T(8,128)(2,1)S(1)}, bf16[4,48,512]{2,1,0:T(8,128)(2,1)S(1)}, u32[]{:S(2)}, u32[]{:S(2)}) collective-permute-start(bf16[4,48,512]{2,1,0:T(8,128)(2,1)S(1)} %get-tuple-element.158), channel_id=1, source_target_pairs={{4,0},{8,4},{12,8},{16,12},{20,16},{24,20},{28,24},{5,1},{9,5},{13... | collective-permute-start | bytes 589832 | tf_op jit(solution)/shard_map/ppermute | solution.py:816
  218.0 8.1 %collective-permute-start.20 = (bf16[4,48,512]{2,1,0:T(8,128)(2,1)}, bf16[4,48,512]{2,1,0:T(8,128)(2,1)S(1)}, u32[]{:S(2)}, u32[]{:S(2)}) collective-permute-start(bf16[4,48,512]{2,1,0:T(8,128)(2,1)} %get-tuple-element.124), channel_id=1, source_target_pairs={{4,0},{8,4},{12,8},{16,12},{20,16},{24,20},{28,24},{5,1},{9,5},{13... | collective-permute-start | bytes 589832 | tf_op jit(solution)/shard_map/ppermute | solution.py:816
  219.5 9.2 %collective-permute-start.19 = (bf16[4,48,512]{2,1,0:T(8,128)(2,1)}, bf16[4,48,512]{2,1,0:T(8,128)(2,1)S(1)}, u32[]{:S(2)}, u32[]{:S(2)}) collective-permute-start(bf16[4,48,512]{2,1,0:T(8,128)(2,1)} %get-tuple-element.123), channel_id=1, source_target_pairs={{0,4},{4,8},{8,12},{12,16},{16,20},{20,24},{24,28},{1,5},{5,9},{9,... | collective-permute-start | bytes 589832 | tf_op jit(solution)/shard_map/ppermute | solution.py:816
  228.9 10.8 %collective-permute-start.21 = (bf16[192,512]{1,0:T(8,128)(2,1)S(1)}, bf16[192,512]{1,0:T(8,128)(2,1)S(1)}, u32[]{:S(2)}, u32[]{:S(2)}) collective-permute-start(bf16[192,512]{1,0:T(8,128)(2,1)S(1)} %get-tuple-element.161), channel_id=1, source_target_pairs={{0,1},{1,2},{2,3},{4,5},{5,6},{6,7},{8,9},{9,10},{10,11},{12,13},{... | collective-permute-start | bytes 589832 | tf_op jit(solution)/shard_map/ppermute | solution.py:816
  249.3 26.1 %all-to-all-start.2 = ((bf16[4,1184,128]{2,1,0:T(8,128)(2,1)}), bf16[4,1184,128]{2,1,0:T(8,128)(2,1)S(1)}, u32[]{:S(2)}, u32[]{:S(2)}) async-start(bf16[4,1184,128]{2,1,0:T(8,128)(2,1)} %get-tuple-element.132), calls=%async_computation.4 | async-start | bytes 2424832 | tf_op jit(solution)/shard_map/all_to_all | solution.py:992
  279.2 33.8 %all-to-all-start.3 = ((bf16[8,576,128]{2,1,0:T(8,128)(2,1)}), bf16[8,576,128]{2,1,0:T(8,128)(2,1)S(1)}, u32[]{:S(2)}, u32[]{:S(2)}) async-start(bf16[8,576,128]{2,1,0:T(8,128)(2,1)} %shard_map.417), calls=%async_computation.5 | async-start | bytes 2359296 | tf_op jit(solution)/shard_map/all_to_all | solution.py:998
  (41 other events, 445.2 us)
Sparse Core Ops, SparseCore 0:
  26.5 15.7 all-gather.7
  49.3 24.5 all-gather.9
  75.4 20.1 all-gather.11
  178.9 24.8 reduce-scatter.2
  218.1 36.0 reduce-scatter.4

commit v3 on v2

--- a/solution.py
+++ b/solution.py
@@ -27,7 +27,7 @@
 f32 = jnp.float32
 i32 = jnp.int32
 MASKED = -1e30
-VMEM = 56 * 1024 * 1024
+MIB = 1024 * 1024
 
 
 def nn(a, b):
@@ -308,7 +308,40 @@
     return [parts[:, g >> 1, g & 1].reshape(96, x.shape[-1]) for g in range(4)]
 
 
-def run(kernel, outs, ins, scratch=(), specs=None, flops=0):
+EVEN_ROW, EVEN_COL = 3, 4
+
+
+def send(place, even, first, second, after, before):
+    for ref, when_even, when_odd in ((first, after, before), (second, before, after)):
+
+        @pl.when(place[even] == 1)
+        def _(ref=ref, value=when_even):
+            ref[...] = value()
+
+        @pl.when(place[even] == 0)
+        def _(ref=ref, value=when_odd):
+            ref[...] = value()
+
+
+def received(place, even, first, second):
+    flag = place[even].astype(f32)
+    one, two = first.astype(f32), second.astype(f32)
+    return two * flag + one * (1.0 - flag), one * flag + two * (1.0 - flag)
+
+
+def store_received(place, even, first, second, before, after):
+    @pl.when(place[even] == 1)
+    def _():
+        before(second)
+        after(first)
+
+    @pl.when(place[even] == 0)
+    def _():
+        before(first)
+        after(second)
+
+
+def run(kernel, outs, ins, scratch=(), specs=None, vmem=16):
     in_specs = [pl.BlockSpec(memory_space=pltpu.VMEM)] * len(ins)
     for index, spec in (specs or {}).items():
         in_specs[index] = spec
@@ -318,8 +351,8 @@
         in_specs=in_specs,
         out_specs=[pl.BlockSpec(memory_space=pltpu.VMEM)] * len(outs),
         scratch_shapes=list(scratch),
-        compiler_params=pltpu.CompilerParams(vmem_limit_bytes=VMEM),
-        cost_estimate=pl.CostEstimate(flops=flops, bytes_accessed=4 << 20, transcendentals=0),
+        compiler_params=pltpu.CompilerParams(vmem_limit_bytes=vmem * MIB),
+        cost_estimate=pl.CostEstimate(flops=0, bytes_accessed=4 << 20, transcendentals=0),
     )(*ins)
 
 
@@ -330,9 +363,9 @@
     return jax.ShapeDtypeStruct(shape, dtype)
 
 
-def pack_kernel(col, conv, qkv, proj, exp, red, head, *refs):
+def pack_kernel(col, conv, qkv, proj, exp, red, head, *refs, across):
     sh = qkv.shape[1]
-    outs, groups = refs[:3], refs[3:]
+    outs, groups = refs[:2], refs[2:]
 
     def cols(x):
         return [x[:, k * 128 : (k + 1) * 128] for k in range(x.shape[1] // 128)]
@@ -346,16 +379,20 @@
         cols(proj[0]) + cols(exp[0]) + reds(red[0]) + cols(qkv[1]),
         cols(proj[1]) + cols(exp[1]) + reds(red[1]) + cols(head[:, :896]) + [tail],
     )
-    for result, group, values in zip(outs, groups, blocks):
+    begin = 0
+    for index, (group, values) in enumerate(zip(groups, blocks)):
         for k, value in enumerate(values):
             group[k * sh : (k + 1) * sh, :] = value.astype(bf16)
         empty = group.shape[0] - len(values) * sh
         if empty:
             group[len(values) * sh :, :] = jnp.zeros((empty, 128), bf16)
-        part = result.shape[1]
+        result = outs[min(index, 1)]
+        begin = begin if index == 2 else 0
+        part = group.shape[0] // across
         mine = group[pl.ds(pl.multiple_of(col[0] * part, 16), part), :]
         for row in range(result.shape[0]):
-            result[row] = mine
+            result[row, begin : begin + part, :] = mine
+        begin += part
 
 
 def weight_of(blocks, first, count):
@@ -415,7 +452,7 @@
             patches[:, lanes] = value.astype(bf16)
 
 
-def front_kernel(patches, early, norms, conv_out, hidden, query, keyval, edge_left, edge_right):
+def front_kernel(place, patches, early, norms, conv_out, hidden, query, keyval, first, second):
     conv = nt(patches[...], weight_of(early, 0, 9))
     conv_out[...] = conv
     h = norm(conv, norms[0:2, :])
@@ -430,16 +467,95 @@
     sub = lax.broadcasted_iota(i32, zero.shape, 1)
     left = jnp.where(sub < 4, zero, pltpu.roll(one, 4, 1))
     right = jnp.where(sub < 4, pltpu.roll(zero, 4, 1), one)
-    edge_left[...] = left.reshape(192, 2 * D).astype(bf16)
-    edge_right[...] = right.reshape(192, 2 * D).astype(bf16)
-
-
-def gather_keys_one(keyval, left, right, above, below, pieces):
-    for p in range(4):
-        own = keyval[p] if p < 2 else (left, right)[p - 2][...]
-        pieces[p, 0:48, :] = above[p]
-        pieces[p, 48:240, :] = own
-        pieces[p, 240:288, :] = below[p]
+    send(
+        place, EVEN_COL, first, second,
+        lambda: right.reshape(192, 2 * D).astype(bf16), lambda: left.reshape(192, 2 * D).astype(bf16),
+    )
+
+
+def ring_kernel(place, keyval, first, second, row_first, row_second):
+    def put(ref, begin):
+        rows = slice(begin, begin + 48)
+        ref[0] = keyval[0, rows, :]
+        ref[1] = keyval[1, rows, :]
+
+        def left(source):
+            ref[2] = source[rows, :]
+
+        def right(source):
+            ref[3] = source[rows, :]
+
+        store_received(place, EVEN_COL, first, second, left, right)
+
+    @pl.when(place[EVEN_ROW] == 1)
+    def _():
+        put(row_first, 144)
+        put(row_second, 0)
+
+    @pl.when(place[EVEN_ROW] == 0)
+    def _():
+        put(row_first, 0)
+        put(row_second, 144)
+
+
+def gather_keys_one(place, keyval, col_first, col_second, row_first, row_second, pieces):
+    pieces[0, 48:240, :] = keyval[0]
+    pieces[1, 48:240, :] = keyval[1]
+
+    def into(index, rows):
+        def put(source):
+            pieces[index, rows, :] = source[...]
+
+        return put
+
+    every = slice(None)
+    middle = slice(48, 240)
+    store_received(place, EVEN_COL, col_first, col_second, into(2, middle), into(3, middle))
+    store_received(
+        place, EVEN_ROW, row_first, row_second, into(every, slice(0, 48)), into(every, slice(240, 288))
+    )
+
+
+def gather_keys_two(place, own, first, second, pieces):
+    pieces[0] = own[...]
+
+    def into(index):
+        def put(source):
+            pieces[index] = source[...]
+
+        return put
+
+    store_received(place, EVEN_COL, first, second, into(1), into(2))
+
+
+def extend_kernel(place, keyval, first, second, result):
+    result[:, 48:144, :] = keyval[...]
+
+    def above(source):
+        result[:, 0:48, :] = source[...]
+
+    def below(source):
+        result[:, 144:192, :] = source[...]
+
+    store_received(place, EVEN_ROW, first, second, above, below)
+
+
+def rim_kernel(place, own, first, second, row_first, row_second):
+    def total(begin):
+        rows = slice(begin, begin + 48)
+        value = own[:, rows, :] + first[:, rows, :].astype(f32) + second[:, rows, :].astype(f32)
+        return value.astype(bf16)
+
+    send(place, EVEN_ROW, row_first, row_second, lambda: total(144), lambda: total(0))
+
+
+def sides_kernel(place, inner, first, second, col_first, col_second):
+    def total(p):
+        above, below = received(place, EVEN_ROW, first[p], second[p])
+        rows = [inner[p, 0:48, :] + above, inner[p, 48:144, :], inner[p, 144:192, :] + below]
+        return jnp.concatenate(rows, 0).astype(bf16)
+
+    send(place, EVEN_COL, col_first, col_second, lambda: total(3), lambda: total(2))
 
 
 def feed_forward(hidden, norms, w_exp, w_red, bias):
@@ -459,12 +575,12 @@
 
 
 def first_block_kernel(
-    place, lay, hidden, query, keyval, left, right, above, below, first_table, late, norms, ebias,
-    att, middle, last, query2, keyval2, up, down,
+    place, lay, hidden, query, keyval, cola, colb, rowa, rowb, first_table, late, norms, ebias,
+    att, middle, last, query2, keyval2, first, second,
     pieces, table, score, prob, group, sem,
 ):
     arrived = fetch(late, group, sem)
-    gather_keys_one(keyval, left, right, above, below, pieces)
+    gather_keys_one(place, keyval, cola, colb, rowa, rowb, pieces)
     spread_table(One, first_table, table)
     attend(One, place, lay, query, pieces, table, att, score, prob)
     arrived()
@@ -476,10 +592,10 @@
     mixed = nn(low, weight_of(group, QKV, 6))
     for g, part in enumerate(grouped(mixed)):
         query2[g * 96 : (g + 1) * 96, :] = part[:, :D].astype(bf16)
-        low = part[:, D:].astype(bf16)
-        keyval2[g] = low
-        up[g] = low[:48]
-        down[g] = low[48:]
+        keyval2[g] = part[:, D:].astype(bf16)
+    send(
+        place, EVEN_ROW, first, second, lambda: keyval2[:, 48:, :], lambda: keyval2[:, :48, :]
+    )
 
 
 def slot_onehot(slots, images):
@@ -493,14 +609,12 @@
 
 
 def second_block_kernel(
-    place, lay, slots, hidden, query, own, left, right, first_table, late, norms, ebias,
+    place, lay, slots, hidden, query, own, cola, colb, first_table, late, norms, ebias,
     att, middle, last, sums,
     pieces, table, score, prob, att_group, att_token, group, sem,
 ):
     arrived = fetch(late, group, sem)
-    pieces[0] = own[...]
-    pieces[1] = left[...]
-    pieces[2] = right[...]
+    gather_keys_two(place, own, cola, colb, pieces)
     spread_table(Two, first_table, table)
     attend(Two, place, lay, query, pieces, table, att_group, score, prob)
     ungroup(att_group[...], att_token)
@@ -557,15 +671,13 @@
 
 
 def second_back_kernel(
-    place, lay, slots, sums, labels, live, hbias, hidden, middle, att, query, own, left, right,
+    place, lay, slots, sums, labels, live, hbias, hidden, middle, att, query, own, cola, colb,
     first_table, late, norms, ebias,
-    loss, grad_head, grad_hbias, dhidden, grads, dnorms, debias, dpos, dquery, down, dleft, dright,
+    loss, grad_head, grad_hbias, dhidden, grads, dnorms, debias, dpos, dquery, down, first, second,
     pieces, table, dtable, score, dscore_f, prob, dscore, dpieces, datt, dq_group, dfirst, dq_token, group, sem,
 ):
     arrived = fetch(late, group, sem)
-    pieces[0] = own[...]
-    pieces[1] = left[...]
-    pieces[2] = right[...]
+    gather_keys_two(place, own, cola, colb, pieces)
     spread_table(Two, first_table, table)
     images = sums.shape[0] - 8
     total = sums[:images, :D]
@@ -621,24 +733,26 @@
     ungroup(dq_group[...], dq_token)
     dquery[...] = dq_token[...].reshape(384, D).astype(bf16)
     down[...] = dpieces[0]
-    dleft[...] = dpieces[1].astype(bf16)
-    dright[...] = dpieces[2].astype(bf16)
+    send(
+        place, EVEN_COL, first, second,
+        lambda: dpieces[2].astype(bf16), lambda: dpieces[1].astype(bf16),
+    )
     dpos[...] = gather_table(Two, dtable, dfirst)
 
 
 def first_back_kernel(
-    place, lay, dhid_in, dquery2, dkv, from_left, from_right, from_above, from_below, hidden, middle, att, query, keyval,
-    left, right, above, below, first_table, late, norms, ebias,
-    dhidden, grads, dnorms, debias, dpos, dquery, inner, up, down,
+    place, lay, dhid_in, dquery2, dkv, dcola, dcolb, drowa, drowb, hidden, middle, att, query, keyval,
+    cola, colb, rowa, rowb, first_table, late, norms, ebias,
+    dhidden, grads, dnorms, debias, dpos, dquery, inner, first, second,
     pieces, table, dtable, score, dscore_f, prob, dscore, dpieces, datt, dq, dfirst, dkv_token, group, sem,
 ):
     arrived = fetch(late, group, sem)
-    gather_keys_one(keyval, left, right, above, below, pieces)
+    gather_keys_one(place, keyval, cola, colb, rowa, rowb, pieces)
     spread_table(One, first_table, table)
     for g in range(4):
         rows = slice(48, 144)
-        total = dkv[g, rows, :] + from_left[g, rows, :].astype(f32) + from_right[g, rows, :].astype(f32)
-        total += jnp.concatenate([from_above[g], from_below[g]], 0).astype(f32)
+        total = dkv[g, rows, :] + dcola[g, rows, :].astype(f32) + dcolb[g, rows, :].astype(f32)
+        total += jnp.concatenate(received(place, EVEN_ROW, drowa[g], drowb[g]), 0)
         dkv_token[:, g >> 1, g & 1] = total.reshape(12, 8, 2 * D)
     dmixed = jnp.concatenate(
         [dquery2[...], dkv_token[...].reshape(384, 2 * D).astype(bf16)], 1
@@ -669,9 +783,11 @@
         score, dscore_f, prob, dscore,
     )
     dquery[...] = dq[...].astype(bf16)
-    up[...] = dpieces[:, 0:48, :].astype(bf16)
     inner[...] = dpieces[:, 48:240, :]
-    down[...] = dpieces[:, 240:288, :].astype(bf16)
+    send(
+        place, EVEN_ROW, first, second,
+        lambda: dpieces[:, 240:288, :].astype(bf16), lambda: dpieces[:, 0:48, :].astype(bf16),
+    )
     dpos[...] = gather_table(One, dtable, dfirst)
 
 
@@ -679,17 +795,18 @@
 
 
 def front_back_kernel(
-    dhid_in, dquery, inner, from_above, from_below, edge_left, edge_right, hidden, conv, patches,
-    early, norms, dnorms1, dnorms2, debias1, debias2, dpos1, dpos2,
+    place, dhid_in, dquery, inner, drowa, drowb, dcola, dcolb, hidden, conv, patches, early,
+    norms, dnorms1, dnorms2, debias1, debias2, dpos1, dpos2,
     grads, small,
 ):
-    left = edge_left[...].astype(f32).reshape(24, 8, 2 * D)
-    right = edge_right[...].astype(f32).reshape(24, 8, 2 * D)
+    left, right = received(place, EVEN_COL, dcola[...], dcolb[...])
+    left, right = left.reshape(24, 8, 2 * D), right.reshape(24, 8, 2 * D)
     sub = lax.broadcasted_iota(i32, left.shape, 1)
 
     def whole(p):
-        top = inner[p, 0:48, :] + from_above[p].astype(f32)
-        bottom = inner[p, 144:192, :] + from_below[p].astype(f32)
+        above, below = received(place, EVEN_ROW, drowa[p], drowb[p])
+        top = inner[p, 0:48, :] + above
+        bottom = inner[p, 144:192, :] + below
         return jnp.concatenate([top, inner[p, 48:144, :], bottom], 0).reshape(24, 8, 2 * D)
 
     zero = whole(0) + jnp.where(sub < 4, left, pltpu.roll(right, 4, 1))
@@ -810,19 +927,34 @@
         update(2, 0, 12 + k, 1, every, lanes)
 
 
-def passed_along(value, axis, steps):
+def onward(value, axis):
     count = lax.axis_size(axis)
-    leading, last = (max(0, -steps), min(count, count - steps))
-    return lax.ppermute(value, axis, [(source, source + steps) for source in range(leading, last)])
+    return lax.ppermute(value, axis, [(i, (i + 1) % count) for i in range(count)])
+
+
+def swaps(first, second, axis):
+    count = lax.axis_size(axis)
+    pairs = [[(i, i + 1) for i in range(begin, count - 1, 2)] for begin in (0, 1)]
+    both = [low + [(j, i) for i, j in low] for low in pairs]
+    return lax.ppermute(first, axis, both[0]), lax.ppermute(second, axis, both[1])
 
 
 def sum_all(value):
     for axis in ("col", "row"):
         count = lax.axis_size(axis)
         step = 1
+
+        def other(flip):
+            return lax.ppermute(value, axis, [(i, i ^ flip) for i in range(count)])
+
         while step < count:
-            value = value + lax.ppermute(value, axis, [(i, i ^ step) for i in range(count)])
-            step *= 2
+            if 4 * step <= count:
+                near, far, both = other(step), other(2 * step), other(3 * step)
+                value = (value + near) + (far + both)
+                step *= 4
+            else:
+                value = value + other(step)
+                step *= 2
     return value
 
 
@@ -839,19 +971,18 @@
     per = [-(-count // nc) for count in (14, 20, 15)]
     row_index, col_index = lax.axis_index("row"), lax.axis_index("col")
     parts = [-(-count // nc) * sh for count in (15, 20, 22)]
-    early, late1, late2 = run(
-        pack_kernel,
-        [out((nr, part, 128), bf16) for part in parts],
+    early, late = run(
+        functools.partial(pack_kernel, across=nc),
+        [out((nr, parts[0], 128), bf16), out((nr, parts[1] + parts[2], 128), bf16)],
         [
             col_index.astype(i32)[None], conv_weight.T, input_proj, output_proj, expand_weight, reduce_weight,
             head_weight,
         ],
         [pltpu.VMEM((part * nc, 128), bf16) for part in parts],
         {0: SMEM},
+        56,
     )
     early = lax.all_to_all(early, "row", 0, 0, tiled=True)
-    early, late = lax.optimization_barrier((early, jnp.concatenate([late1, late2], 1)))
-    late = lax.all_to_all(late, "row", 0, 0, tiled=True)
     norms = small_params[: 12 * D].reshape(12, D)
     start = 12 * D
     ebias = small_params[start : start + LAYERS * FF].reshape(LAYERS, FF)
@@ -864,12 +995,13 @@
         [out((geo.pieces, HEADS * geo.across, 128)) for geo in (One, Two)],
         [jnp.pad(pos_bias, ((0, 0), (0, WIN - 169)))],
     )
-    place = jnp.stack([row_index * 24, col_index * 16, row_index * sh]).astype(i32)
+    place = [row_index * 24, col_index * 16, row_index * sh, (row_index + 1) % 2, (col_index + 1) % 2]
+    place = jnp.stack(place).astype(i32)
     lay_one = layout.reshape(5, 24, 8, 2).transpose(1, 3, 2, 0).reshape(384, 5)
     lay_two = layout.reshape(5, 12, 2, 8, 2).transpose(2, 4, 1, 3, 0).reshape(384, 5)
-    above = passed_along(stem_map[-1:], "row", 1)
+    above = onward(stem_map[-1:], "row")
     rim = jnp.concatenate([above[:, -1:], stem_map[:, -1:]], 0)
-    rim = jnp.broadcast_to(passed_along(rim, "col", 1), (49, 8, 128))
+    rim = jnp.broadcast_to(onward(rim, "col"), (49, 8, 128))
     patches = run(
         patch_kernel,
         [out((384, 1152), bf16)],
@@ -877,23 +1009,21 @@
         [pltpu.VMEM((1536, 128), f32), pltpu.VMEM((32, 128), f32)],
         {0: SMEM},
     )[0]
+    late, _, _ = lax.optimization_barrier((late, above, early))
     early = lax.all_gather(early, "col", axis=0)
-    late, patches = lax.optimization_barrier((late, patches))
+    late = lax.all_to_all(late, "row", 0, 0, tiled=True)
+    rows48, edge = out((4, 48, 2 * D), bf16), out((192, 2 * D), bf16)
+    conv_out, hidden0, query1, keyval1, *edges = run(
+        front_kernel,
+        [out((384, D)), out((384, D)), out((384, D), bf16), out((2, 192, 2 * D), bf16), edge, edge],
+        [place, patches, early, norms],
+        specs={0: SMEM},
+    )
+    late, _ = lax.optimization_barrier((late, edges))
     late1 = lax.all_gather(late[:, : parts[1]], "col", axis=0)
     late2 = lax.all_gather(late[:, parts[1] :], "col", axis=0)
-    conv_out, hidden0, query1, keyval1, edge_left, edge_right = run(
-        front_kernel,
-        [
-            out((384, D)), out((384, D)), out((384, D), bf16), out((2, 192, 2 * D), bf16),
-            out((192, 2 * D), bf16), out((192, 2 * D), bf16),
-        ],
-        [patches, early, norms],
-    )
-    left1 = passed_along(edge_right, "col", 1)
-    right1 = passed_along(edge_left, "col", -1)
-    ring = lambda rows: jnp.concatenate([keyval1[:, rows], left1[None, rows], right1[None, rows]], 0)
-    below1 = passed_along(ring(slice(0, 48)), "row", -1)
-    above1 = passed_along(ring(slice(144, 192)), "row", 1)
+    cols1 = swaps(*edges, "col")
+    rows1 = swaps(*run(ring_kernel, [rows48] * 2, [place, keyval1, *cols1], specs={0: SMEM}), "row")
     anywhere = pl.BlockSpec(memory_space=pl.ANY)
     block = lambda group: [pltpu.VMEM(group.shape, bf16), pltpu.SemaphoreType.DMA((1,))]
 
@@ -910,33 +1040,32 @@
         ]
 
     token5 = lambda width: pltpu.VMEM((12, 2, 2, 8, width), f32)
-    tokens, rows48, ext = out((384, D)), out((4, 48, 2 * D), bf16), out((4, 192, 2 * D), bf16)
+    tokens, ext = out((384, D)), out((4, 192, 2 * D), bf16)
     tokens_low = out((384, D), bf16)
-    near1 = [keyval1, left1, right1, above1, below1, first_one]
-    att1, middle1, last1, query2, keyval2, up2, down2 = run(
+    near1 = [keyval1, *cols1, *rows1, first_one]
+    att1, middle1, last1, query2, keyval2, *edges = run(
         first_block_kernel,
         [tokens_low, tokens, tokens, tokens_low, out((4, 96, 2 * D), bf16), rows48, rows48],
         [place, lay_one, hidden0, query1, *near1, late1, norms, ebias],
         tiles(One, False) + block(late1),
         {0: SMEM, 10: anywhere},
-    )
-    below2 = passed_along(up2, "row", -1)
-    above2 = passed_along(down2, "row", 1)
-    own2 = jnp.concatenate([above2, keyval2, below2], 1)
-    left2 = passed_along(own2, "col", 1)
-    right2 = passed_along(own2, "col", -1)
-    near2 = [own2, left2, right2, first_two]
+        56,
+    )
+    rows2 = swaps(*edges, "row")
+    own2 = run(extend_kernel, [ext], [place, keyval2, *rows2], specs={0: SMEM})[0]
+    near2 = [own2, *swaps(own2, own2, "col"), first_two]
     att2, middle2, last2, sums = run(
         second_block_kernel,
         [tokens_low, tokens, tokens, out((padded + 8, max(D, -(-padded // 128) * 128)))],
         [place, lay_two, lay_one, last1, query2, *near2, late2, norms, ebias],
         tiles(Two, False) + [pltpu.VMEM((384, D), f32), token5(D)] + block(late2),
         {0: SMEM, 9: anywhere},
+        56,
     )
     sums = sum_all(sums)
     pad_images = lambda x: jnp.pad(x, (0, padded - images))[:, None]
     (
-        loss, grad_head, grad_hbias, dhid, grads2, dnorms2, debias2, dpos2, dquery2, down2, dleft2, dright2,
+        loss, grad_head, grad_hbias, dhid, grads2, dnorms2, debias2, dpos2, dquery2, down2, *edges,
     ) = run(
         second_back_kernel,
         [
@@ -950,44 +1079,36 @@
         ],
         tiles(Two, True) + [token5(D)] + block(late2),
         {0: SMEM, 15: anywhere},
-    )
-    from_right = passed_along(dleft2, "col", -1)
-    from_left = passed_along(dright2, "col", 1)
-    rim2 = lambda rows: (
-        down2[:, rows] + from_left[:, rows].astype(f32) + from_right[:, rows].astype(f32)
-    ).astype(bf16)
-    lower2 = passed_along(rim2(slice(0, 48)), "row", -1)
-    upper2 = passed_along(rim2(slice(144, 192)), "row", 1)
+        56,
+    )
+    dcols2 = swaps(*edges, "col")
+    drows2 = swaps(*run(rim_kernel, [rows48] * 2, [place, down2, *dcols2], specs={0: SMEM}), "row")
     grads2 = lax.psum_scatter(grads2, "col", scatter_dimension=0, tiled=False)
-    dhid, grads1, dnorms1, debias1, dpos1, dquery1, inner1, up1, down1 = run(
+    dhid, grads1, dnorms1, debias1, dpos1, dquery1, inner1, *edges = run(
         first_back_kernel,
         [
             tokens, out((nc, per[1] * D, 128), bf16), out((4, D)), out((1, FF)), out((HEADS, WIN)),
             tokens_low, out((4, 192, 2 * D)), rows48, rows48,
         ],
         [
-            place, lay_one, dhid, dquery2, down2, from_left, from_right, upper2, lower2, last1, middle1, att1, query1,
+            place, lay_one, dhid, dquery2, down2, *dcols2, *drows2, last1, middle1, att1, query1,
             *near1, late1, norms, ebias,
         ],
         tiles(One, True) + [token5(2 * D)] + block(late1),
         {0: SMEM, 19: anywhere},
-    )
-    lower1 = passed_along(up1, "row", -1)
-    upper1 = passed_along(down1, "row", 1)
+        56,
+    )
+    drows1 = swaps(*edges, "row")
     grads1 = lax.psum_scatter(grads1, "col", scatter_dimension=0, tiled=False)
-    sides = inner1[2:] + jnp.concatenate(
-        [upper1[2:].astype(f32), jnp.zeros((2, 96, 2 * D), f32), lower1[2:].astype(f32)], 1
-    )
-    sides = sides.astype(bf16)
-    edge_right = passed_along(sides[0], "col", -1)
-    edge_left = passed_along(sides[1], "col", 1)
+    dcols1 = swaps(*run(sides_kernel, [edge] * 2, [place, inner1, *drows1], specs={0: SMEM}), "col")
     grads0, _ = run(
         front_back_kernel,
         [out((nc, per[2] * D + 2 * SMALL_ROWS, 128), bf16), out((SMALL_ROWS, 128))],
         [
-            dhid, dquery1, inner1, upper1, lower1, edge_left, edge_right, hidden0, conv_out, patches,
+            place, dhid, dquery1, inner1, *drows1, *dcols1, hidden0, conv_out, patches,
             early, norms, dnorms1, dnorms2, debias1, debias2, dpos1, dpos2,
         ],
+        specs={0: SMEM},
     )
     grads0 = lax.all_to_all(grads0, "col", 0, 0, tiled=True)
     grads0 = run(

time: 338 us -> 309 us (0.914)
  starting transfers between devices: 101 us -> 72.4 us
  blocking collectives: 7.22 us -> 22.9 us
  Pallas kernels: 88.1 us -> 79.4 us
  waiting for transfers between devices: 98 us -> 93.9 us
  other arithmetic: 7.42 us -> 3.79 us
    ppermute x23 -> x25, starting transfers between devices: 74.7 us -> 47 us  [the longest x8 23.5 us: swaps(): lax.ppermute(first, axis, both[0])]
    all_to_all x0 -> x1, blocking collectives: none -> 16.4 us  [on_device(): early = lax.all_to_all(early, 'row', 0, 0, tiled=True)]
    pallas_call x12 -> x16, Pallas kernels: 88.1 us -> 79.4 us  [run(): pl.pallas_call(kernel, out_shape=outs, in_specs=in_specs, out_specs=[pl.B...]
    all_gather x1, waiting for transfers between devices: 0.95 us -> 8.37 us  [on_device(): late1 = lax.all_gather(late[:, :parts[1]], 'col', axis=0)]
    all_to_all x1 -> x0, starting transfers between devices: 7.25 us -> none  [on_device(): early = lax.all_to_all(early, 'row', 0, 0, tiled=True)]
    all_to_all x1 -> x0, waiting for transfers between devices: 6.85 us -> none  [on_device(): early = lax.all_to_all(early, 'row', 0, 0, tiled=True)]
    ppermute x23 -> x25, waiting for transfers between devices: 41 us -> 35.4 us  [the longest x8 16.6 us: swaps(): lax.ppermute(first, axis, both[0])]
    unnamed x66 -> x132, local copies, waits for them, and re-layouts: 6.42 us -> 11.6 us
  transfers between devices with their start and end apart: 32 -> 33, of which waited for: 23 -> 20; matrix products, arithmetic and copies ran while one was open for 5% -> 3% of each run, Pallas kernels for 13% -> 13%
where the time goes in v3:
time: 309 us; the launch traced here: 307 us
  waiting for transfers between devices  93.9 us (30%)
  Pallas kernels  79.4 us (26%)
  starting transfers between devices  72.4 us (23%)
  blocking collectives  22.9 us (7%)
  local copies, waits for them, and re-layouts  20.4 us (7%)
  between operations  14.7 us (5%)
  other arithmetic  3.79 us (1%)
    pallas_call x16, Pallas kernels, run(): pl.pallas_call(kernel, out_shape=outs, in_specs=in_specs, out_specs=[pl.B...  79.4 us
    all_to_all x1, waiting for transfers between devices, on_device(): grads0 = lax.all_to_all(grads0, 'row', 0, 0, tiled=True)  26.1 us
    ppermute x8, starting transfers between devices, swaps(): lax.ppermute(first, axis, both[0])  23.5 us
    ppermute x7, starting transfers between devices, other(): return lax.ppermute(value, axis, [(i, i ^ flip) for i in range(count)])  16.6 us
    ppermute x8, waiting for transfers between devices, swaps(): lax.ppermute(first, axis, both[0])  16.6 us
    all_to_all x1, blocking collectives, on_device(): early = lax.all_to_all(early, 'row', 0, 0, tiled=True)  16.4 us
    all_to_all x1, waiting for transfers between devices, on_device(): grads0 = lax.all_to_all(grads0, 'col', 0, 0, tiled=True)  16.2 us
    unnamed x132, local copies, waits for them, and re-layouts  11.6 us
  transfers between devices with their start and end apart: 33, of which 20 were waited for; matrix products, arithmetic and copies ran while one was open for 3% of the time, Pallas kernels for 13%

profile of v3, /device:TPU:0, one launch (start us, length us, event | category | flops | bytes accessed | tf_op | source)
XLA Modules:
  0.0 307.4 jit_solution(15705987947130652108)
XLA Ops:
  9.6 16.4 %all_to_all.20 = bf16[8,128,128]{2,1,0:T(8,128)(2,1)} all-to-all(bf16[8,128,128]{2,1,0:T(8,128)(2,1)} %get-tuple-element.90), channel_id=1, replica_groups=mesh['row'=8,'col'=4] {'row'}, dimensions={0} | all-to-all | bytes 524288 | tf_op jit(solution)/shard_map/all_to_all | solution.py:985
  27.5 4.9 %collective-permute-done = bf16[1,32,128]{2,1,0:T(8,128)(2,1)S(1)} collective-permute-done((bf16[1,32,128]{2,1,0:T(8,128)(2,1)S(1)}, bf16[1,32,128]{2,1,0:T(8,128)(2,1)S(1)}, u32[]{:S(2)}, u32[]{:S(2)}) %collective-permute-start) | collective-permute-done | bytes 8224 | tf_op jit(solution)/shard_map/ppermute | solution.py:932
  32.4 4.2 %all-to-all-start.1 = ((bf16[8,352,128]{2,1,0:T(8,128)(2,1)}), bf16[8,352,128]{2,1,0:T(8,128)(2,1)}, u32[]{:S(2)}, u32[]{:S(2)}) async-start(bf16[8,352,128]{2,1,0:T(8,128)(2,1)} %get-tuple-element.100), calls=%async_computation.1 | async-start | bytes 1441792 | tf_op jit(solution)/shard_map/all_to_all | solution.py:1014
  46.0 6.7 %all-to-all-done.1 = bf16[8,352,128]{2,1,0:T(8,128)(2,1)} async-done(((bf16[8,352,128]{2,1,0:T(8,128)(2,1)}), bf16[8,352,128]{2,1,0:T(8,128)(2,1)}, u32[]{:S(2)}, u32[]{:S(2)}) %all-to-all-start.1) | async-done | bytes 720928 | tf_op jit(solution)/shard_map/all_to_all | solution.py:1014
  64.3 8.4 %all-gather.10.cloned.1.call-done = bf16[32,160,128]{2,1,0:T(8,128)(2,1)} async-done(((bf16[8,160,128]{2,1,0:T(8,128)(2,1)}), bf16[32,160,128]{2,1,0:T(8,128)(2,1)}) %all-gather.10.cloned.1.call-update) | async-done | bytes 1310736 | tf_op jit(solution)/shard_map/all_gather | solution.py:1023
  72.7 10.9 %shard_map.413 = (bf16[384,256]{1,0:T(8,128)(2,1)}, f32[384,256]{1,0:T(8,128)}, f32[384,256]{1,0:T(8,128)}, bf16[384,256]{1,0:T(8,128)(2,1)}, bf16[4,96,512]{2,1...) custom-call(s32[5]{0:T(128)} %copy-done.39, s32[384,5]{1,0:T(8,128)} %bitcast.44, ...), custom_call_target="tpu_custom_call" | custom-call | bytes 4194304 | tf_op jit(solution)/shard_map/pallas_call | solution.py:348
  85.7 5.1 %collective-permute-done.6.first = bf16[4,48,512]{2,1,0:T(8,128)(2,1)S(1)} collective-permute-done((bf16[4,48,512]{2,1,0:T(8,128)(2,1)}, bf16[4,48,512]{2,1,0:T(8,128)(2,1)S(1)}, u32[]{:S(2)}, u32[]{:S(2)}) %collective-permute-start.6) | collective-permute-done | bytes 196640 | tf_op jit(solution)/shard_map/ppermute | solution.py:939
  93.2 5.4 %collective-permute-start.8 = (bf16[4,192,512]{2,1,0:T(8,128)(2,1)S(1)}, bf16[4,192,512]{2,1,0:T(8,128)(2,1)}, u32[]{:S(2)}, u32[]{:S(2)}) collective-permute-start(bf16[4,192,512]{2,1,0:T(8,128)(2,1)S(1)} %shard_map.414.own), channel_id=1, source_target_pairs={{0,1},{2,3},{1,0},{3,2},{4,5},{6,7},{5,4},{7,6},{8,9},{10,11},{9,8... | collective-permute-start | bytes 2359304 | tf_op jit(solution)/shard_map/ppermute | solution.py:939
  100.7 12.6 %shard_map.415 = (bf16[384,256]{1,0:T(8,128)(2,1)}, f32[384,256]{1,0:T(8,128)}, f32[384,256]{1,0:T(8,128)}, f32[64,256]{1,0:T(8,128)}) custom-call(s32[5]{0:T(128)} %copy-done.39, s32[384,5]{1,0:T(8,128)} %bitcast.63, s32[384,5]{1,0:T(8,128)} %bitcast.45, f32[384,256]{1,0:T(8,128)} %get-tuple-element.102.hidden, bf16[384,256]{1,0:T(8,128)(2,1)} %get-tuple-element.103.query, ...), custom_call_target="tpu_custom_call" | custom-call | bytes 4194304 | tf_op jit(solution)/shard_map/pallas_call | solution.py:348
  115.1 10.1 %collective-permute-start.11 = (f32[64,256]{1,0:T(8,128)}, f32[64,256]{1,0:T(8,128)S(1)}, u32[]{:S(2)}, u32[]{:S(2)}) collective-permute-start(f32[64,256]{1,0:T(8,128)} %get-tuple-element.108), channel_id=1, source_target_pairs={{0,2},{1,3},{2,0},{3,1},{4,6},{5,7},{6,4},{7,5},{8,10},{9,11},{10,... | collective-permute-start | bytes 196616 | tf_op jit(solution)/shard_map/ppermute | solution.py:948
  125.2 3.3 %collective-permute-done.11 = f32[64,256]{1,0:T(8,128)S(1)} collective-permute-done((f32[64,256]{1,0:T(8,128)}, f32[64,256]{1,0:T(8,128)S(1)}, u32[]{:S(2)}, u32[]{:S(2)}) %collective-permute-start.11) | collective-permute-done | bytes 65568 | tf_op jit(solution)/shard_map/ppermute | solution.py:948
  139.7 4.0 %collective-permute-done.16 = f32[64,256]{1,0:T(8,128)S(1)} collective-permute-done((f32[64,256]{1,0:T(8,128)S(1)}, f32[64,256]{1,0:T(8,128)S(1)}, u32[]{:S(2)}, u32[]{:S(2)}) %collective-permute-start.16) | collective-permute-done | bytes 65568 | tf_op jit(solution)/shard_map/ppermute | solution.py:948
  144.3 20.8 %shard_map.416 = (f32[8,128]{1,0:T(8,128)}, f32[32,1024]{1,0:T(8,128)}, f32[1,1024]{1,0:T(1,128)}, f32[384,256]{1,0:T(8,128)}, bf16[4,1024,128]{2,1,0:T(8,128)(2...) custom-call(s32[5]{0:T(128)} %copy-done.39, ...), custom_call_target="tpu_custom_call" | custom-call | bytes 4194304 | tf_op jit(solution)/shard_map/pallas_call | solution.py:348
  172.4 3.8 %collective-permute-done.19.drowa = bf16[4,48,512]{2,1,0:T(8,128)(2,1)S(1)} collective-permute-done((bf16[4,48,512]{2,1,0:T(8,128)(2,1)S(1)}, bf16[4,48,512]{2,1,0:T(8,128)(2,1)S(1)}, u32[]{:S(2)}, u32[]{:S(2)}) %collective-permute-start.19) | collective-permute-done | bytes 196640 | tf_op jit(solution)/shard_map/ppermute | solution.py:939
  177.0 18.7 %shard_map.418 = (f32[384,256]{1,0:T(8,128)}, bf16[4,1280,128]{2,1,0:T(8,128)(2,1)}, f32[4,256]{1,0:T(4,128)}, f32[1,768]{1,0:T(1,128)}, f32[8,176]{1,0:T(8,128)...) custom-call(s32[5]{0:T(128)} %copy-done.39, ...), custom_call_target="tpu_custom_call" | custom-call | bytes 4194304 | tf_op jit(solution)/shard_map/pallas_call | solution.py:348
  195.8 4.7 %collective-permute-start.21 = (bf16[4,48,512]{2,1,0:T(8,128)(2,1)}, bf16[4,48,512]{2,1,0:T(8,128)(2,1)S(1)}, u32[]{:S(2)}, u32[]{:S(2)}) collective-permute-start(bf16[4,48,512]{2,1,0:T(8,128)(2,1)} %get-tuple-element.127), channel_id=1, source_target_pairs={{0,4},{8,12},{16,20},{24,28},{4,0},{12,8},{20,16},{28,24},{1,5},{9... | collective-permute-start | bytes 589832 | tf_op jit(solution)/shard_map/ppermute | solution.py:939
  201.1 3.2 %collective-permute-done.21.first.drowa = bf16[4,48,512]{2,1,0:T(8,128)(2,1)S(1)} collective-permute-done((bf16[4,48,512]{2,1,0:T(8,128)(2,1)}, bf16[4,48,512]{2,1,0:T(8,128)(2,1)S(1)}, u32[]{:S(2)}, u32[]{:S(2)}) %collective-permute-start.21) | collective-permute-done | bytes 196640 | tf_op jit(solution)/shard_map/ppermute | solution.py:939
  206.6 9.1 %collective-permute-start.23 = (bf16[192,512]{1,0:T(8,128)(2,1)S(1)}, bf16[192,512]{1,0:T(8,128)(2,1)S(1)}, u32[]{:S(2)}, u32[]{:S(2)}) collective-permute-start(bf16[192,512]{1,0:T(8,128)(2,1)S(1)} %get-tuple-element.129), channel_id=1, source_target_pairs={{0,1},{2,3},{1,0},{3,2},{4,5},{6,7},{5,4},{7,6},{8,9},{10,11},{9,8... | collective-permute-start | bytes 589832 | tf_op jit(solution)/shard_map/ppermute | solution.py:939
  217.0 3.4 %shard_map.420 = (bf16[4,1184,128]{2,1,0:T(8,128)(2,1)}, f32[80,128]{1,0:T(8,128)}) custom-call(s32[5]{0:T(128)S(1)} %copy-done.42, f32[384,256]{1,0:T(8,128)S(1)} %copy-done.23, bf16[384,256]{1,0:T(8,128)(2,1)S(1)} %copy-done.29, f32[4,192,512]{2,1,0:T(8,128)S(1)} %copy-done.4, bf16[4,48,512]{2,1,0:T(8,128)(2,1)S(1)} %collective-permute-done.21.first.drowa, ...), custom_call_target="tpu_custom_call" | custom-call | bytes 4194304 | tf_op jit(solution)/shard_map/pallas_call | solution.py:348
  220.4 10.8 %all-to-all-start.2 = ((bf16[4,1184,128]{2,1,0:T(8,128)(2,1)}), bf16[4,1184,128]{2,1,0:T(8,128)(2,1)S(1)}, u32[]{:S(2)}, u32[]{:S(2)}) async-start(bf16[4,1184,128]{2,1,0:T(8,128)(2,1)} %get-tuple-element.138), calls=%async_computation.4 | async-start | bytes 2424832 | tf_op jit(solution)/shard_map/all_to_all | solution.py:1113
  231.2 16.2 %all-to-all-done.2.parts = bf16[4,1184,128]{2,1,0:T(8,128)(2,1)S(1)} async-done(((bf16[4,1184,128]{2,1,0:T(8,128)(2,1)}), bf16[4,1184,128]{2,1,0:T(8,128)(2,1)S(1)}, u32[]{:S(2)}, u32[]{:S(2)}) %all-to-all-start.2) | async-done | bytes 1212448 | tf_op jit(solution)/shard_map/all_to_all | solution.py:1113
  250.6 10.2 %all-to-all-start.3 = ((bf16[8,576,128]{2,1,0:T(8,128)(2,1)}), bf16[8,576,128]{2,1,0:T(8,128)(2,1)S(1)}, u32[]{:S(2)}, u32[]{:S(2)}) async-start(bf16[8,576,128]{2,1,0:T(8,128)(2,1)} %shard_map.421), calls=%async_computation.5 | async-start | bytes 2359296 | tf_op jit(solution)/shard_map/all_to_all | solution.py:1119
  263.0 26.1 %all-to-all-done.3.parts = bf16[8,576,128]{2,1,0:T(8,128)(2,1)S(1)} async-done(((bf16[8,576,128]{2,1,0:T(8,128)(2,1)}), bf16[8,576,128]{2,1,0:T(8,128)(2,1)S(1)}, u32[]{:S(2)}, u32[]{:S(2)}) %all-to-all-start.3) | async-done | bytes 1179680 | tf_op jit(solution)/shard_map/all_to_all | solution.py:1119
  290.1 6.5 %all-gather.3 = bf16[1664,128]{1,0:T(8,128)(2,1)S(1)} all-gather(bf16[416,128]{1,0:T(8,128)(2,1)} %copy-done.38), channel_id=5, replica_groups=mesh['row'=8,'col'=4] {'col'}, dimensions={0}, use_global_device_ids=true | all-gather | bytes 532480 | tf_op jit(solution)/shard_map/all_gather | solution.py:1125
  (236 shorter events, 67.2 us)
Async XLA Ops:
  7.2 34.9 %all-gather.8.cloned.1.call-start = ((), (), s32[]{:S(2)}) async-start(), calls=%async_computation.8 | async-start | bytes 1310720 | tf_op jit(solution)/shard_map/all_gather | solution.py:1013
  26.0 6.4 %collective-permute-start = (bf16[1,32,128]{2,1,0:T(8,128)(2,1)S(1)}, bf16[1,32,128]{2,1,0:T(8,128)(2,1)S(1)}, u32[]{:S(2)}, u32[]{:S(2)}) collective-permute-start(bf16[1,32,128]{2,1,0:T(8,128)(2,1)S(1)} %slice.51), channel_id=1, source_target_pairs={{0,4},{4,8},{8,12},{12,16},{16,20},{20,24},{24,28},{28,0},{1,5},{5... | collective-permute-start | bytes 24584 | tf_op jit(solution)/shard_map/ppermute | solution.py:932
  32.4 20.3 %all-to-all-start.1 = ((bf16[8,352,128]{2,1,0:T(8,128)(2,1)}), bf16[8,352,128]{2,1,0:T(8,128)(2,1)}, u32[]{:S(2)}, u32[]{:S(2)}) async-start(bf16[8,352,128]{2,1,0:T(8,128)(2,1)} %get-tuple-element.100), calls=%async_computation.1 | async-start | bytes 1441792 | tf_op jit(solution)/shard_map/all_to_all | solution.py:1014
  36.6 36.0 %all-gather.10.cloned.1.call-start = ((), (), s32[]{:S(2)}) async-start(), calls=%async_computation.9 | async-start | bytes 1638400 | tf_op jit(solution)/shard_map/all_gather | solution.py:1023
  54.5 45.0 %all-gather.12.cloned.1.call-start = ((), (), s32[]{:S(2)}) async-start(), calls=%async_computation.10 | async-start | bytes 1966080 | tf_op jit(solution)/shard_map/all_gather | solution.py:1024
  56.3 174.9 %reduce-scatter.3.cloned.1.call-start = ((), (), s32[]{:S(2)}) async-start(), calls=%async_computation.6 | async-start | bytes 1310720 | tf_op jit(solution)/shard_map/reduce_scatter | solution.py:1086
  58.5 5.7 %collective-permute-start.4 = (bf16[4,48,512]{2,1,0:T(8,128)(2,1)S(1)}, bf16[4,48,512]{2,1,0:T(8,128)(2,1)S(1)}, u32[]{:S(2)}, u32[]{:S(2)}) collective-permute-start(bf16[4,48,512]{2,1,0:T(8,128)(2,1)S(1)} %get-tuple-element.96), channel_id=1, source_target_pairs={{0,4},{8,12},{16,20},{24,28},{4,0},{12,8},{20,16},{28,24},{1,5},{9... | collective-permute-start | bytes 589832 | tf_op jit(solution)/shard_map/ppermute | solution.py:939
  60.0 4.3 %collective-permute-start.5 = (bf16[4,48,512]{2,1,0:T(8,128)(2,1)S(1)}, bf16[4,48,512]{2,1,0:T(8,128)(2,1)S(1)}, u32[]{:S(2)}, u32[]{:S(2)}) collective-permute-start(bf16[4,48,512]{2,1,0:T(8,128)(2,1)S(1)} %get-tuple-element.97), channel_id=1, source_target_pairs={{4,8},{12,16},{20,24},{8,4},{16,12},{24,20},{5,9},{13,17},{21,25},... | collective-permute-start | bytes 589832 | tf_op jit(solution)/shard_map/ppermute | solution.py:939
  83.6 7.2 %collective-permute-start.6 = (bf16[4,48,512]{2,1,0:T(8,128)(2,1)}, bf16[4,48,512]{2,1,0:T(8,128)(2,1)S(1)}, u32[]{:S(2)}, u32[]{:S(2)}) collective-permute-start(bf16[4,48,512]{2,1,0:T(8,128)(2,1)} %get-tuple-element.105), channel_id=1, source_target_pairs={{0,4},{8,12},{16,20},{24,28},{4,0},{12,8},{20,16},{28,24},{1,5},{9... | collective-permute-start | bytes 589832 | tf_op jit(solution)/shard_map/ppermute | solution.py:939
  85.1 5.8 %collective-permute-start.7 = (bf16[4,48,512]{2,1,0:T(8,128)(2,1)}, bf16[4,48,512]{2,1,0:T(8,128)(2,1)S(1)}, u32[]{:S(2)}, u32[]{:S(2)}) collective-permute-start(bf16[4,48,512]{2,1,0:T(8,128)(2,1)} %get-tuple-element.106), channel_id=1, source_target_pairs={{4,8},{12,16},{20,24},{8,4},{16,12},{24,20},{5,9},{13,17},{21,25},... | collective-permute-start | bytes 589832 | tf_op jit(solution)/shard_map/ppermute | solution.py:939
  92.5 7.0 %collective-permute-start.9 = (bf16[4,192,512]{2,1,0:T(8,128)(2,1)S(1)}, bf16[4,192,512]{2,1,0:T(8,128)(2,1)S(1)}, u32[]{:S(2)}, u32[]{:S(2)}) collective-permute-start(bf16[4,192,512]{2,1,0:T(8,128)(2,1)S(1)} %shard_map.414.own), channel_id=1, source_target_pairs={{1,2},{2,1},{5,6},{6,5},{9,10},{10,9},{13,14},{14,13},{17,18},{18,... | collective-permute-start | bytes 2359304 | tf_op jit(solution)/shard_map/ppermute | solution.py:939
  93.2 7.5 %collective-permute-start.8 = (bf16[4,192,512]{2,1,0:T(8,128)(2,1)S(1)}, bf16[4,192,512]{2,1,0:T(8,128)(2,1)}, u32[]{:S(2)}, u32[]{:S(2)}) collective-permute-start(bf16[4,192,512]{2,1,0:T(8,128)(2,1)S(1)} %shard_map.414.own), channel_id=1, source_target_pairs={{0,1},{2,3},{1,0},{3,2},{4,5},{6,7},{5,4},{7,6},{8,9},{10,11},{9,8... | collective-permute-start | bytes 2359304 | tf_op jit(solution)/shard_map/ppermute | solution.py:939
  113.3 11.9 %collective-permute-start.12 = (f32[64,256]{1,0:T(8,128)}, f32[64,256]{1,0:T(8,128)S(1)}, u32[]{:S(2)}, u32[]{:S(2)}) collective-permute-start(f32[64,256]{1,0:T(8,128)} %get-tuple-element.108), channel_id=1, source_target_pairs={{0,3},{1,2},{2,1},{3,0},{4,7},{5,6},{6,5},{7,4},{8,11},{9,10},{10,... | collective-permute-start | bytes 196616 | tf_op jit(solution)/shard_map/ppermute | solution.py:948
  115.1 13.4 %collective-permute-start.11 = (f32[64,256]{1,0:T(8,128)}, f32[64,256]{1,0:T(8,128)S(1)}, u32[]{:S(2)}, u32[]{:S(2)}) collective-permute-start(f32[64,256]{1,0:T(8,128)} %get-tuple-element.108), channel_id=1, source_target_pairs={{0,2},{1,3},{2,0},{3,1},{4,6},{5,7},{6,4},{7,5},{8,10},{9,11},{10,... | collective-permute-start | bytes 196616 | tf_op jit(solution)/shard_map/ppermute | solution.py:948
  129.4 5.3 %collective-permute-start.15 = (f32[64,256]{1,0:T(8,128)S(1)}, f32[64,256]{1,0:T(8,128)S(1)}, u32[]{:S(2)}, u32[]{:S(2)}) collective-permute-start(f32[64,256]{1,0:T(8,128)S(1)} %add_add_fusion.1), channel_id=1, source_target_pairs={{0,12},{4,8},{8,4},{12,0},{16,28},{20,24},{24,20},{28,16},{1,13},{... | collective-permute-start | bytes 196616 | tf_op jit(solution)/shard_map/ppermute | solution.py:948
  132.0 5.2 %collective-permute-start.14 = (f32[64,256]{1,0:T(8,128)S(1)}, f32[64,256]{1,0:T(8,128)S(1)}, u32[]{:S(2)}, u32[]{:S(2)}) collective-permute-start(f32[64,256]{1,0:T(8,128)S(1)} %add_add_fusion.1), channel_id=1, source_target_pairs={{0,8},{4,12},{8,0},{12,4},{16,24},{20,28},{24,16},{28,20},{1,9},{5... | collective-permute-start | bytes 196616 | tf_op jit(solution)/shard_map/ppermute | solution.py:948
  137.8 5.9 %collective-permute-start.16 = (f32[64,256]{1,0:T(8,128)S(1)}, f32[64,256]{1,0:T(8,128)S(1)}, u32[]{:S(2)}, u32[]{:S(2)}) collective-permute-start(f32[64,256]{1,0:T(8,128)S(1)} %add_add_fusion), channel_id=1, source_target_pairs={{0,16},{4,20},{8,24},{12,28},{16,0},{20,4},{24,8},{28,12},{1,17},{... | collective-permute-start | bytes 196616 | tf_op jit(solution)/shard_map/ppermute | solution.py:948
  165.1 82.3 %reduce-scatter.5.cloned.1.call-start = ((), (), s32[]{:S(2)}) async-start(), calls=%async_computation.7 | async-start | bytes 1638400 | tf_op jit(solution)/shard_map/reduce_scatter | solution.py:1102
  170.5 5.7 %collective-permute-start.19 = (bf16[4,48,512]{2,1,0:T(8,128)(2,1)S(1)}, bf16[4,48,512]{2,1,0:T(8,128)(2,1)S(1)}, u32[]{:S(2)}, u32[]{:S(2)}) collective-permute-start(bf16[4,48,512]{2,1,0:T(8,128)(2,1)S(1)} %get-tuple-element.119), channel_id=1, source_target_pairs={{0,4},{8,12},{16,20},{24,28},{4,0},{12,8},{20,16},{28,24},{1,5},{9... | collective-permute-start | bytes 589832 | tf_op jit(solution)/shard_map/ppermute | solution.py:939
  171.7 4.5 %collective-permute-start.20 = (bf16[4,48,512]{2,1,0:T(8,128)(2,1)S(1)}, bf16[4,48,512]{2,1,0:T(8,128)(2,1)S(1)}, u32[]{:S(2)}, u32[]{:S(2)}) collective-permute-start(bf16[4,48,512]{2,1,0:T(8,128)(2,1)S(1)} %get-tuple-element.120), channel_id=1, source_target_pairs={{4,8},{12,16},{20,24},{8,4},{16,12},{24,20},{5,9},{13,17},{21,25},... | collective-permute-start | bytes 589832 | tf_op jit(solution)/shard_map/ppermute | solution.py:939
  195.8 8.5 %collective-permute-start.21 = (bf16[4,48,512]{2,1,0:T(8,128)(2,1)}, bf16[4,48,512]{2,1,0:T(8,128)(2,1)S(1)}, u32[]{:S(2)}, u32[]{:S(2)}) collective-permute-start(bf16[4,48,512]{2,1,0:T(8,128)(2,1)} %get-tuple-element.127), channel_id=1, source_target_pairs={{0,4},{8,12},{16,20},{24,28},{4,0},{12,8},{20,16},{28,24},{1,5},{9... | collective-permute-start | bytes 589832 | tf_op jit(solution)/shard_map/ppermute | solution.py:939
  206.6 10.3 %collective-permute-start.23 = (bf16[192,512]{1,0:T(8,128)(2,1)S(1)}, bf16[192,512]{1,0:T(8,128)(2,1)S(1)}, u32[]{:S(2)}, u32[]{:S(2)}) collective-permute-start(bf16[192,512]{1,0:T(8,128)(2,1)S(1)} %get-tuple-element.129), channel_id=1, source_target_pairs={{0,1},{2,3},{1,0},{3,2},{4,5},{6,7},{5,4},{7,6},{8,9},{10,11},{9,8... | collective-permute-start | bytes 589832 | tf_op jit(solution)/shard_map/ppermute | solution.py:939
  220.4 27.0 %all-to-all-start.2 = ((bf16[4,1184,128]{2,1,0:T(8,128)(2,1)}), bf16[4,1184,128]{2,1,0:T(8,128)(2,1)S(1)}, u32[]{:S(2)}, u32[]{:S(2)}) async-start(bf16[4,1184,128]{2,1,0:T(8,128)(2,1)} %get-tuple-element.138), calls=%async_computation.4 | async-start | bytes 2424832 | tf_op jit(solution)/shard_map/all_to_all | solution.py:1113
  250.6 38.5 %all-to-all-start.3 = ((bf16[8,576,128]{2,1,0:T(8,128)(2,1)}), bf16[8,576,128]{2,1,0:T(8,128)(2,1)S(1)}, u32[]{:S(2)}, u32[]{:S(2)}) async-start(bf16[8,576,128]{2,1,0:T(8,128)(2,1)} %shard_map.421), calls=%async_computation.5 | async-start | bytes 2359296 | tf_op jit(solution)/shard_map/all_to_all | solution.py:1119
  (76 other events, 1203.0 us)
Sparse Core Ops, SparseCore 0:
  26.1 15.9 all-gather.7
  54.6 17.9 all-gather.9
  74.2 18.8 all-gather.11
  165.3 22.9 reduce-scatter.2
  195.9 38.9 reduce-scatter.4

commit v4 on v3

--- a/solution.py
+++ b/solution.py
@@ -27,6 +27,7 @@
 f32 = jnp.float32
 i32 = jnp.int32
 MASKED = -1e30
+LOG2E = 1.4426950408889634
 MIB = 1024 * 1024
 
 
@@ -74,6 +75,7 @@
 
 class One:
     dilation, queries, across, pieces, steps = 1, 64, 16, 4, 6
+    forward, back = 3, 3
     keys = pieces * 128
 
     @staticmethod
@@ -92,6 +94,7 @@
 
 class Two:
     dilation, queries, across, pieces, steps = 2, 32, 8, 3, 12
+    forward, back = 3, 3
     keys = pieces * 128
 
     @staticmethod
@@ -168,6 +171,7 @@
             for piece in range(geo.pieces):
                 lanes = slice(piece * 128, piece * 128 + 128)
                 value = first_ref[piece, head * geo.across : (head + 1) * geo.across, :]
+                value = value * LOG2E
                 if row:
                     value = pltpu.roll(value, 8 * row, 1)
                 begin = head * geo.queries + row * geo.across
@@ -245,29 +249,37 @@
 
 
 def softmax_rows(score, table, mask):
-    score = score * scale + (table + mask)
-    top = jnp.max(score, -1, keepdims=True)
-    weight = jnp.exp(score - top)
-    return weight * (1.0 / jnp.sum(weight, -1, keepdims=True))
-
-
-def attend(geo, place, lay_ref, query_ref, pieces, table_ref, out_ref, score_ref, prob_ref):
+    score = score * (scale * LOG2E) + (table + mask)
+    weight = jnp.exp2(score - jnp.max(score, -1, keepdims=True))
+    return weight, 1.0 / jnp.sum(weight, -1, keepdims=True)
+
+
+def attend(geo, place, lay_ref, query_ref, pieces, table_ref, out_ref, score_ref, prob_ref, share_ref):
     count = geo.queries
-
-    def step_of(step, carry):
-        rows = pl.ds(pl.multiple_of(step * count, count), count)
-        mask = window_mask(geo, lay_ref[rows, :], step, place[0], place[1])
-        wide = by_head(query_ref[rows, :])
-        score_ref[...] = nt(wide, load_keys(geo, pieces, step, KEY))
+    together = score_ref.shape[0]
+
+    def steps_of(index, carry):
+        steps = [index * together + n for n in range(together)]
+        rows = [pl.ds(pl.multiple_of(step * count, count), count) for step in steps]
+        for n, step in enumerate(steps):
+            score_ref[n] = nt(by_head(query_ref[rows[n], :]), load_keys(geo, pieces, step, KEY))
+        masks = [
+            window_mask(geo, lay_ref[rows[n], :], step, place[0], place[1])
+            for n, step in enumerate(steps)
+        ]
         for h in range(HEADS):
             span = slice(h * count, (h + 1) * count)
-            prob = softmax_rows(score_ref[span, :], table_ref[span, :], mask)
-            prob_ref[span, :] = prob.astype(bf16)
-        out = nn(prob_ref[...], load_keys(geo, pieces, step, VALUE))
-        out_ref[rows, :] = from_heads(out).astype(out_ref.dtype)
+            for n in range(together):
+                weight, share = softmax_rows(score_ref[n, span, :], table_ref[span, :], masks[n])
+                prob_ref[n, span, :] = weight.astype(bf16)
+                share_ref[n, span, :] = jnp.broadcast_to(share, (count, 128))
+        for n, step in enumerate(steps):
+            out = nn(prob_ref[n], load_keys(geo, pieces, step, VALUE))
+            out = out * jnp.concatenate([share_ref[n]] * 2, 1)
+            out_ref[rows[n], :] = from_heads(out).astype(out_ref.dtype)
         return carry
 
-    lax.fori_loop(0, geo.steps, step_of, 0)
+    lax.fori_loop(0, geo.steps // together, steps_of, 0)
 
 
 def attend_back(
@@ -275,32 +287,41 @@
     score_ref, dprob_ref, prob_ref, dscore_ref,
 ):
     count = geo.queries
+    together = score_ref.shape[0]
     dtable_ref[...] = jnp.zeros_like(dtable_ref)
     dpieces[...] = jnp.zeros_like(dpieces)
 
-    def step_of(step, carry):
-        rows = pl.ds(pl.multiple_of(step * count, count), count)
-        mask = window_mask(geo, lay_ref[rows, :], step, place[0], place[1])
-        wide = by_head(query_ref[rows, :])
-        dwide = by_head(dout_ref[rows, :])
-        keys = load_keys(geo, pieces, step, KEY)
-        score_ref[...] = nt(wide, keys)
-        dprob_ref[...] = nt(dwide, load_keys(geo, pieces, step, VALUE))
+    def steps_of(index, carry):
+        steps = [index * together + n for n in range(together)]
+        rows = [pl.ds(pl.multiple_of(step * count, count), count) for step in steps]
+        for n, step in enumerate(steps):
+            score_ref[n] = nt(by_head(query_ref[rows[n], :]), load_keys(geo, pieces, step, KEY))
+            dprob_ref[n] = nt(by_head(dout_ref[rows[n], :]), load_keys(geo, pieces, step, VALUE))
+        masks = [
+            window_mask(geo, lay_ref[rows[n], :], step, place[0], place[1])
+            for n, step in enumerate(steps)
+        ]
         for h in range(HEADS):
             span = slice(h * count, (h + 1) * count)
-            prob = softmax_rows(score_ref[span, :], table_ref[span, :], mask)
-            prob_ref[span, :] = prob.astype(bf16)
-            dprob = dprob_ref[span, :]
-            dscore = prob * (dprob - jnp.sum(prob * dprob, -1, keepdims=True))
-            dtable_ref[span, :] += dscore
-            dscore_ref[span, :] = dscore.astype(bf16)
-        dscore = dscore_ref[...]
-        add_keys(geo, dpieces, step, VALUE, tn(prob_ref[...], dwide))
-        add_keys(geo, dpieces, step, KEY, tn(dscore, wide) * scale)
-        dquery_ref[rows, :] = from_heads(nn(dscore, keys)) * scale
+            total = dtable_ref[span, :]
+            for n in range(together):
+                weight, share = softmax_rows(score_ref[n, span, :], table_ref[span, :], masks[n])
+                prob = weight * share
+                prob_ref[n, span, :] = prob.astype(bf16)
+                dprob = dprob_ref[n, span, :]
+                dscore = prob * (dprob - jnp.sum(prob * dprob, -1, keepdims=True))
+                total += dscore
+                dscore_ref[n, span, :] = dscore.astype(bf16)
+            dtable_ref[span, :] = total
+        for n, step in enumerate(steps):
+            wide, dwide = by_head(query_ref[rows[n], :]), by_head(dout_ref[rows[n], :])
+            dscore = dscore_ref[n]
+            add_keys(geo, dpieces, step, VALUE, tn(prob_ref[n], dwide))
+            add_keys(geo, dpieces, step, KEY, tn(dscore, wide) * scale)
+            dquery_ref[rows[n], :] = from_heads(nn(dscore, load_keys(geo, pieces, step, KEY))) * scale
         return carry
 
-    lax.fori_loop(0, geo.steps, step_of, 0)
+    lax.fori_loop(0, geo.steps // together, steps_of, 0)
 
 
 def grouped(x):
@@ -308,7 +329,7 @@
     return [parts[:, g >> 1, g & 1].reshape(96, x.shape[-1]) for g in range(4)]
 
 
-EVEN_ROW, EVEN_COL = 3, 4
+EVEN_ROW, EVEN_COL, COL = 3, 4, 5
 
 
 def send(place, even, first, second, after, before):
@@ -577,12 +598,12 @@
 def first_block_kernel(
     place, lay, hidden, query, keyval, cola, colb, rowa, rowb, first_table, late, norms, ebias,
     att, middle, last, query2, keyval2, first, second,
-    pieces, table, score, prob, group, sem,
+    pieces, table, score, prob, share, group, sem,
 ):
     arrived = fetch(late, group, sem)
     gather_keys_one(place, keyval, cola, colb, rowa, rowb, pieces)
     spread_table(One, first_table, table)
-    attend(One, place, lay, query, pieces, table, att, score, prob)
+    attend(One, place, lay, query, pieces, table, att, score, prob, share)
     arrived()
     mid = hidden[...] + nn(att[...], weight_of(group, PROJ, 2))
     middle[...] = mid
@@ -611,12 +632,12 @@
 def second_block_kernel(
     place, lay, slots, hidden, query, own, cola, colb, first_table, late, norms, ebias,
     att, middle, last, sums,
-    pieces, table, score, prob, att_group, att_token, group, sem,
+    pieces, table, score, prob, share, att_group, att_token, group, sem,
 ):
     arrived = fetch(late, group, sem)
     gather_keys_two(place, own, cola, colb, pieces)
     spread_table(Two, first_table, table)
-    attend(Two, place, lay, query, pieces, table, att_group, score, prob)
+    attend(Two, place, lay, query, pieces, table, att_group, score, prob, share)
     ungroup(att_group[...], att_token)
     low = att_token[...].reshape(384, D).astype(bf16)
     att[...] = low
@@ -797,6 +818,7 @@
 def front_back_kernel(
     place, dhid_in, dquery, inner, drowa, drowb, dcola, dcolb, hidden, conv, patches, early,
     norms, dnorms1, dnorms2, debias1, debias2, dpos1, dpos2,
+    keep, give,
     grads, small,
 ):
     left, right = received(place, EVEN_COL, dcola[...], dcolb[...])
@@ -837,26 +859,25 @@
     for first, value in ((40, dpos1), (56, dpos2)):
         small[first : first + 8, :] = value[:, :128]
         small[first + 8 : first + 16, : WIN - 128] = value[:, 128:]
-    high, low = two_parts(small[...])
-    begin = grads.shape[1] - 2 * SMALL_ROWS
+    begin = grads.shape[1] - SMALL_ROWS
     for col in range(grads.shape[0]):
-        grads[col, begin : begin + SMALL_ROWS, :] = high
-        grads[col, begin + SMALL_ROWS :, :] = low
-
-
-def small_of(parts, index, begin):
-    high = parts[index, begin : begin + SMALL_ROWS, :].astype(f32)
-    return high + parts[index, begin + SMALL_ROWS : begin + 2 * SMALL_ROWS, :].astype(f32)
-
-
-def add_up(parts, rows):
-    total = parts[0, rows, :].astype(f32)
-    for index in range(1, parts.shape[0]):
-        total += parts[index, rows, :].astype(f32)
-    return total
-
-
-def between_kernel(second, first, parts, result):
+        grads[col, begin:, :] = small[...].astype(bf16)
+    halve(place, 0, grads, keep, give)
+
+
+def halve(place, stage, parts, keep, give):
+    bit = (place[COL] >> stage) & 1
+    for k in range(keep.shape[0]):
+        keep[k] = parts[2 * k + bit]
+        give[k] = parts[2 * k + 1 - bit]
+
+
+def halve_kernel(place, kept, given, keep, give, total, *, stage):
+    total[...] = (kept[...].astype(f32) + given[...].astype(f32)).astype(bf16)
+    halve(place, stage, total, keep, give)
+
+
+def between_kernel(second, first, kept, given, result):
     rows = result.shape[0]
     sh = D // rows
     begin = 0
@@ -864,27 +885,24 @@
         for k in range(group.shape[0] // D):
             result[:, begin : begin + sh, :] = group[k * D : (k + 1) * D, :].reshape(rows, sh, 128)
             begin += sh
-    for k in range(parts.shape[1] // D):
-        total = add_up(parts, slice(k * D, (k + 1) * D)).astype(bf16)
-        result[:, begin : begin + sh, :] = total.reshape(rows, sh, 128)
+    for k in range(kept.shape[1] // D):
+        span = slice(k * D, (k + 1) * D)
+        total = kept[0, span, :].astype(f32) + given[0, span, :].astype(f32)
+        result[:, begin : begin + sh, :] = total.astype(bf16).reshape(rows, sh, 128)
         begin += sh
-    low_rows = parts.shape[1] - 2 * SMALL_ROWS
-    total = small_of(parts, 0, low_rows)
-    for col in range(1, parts.shape[0]):
-        total += small_of(parts, col, low_rows)
-    high, low = two_parts(total)
+    span = slice(kept.shape[1] - SMALL_ROWS, kept.shape[1])
+    small = (kept[0, span, :].astype(f32) + given[0, span, :].astype(f32)).astype(bf16)
     for row in range(rows):
-        result[row, begin : begin + SMALL_ROWS, :] = high
-        result[row, begin + SMALL_ROWS :, :] = low
+        result[row, begin:, :] = small
 
 
 def last_sum_kernel(parts, result, small):
+    total = parts[0].astype(f32)
+    for row in range(1, parts.shape[0]):
+        total += parts[row].astype(f32)
     count = result.shape[0]
-    result[...] = add_up(parts, slice(0, count)).astype(bf16)
-    total = small_of(parts, 0, count)
-    for row in range(1, parts.shape[0]):
-        total += small_of(parts, row, count)
-    small[...] = total
+    result[...] = total[:count].astype(bf16)
+    small[...] = total[count:]
 
 
 def adamw(weight, grad, first, second):
@@ -995,7 +1013,7 @@
         [out((geo.pieces, HEADS * geo.across, 128)) for geo in (One, Two)],
         [jnp.pad(pos_bias, ((0, 0), (0, WIN - 169)))],
     )
-    place = [row_index * 24, col_index * 16, row_index * sh, (row_index + 1) % 2, (col_index + 1) % 2]
+    place = [row_index * 24, col_index * 16, row_index * sh, (row_index + 1) % 2, (col_index + 1) % 2, col_index]
     place = jnp.stack(place).astype(i32)
     lay_one = layout.reshape(5, 24, 8, 2).transpose(1, 3, 2, 0).reshape(384, 5)
     lay_two = layout.reshape(5, 12, 2, 8, 2).transpose(2, 4, 1, 3, 0).reshape(384, 5)
@@ -1030,11 +1048,12 @@
     def tiles(geo, back):
         square = (HEADS * geo.queries, geo.keys)
         shape = (4, 288, 2 * D) if geo is One else (3, 4, 192, 2 * D)
-        wide, narrow = pltpu.VMEM(square, f32), pltpu.VMEM(square, bf16)
+        table, many = pltpu.VMEM(square, f32), (geo.back if back else geo.forward, *square)
+        wide, narrow = pltpu.VMEM(many, f32), pltpu.VMEM(many, bf16)
         if not back:
-            return [pltpu.VMEM(shape, bf16), wide, wide, narrow]
+            return [pltpu.VMEM(shape, bf16), table, wide, narrow, pltpu.VMEM((*many[:2], 128), f32)]
         return [
-            pltpu.VMEM(shape, bf16), wide, wide, wide, wide, narrow, narrow, pltpu.VMEM(shape, f32),
+            pltpu.VMEM(shape, bf16), table, table, wide, wide, narrow, narrow, pltpu.VMEM(shape, f32),
             pltpu.VMEM((384, D), bf16), pltpu.VMEM((384, D), f32),
             pltpu.VMEM((geo.pieces, HEADS * geo.across, 128), f32),
         ]
@@ -1101,26 +1120,40 @@
     drows1 = swaps(*edges, "row")
     grads1 = lax.psum_scatter(grads1, "col", scatter_dimension=0, tiled=False)
     dcols1 = swaps(*run(sides_kernel, [edge] * 2, [place, inner1, *drows1], specs={0: SMEM}), "col")
-    grads0, _ = run(
+    part = per[2] * D + SMALL_ROWS
+    half = lambda count: out((count, part, 128), bf16)
+    kept, given = run(
         front_back_kernel,
-        [out((nc, per[2] * D + 2 * SMALL_ROWS, 128), bf16), out((SMALL_ROWS, 128))],
+        [half(nc // 2), half(nc // 2)],
         [
             place, dhid, dquery1, inner1, *drows1, *dcols1, hidden0, conv_out, patches,
             early, norms, dnorms1, dnorms2, debias1, debias2, dpos1, dpos2,
         ],
-        specs={0: SMEM},
-    )
-    grads0 = lax.all_to_all(grads0, "col", 0, 0, tiled=True)
-    grads0 = run(
+        [pltpu.VMEM((nc, part, 128), bf16), pltpu.VMEM((SMALL_ROWS, 128), f32)],
+        {0: SMEM},
+    )
+    stage = 0
+    while True:
+        given = lax.ppermute(given, "col", [(i, i ^ (1 << stage)) for i in range(nc)])
+        stage += 1
+        if 1 << stage == nc:
+            break
+        count = nc >> (stage + 1)
+        kept, given = run(
+            functools.partial(halve_kernel, stage=stage),
+            [half(count), half(count)],
+            [place, kept, given],
+            [pltpu.VMEM((2 * count, part, 128), bf16)],
+            {0: SMEM},
+        )
+    mine = run(
         between_kernel,
-        [out((nr, sum(per) * sh + 2 * SMALL_ROWS, 128), bf16)],
-        [grads2, grads1, grads0],
+        [out((nr, sum(per) * sh + SMALL_ROWS, 128), bf16)],
+        [grads2, grads1, kept, given],
     )[0]
-    grads0 = lax.all_to_all(grads0, "row", 0, 0, tiled=True)
+    mine = lax.all_to_all(mine, "row", 0, 0, tiled=True)
     mine, small = run(
-        last_sum_kernel,
-        [out((sum(per) * sh, 128), bf16), out((SMALL_ROWS, 128))],
-        [grads0],
+        last_sum_kernel, [out((sum(per) * sh, 128), bf16), out((SMALL_ROWS, 128))], [mine]
     )
     grads = lax.all_gather(mine, "col", axis=0)
     wide = [

time: 309 us -> 282 us (0.913)
  Pallas kernels: 79.4 us -> 66.2 us
  waiting for transfers between devices: 93.9 us -> 82.7 us
    all_to_all x2 -> x1, waiting for transfers between devices: 42.3 us -> 21.5 us  [on_device(): mine = lax.all_to_all(mine, 'row', 0, 0, tiled=True)]
    pallas_call x16 -> x17, Pallas kernels: 79.4 us -> 66.2 us  [run(): pl.pallas_call(kernel, out_shape=outs, in_specs=in_specs, out_specs=[pl.B...]
    all_to_all x2 -> x1, starting transfers between devices: 21 us -> 9.03 us  [on_device(): mine = lax.all_to_all(mine, 'row', 0, 0, tiled=True)]
    ppermute x0 -> x2, starting transfers between devices: none -> 10.1 us  [on_device(): given = lax.ppermute(given, 'col', [(i, i ^ 1 << stage) for i in range(nc)])]
    ppermute x0 -> x2, waiting for transfers between devices: none -> 9.87 us  [on_device(): given = lax.ppermute(given, 'col', [(i, i ^ 1 << stage) for i in range(nc)])]
    unnamed x132 -> x122, local copies, waits for them, and re-layouts: 11.6 us -> 10.2 us
  transfers between devices with their start and end apart: 33 -> 34, of which waited for: 20 -> 21; matrix products, arithmetic and copies ran while one was open for 3% -> 3% of each run, Pallas kernels for 13% -> 13%
where the time goes in v4:
time: 282 us; the launch traced here: 281 us
  waiting for transfers between devices  82.7 us (29%)
  starting transfers between devices  70.6 us (25%)
  Pallas kernels  66.2 us (23%)
  blocking collectives  22.9 us (8%)
  local copies, waits for them, and re-layouts  19.2 us (7%)
  between operations  14.8 us (5%)
  other arithmetic  4.88 us (2%)
    pallas_call x17, Pallas kernels, run(): pl.pallas_call(kernel, out_shape=outs, in_specs=in_specs, out_specs=[pl.B...  66.2 us
    ppermute x8, starting transfers between devices, swaps(): lax.ppermute(first, axis, both[0])  23.5 us
    all_to_all x1, waiting for transfers between devices, on_device(): mine = lax.all_to_all(mine, 'row', 0, 0, tiled=True)  21.5 us
    ppermute x7, starting transfers between devices, other(): return lax.ppermute(value, axis, [(i, i ^ flip) for i in range(count)])  16.7 us
    ppermute x8, waiting for transfers between devices, swaps(): lax.ppermute(first, axis, both[0])  16.5 us
    all_to_all x1, blocking collectives, on_device(): early = lax.all_to_all(early, 'row', 0, 0, tiled=True)  16.3 us
    ppermute x7, waiting for transfers between devices, other(): return lax.ppermute(value, axis, [(i, i ^ flip) for i in range(count)])  10.8 us
    unnamed x122, local copies, waits for them, and re-layouts  10.2 us
  transfers between devices with their start and end apart: 34, of which 21 were waited for; matrix products, arithmetic and copies ran while one was open for 3% of the time, Pallas kernels for 13%

profile of v4, /device:TPU:0, one launch (start us, length us, event | category | flops | bytes accessed | tf_op | source)
XLA Modules:
  0.0 281.3 jit_solution(8670093567118816809)
XLA Ops:
  9.6 16.3 %all_to_all.15 = bf16[8,128,128]{2,1,0:T(8,128)(2,1)} all-to-all(bf16[8,128,128]{2,1,0:T(8,128)(2,1)} %get-tuple-element.93), channel_id=1, replica_groups=mesh['row'=8,'col'=4] {'row'}, dimensions={0} | all-to-all | bytes 524288 | tf_op jit(solution)/shard_map/all_to_all | solution.py:1003
  27.4 4.9 %collective-permute-done = bf16[1,32,128]{2,1,0:T(8,128)(2,1)S(1)} collective-permute-done((bf16[1,32,128]{2,1,0:T(8,128)(2,1)S(1)}, bf16[1,32,128]{2,1,0:T(8,128)(2,1)S(1)}, u32[]{:S(2)}, u32[]{:S(2)}) %collective-permute-start) | collective-permute-done | bytes 8224 | tf_op jit(solution)/shard_map/ppermute | solution.py:950
  32.3 4.2 %all-to-all-start.1 = ((bf16[8,352,128]{2,1,0:T(8,128)(2,1)}), bf16[8,352,128]{2,1,0:T(8,128)(2,1)}, u32[]{:S(2)}, u32[]{:S(2)}) async-start(bf16[8,352,128]{2,1,0:T(8,128)(2,1)} %get-tuple-element.103), calls=%async_computation.1 | async-start | bytes 1441792 | tf_op jit(solution)/shard_map/all_to_all | solution.py:1032
  37.1 3.0 %collective-permute-done.1 = bf16[49,1,128]{2,0,1:T(8,128)(2,1)S(1)} collective-permute-done((bf16[49,1,128]{2,0,1:T(8,128)(2,1)S(1)}, bf16[49,1,128]{2,0,1:T(8,128)(2,1)S(1)}, u32[]{:S(2)}, u32[]{:S(2)}) %collective-permute-start.1) | collective-permute-done | bytes 12576 | tf_op jit(solution)/shard_map/ppermute | solution.py:950
  45.9 6.7 %all-to-all-done.1 = bf16[8,352,128]{2,1,0:T(8,128)(2,1)} async-done(((bf16[8,352,128]{2,1,0:T(8,128)(2,1)}), bf16[8,352,128]{2,1,0:T(8,128)(2,1)}, u32[]{:S(2)}, u32[]{:S(2)}) %all-to-all-start.1) | async-done | bytes 720928 | tf_op jit(solution)/shard_map/all_to_all | solution.py:1032
  64.2 8.4 %all-gather.10.cloned.1.call-done = bf16[32,160,128]{2,1,0:T(8,128)(2,1)} async-done(((bf16[8,160,128]{2,1,0:T(8,128)(2,1)}), bf16[32,160,128]{2,1,0:T(8,128)(2,1)}) %all-gather.10.cloned.1.call-update) | async-done | bytes 1310736 | tf_op jit(solution)/shard_map/all_gather | solution.py:1041
  72.6 8.3 %shard_map.413 = (bf16[384,256]{1,0:T(8,128)(2,1)}, f32[384,256]{1,0:T(8,128)}, f32[384,256]{1,0:T(8,128)}, bf16[384,256]{1,0:T(8,128)(2,1)}, bf16[4,96,512]{2,1...) custom-call(s32[6]{0:T(128)} %copy-done.38, s32[384,5]{1,0:T(8,128)} %bitcast.44, ...), custom_call_target="tpu_custom_call" | custom-call | bytes 4194304 | tf_op jit(solution)/shard_map/pallas_call | solution.py:369
  83.0 5.1 %collective-permute-done.6.first = bf16[4,48,512]{2,1,0:T(8,128)(2,1)S(1)} collective-permute-done((bf16[4,48,512]{2,1,0:T(8,128)(2,1)}, bf16[4,48,512]{2,1,0:T(8,128)(2,1)S(1)}, u32[]{:S(2)}, u32[]{:S(2)}) %collective-permute-start.6) | collective-permute-done | bytes 196640 | tf_op jit(solution)/shard_map/ppermute | solution.py:957
  90.5 5.4 %collective-permute-start.8 = (bf16[4,192,512]{2,1,0:T(8,128)(2,1)S(1)}, bf16[4,192,512]{2,1,0:T(8,128)(2,1)}, u32[]{:S(2)}, u32[]{:S(2)}) collective-permute-start(bf16[4,192,512]{2,1,0:T(8,128)(2,1)S(1)} %shard_map.414.own), channel_id=1, source_target_pairs={{0,1},{2,3},{1,0},{3,2},{4,5},{6,7},{5,4},{7,6},{8,9},{10,11},{9,8... | collective-permute-start | bytes 2359304 | tf_op jit(solution)/shard_map/ppermute | solution.py:957
  97.9 8.2 %shard_map.415 = (bf16[384,256]{1,0:T(8,128)(2,1)}, f32[384,256]{1,0:T(8,128)}, f32[384,256]{1,0:T(8,128)}, f32[64,256]{1,0:T(8,128)}) custom-call(s32[6]{0:T(128)} %copy-done.38, s32[384,5]{1,0:T(8,128)} %bitcast.63, s32[384,5]{1,0:T(8,128)} %bitcast.45, f32[384,256]{1,0:T(8,128)} %get-tuple-element.105.hidden, bf16[384,256]{1,0:T(8,128)(2,1)} %get-tuple-element.106.query, ...), custom_call_target="tpu_custom_call" | custom-call | bytes 4194304 | tf_op jit(solution)/shard_map/pallas_call | solution.py:369
  108.0 10.1 %collective-permute-start.11 = (f32[64,256]{1,0:T(8,128)}, f32[64,256]{1,0:T(8,128)S(1)}, u32[]{:S(2)}, u32[]{:S(2)}) collective-permute-start(f32[64,256]{1,0:T(8,128)} %get-tuple-element.111), channel_id=1, source_target_pairs={{0,2},{1,3},{2,0},{3,1},{4,6},{5,7},{6,4},{7,5},{8,10},{9,11},{10,... | collective-permute-start | bytes 196616 | tf_op jit(solution)/shard_map/ppermute | solution.py:966
  118.1 3.3 %collective-permute-done.11 = f32[64,256]{1,0:T(8,128)S(1)} collective-permute-done((f32[64,256]{1,0:T(8,128)}, f32[64,256]{1,0:T(8,128)S(1)}, u32[]{:S(2)}, u32[]{:S(2)}) %collective-permute-start.11) | collective-permute-done | bytes 65568 | tf_op jit(solution)/shard_map/ppermute | solution.py:966
  132.7 3.9 %collective-permute-done.16 = f32[64,256]{1,0:T(8,128)S(1)} collective-permute-done((f32[64,256]{1,0:T(8,128)S(1)}, f32[64,256]{1,0:T(8,128)S(1)}, u32[]{:S(2)}, u32[]{:S(2)}) %collective-permute-start.16) | collective-permute-done | bytes 65568 | tf_op jit(solution)/shard_map/ppermute | solution.py:966
  137.2 16.8 %shard_map.416 = (f32[8,128]{1,0:T(8,128)}, f32[32,1024]{1,0:T(8,128)}, f32[1,1024]{1,0:T(1,128)}, f32[384,256]{1,0:T(8,128)}, bf16[4,1024,128]{2,1,0:T(8,128)(2...) custom-call(s32[6]{0:T(128)} %copy-done.38, ...), custom_call_target="tpu_custom_call" | custom-call | bytes 4194304 | tf_op jit(solution)/shard_map/pallas_call | solution.py:369
  161.3 3.8 %collective-permute-done.19.drowa = bf16[4,48,512]{2,1,0:T(8,128)(2,1)S(1)} collective-permute-done((bf16[4,48,512]{2,1,0:T(8,128)(2,1)S(1)}, bf16[4,48,512]{2,1,0:T(8,128)(2,1)S(1)}, u32[]{:S(2)}, u32[]{:S(2)}) %collective-permute-start.19) | collective-permute-done | bytes 196640 | tf_op jit(solution)/shard_map/ppermute | solution.py:957
  165.9 17.0 %shard_map.418 = (f32[384,256]{1,0:T(8,128)}, bf16[4,1280,128]{2,1,0:T(8,128)(2,1)}, f32[4,256]{1,0:T(4,128)}, f32[1,768]{1,0:T(1,128)}, f32[8,176]{1,0:T(8,128)...) custom-call(s32[6]{0:T(128)} %copy-done.38, ...), custom_call_target="tpu_custom_call" | custom-call | bytes 4194304 | tf_op jit(solution)/shard_map/pallas_call | solution.py:369
  183.0 4.6 %collective-permute-start.21 = (bf16[4,48,512]{2,1,0:T(8,128)(2,1)}, bf16[4,48,512]{2,1,0:T(8,128)(2,1)S(1)}, u32[]{:S(2)}, u32[]{:S(2)}) collective-permute-start(bf16[4,48,512]{2,1,0:T(8,128)(2,1)} %get-tuple-element.130), channel_id=1, source_target_pairs={{0,4},{8,12},{16,20},{24,28},{4,0},{12,8},{20,16},{28,24},{1,5},{9... | collective-permute-start | bytes 589832 | tf_op jit(solution)/shard_map/ppermute | solution.py:957
  188.3 3.2 %collective-permute-done.21.first.drowa = bf16[4,48,512]{2,1,0:T(8,128)(2,1)S(1)} collective-permute-done((bf16[4,48,512]{2,1,0:T(8,128)(2,1)}, bf16[4,48,512]{2,1,0:T(8,128)(2,1)S(1)}, u32[]{:S(2)}, u32[]{:S(2)}) %collective-permute-start.21) | collective-permute-done | bytes 196640 | tf_op jit(solution)/shard_map/ppermute | solution.py:957
  193.6 9.1 %collective-permute-start.23 = (bf16[192,512]{1,0:T(8,128)(2,1)S(1)}, bf16[192,512]{1,0:T(8,128)(2,1)S(1)}, u32[]{:S(2)}, u32[]{:S(2)}) collective-permute-start(bf16[192,512]{1,0:T(8,128)(2,1)S(1)} %get-tuple-element.132), channel_id=1, source_target_pairs={{0,1},{2,3},{1,0},{3,2},{4,5},{6,7},{5,4},{7,6},{8,9},{10,11},{9,8... | collective-permute-start | bytes 589832 | tf_op jit(solution)/shard_map/ppermute | solution.py:957
  206.3 8.1 %collective-permute-start.25 = (bf16[2,1104,128]{2,1,0:T(8,128)(2,1)S(1)}, bf16[2,1104,128]{2,1,0:T(8,128)(2,1)S(1)}, u32[]{:S(2)}, u32[]{:S(2)}) collective-permute-start(bf16[2,1104,128]{2,1,0:T(8,128)(2,1)S(1)} %get-tuple-element.142), channel_id=1, source_target_pairs={{0,1},{1,0},{2,3},{3,2},{4,5},{5,4},{6,7},{7,6},{8,9},{9,8},{10,11... | collective-permute-start | bytes 1695752 | tf_op jit(solution)/shard_map/ppermute | solution.py:1137
  218.9 8.3 %collective-permute-done.26.given = bf16[1,1104,128]{2,1,0:T(8,128)(2,1)S(1)} collective-permute-done((bf16[1,1104,128]{2,1,0:T(8,128)(2,1)S(1)}, bf16[1,1104,128]{2,1,0:T(8,128)(2,1)S(1)}, u32[]{:S(2)}, u32[]{:S(2)}) %collective-permute-start.26) | collective-permute-done | bytes 282656 | tf_op jit(solution)/shard_map/ppermute | solution.py:1137
  230.2 9.0 %all-to-all-start.2 = ((bf16[8,496,128]{2,1,0:T(8,128)(2,1)}), bf16[8,496,128]{2,1,0:T(8,128)(2,1)S(1)}, u32[]{:S(2)}, u32[]{:S(2)}) async-start(bf16[8,496,128]{2,1,0:T(8,128)(2,1)} %shard_map.422), calls=%async_computation.4 | async-start | bytes 2031616 | tf_op jit(solution)/shard_map/all_to_all | solution.py:1154
  242.7 21.5 %all-to-all-done.2.parts = bf16[8,496,128]{2,1,0:T(8,128)(2,1)S(1)} async-done(((bf16[8,496,128]{2,1,0:T(8,128)(2,1)}), bf16[8,496,128]{2,1,0:T(8,128)(2,1)S(1)}, u32[]{:S(2)}, u32[]{:S(2)}) %all-to-all-start.2) | async-done | bytes 1015840 | tf_op jit(solution)/shard_map/all_to_all | solution.py:1154
  264.5 6.7 %all-gather.3 = bf16[1664,128]{1,0:T(8,128)(2,1)S(1)} all-gather(bf16[416,128]{1,0:T(8,128)(2,1)S(1)} %get-tuple-element.145), channel_id=5, replica_groups=mesh['row'=8,'col'=4] {'col'}, dimensions={0}, use_global_device_ids=true | all-gather | bytes 532480 | tf_op jit(solution)/shard_map/all_gather | solution.py:1158
  (229 shorter events, 70.6 us)
Async XLA Ops:
  7.2 34.8 %all-gather.8.cloned.1.call-start = ((), (), s32[]{:S(2)}) async-start(), calls=%async_computation.7 | async-start | bytes 1310720 | tf_op jit(solution)/shard_map/all_gather | solution.py:1031
  25.9 6.4 %collective-permute-start = (bf16[1,32,128]{2,1,0:T(8,128)(2,1)S(1)}, bf16[1,32,128]{2,1,0:T(8,128)(2,1)S(1)}, u32[]{:S(2)}, u32[]{:S(2)}) collective-permute-start(bf16[1,32,128]{2,1,0:T(8,128)(2,1)S(1)} %slice.51), channel_id=1, source_target_pairs={{0,4},{4,8},{8,12},{12,16},{16,20},{20,24},{24,28},{28,0},{1,5},{5... | collective-permute-start | bytes 24584 | tf_op jit(solution)/shard_map/ppermute | solution.py:950
  32.3 20.3 %all-to-all-start.1 = ((bf16[8,352,128]{2,1,0:T(8,128)(2,1)}), bf16[8,352,128]{2,1,0:T(8,128)(2,1)}, u32[]{:S(2)}, u32[]{:S(2)}) async-start(bf16[8,352,128]{2,1,0:T(8,128)(2,1)} %get-tuple-element.103), calls=%async_computation.1 | async-start | bytes 1441792 | tf_op jit(solution)/shard_map/all_to_all | solution.py:1032
  36.6 36.0 %all-gather.10.cloned.1.call-start = ((), (), s32[]{:S(2)}) async-start(), calls=%async_computation.8 | async-start | bytes 1638400 | tf_op jit(solution)/shard_map/all_gather | solution.py:1041
  54.4 42.4 %all-gather.12.cloned.1.call-start = ((), (), s32[]{:S(2)}) async-start(), calls=%async_computation.9 | async-start | bytes 1966080 | tf_op jit(solution)/shard_map/all_gather | solution.py:1042
  56.3 162.6 %reduce-scatter.3.cloned.1.call-start = ((), (), s32[]{:S(2)}) async-start(), calls=%async_computation.5 | async-start | bytes 1310720 | tf_op jit(solution)/shard_map/reduce_scatter | solution.py:1105
  58.4 5.7 %collective-permute-start.4 = (bf16[4,48,512]{2,1,0:T(8,128)(2,1)S(1)}, bf16[4,48,512]{2,1,0:T(8,128)(2,1)S(1)}, u32[]{:S(2)}, u32[]{:S(2)}) collective-permute-start(bf16[4,48,512]{2,1,0:T(8,128)(2,1)S(1)} %get-tuple-element.99), channel_id=1, source_target_pairs={{0,4},{8,12},{16,20},{24,28},{4,0},{12,8},{20,16},{28,24},{1,5},{9... | collective-permute-start | bytes 589832 | tf_op jit(solution)/shard_map/ppermute | solution.py:957
  80.9 7.2 %collective-permute-start.6 = (bf16[4,48,512]{2,1,0:T(8,128)(2,1)}, bf16[4,48,512]{2,1,0:T(8,128)(2,1)S(1)}, u32[]{:S(2)}, u32[]{:S(2)}) collective-permute-start(bf16[4,48,512]{2,1,0:T(8,128)(2,1)} %get-tuple-element.108), channel_id=1, source_target_pairs={{0,4},{8,12},{16,20},{24,28},{4,0},{12,8},{20,16},{28,24},{1,5},{9... | collective-permute-start | bytes 589832 | tf_op jit(solution)/shard_map/ppermute | solution.py:957
  82.3 5.8 %collective-permute-start.7 = (bf16[4,48,512]{2,1,0:T(8,128)(2,1)}, bf16[4,48,512]{2,1,0:T(8,128)(2,1)S(1)}, u32[]{:S(2)}, u32[]{:S(2)}) collective-permute-start(bf16[4,48,512]{2,1,0:T(8,128)(2,1)} %get-tuple-element.109), channel_id=1, source_target_pairs={{4,8},{12,16},{20,24},{8,4},{16,12},{24,20},{5,9},{13,17},{21,25},... | collective-permute-start | bytes 589832 | tf_op jit(solution)/shard_map/ppermute | solution.py:957
  89.7 7.0 %collective-permute-start.9 = (bf16[4,192,512]{2,1,0:T(8,128)(2,1)S(1)}, bf16[4,192,512]{2,1,0:T(8,128)(2,1)S(1)}, u32[]{:S(2)}, u32[]{:S(2)}) collective-permute-start(bf16[4,192,512]{2,1,0:T(8,128)(2,1)S(1)} %shard_map.414.own), channel_id=1, source_target_pairs={{1,2},{2,1},{5,6},{6,5},{9,10},{10,9},{13,14},{14,13},{17,18},{18,... | collective-permute-start | bytes 2359304 | tf_op jit(solution)/shard_map/ppermute | solution.py:957
  90.5 7.5 %collective-permute-start.8 = (bf16[4,192,512]{2,1,0:T(8,128)(2,1)S(1)}, bf16[4,192,512]{2,1,0:T(8,128)(2,1)}, u32[]{:S(2)}, u32[]{:S(2)}) collective-permute-start(bf16[4,192,512]{2,1,0:T(8,128)(2,1)S(1)} %shard_map.414.own), channel_id=1, source_target_pairs={{0,1},{2,3},{1,0},{3,2},{4,5},{6,7},{5,4},{7,6},{8,9},{10,11},{9,8... | collective-permute-start | bytes 2359304 | tf_op jit(solution)/shard_map/ppermute | solution.py:957
  106.2 11.9 %collective-permute-start.12 = (f32[64,256]{1,0:T(8,128)}, f32[64,256]{1,0:T(8,128)S(1)}, u32[]{:S(2)}, u32[]{:S(2)}) collective-permute-start(f32[64,256]{1,0:T(8,128)} %get-tuple-element.111), channel_id=1, source_target_pairs={{0,3},{1,2},{2,1},{3,0},{4,7},{5,6},{6,5},{7,4},{8,11},{9,10},{10,... | collective-permute-start | bytes 196616 | tf_op jit(solution)/shard_map/ppermute | solution.py:966
  108.0 13.4 %collective-permute-start.11 = (f32[64,256]{1,0:T(8,128)}, f32[64,256]{1,0:T(8,128)S(1)}, u32[]{:S(2)}, u32[]{:S(2)}) collective-permute-start(f32[64,256]{1,0:T(8,128)} %get-tuple-element.111), channel_id=1, source_target_pairs={{0,2},{1,3},{2,0},{3,1},{4,6},{5,7},{6,4},{7,5},{8,10},{9,11},{10,... | collective-permute-start | bytes 196616 | tf_op jit(solution)/shard_map/ppermute | solution.py:966
  122.3 5.3 %collective-permute-start.15 = (f32[64,256]{1,0:T(8,128)S(1)}, f32[64,256]{1,0:T(8,128)S(1)}, u32[]{:S(2)}, u32[]{:S(2)}) collective-permute-start(f32[64,256]{1,0:T(8,128)S(1)} %add_add_fusion.1), channel_id=1, source_target_pairs={{0,12},{4,8},{8,4},{12,0},{16,28},{20,24},{24,20},{28,16},{1,13},{... | collective-permute-start | bytes 196616 | tf_op jit(solution)/shard_map/ppermute | solution.py:966
  124.9 5.2 %collective-permute-start.14 = (f32[64,256]{1,0:T(8,128)S(1)}, f32[64,256]{1,0:T(8,128)S(1)}, u32[]{:S(2)}, u32[]{:S(2)}) collective-permute-start(f32[64,256]{1,0:T(8,128)S(1)} %add_add_fusion.1), channel_id=1, source_target_pairs={{0,8},{4,12},{8,0},{12,4},{16,24},{20,28},{24,16},{28,20},{1,9},{5... | collective-permute-start | bytes 196616 | tf_op jit(solution)/shard_map/ppermute | solution.py:966
  130.7 5.9 %collective-permute-start.16 = (f32[64,256]{1,0:T(8,128)S(1)}, f32[64,256]{1,0:T(8,128)S(1)}, u32[]{:S(2)}, u32[]{:S(2)}) collective-permute-start(f32[64,256]{1,0:T(8,128)S(1)} %add_add_fusion), channel_id=1, source_target_pairs={{0,16},{4,20},{8,24},{12,28},{16,0},{20,4},{24,8},{28,12},{1,17},{... | collective-permute-start | bytes 196616 | tf_op jit(solution)/shard_map/ppermute | solution.py:966
  154.1 73.1 %reduce-scatter.5.cloned.1.call-start = ((), (), s32[]{:S(2)}) async-start(), calls=%async_computation.6 | async-start | bytes 1638400 | tf_op jit(solution)/shard_map/reduce_scatter | solution.py:1121
  159.4 5.7 %collective-permute-start.19 = (bf16[4,48,512]{2,1,0:T(8,128)(2,1)S(1)}, bf16[4,48,512]{2,1,0:T(8,128)(2,1)S(1)}, u32[]{:S(2)}, u32[]{:S(2)}) collective-permute-start(bf16[4,48,512]{2,1,0:T(8,128)(2,1)S(1)} %get-tuple-element.122), channel_id=1, source_target_pairs={{0,4},{8,12},{16,20},{24,28},{4,0},{12,8},{20,16},{28,24},{1,5},{9... | collective-permute-start | bytes 589832 | tf_op jit(solution)/shard_map/ppermute | solution.py:957
  160.7 4.5 %collective-permute-start.20 = (bf16[4,48,512]{2,1,0:T(8,128)(2,1)S(1)}, bf16[4,48,512]{2,1,0:T(8,128)(2,1)S(1)}, u32[]{:S(2)}, u32[]{:S(2)}) collective-permute-start(bf16[4,48,512]{2,1,0:T(8,128)(2,1)S(1)} %get-tuple-element.123), channel_id=1, source_target_pairs={{4,8},{12,16},{20,24},{8,4},{16,12},{24,20},{5,9},{13,17},{21,25},... | collective-permute-start | bytes 589832 | tf_op jit(solution)/shard_map/ppermute | solution.py:957
  183.0 8.5 %collective-permute-start.21 = (bf16[4,48,512]{2,1,0:T(8,128)(2,1)}, bf16[4,48,512]{2,1,0:T(8,128)(2,1)S(1)}, u32[]{:S(2)}, u32[]{:S(2)}) collective-permute-start(bf16[4,48,512]{2,1,0:T(8,128)(2,1)} %get-tuple-element.130), channel_id=1, source_target_pairs={{0,4},{8,12},{16,20},{24,28},{4,0},{12,8},{20,16},{28,24},{1,5},{9... | collective-permute-start | bytes 589832 | tf_op jit(solution)/shard_map/ppermute | solution.py:957
  193.6 10.2 %collective-permute-start.23 = (bf16[192,512]{1,0:T(8,128)(2,1)S(1)}, bf16[192,512]{1,0:T(8,128)(2,1)S(1)}, u32[]{:S(2)}, u32[]{:S(2)}) collective-permute-start(bf16[192,512]{1,0:T(8,128)(2,1)S(1)} %get-tuple-element.132), channel_id=1, source_target_pairs={{0,1},{2,3},{1,0},{3,2},{4,5},{6,7},{5,4},{7,6},{8,9},{10,11},{9,8... | collective-permute-start | bytes 589832 | tf_op jit(solution)/shard_map/ppermute | solution.py:957
  206.3 9.6 %collective-permute-start.25 = (bf16[2,1104,128]{2,1,0:T(8,128)(2,1)S(1)}, bf16[2,1104,128]{2,1,0:T(8,128)(2,1)S(1)}, u32[]{:S(2)}, u32[]{:S(2)}) collective-permute-start(bf16[2,1104,128]{2,1,0:T(8,128)(2,1)S(1)} %get-tuple-element.142), channel_id=1, source_target_pairs={{0,1},{1,0},{2,3},{3,2},{4,5},{5,4},{6,7},{7,6},{8,9},{9,8},{10,11... | collective-permute-start | bytes 1695752 | tf_op jit(solution)/shard_map/ppermute | solution.py:1137
  216.8 10.3 %collective-permute-start.26 = (bf16[1,1104,128]{2,1,0:T(8,128)(2,1)S(1)}, bf16[1,1104,128]{2,1,0:T(8,128)(2,1)S(1)}, u32[]{:S(2)}, u32[]{:S(2)}) collective-permute-start(bf16[1,1104,128]{2,1,0:T(8,128)(2,1)S(1)} %get-tuple-element.144), channel_id=1, source_target_pairs={{0,2},{1,3},{2,0},{3,1},{4,6},{5,7},{6,4},{7,5},{8,10},{9,11},{10,... | collective-permute-start | bytes 847880 | tf_op jit(solution)/shard_map/ppermute | solution.py:1137
  230.2 34.0 %all-to-all-start.2 = ((bf16[8,496,128]{2,1,0:T(8,128)(2,1)}), bf16[8,496,128]{2,1,0:T(8,128)(2,1)S(1)}, u32[]{:S(2)}, u32[]{:S(2)}) async-start(bf16[8,496,128]{2,1,0:T(8,128)(2,1)} %shard_map.422), calls=%async_computation.4 | async-start | bytes 2031616 | tf_op jit(solution)/shard_map/all_to_all | solution.py:1154
  (72 other events, 1194.8 us)
Sparse Core Ops, SparseCore 0:
  26.0 15.9 all-gather.7
  54.5 17.9 all-gather.9
  74.1 18.8 all-gather.11
  154.2 22.9 reduce-scatter.2
  183.2 40.1 reduce-scatter.4

commit v5 on v4

--- a/solution.py
+++ b/solution.py
@@ -75,7 +75,7 @@
 
 class One:
     dilation, queries, across, pieces, steps = 1, 64, 16, 4, 6
-    forward, back = 3, 3
+    together = 3
     keys = pieces * 128
 
     @staticmethod
@@ -94,7 +94,7 @@
 
 class Two:
     dilation, queries, across, pieces, steps = 2, 32, 8, 3, 12
-    forward, back = 3, 3
+    together = 3
     keys = pieces * 128
 
     @staticmethod
@@ -251,12 +251,16 @@
 def softmax_rows(score, table, mask):
     score = score * (scale * LOG2E) + (table + mask)
     weight = jnp.exp2(score - jnp.max(score, -1, keepdims=True))
-    return weight, 1.0 / jnp.sum(weight, -1, keepdims=True)
-
-
-def attend(geo, place, lay_ref, query_ref, pieces, table_ref, out_ref, score_ref, prob_ref, share_ref):
+    return weight * (1.0 / jnp.sum(weight, -1, keepdims=True))
+
+
+def attend(geo, place, lay_ref, query_ref, pieces, table_ref, out_ref, score_ref, prob_ref, kept, sems):
     count = geo.queries
     together = score_ref.shape[0]
+
+    def keep(index):
+        span = pl.ds(index * together, together)
+        return pltpu.make_async_copy(prob_ref.at[span], kept.at[span], sems.at[index])
 
     def steps_of(index, carry):
         steps = [index * together + n for n in range(together)]
@@ -269,25 +273,24 @@
         ]
         for h in range(HEADS):
             span = slice(h * count, (h + 1) * count)
-            for n in range(together):
-                weight, share = softmax_rows(score_ref[n, span, :], table_ref[span, :], masks[n])
-                prob_ref[n, span, :] = weight.astype(bf16)
-                share_ref[n, span, :] = jnp.broadcast_to(share, (count, 128))
+            for n, step in enumerate(steps):
+                prob = softmax_rows(score_ref[n, span, :], table_ref[span, :], masks[n])
+                prob_ref[step, span, :] = prob.astype(bf16)
+        keep(index).start()
         for n, step in enumerate(steps):
-            out = nn(prob_ref[n], load_keys(geo, pieces, step, VALUE))
-            out = out * jnp.concatenate([share_ref[n]] * 2, 1)
+            out = nn(prob_ref[step], load_keys(geo, pieces, step, VALUE))
             out_ref[rows[n], :] = from_heads(out).astype(out_ref.dtype)
         return carry
 
     lax.fori_loop(0, geo.steps // together, steps_of, 0)
+    return [keep(index) for index in range(geo.steps // together)]
 
 
 def attend_back(
-    geo, place, lay_ref, query_ref, dout_ref, pieces, table_ref, dquery_ref, dpieces, dtable_ref,
-    score_ref, dprob_ref, prob_ref, dscore_ref,
+    geo, query_ref, dout_ref, pieces, prob_ref, dquery_ref, dpieces, dtable_ref, dprob_ref, dscore_ref,
 ):
     count = geo.queries
-    together = score_ref.shape[0]
+    together = dprob_ref.shape[0]
     dtable_ref[...] = jnp.zeros_like(dtable_ref)
     dpieces[...] = jnp.zeros_like(dpieces)
 
@@ -295,19 +298,12 @@
         steps = [index * together + n for n in range(together)]
         rows = [pl.ds(pl.multiple_of(step * count, count), count) for step in steps]
         for n, step in enumerate(steps):
-            score_ref[n] = nt(by_head(query_ref[rows[n], :]), load_keys(geo, pieces, step, KEY))
             dprob_ref[n] = nt(by_head(dout_ref[rows[n], :]), load_keys(geo, pieces, step, VALUE))
-        masks = [
-            window_mask(geo, lay_ref[rows[n], :], step, place[0], place[1])
-            for n, step in enumerate(steps)
-        ]
         for h in range(HEADS):
             span = slice(h * count, (h + 1) * count)
             total = dtable_ref[span, :]
-            for n in range(together):
-                weight, share = softmax_rows(score_ref[n, span, :], table_ref[span, :], masks[n])
-                prob = weight * share
-                prob_ref[n, span, :] = prob.astype(bf16)
+            for n, step in enumerate(steps):
+                prob = prob_ref[step, span, :].astype(f32)
                 dprob = dprob_ref[n, span, :]
                 dscore = prob * (dprob - jnp.sum(prob * dprob, -1, keepdims=True))
                 total += dscore
@@ -316,7 +312,7 @@
         for n, step in enumerate(steps):
             wide, dwide = by_head(query_ref[rows[n], :]), by_head(dout_ref[rows[n], :])
             dscore = dscore_ref[n]
-            add_keys(geo, dpieces, step, VALUE, tn(prob_ref[n], dwide))
+            add_keys(geo, dpieces, step, VALUE, tn(prob_ref[step], dwide))
             add_keys(geo, dpieces, step, KEY, tn(dscore, wide) * scale)
             dquery_ref[rows[n], :] = from_heads(nn(dscore, load_keys(geo, pieces, step, KEY))) * scale
         return carry
@@ -362,15 +358,18 @@
         after(second)
 
 
-def run(kernel, outs, ins, scratch=(), specs=None, vmem=16):
+def run(kernel, outs, ins, scratch=(), specs=None, vmem=16, out_specs=None):
     in_specs = [pl.BlockSpec(memory_space=pltpu.VMEM)] * len(ins)
     for index, spec in (specs or {}).items():
         in_specs[index] = spec
+    results = [pl.BlockSpec(memory_space=pltpu.VMEM)] * len(outs)
+    for index, spec in (out_specs or {}).items():
+        results[index] = spec
     return pl.pallas_call(
         kernel,
         out_shape=outs,
         in_specs=in_specs,
-        out_specs=[pl.BlockSpec(memory_space=pltpu.VMEM)] * len(outs),
+        out_specs=results,
         scratch_shapes=list(scratch),
         compiler_params=pltpu.CompilerParams(vmem_limit_bytes=vmem * MIB),
         cost_estimate=pl.CostEstimate(flops=0, bytes_accessed=4 << 20, transcendentals=0),
@@ -519,34 +518,58 @@
         put(row_second, 144)
 
 
-def gather_keys_one(place, keyval, col_first, col_second, row_first, row_second, pieces):
-    pieces[0, 48:240, :] = keyval[0]
-    pieces[1, 48:240, :] = keyval[1]
-
-    def into(index, rows):
-        def put(source):
-            pieces[index, rows, :] = source[...]
-
-        return put
-
-    every = slice(None)
-    middle = slice(48, 240)
-    store_received(place, EVEN_COL, col_first, col_second, into(2, middle), into(3, middle))
-    store_received(
-        place, EVEN_ROW, row_first, row_second, into(every, slice(0, 48)), into(every, slice(240, 288))
-    )
-
-
-def gather_keys_two(place, own, first, second, pieces):
-    pieces[0] = own[...]
-
-    def into(index):
-        def put(source):
-            pieces[index] = source[...]
-
-        return put
-
-    store_received(place, EVEN_COL, first, second, into(1), into(2))
+class Copies:
+    def __init__(self, sems):
+        self.sems, self.used = sems, 0
+
+    def semaphore(self):
+        self.used += 1
+        return self.sems.at[self.used - 1]
+
+    def start(self, source, target):
+        copy = pltpu.make_async_copy(source, target, self.semaphore())
+        copy.start()
+        return [copy]
+
+    def start_received(self, place, even, first, second, before, after):
+        one, two = self.semaphore(), self.semaphore()
+
+        @pl.when(place[even] == 1)
+        def _():
+            pltpu.make_async_copy(second, before, one).start()
+            pltpu.make_async_copy(first, after, two).start()
+
+        @pl.when(place[even] == 0)
+        def _():
+            pltpu.make_async_copy(first, before, one).start()
+            pltpu.make_async_copy(second, after, two).start()
+
+        return [pltpu.make_async_copy(first, before, one), pltpu.make_async_copy(first, after, two)]
+
+
+def wait_for(copies):
+    for copy in copies:
+        copy.wait()
+
+
+def gather_keys_one(copies, place, keyval, col_first, col_second, row_first, row_second, pieces):
+    inner = pl.ds(48, 192)
+    return (
+        copies.start(keyval, pieces.at[pl.ds(0, 2), inner, :])
+        + copies.start_received(
+            place, EVEN_COL, col_first, col_second, pieces.at[2, inner, :], pieces.at[3, inner, :]
+        )
+        + copies.start_received(
+            place, EVEN_ROW, row_first, row_second,
+            pieces.at[:, pl.ds(0, 48), :], pieces.at[:, pl.ds(240, 48), :],
+        )
+    )
+
+
+def gather_keys_two(copies, place, own, first, second, pieces):
+    return copies.start(own, pieces.at[0]) + copies.start_received(
+        place, EVEN_COL, first, second, pieces.at[1], pieces.at[2]
+    )
 
 
 def extend_kernel(place, keyval, first, second, result):
@@ -561,22 +584,24 @@
     store_received(place, EVEN_ROW, first, second, above, below)
 
 
-def rim_kernel(place, own, first, second, row_first, row_second):
-    def total(begin):
-        rows = slice(begin, begin + 48)
-        value = own[:, rows, :] + first[:, rows, :].astype(f32) + second[:, rows, :].astype(f32)
+def rim_kernel(place, rims, first, second, row_first, row_second):
+    def total(part):
+        rows = slice(144 * part, 144 * part + 48)
+        value = rims[:, 48 * part : 48 * part + 48, :].astype(f32)
+        value += first[:, rows, :].astype(f32) + second[:, rows, :].astype(f32)
         return value.astype(bf16)
 
-    send(place, EVEN_ROW, row_first, row_second, lambda: total(144), lambda: total(0))
-
-
-def sides_kernel(place, inner, first, second, col_first, col_second):
+    send(place, EVEN_ROW, row_first, row_second, lambda: total(1), lambda: total(0))
+
+
+def sides_kernel(place, sides, first, second, col_first, col_second):
     def total(p):
-        above, below = received(place, EVEN_ROW, first[p], second[p])
-        rows = [inner[p, 0:48, :] + above, inner[p, 48:144, :], inner[p, 144:192, :] + below]
+        above, below = received(place, EVEN_ROW, first[2 + p], second[2 + p])
+        own = sides[p].astype(f32)
+        rows = [own[0:48] + above, own[48:144], own[144:192] + below]
         return jnp.concatenate(rows, 0).astype(bf16)
 
-    send(place, EVEN_COL, col_first, col_second, lambda: total(3), lambda: total(2))
+    send(place, EVEN_COL, col_first, col_second, lambda: total(1), lambda: total(0))
 
 
 def feed_forward(hidden, norms, w_exp, w_red, bias):
@@ -589,23 +614,19 @@
 PROJ, EXP, RED, QKV, HEAD = 0, 2, 8, 14, 14
 
 
-def fetch(source, buffer, sem):
-    copy = pltpu.make_async_copy(source, buffer, sem.at[0])
-    copy.start()
-    return copy.wait
-
-
 def first_block_kernel(
     place, lay, hidden, query, keyval, cola, colb, rowa, rowb, first_table, late, norms, ebias,
-    att, middle, last, query2, keyval2, first, second,
-    pieces, table, score, prob, share, group, sem,
+    kept, att, middle, last, query2, keyval2, first, second,
+    pieces, table, score, prob, group, before, sems, keep_sems,
 ):
-    arrived = fetch(late, group, sem)
-    gather_keys_one(place, keyval, cola, colb, rowa, rowb, pieces)
+    copies = Copies(sems)
+    near = gather_keys_one(copies, place, keyval, cola, colb, rowa, rowb, pieces)
+    arrived = copies.start(late, group) + copies.start(hidden, before)
     spread_table(One, first_table, table)
-    attend(One, place, lay, query, pieces, table, att, score, prob, share)
-    arrived()
-    mid = hidden[...] + nn(att[...], weight_of(group, PROJ, 2))
+    wait_for(near)
+    leaving = attend(One, place, lay, query, pieces, table, att, score, prob, kept, keep_sems)
+    wait_for(arrived)
+    mid = before[...] + nn(att[...], weight_of(group, PROJ, 2))
     middle[...] = mid
     end = feed_forward(mid, norms[4:6, :], weight_of(group, EXP, 6), weight_red(group, RED), ebias[0:1, :])
     last[...] = end
@@ -617,6 +638,7 @@
     send(
         place, EVEN_ROW, first, second, lambda: keyval2[:, 48:, :], lambda: keyval2[:, :48, :]
     )
+    wait_for(leaving)
 
 
 def slot_onehot(slots, images):
@@ -631,18 +653,20 @@
 
 def second_block_kernel(
     place, lay, slots, hidden, query, own, cola, colb, first_table, late, norms, ebias,
-    att, middle, last, sums,
-    pieces, table, score, prob, share, att_group, att_token, group, sem,
+    kept, att, middle, last, sums,
+    pieces, table, score, prob, group, before, att_group, att_token, sems, keep_sems,
 ):
-    arrived = fetch(late, group, sem)
-    gather_keys_two(place, own, cola, colb, pieces)
+    copies = Copies(sems)
+    near = gather_keys_two(copies, place, own, cola, colb, pieces)
+    arrived = copies.start(late, group) + copies.start(hidden, before)
     spread_table(Two, first_table, table)
-    attend(Two, place, lay, query, pieces, table, att_group, score, prob, share)
+    wait_for(near)
+    leaving = attend(Two, place, lay, query, pieces, table, att_group, score, prob, kept, keep_sems)
     ungroup(att_group[...], att_token)
     low = att_token[...].reshape(384, D).astype(bf16)
     att[...] = low
-    arrived()
-    mid = hidden[...] + nn(low, weight_of(group, PROJ, 2))
+    wait_for(arrived)
+    mid = before[...] + nn(low, weight_of(group, PROJ, 2))
     middle[...] = mid
     end = feed_forward(mid, norms[8:10, :], weight_of(group, EXP, 6), weight_red(group, RED), ebias[1:2, :])
     last[...] = end
@@ -653,6 +677,7 @@
     sums[...] = jnp.zeros_like(sums)
     sums[:images, :D] = tn(where, high) + tn(where, low)
     sums[images:, :images] = tn(jnp.ones((384, 8), bf16), where)
+    wait_for(leaving)
 
 
 def feed_forward_back(dhid, mid, gain_bias, w_exp, w_red, bias):
@@ -692,14 +717,14 @@
 
 
 def second_back_kernel(
-    place, lay, slots, sums, labels, live, hbias, hidden, middle, att, query, own, cola, colb,
-    first_table, late, norms, ebias,
-    loss, grad_head, grad_hbias, dhidden, grads, dnorms, debias, dpos, dquery, down, first, second,
-    pieces, table, dtable, score, dscore_f, prob, dscore, dpieces, datt, dq_group, dfirst, dq_token, group, sem,
+    place, slots, sums, labels, live, hbias, hidden, middle, att, query, own, cola, colb, kept, late,
+    norms, ebias,
+    loss, grad_head, grad_hbias, dhidden, grads, dnorms, debias, dtable, dquery, inner, rims, first, second,
+    pieces, prob, dprob, dscore, dpieces, datt, dq_group, group, grads_out, dq_token, sems,
 ):
-    arrived = fetch(late, group, sem)
-    gather_keys_two(place, own, cola, colb, pieces)
-    spread_table(Two, first_table, table)
+    copies = Copies(sems)
+    weights = copies.start(late, group)
+    near = gather_keys_two(copies, place, own, cola, colb, pieces) + copies.start(kept, prob)
     images = sums.shape[0] - 8
     total = sums[:images, :D]
     diagonal = lax.broadcasted_iota(i32, (images, images), 0)
@@ -708,7 +733,7 @@
     area = jnp.sum(area, -1, keepdims=True)
     spread_area = jnp.maximum(area, 1.0)
     pooled = (total / spread_area).astype(bf16)
-    arrived()
+    wait_for(weights)
     w_head = weight_of(group, HEAD, 8)
     logits = nn(pooled, w_head) + hbias[...]
     weight = live[...] * jnp.where(area > 0.5, 1.0, 0.0)
@@ -735,81 +760,90 @@
     dhid, grad_red, grad_exp, grad_bias, dgain, dbias = feed_forward_back(
         dhid, middle[...], norms[8:10, :], weight_of(group, EXP, 6), weight_red(group, RED), ebias[1:2, :]
     )
-    put_cols(grads, 0, grad_exp)
-    put_red(grads, 6, grad_red, share)
+    put_cols(grads_out, 0, grad_exp)
+    put_red(grads_out, 6, grad_red, share)
     debias[...] = grad_bias
     dnorms[0:1, :] = dgain
     dnorms[1:2, :] = dbias
     dhidden[...] = dhid
     dy = dhid.astype(bf16)
-    put_cols(grads, 12, tn(att[...], dy))
-    put_zeros(grads, 14)
+    put_cols(grads_out, 12, tn(att[...], dy))
+    put_zeros(grads_out, 14)
+    leaving = copies.start(grads_out, grads)
     back = nt(dy, weight_of(group, PROJ, 2))
     for g, part in enumerate(grouped(back)):
         datt[g * 96 : (g + 1) * 96, :] = part.astype(bf16)
-    attend_back(
-        Two, place, lay, query, datt, pieces, table, dq_group, dpieces, dtable,
-        score, dscore_f, prob, dscore,
-    )
+    wait_for(near)
+    attend_back(Two, query, datt, pieces, prob, dq_group, dpieces, dtable, dprob, dscore)
     ungroup(dq_group[...], dq_token)
     dquery[...] = dq_token[...].reshape(384, D).astype(bf16)
-    down[...] = dpieces[0]
+    inner[...] = dpieces[0, :, 48:144, :]
+    rims[:, 0:48, :] = dpieces[0, :, 0:48, :].astype(bf16)
+    rims[:, 48:96, :] = dpieces[0, :, 144:192, :].astype(bf16)
     send(
         place, EVEN_COL, first, second,
         lambda: dpieces[2].astype(bf16), lambda: dpieces[1].astype(bf16),
     )
-    dpos[...] = gather_table(Two, dtable, dfirst)
+    wait_for(leaving)
+
+
+def position_kernel(dtable, dpos, dfirst, *, geo):
+    dpos[...] = gather_table(geo, dtable, dfirst)
 
 
 def first_back_kernel(
-    place, lay, dhid_in, dquery2, dkv, dcola, dcolb, drowa, drowb, hidden, middle, att, query, keyval,
-    cola, colb, rowa, rowb, first_table, late, norms, ebias,
-    dhidden, grads, dnorms, debias, dpos, dquery, inner, first, second,
-    pieces, table, dtable, score, dscore_f, prob, dscore, dpieces, datt, dq, dfirst, dkv_token, group, sem,
+    place, dhid_in, dquery2, dkv, dcola, dcolb, drowa, drowb, hidden, middle, att, query,
+    keyval, cola, colb, rowa, rowb, kept, late, norms, ebias,
+    dhidden, grads, dnorms, debias, dtable, dquery, inner, sides, first, second,
+    pieces, prob, dprob, dscore, dpieces, datt, dq, group, grads_out, parta, partb, dkv_token, sems,
 ):
-    arrived = fetch(late, group, sem)
-    gather_keys_one(place, keyval, cola, colb, rowa, rowb, pieces)
-    spread_table(One, first_table, table)
+    copies = Copies(sems)
+    rows = pl.ds(48, 96)
+    parts = copies.start(dcola.at[:, rows, :], parta) + copies.start(dcolb.at[:, rows, :], partb)
+    weights = copies.start(late, group)
+    near = gather_keys_one(copies, place, keyval, cola, colb, rowa, rowb, pieces)
+    near += copies.start(kept, prob)
+    wait_for(parts)
     for g in range(4):
-        rows = slice(48, 144)
-        total = dkv[g, rows, :] + dcola[g, rows, :].astype(f32) + dcolb[g, rows, :].astype(f32)
+        total = dkv[g] + parta[g].astype(f32) + partb[g].astype(f32)
         total += jnp.concatenate(received(place, EVEN_ROW, drowa[g], drowb[g]), 0)
         dkv_token[:, g >> 1, g & 1] = total.reshape(12, 8, 2 * D)
     dmixed = jnp.concatenate(
         [dquery2[...], dkv_token[...].reshape(384, 2 * D).astype(bf16)], 1
     )
     low = norm(hidden[...], norms[6:8, :]).astype(bf16)
-    put_cols(grads, 0, tn(low, dmixed))
-    arrived()
+    put_cols(grads_out, 0, tn(low, dmixed))
+    wait_for(weights)
     dx, dgain, dbias = norm_back(
         hidden[...], norms[6:8, :], nt(dmixed, weight_of(group, QKV, 6))
     )
     dnorms[2:3, :] = dgain
     dnorms[3:4, :] = dbias
     dhid, grad_red, grad_exp, grad_bias, dgain, dbias = feed_forward_back(
-        dhid_in[...] + dx, middle[...], norms[4:6, :], weight_of(group, EXP, 6), weight_red(group, RED), ebias[0:1, :]
-    )
-    put_cols(grads, 6, grad_exp)
-    put_red(grads, 12, grad_red, D // late.shape[1])
+        dhid_in[...] + dx, middle[...], norms[4:6, :], weight_of(group, EXP, 6), weight_red(group, RED),
+        ebias[0:1, :],
+    )
+    put_cols(grads_out, 6, grad_exp)
+    put_red(grads_out, 12, grad_red, D // late.shape[1])
     debias[...] = grad_bias
     dnorms[0:1, :] = dgain
     dnorms[1:2, :] = dbias
     dhidden[...] = dhid
     dy = dhid.astype(bf16)
-    put_cols(grads, 18, tn(att[...], dy))
-    put_zeros(grads, 20)
+    put_cols(grads_out, 18, tn(att[...], dy))
+    put_zeros(grads_out, 20)
+    leaving = copies.start(grads_out, grads)
     datt[...] = nt(dy, weight_of(group, PROJ, 2)).astype(bf16)
-    attend_back(
-        One, place, lay, query, datt, pieces, table, dq, dpieces, dtable,
-        score, dscore_f, prob, dscore,
-    )
+    wait_for(near)
+    attend_back(One, query, datt, pieces, prob, dq, dpieces, dtable, dprob, dscore)
     dquery[...] = dq[...].astype(bf16)
-    inner[...] = dpieces[:, 48:240, :]
+    inner[...] = dpieces[0:2, 48:240, :]
+    sides[...] = dpieces[2:4, 48:240, :].astype(bf16)
     send(
         place, EVEN_ROW, first, second,
         lambda: dpieces[:, 240:288, :].astype(bf16), lambda: dpieces[:, 0:48, :].astype(bf16),
     )
-    dpos[...] = gather_table(One, dtable, dfirst)
+    wait_for(leaving)
 
 
 SMALL_ROWS = 80
@@ -1042,84 +1076,100 @@
     late2 = lax.all_gather(late[:, parts[1] :], "col", axis=0)
     cols1 = swaps(*edges, "col")
     rows1 = swaps(*run(ring_kernel, [rows48] * 2, [place, keyval1, *cols1], specs={0: SMEM}), "row")
-    anywhere = pl.BlockSpec(memory_space=pl.ANY)
-    block = lambda group: [pltpu.VMEM(group.shape, bf16), pltpu.SemaphoreType.DMA((1,))]
+    hbm = pl.BlockSpec(memory_space=pl.ANY)
+    tokens, tokens_low, ext = out((384, D)), out((384, D), bf16), out((4, 192, 2 * D), bf16)
+    token5 = lambda width: pltpu.VMEM((12, 2, 2, 8, width), f32)
+    like = lambda x: pltpu.VMEM(x.shape, x.dtype)
+    copy_sems = lambda count: pltpu.SemaphoreType.DMA((count,))
 
     def tiles(geo, back):
         square = (HEADS * geo.queries, geo.keys)
         shape = (4, 288, 2 * D) if geo is One else (3, 4, 192, 2 * D)
-        table, many = pltpu.VMEM(square, f32), (geo.back if back else geo.forward, *square)
-        wide, narrow = pltpu.VMEM(many, f32), pltpu.VMEM(many, bf16)
+        pieces, prob = pltpu.VMEM(shape, bf16), pltpu.VMEM((geo.steps, *square), bf16)
+        many = (geo.together, *square)
         if not back:
-            return [pltpu.VMEM(shape, bf16), table, wide, narrow, pltpu.VMEM((*many[:2], 128), f32)]
+            return [pieces, pltpu.VMEM(square, f32), pltpu.VMEM(many, f32), prob]
         return [
-            pltpu.VMEM(shape, bf16), table, table, wide, wide, narrow, narrow, pltpu.VMEM(shape, f32),
+            pieces, prob, pltpu.VMEM(many, f32), pltpu.VMEM(many, bf16), pltpu.VMEM(shape, f32),
             pltpu.VMEM((384, D), bf16), pltpu.VMEM((384, D), f32),
-            pltpu.VMEM((geo.pieces, HEADS * geo.across, 128), f32),
         ]
 
-    token5 = lambda width: pltpu.VMEM((12, 2, 2, 8, width), f32)
-    tokens, ext = out((384, D)), out((4, 192, 2 * D), bf16)
-    tokens_low = out((384, D), bf16)
-    near1 = [keyval1, *cols1, *rows1, first_one]
-    att1, middle1, last1, query2, keyval2, *edges = run(
+    probs = lambda geo: out((geo.steps, HEADS * geo.queries, geo.keys), bf16)
+    dtable = lambda geo: out((HEADS * geo.queries, geo.keys))
+    turns = lambda geo: copy_sems(geo.steps // geo.together)
+    near1 = [keyval1, *cols1, *rows1]
+    kept1, att1, middle1, last1, query2, keyval2, *edges = run(
         first_block_kernel,
-        [tokens_low, tokens, tokens, tokens_low, out((4, 96, 2 * D), bf16), rows48, rows48],
-        [place, lay_one, hidden0, query1, *near1, late1, norms, ebias],
-        tiles(One, False) + block(late1),
-        {0: SMEM, 10: anywhere},
+        [probs(One), tokens_low, tokens, tokens, tokens_low, out((4, 96, 2 * D), bf16), rows48, rows48],
+        [place, lay_one, hidden0, query1, *near1, first_one, late1, norms, ebias],
+        tiles(One, False) + [like(late1), like(hidden0), copy_sems(7), turns(One)],
+        {0: SMEM, **dict.fromkeys((2, 4, 5, 6, 7, 8, 10), hbm)},
         56,
+        {0: hbm},
     )
     rows2 = swaps(*edges, "row")
     own2 = run(extend_kernel, [ext], [place, keyval2, *rows2], specs={0: SMEM})[0]
-    near2 = [own2, *swaps(own2, own2, "col"), first_two]
-    att2, middle2, last2, sums = run(
+    near2 = [own2, *swaps(own2, own2, "col")]
+    kept2, att2, middle2, last2, sums = run(
         second_block_kernel,
-        [tokens_low, tokens, tokens, out((padded + 8, max(D, -(-padded // 128) * 128)))],
-        [place, lay_two, lay_one, last1, query2, *near2, late2, norms, ebias],
-        tiles(Two, False) + [pltpu.VMEM((384, D), f32), token5(D)] + block(late2),
-        {0: SMEM, 9: anywhere},
+        [probs(Two), tokens_low, tokens, tokens, out((padded + 8, max(D, -(-padded // 128) * 128)))],
+        [place, lay_two, lay_one, last1, query2, *near2, first_two, late2, norms, ebias],
+        tiles(Two, False)
+        + [like(late2), like(last1), pltpu.VMEM((384, D), f32), token5(D), copy_sems(5), turns(Two)],
+        {0: SMEM, **dict.fromkeys((3, 5, 6, 7, 9), hbm)},
         56,
+        {0: hbm},
     )
     sums = sum_all(sums)
     pad_images = lambda x: jnp.pad(x, (0, padded - images))[:, None]
+    grads_of = lambda group: out((nc, per[group] * D, 128), bf16)
     (
-        loss, grad_head, grad_hbias, dhid, grads2, dnorms2, debias2, dpos2, dquery2, down2, *edges,
+        loss, grad_head, grad_hbias, dhid, grads2, dnorms2, debias2, dtable2, dquery2, inner2, rims2, *edges,
     ) = run(
         second_back_kernel,
         [
-            out((8, 128)), out((sh, 1024)), out((1, 1024)), tokens, out((nc, per[0] * D, 128), bf16),
-            out((4, D)), out((1, FF)), out((HEADS, WIN)), tokens_low,
-            out((4, 192, 2 * D)), ext, ext,
+            out((8, 128)), out((sh, 1024)), out((1, 1024)), tokens, grads_of(0),
+            out((4, D)), out((1, FF)), dtable(Two), tokens_low,
+            out((4, 96, 2 * D)), out((4, 96, 2 * D), bf16), ext, ext,
         ],
         [
-            place, lay_two, lay_one, sums, pad_images(labels), pad_images(live.astype(f32)), hbias,
-            last2, middle2, att2, query2, *near2, late2, norms, ebias,
+            place, lay_one, sums, pad_images(labels), pad_images(live.astype(f32)), hbias,
+            last2, middle2, att2, query2, *near2, kept2, late2, norms, ebias,
         ],
-        tiles(Two, True) + [token5(D)] + block(late2),
-        {0: SMEM, 15: anywhere},
+        tiles(Two, True) + [like(late2), like(grads_of(0)), token5(D), copy_sems(6)],
+        {0: SMEM, **dict.fromkeys((10, 11, 12, 13, 14), hbm)},
         56,
+        {4: hbm},
     )
     dcols2 = swaps(*edges, "col")
-    drows2 = swaps(*run(rim_kernel, [rows48] * 2, [place, down2, *dcols2], specs={0: SMEM}), "row")
+    drows2 = swaps(*run(rim_kernel, [rows48] * 2, [place, rims2, *dcols2], specs={0: SMEM}), "row")
     grads2 = lax.psum_scatter(grads2, "col", scatter_dimension=0, tiled=False)
-    dhid, grads1, dnorms1, debias1, dpos1, dquery1, inner1, *edges = run(
+
+    def position(geo, table):
+        scratch = [pltpu.VMEM((geo.pieces, HEADS * geo.across, 128), f32)]
+        return run(functools.partial(position_kernel, geo=geo), [out((HEADS, WIN))], [table], scratch)[0]
+
+    dpos2 = position(Two, dtable2)
+    part2 = pltpu.VMEM((4, 96, 2 * D), bf16)
+    dhid, grads1, dnorms1, debias1, dtable1, dquery1, inner1, sides1, *edges = run(
         first_back_kernel,
         [
-            tokens, out((nc, per[1] * D, 128), bf16), out((4, D)), out((1, FF)), out((HEADS, WIN)),
-            tokens_low, out((4, 192, 2 * D)), rows48, rows48,
+            tokens, grads_of(1), out((4, D)), out((1, FF)), dtable(One),
+            tokens_low, out((2, 192, 2 * D)), out((2, 192, 2 * D), bf16), rows48, rows48,
         ],
         [
-            place, lay_one, dhid, dquery2, down2, *dcols2, *drows2, last1, middle1, att1, query1,
-            *near1, late1, norms, ebias,
+            place, dhid, dquery2, inner2, *dcols2, *drows2, last1, middle1, att1, query1,
+            *near1, kept1, late1, norms, ebias,
         ],
-        tiles(One, True) + [token5(2 * D)] + block(late1),
-        {0: SMEM, 19: anywhere},
+        tiles(One, True) + [like(late1), like(grads_of(1)), part2, part2, token5(2 * D), copy_sems(10)],
+        {0: SMEM, **dict.fromkeys((4, 5, 12, 13, 14, 15, 16, 17, 18), hbm)},
         56,
+        {1: hbm},
     )
     drows1 = swaps(*edges, "row")
     grads1 = lax.psum_scatter(grads1, "col", scatter_dimension=0, tiled=False)
-    dcols1 = swaps(*run(sides_kernel, [edge] * 2, [place, inner1, *drows1], specs={0: SMEM}), "col")
+    dpos1 = position(One, dtable1)
+    dcols1 = swaps(*run(sides_kernel, [edge] * 2, [place, sides1, *drows1], specs={0: SMEM}), "col")
     part = per[2] * D + SMALL_ROWS
     half = lambda count: out((count, part, 128), bf16)
     kept, given = run(
@@ -1150,6 +1200,7 @@
         between_kernel,
         [out((nr, sum(per) * sh + SMALL_ROWS, 128), bf16)],
         [grads2, grads1, kept, given],
+        vmem=56,
     )[0]
     mine = lax.all_to_all(mine, "row", 0, 0, tiled=True)
     mine, small = run(

time: 282 us -> 274 us (0.972)
  starting transfers between devices: 70.6 us -> 64.5 us
  local copies, waits for them, and re-layouts: 19.2 us -> 22.3 us
  waiting for transfers between devices: 82.7 us -> 79.8 us
    unnamed x122 -> x128, local copies, waits for them, and re-layouts: 10.2 us -> 15.3 us
    ppermute x2, starting transfers between devices: 10.1 us -> 6.94 us  [on_device(): given = lax.ppermute(given, 'col', [(i, i ^ 1 << stage) for i in range(nc)])]
    pallas_call x17 -> x19, Pallas kernels: 66.2 us -> 63.6 us  [run(): pl.pallas_call(kernel, out_shape=outs, in_specs=in_specs, out_specs=resul...]
  transfers between devices with their start and end apart: 34 -> 34, of which waited for: 21 -> 20; matrix products, arithmetic and copies ran while one was open for 3% -> 3% of each run, Pallas kernels for 13% -> 13%
where the time goes in v5:
time: 274 us; the launch traced here: 273 us
  waiting for transfers between devices  79.8 us (29%)
  starting transfers between devices  64.5 us (24%)
  Pallas kernels  63.6 us (23%)
  blocking collectives  22.9 us (8%)
  local copies, waits for them, and re-layouts  22.3 us (8%)
  between operations  14.7 us (5%)
  other arithmetic  4.88 us (2%)
    pallas_call x19, Pallas kernels, run(): pl.pallas_call(kernel, out_shape=outs, in_specs=in_specs, out_specs=resul...  63.6 us
    ppermute x8, starting transfers between devices, swaps(): lax.ppermute(first, axis, both[0])  22.5 us
    all_to_all x1, waiting for transfers between devices, on_device(): mine = lax.all_to_all(mine, 'row', 0, 0, tiled=True)  21.5 us
    ppermute x8, waiting for transfers between devices, swaps(): lax.ppermute(first, axis, both[0])  18.3 us
    all_to_all x1, blocking collectives, on_device(): early = lax.all_to_all(early, 'row', 0, 0, tiled=True)  16.3 us
    ppermute x7, starting transfers between devices, other(): return lax.ppermute(value, axis, [(i, i ^ flip) for i in range(count)])  16 us
    unnamed x128, local copies, waits for them, and re-layouts  15.3 us
    ppermute x2, waiting for transfers between devices, on_device(): given = lax.ppermute(given, 'col', [(i, i ^ 1 << stage) for i in range(nc)])  9.05 us
  transfers between devices with their start and end apart: 34, of which 20 were waited for; matrix products, arithmetic and copies ran while one was open for 3% of the time, Pallas kernels for 13%

profile of v5, /device:TPU:0, one launch (start us, length us, event | category | flops | bytes accessed | tf_op | source)
XLA Modules:
  0.0 272.8 jit_solution(14405350473486333983)
XLA Ops:
  9.6 16.3 %all_to_all.15 = bf16[8,128,128]{2,1,0:T(8,128)(2,1)} all-to-all(bf16[8,128,128]{2,1,0:T(8,128)(2,1)} %get-tuple-element.97), channel_id=1, replica_groups=mesh['row'=8,'col'=4] {'row'}, dimensions={0} | all-to-all | bytes 524288 | tf_op jit(solution)/shard_map/all_to_all | solution.py:1037
  27.4 4.9 %collective-permute-done = bf16[1,32,128]{2,1,0:T(8,128)(2,1)S(1)} collective-permute-done((bf16[1,32,128]{2,1,0:T(8,128)(2,1)S(1)}, bf16[1,32,128]{2,1,0:T(8,128)(2,1)S(1)}, u32[]{:S(2)}, u32[]{:S(2)}) %collective-permute-start) | collective-permute-done | bytes 8224 | tf_op jit(solution)/shard_map/ppermute | solution.py:984
  32.3 3.5 %all-to-all-start.1 = ((bf16[8,352,128]{2,1,0:T(8,128)(2,1)}), bf16[8,352,128]{2,1,0:T(8,128)(2,1)S(1)}, u32[]{:S(2)}, u32[]{:S(2)}) async-start(bf16[8,352,128]{2,1,0:T(8,128)(2,1)} %get-tuple-element.107), calls=%async_computation.1 | async-start | bytes 1441792 | tf_op jit(solution)/shard_map/all_to_all | solution.py:1066
  36.5 3.0 %collective-permute-done.1 = bf16[49,1,128]{2,0,1:T(8,128)(2,1)S(1)} collective-permute-done((bf16[49,1,128]{2,0,1:T(8,128)(2,1)S(1)}, bf16[49,1,128]{2,0,1:T(8,128)(2,1)S(1)}, u32[]{:S(2)}, u32[]{:S(2)}) %collective-permute-start.1) | collective-permute-done | bytes 12576 | tf_op jit(solution)/shard_map/ppermute | solution.py:984
  47.4 4.5 %all-to-all-done.1 = bf16[8,352,128]{2,1,0:T(8,128)(2,1)S(1)} async-done(((bf16[8,352,128]{2,1,0:T(8,128)(2,1)}), bf16[8,352,128]{2,1,0:T(8,128)(2,1)S(1)}, u32[]{:S(2)}, u32[]{:S(2)}) %all-to-all-start.1) | async-done | bytes 720928 | tf_op jit(solution)/shard_map/all_to_all | solution.py:1066
  61.4 8.6 %all-gather.10.cloned.1.call-done = bf16[32,160,128]{2,1,0:T(8,128)(2,1)} async-done(((bf16[8,160,128]{2,1,0:T(8,128)(2,1)}), bf16[32,160,128]{2,1,0:T(8,128)(2,1)}) %all-gather.10.cloned.1.call-update) | async-done | bytes 1310736 | tf_op jit(solution)/shard_map/all_gather | solution.py:1075
  70.1 9.0 %shard_map.413 = (bf16[6,512,512]{2,1,0:T(8,128)(2,1)}, bf16[384,256]{1,0:T(8,128)(2,1)}, f32[384,256]{1,0:T(8,128)}, f32[384,256]{1,0:T(8,128)}, bf16[384,256]{...) custom-call(s32[6]{0:T(128)} %copy-done.41, ...), custom_call_target="tpu_custom_call" | custom-call | bytes 4194304 | tf_op jit(solution)/shard_map/pallas_call | solution.py:368
  81.3 8.4 %collective-permute-done.6.first = bf16[4,48,512]{2,1,0:T(8,128)(2,1)S(1)} collective-permute-done((bf16[4,48,512]{2,1,0:T(8,128)(2,1)}, bf16[4,48,512]{2,1,0:T(8,128)(2,1)S(1)}, u32[]{:S(2)}, u32[]{:S(2)}) %collective-permute-start.6) | collective-permute-done | bytes 196640 | tf_op jit(solution)/shard_map/ppermute | solution.py:991
  92.3 2.9 %collective-permute-start.8 = (bf16[4,192,512]{2,1,0:T(8,128)(2,1)S(1)}, bf16[4,192,512]{2,1,0:T(8,128)(2,1)S(1)}, u32[]{:S(2)}, u32[]{:S(2)}) collective-permute-start(bf16[4,192,512]{2,1,0:T(8,128)(2,1)S(1)} %shard_map.414.own), channel_id=1, source_target_pairs={{0,1},{2,3},{1,0},{3,2},{4,5},{6,7},{5,4},{7,6},{8,9},{10,11},{9,8... | collective-permute-start | bytes 2359304 | tf_op jit(solution)/shard_map/ppermute | solution.py:991
  98.0 9.1 %shard_map.415 = (bf16[12,256,384]{2,1,0:T(8,128)(2,1)}, bf16[384,256]{1,0:T(8,128)(2,1)}, f32[384,256]{1,0:T(8,128)}, f32[384,256]{1,0:T(8,128)}, f32[64,256]{1,0:T(8,128)}) custom-call(s32[6]{0:T(128)} %copy-done.41, s32[384,5]{1,0:T(8,128)} %bitcast.60, s32[384,5]{1,0:T(8,128)} %bitcast.45, f32[384,256]{1,0:T(8,128)} %get-tuple-element.109.hidden, ...), custom_call_target="tpu_custom_call" | custom-call | bytes 4194304 | tf_op jit(solution)/shard_map/pallas_call | solution.py:368
  107.3 9.5 %collective-permute-start.11 = (f32[64,256]{1,0:T(8,128)}, f32[64,256]{1,0:T(8,128)S(1)}, u32[]{:S(2)}, u32[]{:S(2)}) collective-permute-start(f32[64,256]{1,0:T(8,128)} %get-tuple-element.115), channel_id=1, source_target_pairs={{0,2},{1,3},{2,0},{3,1},{4,6},{5,7},{6,4},{7,5},{8,10},{9,11},{10,... | collective-permute-start | bytes 196616 | tf_op jit(solution)/shard_map/ppermute | solution.py:1000
  116.8 3.2 %collective-permute-done.11 = f32[64,256]{1,0:T(8,128)S(1)} collective-permute-done((f32[64,256]{1,0:T(8,128)}, f32[64,256]{1,0:T(8,128)S(1)}, u32[]{:S(2)}, u32[]{:S(2)}) %collective-permute-start.11) | collective-permute-done | bytes 65568 | tf_op jit(solution)/shard_map/ppermute | solution.py:1000
  120.9 3.3 %collective-permute-start.15 = (f32[64,256]{1,0:T(8,128)S(1)}, f32[64,256]{1,0:T(8,128)S(1)}, u32[]{:S(2)}, u32[]{:S(2)}) collective-permute-start(f32[64,256]{1,0:T(8,128)S(1)} %add_add_fusion.1), channel_id=1, source_target_pairs={{0,12},{4,8},{8,4},{12,0},{16,28},{20,24},{24,20},{28,16},{1,13},{... | collective-permute-start | bytes 196616 | tf_op jit(solution)/shard_map/ppermute | solution.py:1000
  134.9 12.8 %shard_map.416 = (f32[8,128]{1,0:T(8,128)}, f32[32,1024]{1,0:T(8,128)}, f32[1,1024]{1,0:T(1,128)}, f32[384,256]{1,0:T(8,128)}, bf16[4,1024,128]{2,1,0:T(8,128)(2...) custom-call(s32[6]{0:T(128)} %copy-done.41, ...), custom_call_target="tpu_custom_call" | custom-call | bytes 4194304 | tf_op jit(solution)/shard_map/pallas_call | solution.py:368
  155.3 2.9 %collective-permute-done.19.drowa = bf16[4,48,512]{2,1,0:T(8,128)(2,1)S(1)} collective-permute-done((bf16[4,48,512]{2,1,0:T(8,128)(2,1)S(1)}, bf16[4,48,512]{2,1,0:T(8,128)(2,1)S(1)}, u32[]{:S(2)}, u32[]{:S(2)}) %collective-permute-start.19) | collective-permute-done | bytes 196640 | tf_op jit(solution)/shard_map/ppermute | solution.py:991
  158.9 12.8 %shard_map.418 = (f32[384,256]{1,0:T(8,128)}, bf16[4,1280,128]{2,1,0:T(8,128)(2,1)}, f32[4,256]{1,0:T(4,128)}, f32[1,768]{1,0:T(1,128)}, f32[512,512]{1,0:T(8,12...) custom-call(s32[6]{0:T(128)} %copy-done.41, ...), custom_call_target="tpu_custom_call" | custom-call | bytes 4194304 | tf_op jit(solution)/shard_map/pallas_call | solution.py:368
  171.8 4.9 %collective-permute-start.21 = (bf16[4,48,512]{2,1,0:T(8,128)(2,1)}, bf16[4,48,512]{2,1,0:T(8,128)(2,1)S(1)}, u32[]{:S(2)}, u32[]{:S(2)}) collective-permute-start(bf16[4,48,512]{2,1,0:T(8,128)(2,1)} %get-tuple-element.137), channel_id=1, source_target_pairs={{0,4},{8,12},{16,20},{24,28},{4,0},{12,8},{20,16},{28,24},{1,5},{9... | collective-permute-start | bytes 589832 | tf_op jit(solution)/shard_map/ppermute | solution.py:991
  177.3 3.2 %collective-permute-done.21.first.drowa = bf16[4,48,512]{2,1,0:T(8,128)(2,1)S(1)} collective-permute-done((bf16[4,48,512]{2,1,0:T(8,128)(2,1)}, bf16[4,48,512]{2,1,0:T(8,128)(2,1)S(1)}, u32[]{:S(2)}, u32[]{:S(2)}) %collective-permute-start.21) | collective-permute-done | bytes 196640 | tf_op jit(solution)/shard_map/ppermute | solution.py:991
  182.2 9.6 %collective-permute-start.23 = (bf16[192,512]{1,0:T(8,128)(2,1)S(1)}, bf16[192,512]{1,0:T(8,128)(2,1)S(1)}, u32[]{:S(2)}, u32[]{:S(2)}) collective-permute-start(bf16[192,512]{1,0:T(8,128)(2,1)S(1)} %get-tuple-element.140), channel_id=1, source_target_pairs={{0,1},{2,3},{1,0},{3,2},{4,5},{6,7},{5,4},{7,6},{8,9},{10,11},{9,8... | collective-permute-start | bytes 589832 | tf_op jit(solution)/shard_map/ppermute | solution.py:991
  202.1 5.4 %collective-permute-start.25 = (bf16[2,1104,128]{2,1,0:T(8,128)(2,1)S(1)}, bf16[2,1104,128]{2,1,0:T(8,128)(2,1)S(1)}, u32[]{:S(2)}, u32[]{:S(2)}) collective-permute-start(bf16[2,1104,128]{2,1,0:T(8,128)(2,1)S(1)} %get-tuple-element.150), channel_id=1, source_target_pairs={{0,1},{1,0},{2,3},{3,2},{4,5},{5,4},{6,7},{7,6},{8,9},{9,8},{10,11... | collective-permute-start | bytes 1695752 | tf_op jit(solution)/shard_map/ppermute | solution.py:1187
  212.3 7.5 %collective-permute-done.26.given = bf16[1,1104,128]{2,1,0:T(8,128)(2,1)S(1)} collective-permute-done((bf16[1,1104,128]{2,1,0:T(8,128)(2,1)S(1)}, bf16[1,1104,128]{2,1,0:T(8,128)(2,1)S(1)}, u32[]{:S(2)}, u32[]{:S(2)}) %collective-permute-start.26) | collective-permute-done | bytes 282656 | tf_op jit(solution)/shard_map/ppermute | solution.py:1187
  222.7 7.9 %all-to-all-start.2 = ((bf16[8,496,128]{2,1,0:T(8,128)(2,1)}), bf16[8,496,128]{2,1,0:T(8,128)(2,1)S(1)}, u32[]{:S(2)}, u32[]{:S(2)}) async-start(bf16[8,496,128]{2,1,0:T(8,128)(2,1)} %shard_map.424), calls=%async_computation.4 | async-start | bytes 2031616 | tf_op jit(solution)/shard_map/all_to_all | solution.py:1205
  234.2 21.5 %all-to-all-done.2.parts = bf16[8,496,128]{2,1,0:T(8,128)(2,1)S(1)} async-done(((bf16[8,496,128]{2,1,0:T(8,128)(2,1)}), bf16[8,496,128]{2,1,0:T(8,128)(2,1)S(1)}, u32[]{:S(2)}, u32[]{:S(2)}) %all-to-all-start.2) | async-done | bytes 1015840 | tf_op jit(solution)/shard_map/all_to_all | solution.py:1205
  256.0 6.7 %all-gather.3 = bf16[1664,128]{1,0:T(8,128)(2,1)S(1)} all-gather(bf16[416,128]{1,0:T(8,128)(2,1)S(1)} %get-tuple-element.153), channel_id=5, replica_groups=mesh['row'=8,'col'=4] {'col'}, dimensions={0}, use_global_device_ids=true | all-gather | bytes 532480 | tf_op jit(solution)/shard_map/all_gather | solution.py:1209
  (237 shorter events, 76.5 us)
Async XLA Ops:
  7.2 34.8 %all-gather.8.cloned.1.call-start = ((), (), s32[]{:S(2)}) async-start(), calls=%async_computation.7 | async-start | bytes 1310720 | tf_op jit(solution)/shard_map/all_gather | solution.py:1065
  25.9 6.4 %collective-permute-start = (bf16[1,32,128]{2,1,0:T(8,128)(2,1)S(1)}, bf16[1,32,128]{2,1,0:T(8,128)(2,1)S(1)}, u32[]{:S(2)}, u32[]{:S(2)}) collective-permute-start(bf16[1,32,128]{2,1,0:T(8,128)(2,1)S(1)} %slice.51), channel_id=1, source_target_pairs={{0,4},{4,8},{8,12},{12,16},{16,20},{20,24},{24,28},{28,0},{1,5},{5... | collective-permute-start | bytes 24584 | tf_op jit(solution)/shard_map/ppermute | solution.py:984
  32.3 19.6 %all-to-all-start.1 = ((bf16[8,352,128]{2,1,0:T(8,128)(2,1)}), bf16[8,352,128]{2,1,0:T(8,128)(2,1)S(1)}, u32[]{:S(2)}, u32[]{:S(2)}) async-start(bf16[8,352,128]{2,1,0:T(8,128)(2,1)} %get-tuple-element.107), calls=%async_computation.1 | async-start | bytes 1441792 | tf_op jit(solution)/shard_map/all_to_all | solution.py:1066
  35.9 34.2 %all-gather.10.cloned.1.call-start = ((), (), s32[]{:S(2)}) async-start(), calls=%async_computation.8 | async-start | bytes 1638400 | tf_op jit(solution)/shard_map/all_gather | solution.py:1075
  52.7 43.4 %all-gather.12.cloned.1.call-start = ((), (), s32[]{:S(2)}) async-start(), calls=%async_computation.9 | async-start | bytes 1966080 | tf_op jit(solution)/shard_map/all_gather | solution.py:1076
  53.5 158.7 %reduce-scatter.3.cloned.1.call-start = ((), (), s32[]{:S(2)}) async-start(), calls=%async_computation.5 | async-start | bytes 1310720 | tf_op jit(solution)/shard_map/reduce_scatter | solution.py:1146
  55.7 5.7 %collective-permute-start.4 = (bf16[4,48,512]{2,1,0:T(8,128)(2,1)S(1)}, bf16[4,48,512]{2,1,0:T(8,128)(2,1)S(1)}, u32[]{:S(2)}, u32[]{:S(2)}) collective-permute-start(bf16[4,48,512]{2,1,0:T(8,128)(2,1)S(1)} %get-tuple-element.103), channel_id=1, source_target_pairs={{0,4},{8,12},{16,20},{24,28},{4,0},{12,8},{20,16},{28,24},{1,5},{9... | collective-permute-start | bytes 589832 | tf_op jit(solution)/shard_map/ppermute | solution.py:991
  57.2 4.3 %collective-permute-start.5 = (bf16[4,48,512]{2,1,0:T(8,128)(2,1)S(1)}, bf16[4,48,512]{2,1,0:T(8,128)(2,1)S(1)}, u32[]{:S(2)}, u32[]{:S(2)}) collective-permute-start(bf16[4,48,512]{2,1,0:T(8,128)(2,1)S(1)} %get-tuple-element.104), channel_id=1, source_target_pairs={{4,8},{12,16},{20,24},{8,4},{16,12},{24,20},{5,9},{13,17},{21,25},... | collective-permute-start | bytes 589832 | tf_op jit(solution)/shard_map/ppermute | solution.py:991
  79.1 10.6 %collective-permute-start.6 = (bf16[4,48,512]{2,1,0:T(8,128)(2,1)}, bf16[4,48,512]{2,1,0:T(8,128)(2,1)S(1)}, u32[]{:S(2)}, u32[]{:S(2)}) collective-permute-start(bf16[4,48,512]{2,1,0:T(8,128)(2,1)} %get-tuple-element.112), channel_id=1, source_target_pairs={{0,4},{8,12},{16,20},{24,28},{4,0},{12,8},{20,16},{28,24},{1,5},{9... | collective-permute-start | bytes 589832 | tf_op jit(solution)/shard_map/ppermute | solution.py:991
  80.7 9.1 %collective-permute-start.7 = (bf16[4,48,512]{2,1,0:T(8,128)(2,1)}, bf16[4,48,512]{2,1,0:T(8,128)(2,1)S(1)}, u32[]{:S(2)}, u32[]{:S(2)}) collective-permute-start(bf16[4,48,512]{2,1,0:T(8,128)(2,1)} %get-tuple-element.113), channel_id=1, source_target_pairs={{4,8},{12,16},{20,24},{8,4},{16,12},{24,20},{5,9},{13,17},{21,25},... | collective-permute-start | bytes 589832 | tf_op jit(solution)/shard_map/ppermute | solution.py:991
  91.4 4.7 %collective-permute-start.9 = (bf16[4,192,512]{2,1,0:T(8,128)(2,1)S(1)}, bf16[4,192,512]{2,1,0:T(8,128)(2,1)S(1)}, u32[]{:S(2)}, u32[]{:S(2)}) collective-permute-start(bf16[4,192,512]{2,1,0:T(8,128)(2,1)S(1)} %shard_map.414.own), channel_id=1, source_target_pairs={{1,2},{2,1},{5,6},{6,5},{9,10},{10,9},{13,14},{14,13},{17,18},{18,... | collective-permute-start | bytes 2359304 | tf_op jit(solution)/shard_map/ppermute | solution.py:991
  92.3 4.8 %collective-permute-start.8 = (bf16[4,192,512]{2,1,0:T(8,128)(2,1)S(1)}, bf16[4,192,512]{2,1,0:T(8,128)(2,1)S(1)}, u32[]{:S(2)}, u32[]{:S(2)}) collective-permute-start(bf16[4,192,512]{2,1,0:T(8,128)(2,1)S(1)} %shard_map.414.own), channel_id=1, source_target_pairs={{0,1},{2,3},{1,0},{3,2},{4,5},{6,7},{5,4},{7,6},{8,9},{10,11},{9,8... | collective-permute-start | bytes 2359304 | tf_op jit(solution)/shard_map/ppermute | solution.py:991
  107.2 9.6 %collective-permute-start.12 = (f32[64,256]{1,0:T(8,128)}, f32[64,256]{1,0:T(8,128)S(1)}, u32[]{:S(2)}, u32[]{:S(2)}) collective-permute-start(f32[64,256]{1,0:T(8,128)} %get-tuple-element.115), channel_id=1, source_target_pairs={{0,3},{1,2},{2,1},{3,0},{4,7},{5,6},{6,5},{7,4},{8,11},{9,10},{10,... | collective-permute-start | bytes 196616 | tf_op jit(solution)/shard_map/ppermute | solution.py:1000
  107.3 12.8 %collective-permute-start.11 = (f32[64,256]{1,0:T(8,128)}, f32[64,256]{1,0:T(8,128)S(1)}, u32[]{:S(2)}, u32[]{:S(2)}) collective-permute-start(f32[64,256]{1,0:T(8,128)} %get-tuple-element.115), channel_id=1, source_target_pairs={{0,2},{1,3},{2,0},{3,1},{4,6},{5,7},{6,4},{7,5},{8,10},{9,11},{10,... | collective-permute-start | bytes 196616 | tf_op jit(solution)/shard_map/ppermute | solution.py:1000
  120.9 6.2 %collective-permute-start.15 = (f32[64,256]{1,0:T(8,128)S(1)}, f32[64,256]{1,0:T(8,128)S(1)}, u32[]{:S(2)}, u32[]{:S(2)}) collective-permute-start(f32[64,256]{1,0:T(8,128)S(1)} %add_add_fusion.1), channel_id=1, source_target_pairs={{0,12},{4,8},{8,4},{12,0},{16,28},{20,24},{24,20},{28,16},{1,13},{... | collective-permute-start | bytes 196616 | tf_op jit(solution)/shard_map/ppermute | solution.py:1000
  129.1 5.2 %collective-permute-start.16 = (f32[64,256]{1,0:T(8,128)S(1)}, f32[64,256]{1,0:T(8,128)S(1)}, u32[]{:S(2)}, u32[]{:S(2)}) collective-permute-start(f32[64,256]{1,0:T(8,128)S(1)} %add_add_fusion), channel_id=1, source_target_pairs={{0,16},{4,20},{8,24},{12,28},{16,0},{20,4},{24,8},{28,12},{1,17},{... | collective-permute-start | bytes 196616 | tf_op jit(solution)/shard_map/ppermute | solution.py:1000
  147.8 72.0 %reduce-scatter.5.cloned.1.call-start = ((), (), s32[]{:S(2)}) async-start(), calls=%async_computation.6 | async-start | bytes 1638400 | tf_op jit(solution)/shard_map/reduce_scatter | solution.py:1170
  152.4 5.7 %collective-permute-start.19 = (bf16[4,48,512]{2,1,0:T(8,128)(2,1)S(1)}, bf16[4,48,512]{2,1,0:T(8,128)(2,1)S(1)}, u32[]{:S(2)}, u32[]{:S(2)}) collective-permute-start(bf16[4,48,512]{2,1,0:T(8,128)(2,1)S(1)} %get-tuple-element.128), channel_id=1, source_target_pairs={{0,4},{8,12},{16,20},{24,28},{4,0},{12,8},{20,16},{28,24},{1,5},{9... | collective-permute-start | bytes 589832 | tf_op jit(solution)/shard_map/ppermute | solution.py:991
  171.8 8.7 %collective-permute-start.21 = (bf16[4,48,512]{2,1,0:T(8,128)(2,1)}, bf16[4,48,512]{2,1,0:T(8,128)(2,1)S(1)}, u32[]{:S(2)}, u32[]{:S(2)}) collective-permute-start(bf16[4,48,512]{2,1,0:T(8,128)(2,1)} %get-tuple-element.137), channel_id=1, source_target_pairs={{0,4},{8,12},{16,20},{24,28},{4,0},{12,8},{20,16},{28,24},{1,5},{9... | collective-permute-start | bytes 589832 | tf_op jit(solution)/shard_map/ppermute | solution.py:991
  182.2 14.1 %collective-permute-start.23 = (bf16[192,512]{1,0:T(8,128)(2,1)S(1)}, bf16[192,512]{1,0:T(8,128)(2,1)S(1)}, u32[]{:S(2)}, u32[]{:S(2)}) collective-permute-start(bf16[192,512]{1,0:T(8,128)(2,1)S(1)} %get-tuple-element.140), channel_id=1, source_target_pairs={{0,1},{2,3},{1,0},{3,2},{4,5},{6,7},{5,4},{7,6},{8,9},{10,11},{9,8... | collective-permute-start | bytes 589832 | tf_op jit(solution)/shard_map/ppermute | solution.py:991
  191.8 4.4 %collective-permute-start.24 = (bf16[192,512]{1,0:T(8,128)(2,1)S(1)}, bf16[192,512]{1,0:T(8,128)(2,1)S(1)}, u32[]{:S(2)}, u32[]{:S(2)}) collective-permute-start(bf16[192,512]{1,0:T(8,128)(2,1)S(1)} %get-tuple-element.141), channel_id=1, source_target_pairs={{1,2},{2,1},{5,6},{6,5},{9,10},{10,9},{13,14},{14,13},{17,18},{18,... | collective-permute-start | bytes 589832 | tf_op jit(solution)/shard_map/ppermute | solution.py:991
  202.1 7.0 %collective-permute-start.25 = (bf16[2,1104,128]{2,1,0:T(8,128)(2,1)S(1)}, bf16[2,1104,128]{2,1,0:T(8,128)(2,1)S(1)}, u32[]{:S(2)}, u32[]{:S(2)}) collective-permute-start(bf16[2,1104,128]{2,1,0:T(8,128)(2,1)S(1)} %get-tuple-element.150), channel_id=1, source_target_pairs={{0,1},{1,0},{2,3},{3,2},{4,5},{5,4},{6,7},{7,6},{8,9},{9,8},{10,11... | collective-permute-start | bytes 1695752 | tf_op jit(solution)/shard_map/ppermute | solution.py:1187
  210.7 9.0 %collective-permute-start.26 = (bf16[1,1104,128]{2,1,0:T(8,128)(2,1)S(1)}, bf16[1,1104,128]{2,1,0:T(8,128)(2,1)S(1)}, u32[]{:S(2)}, u32[]{:S(2)}) collective-permute-start(bf16[1,1104,128]{2,1,0:T(8,128)(2,1)S(1)} %get-tuple-element.152), channel_id=1, source_target_pairs={{0,2},{1,3},{2,0},{3,1},{4,6},{5,7},{6,4},{7,5},{8,10},{9,11},{10,... | collective-permute-start | bytes 847880 | tf_op jit(solution)/shard_map/ppermute | solution.py:1187
  222.7 32.9 %all-to-all-start.2 = ((bf16[8,496,128]{2,1,0:T(8,128)(2,1)}), bf16[8,496,128]{2,1,0:T(8,128)(2,1)S(1)}, u32[]{:S(2)}, u32[]{:S(2)}) async-start(bf16[8,496,128]{2,1,0:T(8,128)(2,1)} %shard_map.424), calls=%async_computation.4 | async-start | bytes 2031616 | tf_op jit(solution)/shard_map/all_to_all | solution.py:1205
  (75 other events, 1133.0 us)
Sparse Core Ops, SparseCore 0:
  26.0 15.9 all-gather.7
  52.8 17.2 all-gather.9
  71.6 19.6 all-gather.11
  147.9 24.9 reduce-scatter.2
  175.4 37.3 reduce-scatter.4

commit v6 on v5

--- a/solution.py
+++ b/solution.py
@@ -472,9 +472,8 @@
             patches[:, lanes] = value.astype(bf16)
 
 
-def front_kernel(place, patches, early, norms, conv_out, hidden, query, keyval, first, second):
+def front_kernel(place, patches, early, norms, hidden, query, keyval, first, second):
     conv = nt(patches[...], weight_of(early, 0, 9))
-    conv_out[...] = conv
     h = norm(conv, norms[0:2, :])
     hidden[...] = h
     low = norm(h, norms[2:4, :]).astype(bf16)
@@ -716,15 +715,22 @@
         put_block(grads, k, jnp.zeros((D, 128), f32))
 
 
+def put_bias(dsmall, value):
+    for k in range(3):
+        dsmall[4 + k : 5 + k, :] = value[:, k * D : (k + 1) * D]
+    dsmall[7:8, :] = jnp.zeros((1, D), f32)
+
+
 def second_back_kernel(
-    place, slots, sums, labels, live, hbias, hidden, middle, att, query, own, cola, colb, kept, late,
+    place, slots, sums_a, sums_b, labels, live, hbias, hidden, middle, att, query, own, cola, colb, kept, late,
     norms, ebias,
-    loss, grad_head, grad_hbias, dhidden, grads, dnorms, debias, dtable, dquery, inner, rims, first, second,
+    loss, grad_head, grad_hbias, dhidden, grads, dsmall, dtable, dquery, inner, rims, first, second,
     pieces, prob, dprob, dscore, dpieces, datt, dq_group, group, grads_out, dq_token, sems,
 ):
     copies = Copies(sems)
     weights = copies.start(late, group)
     near = gather_keys_two(copies, place, own, cola, colb, pieces) + copies.start(kept, prob)
+    sums = sums_a[...] + sums_b[...]
     images = sums.shape[0] - 8
     total = sums[:images, :D]
     diagonal = lax.broadcasted_iota(i32, (images, images), 0)
@@ -755,16 +761,16 @@
     where = slot_onehot(slots, images)
     dfinal = nn(where, high) + nn(where, low)
     dhid, dgain, dbias = norm_back(hidden[...], norms[10:12, :], dfinal)
-    dnorms[2:3, :] = dgain
-    dnorms[3:4, :] = dbias
+    dsmall[2:3, :] = dgain
+    dsmall[3:4, :] = dbias
     dhid, grad_red, grad_exp, grad_bias, dgain, dbias = feed_forward_back(
         dhid, middle[...], norms[8:10, :], weight_of(group, EXP, 6), weight_red(group, RED), ebias[1:2, :]
     )
     put_cols(grads_out, 0, grad_exp)
     put_red(grads_out, 6, grad_red, share)
-    debias[...] = grad_bias
-    dnorms[0:1, :] = dgain
-    dnorms[1:2, :] = dbias
+    put_bias(dsmall, grad_bias)
+    dsmall[0:1, :] = dgain
+    dsmall[1:2, :] = dbias
     dhidden[...] = dhid
     dy = dhid.astype(bf16)
     put_cols(grads_out, 12, tn(att[...], dy))
@@ -794,7 +800,7 @@
 def first_back_kernel(
     place, dhid_in, dquery2, dkv, dcola, dcolb, drowa, drowb, hidden, middle, att, query,
     keyval, cola, colb, rowa, rowb, kept, late, norms, ebias,
-    dhidden, grads, dnorms, debias, dtable, dquery, inner, sides, first, second,
+    dhidden, grads, dsmall, dtable, dquery, inner, sides, first, second,
     pieces, prob, dprob, dscore, dpieces, datt, dq, group, grads_out, parta, partb, dkv_token, sems,
 ):
     copies = Copies(sems)
@@ -817,17 +823,17 @@
     dx, dgain, dbias = norm_back(
         hidden[...], norms[6:8, :], nt(dmixed, weight_of(group, QKV, 6))
     )
-    dnorms[2:3, :] = dgain
-    dnorms[3:4, :] = dbias
+    dsmall[2:3, :] = dgain
+    dsmall[3:4, :] = dbias
     dhid, grad_red, grad_exp, grad_bias, dgain, dbias = feed_forward_back(
         dhid_in[...] + dx, middle[...], norms[4:6, :], weight_of(group, EXP, 6), weight_red(group, RED),
         ebias[0:1, :],
     )
     put_cols(grads_out, 6, grad_exp)
     put_red(grads_out, 12, grad_red, D // late.shape[1])
-    debias[...] = grad_bias
-    dnorms[0:1, :] = dgain
-    dnorms[1:2, :] = dbias
+    put_bias(dsmall, grad_bias)
+    dsmall[0:1, :] = dgain
+    dsmall[1:2, :] = dbias
     dhidden[...] = dhid
     dy = dhid.astype(bf16)
     put_cols(grads_out, 18, tn(att[...], dy))
@@ -846,12 +852,12 @@
     wait_for(leaving)
 
 
-SMALL_ROWS = 80
+SMALL_ROWS = 64
 
 
 def front_back_kernel(
-    place, dhid_in, dquery, inner, drowa, drowb, dcola, dcolb, hidden, conv, patches, early,
-    norms, dnorms1, dnorms2, debias1, debias2, dpos1, dpos2,
+    place, dhid_in, dquery, inner, drowa, drowb, dcola, dcolb, patches, early,
+    norms, dsmall1, dsmall2, dpos1, dpos2,
     keep, give,
     grads, small,
 ):
@@ -869,12 +875,13 @@
     one = whole(1) + jnp.where(sub < 4, pltpu.roll(left, 4, 1), right)
     dkv = jnp.stack([zero, one], 1).reshape(384, 2 * D).astype(bf16)
     dmixed = jnp.concatenate([dquery[...], dkv], 1)
-    h = hidden[...]
+    conv = nt(patches[...], weight_of(early, 0, 9))
+    h = norm(conv, norms[0:2, :])
     low = norm(h, norms[2:4, :]).astype(bf16)
     put_cols(grads, 9, tn(low, dmixed))
     w_qkv = weight_of(early, 9, 6)
     dx, dgain1, dbias1 = norm_back(h, norms[2:4, :], nt(dmixed, w_qkv))
-    dconv, dgain0, dbias0 = norm_back(conv[...], norms[0:2, :], dhid_in[...] + dx)
+    dconv, dgain0, dbias0 = norm_back(conv, norms[0:2, :], dhid_in[...] + dx)
     put_cols(grads, 0, tn(dconv.astype(bf16), patches[...]))
     put_zeros(grads, 15)
 
@@ -886,13 +893,14 @@
     for k, value in enumerate((dgain0, dbias0, dgain1, dbias1)):
         place_row(2 * k, value)
     for k in range(4):
-        place_row(8 + 2 * k, dnorms1[k : k + 1, :])
-        place_row(16 + 2 * k, dnorms2[k : k + 1, :])
-    place_row(24, debias1[...])
-    place_row(30, debias2[...])
-    for first, value in ((40, dpos1), (56, dpos2)):
-        small[first : first + 8, :] = value[:, :128]
-        small[first + 8 : first + 16, : WIN - 128] = value[:, 128:]
+        place_row(8 + 2 * k, dsmall1[k : k + 1, :])
+        place_row(16 + 2 * k, dsmall2[k : k + 1, :])
+    for k in range(3):
+        place_row(24 + 2 * k, dsmall1[4 + k : 5 + k, :])
+        place_row(30 + 2 * k, dsmall2[4 + k : 5 + k, :])
+    for layer, value in enumerate((dpos1, dpos2)):
+        small[40 + 8 * layer : 48 + 8 * layer, :] = value[:, :128]
+        small[56:64, 64 * layer : 64 * layer + WIN - 128] = value[:, 128:]
     begin = grads.shape[1] - SMALL_ROWS
     for col in range(grads.shape[0]):
         grads[col, begin:, :] = small[...].astype(bf16)
@@ -992,22 +1000,24 @@
 
 
 def sum_all(value):
-    for axis in ("col", "row"):
+    axes = [axis for axis in ("col", "row") if lax.axis_size(axis) > 1]
+    terms = [value, jnp.zeros_like(value)]
+    for axis in axes:
         count = lax.axis_size(axis)
-        step = 1
-
-        def other(flip):
-            return lax.ppermute(value, axis, [(i, i ^ flip) for i in range(count)])
-
-        while step < count:
-            if 4 * step <= count:
-                near, far, both = other(step), other(2 * step), other(3 * step)
-                value = (value + near) + (far + both)
-                step *= 4
-            else:
-                value = value + other(step)
-                step *= 2
-    return value
+        first = 1
+        while first < count:
+            group = min(4, count // first)
+
+            def other(flip):
+                return lax.ppermute(value, axis, [(i, i ^ (flip * first)) for i in range(count)])
+
+            terms = [value, *(other(flip) for flip in range(1, group))]
+            while len(terms) > 2:
+                terms = [a + b for a, b in zip(terms[::2], terms[1::2])]
+            first *= group
+            if axis != axes[-1] or first < count:
+                value = terms[0] + terms[1]
+    return terms
 
 
 def on_device(
@@ -1051,7 +1061,7 @@
     place = jnp.stack(place).astype(i32)
     lay_one = layout.reshape(5, 24, 8, 2).transpose(1, 3, 2, 0).reshape(384, 5)
     lay_two = layout.reshape(5, 12, 2, 8, 2).transpose(2, 4, 1, 3, 0).reshape(384, 5)
-    above = onward(stem_map[-1:], "row")
+    early, above = lax.optimization_barrier((early, onward(stem_map[-1:], "row")))
     rim = jnp.concatenate([above[:, -1:], stem_map[:, -1:]], 0)
     rim = jnp.broadcast_to(onward(rim, "col"), (49, 8, 128))
     patches = run(
@@ -1061,13 +1071,13 @@
         [pltpu.VMEM((1536, 128), f32), pltpu.VMEM((32, 128), f32)],
         {0: SMEM},
     )[0]
-    late, _, _ = lax.optimization_barrier((late, above, early))
+    late, _ = lax.optimization_barrier((late, early))
     early = lax.all_gather(early, "col", axis=0)
     late = lax.all_to_all(late, "row", 0, 0, tiled=True)
     rows48, edge = out((4, 48, 2 * D), bf16), out((192, 2 * D), bf16)
-    conv_out, hidden0, query1, keyval1, *edges = run(
+    hidden0, query1, keyval1, *edges = run(
         front_kernel,
-        [out((384, D)), out((384, D)), out((384, D), bf16), out((2, 192, 2 * D), bf16), edge, edge],
+        [out((384, D)), out((384, D), bf16), out((2, 192, 2 * D), bf16), edge, edge],
         [place, patches, early, norms],
         specs={0: SMEM},
     )
@@ -1120,24 +1130,24 @@
         56,
         {0: hbm},
     )
-    sums = sum_all(sums)
+    sums_a, sums_b = sum_all(sums)
     pad_images = lambda x: jnp.pad(x, (0, padded - images))[:, None]
     grads_of = lambda group: out((nc, per[group] * D, 128), bf16)
     (
-        loss, grad_head, grad_hbias, dhid, grads2, dnorms2, debias2, dtable2, dquery2, inner2, rims2, *edges,
+        loss, grad_head, grad_hbias, dhid, grads2, dsmall2, dtable2, dquery2, inner2, rims2, *edges,
     ) = run(
         second_back_kernel,
         [
             out((8, 128)), out((sh, 1024)), out((1, 1024)), tokens, grads_of(0),
-            out((4, D)), out((1, FF)), dtable(Two), tokens_low,
+            out((8, D)), dtable(Two), tokens_low,
             out((4, 96, 2 * D)), out((4, 96, 2 * D), bf16), ext, ext,
         ],
         [
-            place, lay_one, sums, pad_images(labels), pad_images(live.astype(f32)), hbias,
+            place, lay_one, sums_a, sums_b, pad_images(labels), pad_images(live.astype(f32)), hbias,
             last2, middle2, att2, query2, *near2, kept2, late2, norms, ebias,
         ],
         tiles(Two, True) + [like(late2), like(grads_of(0)), token5(D), copy_sems(6)],
-        {0: SMEM, **dict.fromkeys((10, 11, 12, 13, 14), hbm)},
+        {0: SMEM, **dict.fromkeys((11, 12, 13, 14, 15), hbm)},
         56,
         {4: hbm},
     )
@@ -1151,10 +1161,10 @@
 
     dpos2 = position(Two, dtable2)
     part2 = pltpu.VMEM((4, 96, 2 * D), bf16)
-    dhid, grads1, dnorms1, debias1, dtable1, dquery1, inner1, sides1, *edges = run(
+    dhid, grads1, dsmall1, dtable1, dquery1, inner1, sides1, *edges = run(
         first_back_kernel,
         [
-            tokens, grads_of(1), out((4, D)), out((1, FF)), dtable(One),
+            tokens, grads_of(1), out((8, D)), dtable(One),
             tokens_low, out((2, 192, 2 * D)), out((2, 192, 2 * D), bf16), rows48, rows48,
         ],
         [
@@ -1176,8 +1186,8 @@
         front_back_kernel,
         [half(nc // 2), half(nc // 2)],
         [
-            place, dhid, dquery1, inner1, *drows1, *dcols1, hidden0, conv_out, patches,
-            early, norms, dnorms1, dnorms2, debias1, debias2, dpos1, dpos2,
+            place, dhid, dquery1, inner1, *drows1, *dcols1, patches,
+            early, norms, dsmall1, dsmall2, dpos1, dpos2,
         ],
         [pltpu.VMEM((nc, part, 128), bf16), pltpu.VMEM((SMALL_ROWS, 128), f32)],
         {0: SMEM},
@@ -1217,8 +1227,8 @@
     )
     new = [x.T for x in new[:3]] + list(new[3:])
     pos = [
-        jnp.concatenate([small[k : k + 8], small[k + 8 : k + 16, : 169 - 128]], 1).reshape(-1)
-        for k in (40, 56)
+        jnp.concatenate([small[40 + 8 * k : 48 + 8 * k], small[56:64, 64 * k : 64 * k + 41]], 1).reshape(-1)
+        for k in range(2)
     ]
     grad_small = jnp.concatenate([small[:36].reshape(-1), grad_hbias[0, :CLASSES], *pos])
     head = adamw(head_weight, grad_head[:, :CLASSES], first_head, second_head)

time: 274 us -> 268 us (0.978)
  blocking collectives: 22.9 us -> 6.65 us
  starting transfers between devices: 64.5 us -> 72.1 us
  waiting for transfers between devices: 79.8 us -> 83.4 us
    all_to_all x1 -> x0, blocking collectives: 16.3 us -> none  [on_device(): early = lax.all_to_all(early, 'row', 0, 0, tiled=True)]
    all_to_all x0 -> x1, starting transfers between devices: none -> 7.25 us  [on_device(): early = lax.all_to_all(early, 'row', 0, 0, tiled=True)]
    all_gather x1, waiting for transfers between devices: 1.6 us -> 7.68 us  [on_device(): early = lax.all_gather(early, 'col', axis=0)]
    all_to_all x1, waiting for transfers between devices: 4.51 us -> 1.39 us  [on_device(): late = lax.all_to_all(late, 'row', 0, 0, tiled=True)]
    unnamed x128 -> x124, local copies, waits for them, and re-layouts: 15.3 us -> 13.1 us
  transfers between devices with their start and end apart: 34 -> 35, of which waited for: 20 -> 20; matrix products, arithmetic and copies ran while one was open for 3% -> 3% of each run, Pallas kernels for 13% -> 13%
where the time goes in v6:
time: 268 us; the launch traced here: 266 us
  waiting for transfers between devices  83.4 us (31%)
  starting transfers between devices  72.1 us (27%)
  Pallas kernels  64.5 us (24%)
  local copies, waits for them, and re-layouts  20.9 us (8%)
  between operations  14.7 us (5%)
  blocking collectives  6.65 us (2%)
  other arithmetic  4.23 us (2%)
    pallas_call x19, Pallas kernels, run(): pl.pallas_call(kernel, out_shape=outs, in_specs=in_specs, out_specs=resul...  64.5 us
    ppermute x8, starting transfers between devices, swaps(): lax.ppermute(first, axis, both[0])  22.4 us
    all_to_all x1, waiting for transfers between devices, on_device(): mine = lax.all_to_all(mine, 'row', 0, 0, tiled=True)  20.8 us
    ppermute x8, waiting for transfers between devices, swaps(): lax.ppermute(first, axis, both[0])  18.3 us
    ppermute x7, starting transfers between devices, other(): lax.ppermute(value, axis, [(i, i ^ flip * first) for i in range(count)])  16.2 us
    unnamed x124, local copies, waits for them, and re-layouts  13.1 us
    ppermute x2, waiting for transfers between devices, onward(): lax.ppermute(value, axis, [(i, (i + 1) % count) for i in range(count)])  9.48 us
    ppermute x2, waiting for transfers between devices, on_device(): given = lax.ppermute(given, 'col', [(i, i ^ 1 << stage) for i in range(nc)])  9 us
  transfers between devices with their start and end apart: 35, of which 20 were waited for; matrix products, arithmetic and copies ran while one was open for 3% of the time, Pallas kernels for 13%

profile of v6, /device:TPU:0, one launch (start us, length us, event | category | flops | bytes accessed | tf_op | source)
XLA Modules:
  0.0 266.5 jit_solution(7227264018798766900)
XLA Ops:
  9.6 7.3 %all-to-all-start = ((bf16[8,128,128]{2,1,0:T(8,128)(2,1)}), bf16[8,128,128]{2,1,0:T(8,128)(2,1)S(1)}, u32[]{:S(2)}, u32[]{:S(2)}) async-start(bf16[8,128,128]{2,1,0:T(8,128)(2,1)} %get-tuple-element.96), calls=%async_computation | async-start | bytes 524288 | tf_op jit(solution)/shard_map/all_to_all | solution.py:1047
  19.5 6.7 %collective-permute-done = bf16[1,32,128]{2,1,0:T(8,128)(2,1)S(1)} collective-permute-done((bf16[1,32,128]{2,1,0:T(8,128)(2,1)S(1)}, bf16[1,32,128]{2,1,0:T(8,128)(2,1)S(1)}, u32[]{:S(2)}, u32[]{:S(2)}) %collective-permute-start) | collective-permute-done | bytes 8224 | tf_op jit(solution)/shard_map/ppermute | solution.py:992
  27.0 3.6 %all-to-all-start.1 = ((bf16[8,352,128]{2,1,0:T(8,128)(2,1)}), bf16[8,352,128]{2,1,0:T(8,128)(2,1)S(1)}, u32[]{:S(2)}, u32[]{:S(2)}) async-start(bf16[8,352,128]{2,1,0:T(8,128)(2,1)} %get-tuple-element.108), calls=%async_computation.1 | async-start | bytes 1441792 | tf_op jit(solution)/shard_map/all_to_all | solution.py:1076
  34.8 7.7 %all-gather.8.cloned.1.call-done = bf16[32,128,128]{2,1,0:T(8,128)(2,1)} async-done(((bf16[8,128,128]{2,1,0:T(8,128)(2,1)}), bf16[32,128,128]{2,1,0:T(8,128)(2,1)}) %all-gather.8.cloned.1.call-update) | async-done | bytes 1048592 | tf_op jit(solution)/shard_map/all_gather | solution.py:1075
  58.0 8.6 %all-gather.10.cloned.1.call-done = bf16[32,160,128]{2,1,0:T(8,128)(2,1)} async-done(((bf16[8,160,128]{2,1,0:T(8,128)(2,1)}), bf16[32,160,128]{2,1,0:T(8,128)(2,1)}) %all-gather.10.cloned.1.call-update) | async-done | bytes 1310736 | tf_op jit(solution)/shard_map/all_gather | solution.py:1085
  66.7 9.0 %shard_map.413 = (bf16[6,512,512]{2,1,0:T(8,128)(2,1)}, bf16[384,256]{1,0:T(8,128)(2,1)}, f32[384,256]{1,0:T(8,128)}, f32[384,256]{1,0:T(8,128)}, bf16[384,256]{...) custom-call(s32[6]{0:T(128)} %copy-done.38, ...), custom_call_target="tpu_custom_call" | custom-call | bytes 4194304 | tf_op jit(solution)/shard_map/pallas_call | solution.py:368
  78.0 8.4 %collective-permute-done.6.first = bf16[4,48,512]{2,1,0:T(8,128)(2,1)S(1)} collective-permute-done((bf16[4,48,512]{2,1,0:T(8,128)(2,1)}, bf16[4,48,512]{2,1,0:T(8,128)(2,1)S(1)}, u32[]{:S(2)}, u32[]{:S(2)}) %collective-permute-start.6) | collective-permute-done | bytes 196640 | tf_op jit(solution)/shard_map/ppermute | solution.py:999
  88.9 2.8 %collective-permute-start.8 = (bf16[4,192,512]{2,1,0:T(8,128)(2,1)S(1)}, bf16[4,192,512]{2,1,0:T(8,128)(2,1)S(1)}, u32[]{:S(2)}, u32[]{:S(2)}) collective-permute-start(bf16[4,192,512]{2,1,0:T(8,128)(2,1)S(1)} %shard_map.414.own), channel_id=1, source_target_pairs={{0,1},{2,3},{1,0},{3,2},{4,5},{6,7},{5,4},{7,6},{8,9},{10,11},{9,8... | collective-permute-start | bytes 2359304 | tf_op jit(solution)/shard_map/ppermute | solution.py:999
  94.6 9.1 %shard_map.415 = (bf16[12,256,384]{2,1,0:T(8,128)(2,1)}, bf16[384,256]{1,0:T(8,128)(2,1)}, f32[384,256]{1,0:T(8,128)}, f32[384,256]{1,0:T(8,128)}, f32[64,256]{1,0:T(8,128)}) custom-call(s32[6]{0:T(128)} %copy-done.38, s32[384,5]{1,0:T(8,128)} %bitcast.60, s32[384,5]{1,0:T(8,128)} %bitcast.45, f32[384,256]{1,0:T(8,128)} %get-tuple-element.110.hidden, ...), custom_call_target="tpu_custom_call" | custom-call | bytes 4194304 | tf_op jit(solution)/shard_map/pallas_call | solution.py:368
  103.8 9.5 %collective-permute-start.11 = (f32[64,256]{1,0:T(8,128)}, f32[64,256]{1,0:T(8,128)S(1)}, u32[]{:S(2)}, u32[]{:S(2)}) collective-permute-start(f32[64,256]{1,0:T(8,128)} %get-tuple-element.116), channel_id=1, source_target_pairs={{0,2},{1,3},{2,0},{3,1},{4,6},{5,7},{6,4},{7,5},{8,10},{9,11},{10,... | collective-permute-start | bytes 196616 | tf_op jit(solution)/shard_map/ppermute | solution.py:1012
  113.3 3.2 %collective-permute-done.11 = f32[64,256]{1,0:T(8,128)S(1)} collective-permute-done((f32[64,256]{1,0:T(8,128)}, f32[64,256]{1,0:T(8,128)S(1)}, u32[]{:S(2)}, u32[]{:S(2)}) %collective-permute-start.11) | collective-permute-done | bytes 65568 | tf_op jit(solution)/shard_map/ppermute | solution.py:1012
  117.4 3.4 %collective-permute-start.15 = (f32[64,256]{1,0:T(8,128)S(1)}, f32[64,256]{1,0:T(8,128)S(1)}, u32[]{:S(2)}, u32[]{:S(2)}) collective-permute-start(f32[64,256]{1,0:T(8,128)S(1)} %add_add_fusion.1), channel_id=1, source_target_pairs={{0,12},{4,8},{8,4},{12,0},{16,28},{20,24},{24,20},{28,16},{1,13},{... | collective-permute-start | bytes 196616 | tf_op jit(solution)/shard_map/ppermute | solution.py:1012
  131.5 12.8 %shard_map.416 = (f32[8,128]{1,0:T(8,128)}, f32[32,1024]{1,0:T(8,128)}, f32[1,1024]{1,0:T(1,128)}, f32[384,256]{1,0:T(8,128)}, bf16[4,1024,128]{2,1,0:T(8,128)(2...) custom-call(s32[6]{0:T(128)} %copy-done.38, ...), custom_call_target="tpu_custom_call" | custom-call | bytes 4194304 | tf_op jit(solution)/shard_map/pallas_call | solution.py:368
  151.8 2.9 %collective-permute-done.19.drowa = bf16[4,48,512]{2,1,0:T(8,128)(2,1)S(1)} collective-permute-done((bf16[4,48,512]{2,1,0:T(8,128)(2,1)S(1)}, bf16[4,48,512]{2,1,0:T(8,128)(2,1)S(1)}, u32[]{:S(2)}, u32[]{:S(2)}) %collective-permute-start.19) | collective-permute-done | bytes 196640 | tf_op jit(solution)/shard_map/ppermute | solution.py:999
  155.4 12.8 %shard_map.418 = (f32[384,256]{1,0:T(8,128)}, bf16[4,1280,128]{2,1,0:T(8,128)(2,1)}, f32[8,256]{1,0:T(8,128)}, f32[512,512]{1,0:T(8,128)}, bf16[384,256]{1,0:T(8...) custom-call(s32[6]{0:T(128)} %copy-done.38, ...), custom_call_target="tpu_custom_call" | custom-call | bytes 4194304 | tf_op jit(solution)/shard_map/pallas_call | solution.py:368
  168.3 4.9 %collective-permute-start.21 = (bf16[4,48,512]{2,1,0:T(8,128)(2,1)}, bf16[4,48,512]{2,1,0:T(8,128)(2,1)S(1)}, u32[]{:S(2)}, u32[]{:S(2)}) collective-permute-start(bf16[4,48,512]{2,1,0:T(8,128)(2,1)} %get-tuple-element.138), channel_id=1, source_target_pairs={{0,4},{8,12},{16,20},{24,28},{4,0},{12,8},{20,16},{28,24},{1,5},{9... | collective-permute-start | bytes 589832 | tf_op jit(solution)/shard_map/ppermute | solution.py:999
  173.8 3.2 %collective-permute-done.21.first.drowa = bf16[4,48,512]{2,1,0:T(8,128)(2,1)S(1)} collective-permute-done((bf16[4,48,512]{2,1,0:T(8,128)(2,1)}, bf16[4,48,512]{2,1,0:T(8,128)(2,1)S(1)}, u32[]{:S(2)}, u32[]{:S(2)}) %collective-permute-start.21) | collective-permute-done | bytes 196640 | tf_op jit(solution)/shard_map/ppermute | solution.py:999
  178.7 9.6 %collective-permute-start.23 = (bf16[192,512]{1,0:T(8,128)(2,1)S(1)}, bf16[192,512]{1,0:T(8,128)(2,1)S(1)}, u32[]{:S(2)}, u32[]{:S(2)}) collective-permute-start(bf16[192,512]{1,0:T(8,128)(2,1)S(1)} %get-tuple-element.141), channel_id=1, source_target_pairs={{0,1},{2,3},{1,0},{3,2},{4,5},{6,7},{5,4},{7,6},{8,9},{10,11},{9,8... | collective-permute-start | bytes 589832 | tf_op jit(solution)/shard_map/ppermute | solution.py:999
  193.5 3.4 %shard_map.422 = (bf16[2,1088,128]{2,1,0:T(8,128)(2,1)S(1)}, bf16[2,1088,128]{2,1,0:T(8,128)(2,1)S(1)}) custom-call(s32[6]{0:T(128)S(1)} %copy-done.41, f32[384,256]{1,0:T(8,128)S(1)} %copy-done.19, bf16[384,256]{1,0:T(8,128)(2,1)S(1)} %copy-done.28, f32[2,192,512]{2,1,0:T(8,128)S(1)} %copy-done.12, ...), custom_call_target="tpu_custom_call" | custom-call | bytes 4194304 | tf_op jit(solution)/shard_map/pallas_call | solution.py:368
  196.9 5.4 %collective-permute-start.25 = (bf16[2,1088,128]{2,1,0:T(8,128)(2,1)S(1)}, bf16[2,1088,128]{2,1,0:T(8,128)(2,1)S(1)}, u32[]{:S(2)}, u32[]{:S(2)}) collective-permute-start(bf16[2,1088,128]{2,1,0:T(8,128)(2,1)S(1)} %get-tuple-element.148), channel_id=1, source_target_pairs={{0,1},{1,0},{2,3},{3,2},{4,5},{5,4},{6,7},{7,6},{8,9},{9,8},{10,11... | collective-permute-start | bytes 1671176 | tf_op jit(solution)/shard_map/ppermute | solution.py:1197
  207.0 7.4 %collective-permute-done.26.given = bf16[1,1088,128]{2,1,0:T(8,128)(2,1)S(1)} collective-permute-done((bf16[1,1088,128]{2,1,0:T(8,128)(2,1)S(1)}, bf16[1,1088,128]{2,1,0:T(8,128)(2,1)S(1)}, u32[]{:S(2)}, u32[]{:S(2)}) %collective-permute-start.26) | collective-permute-done | bytes 278560 | tf_op jit(solution)/shard_map/ppermute | solution.py:1197
  217.4 7.7 %all-to-all-start.2 = ((bf16[8,480,128]{2,1,0:T(8,128)(2,1)}), bf16[8,480,128]{2,1,0:T(8,128)(2,1)S(1)}, u32[]{:S(2)}, u32[]{:S(2)}) async-start(bf16[8,480,128]{2,1,0:T(8,128)(2,1)} %shard_map.424), calls=%async_computation.4 | async-start | bytes 1966080 | tf_op jit(solution)/shard_map/all_to_all | solution.py:1215
  228.5 20.8 %all-to-all-done.2.parts = bf16[8,480,128]{2,1,0:T(8,128)(2,1)S(1)} async-done(((bf16[8,480,128]{2,1,0:T(8,128)(2,1)}), bf16[8,480,128]{2,1,0:T(8,128)(2,1)S(1)}, u32[]{:S(2)}, u32[]{:S(2)}) %all-to-all-start.2) | async-done | bytes 983072 | tf_op jit(solution)/shard_map/all_to_all | solution.py:1215
  249.7 6.6 %all-gather.3 = bf16[1664,128]{1,0:T(8,128)(2,1)S(1)} all-gather(bf16[416,128]{1,0:T(8,128)(2,1)S(1)} %get-tuple-element.151), channel_id=5, replica_groups=mesh['row'=8,'col'=4] {'col'}, dimensions={0}, use_global_device_ids=true | all-gather | bytes 532480 | tf_op jit(solution)/shard_map/all_gather | solution.py:1219
  (233 shorter events, 74.9 us)
Async XLA Ops:
  9.6 16.7 %all-to-all-start = ((bf16[8,128,128]{2,1,0:T(8,128)(2,1)}), bf16[8,128,128]{2,1,0:T(8,128)(2,1)S(1)}, u32[]{:S(2)}, u32[]{:S(2)}) async-start(bf16[8,128,128]{2,1,0:T(8,128)(2,1)} %get-tuple-element.96), calls=%async_computation | async-start | bytes 524288 | tf_op jit(solution)/shard_map/all_to_all | solution.py:1047
  16.8 25.6 %all-gather.8.cloned.1.call-start = ((), (), s32[]{:S(2)}) async-start(), calls=%async_computation.7 | async-start | bytes 1310720 | tf_op jit(solution)/shard_map/all_gather | solution.py:1075
  17.6 8.7 %collective-permute-start = (bf16[1,32,128]{2,1,0:T(8,128)(2,1)S(1)}, bf16[1,32,128]{2,1,0:T(8,128)(2,1)S(1)}, u32[]{:S(2)}, u32[]{:S(2)}) collective-permute-start(bf16[1,32,128]{2,1,0:T(8,128)(2,1)S(1)} %slice.51), channel_id=1, source_target_pairs={{0,4},{4,8},{8,12},{12,16},{16,20},{20,24},{24,28},{28,0},{1,5},{5... | collective-permute-start | bytes 24584 | tf_op jit(solution)/shard_map/ppermute | solution.py:992
  27.0 21.5 %all-to-all-start.1 = ((bf16[8,352,128]{2,1,0:T(8,128)(2,1)}), bf16[8,352,128]{2,1,0:T(8,128)(2,1)S(1)}, u32[]{:S(2)}, u32[]{:S(2)}) async-start(bf16[8,352,128]{2,1,0:T(8,128)(2,1)} %get-tuple-element.108), calls=%async_computation.1 | async-start | bytes 1441792 | tf_op jit(solution)/shard_map/all_to_all | solution.py:1076
  30.6 36.1 %all-gather.10.cloned.1.call-start = ((), (), s32[]{:S(2)}) async-start(), calls=%async_computation.8 | async-start | bytes 1638400 | tf_op jit(solution)/shard_map/all_gather | solution.py:1085
  49.2 43.4 %all-gather.12.cloned.1.call-start = ((), (), s32[]{:S(2)}) async-start(), calls=%async_computation.9 | async-start | bytes 1966080 | tf_op jit(solution)/shard_map/all_gather | solution.py:1086
  50.1 156.8 %reduce-scatter.3.cloned.1.call-start = ((), (), s32[]{:S(2)}) async-start(), calls=%async_computation.5 | async-start | bytes 1310720 | tf_op jit(solution)/shard_map/reduce_scatter | solution.py:1156
  52.3 5.7 %collective-permute-start.4 = (bf16[4,48,512]{2,1,0:T(8,128)(2,1)S(1)}, bf16[4,48,512]{2,1,0:T(8,128)(2,1)S(1)}, u32[]{:S(2)}, u32[]{:S(2)}) collective-permute-start(bf16[4,48,512]{2,1,0:T(8,128)(2,1)S(1)} %get-tuple-element.104), channel_id=1, source_target_pairs={{0,4},{8,12},{16,20},{24,28},{4,0},{12,8},{20,16},{28,24},{1,5},{9... | collective-permute-start | bytes 589832 | tf_op jit(solution)/shard_map/ppermute | solution.py:999
  75.8 10.6 %collective-permute-start.6 = (bf16[4,48,512]{2,1,0:T(8,128)(2,1)}, bf16[4,48,512]{2,1,0:T(8,128)(2,1)S(1)}, u32[]{:S(2)}, u32[]{:S(2)}) collective-permute-start(bf16[4,48,512]{2,1,0:T(8,128)(2,1)} %get-tuple-element.113), channel_id=1, source_target_pairs={{0,4},{8,12},{16,20},{24,28},{4,0},{12,8},{20,16},{28,24},{1,5},{9... | collective-permute-start | bytes 589832 | tf_op jit(solution)/shard_map/ppermute | solution.py:999
  77.3 9.1 %collective-permute-start.7 = (bf16[4,48,512]{2,1,0:T(8,128)(2,1)}, bf16[4,48,512]{2,1,0:T(8,128)(2,1)S(1)}, u32[]{:S(2)}, u32[]{:S(2)}) collective-permute-start(bf16[4,48,512]{2,1,0:T(8,128)(2,1)} %get-tuple-element.114), channel_id=1, source_target_pairs={{4,8},{12,16},{20,24},{8,4},{16,12},{24,20},{5,9},{13,17},{21,25},... | collective-permute-start | bytes 589832 | tf_op jit(solution)/shard_map/ppermute | solution.py:999
  88.0 4.6 %collective-permute-start.9 = (bf16[4,192,512]{2,1,0:T(8,128)(2,1)S(1)}, bf16[4,192,512]{2,1,0:T(8,128)(2,1)S(1)}, u32[]{:S(2)}, u32[]{:S(2)}) collective-permute-start(bf16[4,192,512]{2,1,0:T(8,128)(2,1)S(1)} %shard_map.414.own), channel_id=1, source_target_pairs={{1,2},{2,1},{5,6},{6,5},{9,10},{10,9},{13,14},{14,13},{17,18},{18,... | collective-permute-start | bytes 2359304 | tf_op jit(solution)/shard_map/ppermute | solution.py:999
  88.9 4.7 %collective-permute-start.8 = (bf16[4,192,512]{2,1,0:T(8,128)(2,1)S(1)}, bf16[4,192,512]{2,1,0:T(8,128)(2,1)S(1)}, u32[]{:S(2)}, u32[]{:S(2)}) collective-permute-start(bf16[4,192,512]{2,1,0:T(8,128)(2,1)S(1)} %shard_map.414.own), channel_id=1, source_target_pairs={{0,1},{2,3},{1,0},{3,2},{4,5},{6,7},{5,4},{7,6},{8,9},{10,11},{9,8... | collective-permute-start | bytes 2359304 | tf_op jit(solution)/shard_map/ppermute | solution.py:999
  103.7 9.6 %collective-permute-start.12 = (f32[64,256]{1,0:T(8,128)}, f32[64,256]{1,0:T(8,128)S(1)}, u32[]{:S(2)}, u32[]{:S(2)}) collective-permute-start(f32[64,256]{1,0:T(8,128)} %get-tuple-element.116), channel_id=1, source_target_pairs={{0,3},{1,2},{2,1},{3,0},{4,7},{5,6},{6,5},{7,4},{8,11},{9,10},{10,... | collective-permute-start | bytes 196616 | tf_op jit(solution)/shard_map/ppermute | solution.py:1012
  103.8 12.8 %collective-permute-start.11 = (f32[64,256]{1,0:T(8,128)}, f32[64,256]{1,0:T(8,128)S(1)}, u32[]{:S(2)}, u32[]{:S(2)}) collective-permute-start(f32[64,256]{1,0:T(8,128)} %get-tuple-element.116), channel_id=1, source_target_pairs={{0,2},{1,3},{2,0},{3,1},{4,6},{5,7},{6,4},{7,5},{8,10},{9,11},{10,... | collective-permute-start | bytes 196616 | tf_op jit(solution)/shard_map/ppermute | solution.py:1012
  117.4 6.3 %collective-permute-start.15 = (f32[64,256]{1,0:T(8,128)S(1)}, f32[64,256]{1,0:T(8,128)S(1)}, u32[]{:S(2)}, u32[]{:S(2)}) collective-permute-start(f32[64,256]{1,0:T(8,128)S(1)} %add_add_fusion.1), channel_id=1, source_target_pairs={{0,12},{4,8},{8,4},{12,0},{16,28},{20,24},{24,20},{28,16},{1,13},{... | collective-permute-start | bytes 196616 | tf_op jit(solution)/shard_map/ppermute | solution.py:1012
  125.6 5.2 %collective-permute-start.16 = (f32[64,256]{1,0:T(8,128)S(1)}, f32[64,256]{1,0:T(8,128)S(1)}, u32[]{:S(2)}, u32[]{:S(2)}) collective-permute-start(f32[64,256]{1,0:T(8,128)S(1)} %add_add_fusion.sums_a), channel_id=1, source_target_pairs={{0,16},{4,20},{8,24},{12,28},{16,0},{20,4},{24,8},{28,12},{1,17},{... | collective-permute-start | bytes 196616 | tf_op jit(solution)/shard_map/ppermute | solution.py:1012
  144.3 70.1 %reduce-scatter.5.cloned.1.call-start = ((), (), s32[]{:S(2)}) async-start(), calls=%async_computation.6 | async-start | bytes 1638400 | tf_op jit(solution)/shard_map/reduce_scatter | solution.py:1180
  149.0 5.7 %collective-permute-start.19 = (bf16[4,48,512]{2,1,0:T(8,128)(2,1)S(1)}, bf16[4,48,512]{2,1,0:T(8,128)(2,1)S(1)}, u32[]{:S(2)}, u32[]{:S(2)}) collective-permute-start(bf16[4,48,512]{2,1,0:T(8,128)(2,1)S(1)} %get-tuple-element.129), channel_id=1, source_target_pairs={{0,4},{8,12},{16,20},{24,28},{4,0},{12,8},{20,16},{28,24},{1,5},{9... | collective-permute-start | bytes 589832 | tf_op jit(solution)/shard_map/ppermute | solution.py:999
  168.3 8.7 %collective-permute-start.21 = (bf16[4,48,512]{2,1,0:T(8,128)(2,1)}, bf16[4,48,512]{2,1,0:T(8,128)(2,1)S(1)}, u32[]{:S(2)}, u32[]{:S(2)}) collective-permute-start(bf16[4,48,512]{2,1,0:T(8,128)(2,1)} %get-tuple-element.138), channel_id=1, source_target_pairs={{0,4},{8,12},{16,20},{24,28},{4,0},{12,8},{20,16},{28,24},{1,5},{9... | collective-permute-start | bytes 589832 | tf_op jit(solution)/shard_map/ppermute | solution.py:999
  178.7 14.0 %collective-permute-start.23 = (bf16[192,512]{1,0:T(8,128)(2,1)S(1)}, bf16[192,512]{1,0:T(8,128)(2,1)S(1)}, u32[]{:S(2)}, u32[]{:S(2)}) collective-permute-start(bf16[192,512]{1,0:T(8,128)(2,1)S(1)} %get-tuple-element.141), channel_id=1, source_target_pairs={{0,1},{2,3},{1,0},{3,2},{4,5},{6,7},{5,4},{7,6},{8,9},{10,11},{9,8... | collective-permute-start | bytes 589832 | tf_op jit(solution)/shard_map/ppermute | solution.py:999
  188.3 4.4 %collective-permute-start.24 = (bf16[192,512]{1,0:T(8,128)(2,1)S(1)}, bf16[192,512]{1,0:T(8,128)(2,1)S(1)}, u32[]{:S(2)}, u32[]{:S(2)}) collective-permute-start(bf16[192,512]{1,0:T(8,128)(2,1)S(1)} %get-tuple-element.142), channel_id=1, source_target_pairs={{1,2},{2,1},{5,6},{6,5},{9,10},{10,9},{13,14},{14,13},{17,18},{18,... | collective-permute-start | bytes 589832 | tf_op jit(solution)/shard_map/ppermute | solution.py:999
  196.9 7.0 %collective-permute-start.25 = (bf16[2,1088,128]{2,1,0:T(8,128)(2,1)S(1)}, bf16[2,1088,128]{2,1,0:T(8,128)(2,1)S(1)}, u32[]{:S(2)}, u32[]{:S(2)}) collective-permute-start(bf16[2,1088,128]{2,1,0:T(8,128)(2,1)S(1)} %get-tuple-element.148), channel_id=1, source_target_pairs={{0,1},{1,0},{2,3},{3,2},{4,5},{5,4},{6,7},{7,6},{8,9},{9,8},{10,11... | collective-permute-start | bytes 1671176 | tf_op jit(solution)/shard_map/ppermute | solution.py:1197
  205.4 8.9 %collective-permute-start.26 = (bf16[1,1088,128]{2,1,0:T(8,128)(2,1)S(1)}, bf16[1,1088,128]{2,1,0:T(8,128)(2,1)S(1)}, u32[]{:S(2)}, u32[]{:S(2)}) collective-permute-start(bf16[1,1088,128]{2,1,0:T(8,128)(2,1)S(1)} %get-tuple-element.150), channel_id=1, source_target_pairs={{0,2},{1,3},{2,0},{3,1},{4,6},{5,7},{6,4},{7,5},{8,10},{9,11},{10,... | collective-permute-start | bytes 835592 | tf_op jit(solution)/shard_map/ppermute | solution.py:1197
  217.4 32.0 %all-to-all-start.2 = ((bf16[8,480,128]{2,1,0:T(8,128)(2,1)}), bf16[8,480,128]{2,1,0:T(8,128)(2,1)S(1)}, u32[]{:S(2)}, u32[]{:S(2)}) async-start(bf16[8,480,128]{2,1,0:T(8,128)(2,1)} %shard_map.424), calls=%async_computation.4 | async-start | bytes 1966080 | tf_op jit(solution)/shard_map/all_to_all | solution.py:1215
  (74 other events, 1090.1 us)
Sparse Core Ops, SparseCore 0:
  27.1 15.3 all-gather.7
  49.4 17.2 all-gather.9
  68.2 19.6 all-gather.11
  144.4 25.0 reduce-scatter.2
  172.1 37.3 reduce-scatter.4

commit v7 on v6

--- a/solution.py
+++ b/solution.py
@@ -793,7 +793,8 @@
     wait_for(leaving)
 
 
-def position_kernel(dtable, dpos, dfirst, *, geo):
+def position_kernel(dtable, rims, dpos, near, dfirst, *, geo):
+    near[...] = rims[...]
     dpos[...] = gather_table(geo, dtable, dfirst)
 
 
@@ -856,7 +857,7 @@
 
 
 def front_back_kernel(
-    place, dhid_in, dquery, inner, drowa, drowb, dcola, dcolb, patches, early,
+    place, dhid_in, dquery, inner, drowa, drowb, dcolb, dcola, patches, early,
     norms, dsmall1, dsmall2, dpos1, dpos2,
     keep, give,
     grads, small,
@@ -1151,15 +1152,20 @@
         56,
         {4: hbm},
     )
-    dcols2 = swaps(*edges, "col")
+    def position(geo, table, rims):
+        scratch = [pltpu.VMEM((geo.pieces, HEADS * geo.across, 128), f32)]
+        return run(
+            functools.partial(position_kernel, geo=geo),
+            [out((HEADS, WIN)), out(rims.shape, bf16)],
+            [table, rims],
+            scratch,
+        )
+
+    dpos2, rims2 = position(Two, dtable2, rims2)
+    dcols2 = swaps(*edges, "col")[::-1]
     drows2 = swaps(*run(rim_kernel, [rows48] * 2, [place, rims2, *dcols2], specs={0: SMEM}), "row")
     grads2 = lax.psum_scatter(grads2, "col", scatter_dimension=0, tiled=False)
 
-    def position(geo, table):
-        scratch = [pltpu.VMEM((geo.pieces, HEADS * geo.across, 128), f32)]
-        return run(functools.partial(position_kernel, geo=geo), [out((HEADS, WIN))], [table], scratch)[0]
-
-    dpos2 = position(Two, dtable2)
     part2 = pltpu.VMEM((4, 96, 2 * D), bf16)
     dhid, grads1, dsmall1, dtable1, dquery1, inner1, sides1, *edges = run(
         first_back_kernel,
@@ -1178,7 +1184,7 @@
     )
     drows1 = swaps(*edges, "row")
     grads1 = lax.psum_scatter(grads1, "col", scatter_dimension=0, tiled=False)
-    dpos1 = position(One, dtable1)
+    dpos1, sides1 = position(One, dtable1, sides1)
     dcols1 = swaps(*run(sides_kernel, [edge] * 2, [place, sides1, *drows1], specs={0: SMEM}), "col")
     part = per[2] * D + SMALL_ROWS
     half = lambda count: out((count, part, 128), bf16)
@@ -1186,7 +1192,7 @@
         front_back_kernel,
         [half(nc // 2), half(nc // 2)],
         [
-            place, dhid, dquery1, inner1, *drows1, *dcols1, patches,
+            place, dhid, dquery1, inner1, *drows1, *dcols1[::-1], patches,
             early, norms, dsmall1, dsmall2, dpos1, dpos2,
         ],
         [pltpu.VMEM((nc, part, 128), bf16), pltpu.VMEM((SMALL_ROWS, 128), f32)],

time: 268 us -> 264 us (0.985)
  transfers between devices with their start and end apart: 35 -> 35, of which waited for: 20 -> 20; matrix products, arithmetic and copies ran while one was open for 3% -> 3% of each run, Pallas kernels for 13% -> 14%
where the time goes in v7:
time: 264 us; the launch traced here: 263 us
  waiting for transfers between devices  83.1 us (31%)
  starting transfers between devices  70 us (27%)
  Pallas kernels  64.7 us (25%)
  local copies, waits for them, and re-layouts  20 us (8%)
  between operations  14.7 us (6%)
  blocking collectives  6.24 us (2%)
  other arithmetic  4.24 us (2%)
    pallas_call x19, Pallas kernels, run(): pl.pallas_call(kernel, out_shape=outs, in_specs=in_specs, out_specs=resul...  64.7 us
    ppermute x8, starting transfers between devices, swaps(): lax.ppermute(first, axis, both[0])  25.1 us
    all_to_all x1, waiting for transfers between devices, on_device(): mine = lax.all_to_all(mine, 'row', 0, 0, tiled=True)  21 us
    ppermute x7, starting transfers between devices, other(): lax.ppermute(value, axis, [(i, i ^ flip * first) for i in range(count)])  16.2 us
    ppermute x8, waiting for transfers between devices, swaps(): lax.ppermute(first, axis, both[0])  16 us
    unnamed x124, local copies, waits for them, and re-layouts  12.2 us
    ppermute x2, waiting for transfers between devices, on_device(): given = lax.ppermute(given, 'col', [(i, i ^ 1 << stage) for i in range(nc)])  10.9 us
    ppermute x2, waiting for transfers between devices, onward(): lax.ppermute(value, axis, [(i, (i + 1) % count) for i in range(count)])  9.48 us
  transfers between devices with their start and end apart: 35, of which 20 were waited for; matrix products, arithmetic and copies ran while one was open for 3% of the time, Pallas kernels for 14%

profile of v7, /device:TPU:0, one launch (start us, length us, event | category | flops | bytes accessed | tf_op | source)
XLA Modules:
  0.0 262.8 jit_solution(6742626447549114053)
XLA Ops:
  9.6 7.3 %all-to-all-start = ((bf16[8,128,128]{2,1,0:T(8,128)(2,1)}), bf16[8,128,128]{2,1,0:T(8,128)(2,1)S(1)}, u32[]{:S(2)}, u32[]{:S(2)}) async-start(bf16[8,128,128]{2,1,0:T(8,128)(2,1)} %get-tuple-element.100), calls=%async_computation | async-start | bytes 524288 | tf_op jit(solution)/shard_map/all_to_all | solution.py:1048
  19.6 6.7 %collective-permute-done = bf16[1,32,128]{2,1,0:T(8,128)(2,1)S(1)} collective-permute-done((bf16[1,32,128]{2,1,0:T(8,128)(2,1)S(1)}, bf16[1,32,128]{2,1,0:T(8,128)(2,1)S(1)}, u32[]{:S(2)}, u32[]{:S(2)}) %collective-permute-start) | collective-permute-done | bytes 8224 | tf_op jit(solution)/shard_map/ppermute | solution.py:993
  27.0 3.6 %all-to-all-start.1 = ((bf16[8,352,128]{2,1,0:T(8,128)(2,1)}), bf16[8,352,128]{2,1,0:T(8,128)(2,1)S(1)}, u32[]{:S(2)}, u32[]{:S(2)}) async-start(bf16[8,352,128]{2,1,0:T(8,128)(2,1)} %get-tuple-element.112), calls=%async_computation.1 | async-start | bytes 1441792 | tf_op jit(solution)/shard_map/all_to_all | solution.py:1077
  31.2 2.8 %collective-permute-done.1 = bf16[49,1,128]{2,0,1:T(8,128)(2,1)S(1)} collective-permute-done((bf16[49,1,128]{2,0,1:T(8,128)(2,1)S(1)}, bf16[49,1,128]{2,0,1:T(8,128)(2,1)S(1)}, u32[]{:S(2)}, u32[]{:S(2)}) %collective-permute-start.1) | collective-permute-done | bytes 12576 | tf_op jit(solution)/shard_map/ppermute | solution.py:993
  34.8 7.7 %all-gather.8.cloned.1.call-done = bf16[32,128,128]{2,1,0:T(8,128)(2,1)} async-done(((bf16[8,128,128]{2,1,0:T(8,128)(2,1)}), bf16[32,128,128]{2,1,0:T(8,128)(2,1)}) %all-gather.8.cloned.1.call-update) | async-done | bytes 1048592 | tf_op jit(solution)/shard_map/all_gather | solution.py:1076
  58.1 8.6 %all-gather.10.cloned.1.call-done = bf16[32,160,128]{2,1,0:T(8,128)(2,1)} async-done(((bf16[8,160,128]{2,1,0:T(8,128)(2,1)}), bf16[32,160,128]{2,1,0:T(8,128)(2,1)}) %all-gather.10.cloned.1.call-update) | async-done | bytes 1310736 | tf_op jit(solution)/shard_map/all_gather | solution.py:1086
  66.7 9.0 %shard_map.413 = (bf16[6,512,512]{2,1,0:T(8,128)(2,1)}, bf16[384,256]{1,0:T(8,128)(2,1)}, f32[384,256]{1,0:T(8,128)}, f32[384,256]{1,0:T(8,128)}, bf16[384,256]{...) custom-call(s32[6]{0:T(128)} %copy-done.38, ...), custom_call_target="tpu_custom_call" | custom-call | bytes 4194304 | tf_op jit(solution)/shard_map/pallas_call | solution.py:368
  78.0 8.4 %collective-permute-done.6.first = bf16[4,48,512]{2,1,0:T(8,128)(2,1)S(1)} collective-permute-done((bf16[4,48,512]{2,1,0:T(8,128)(2,1)}, bf16[4,48,512]{2,1,0:T(8,128)(2,1)S(1)}, u32[]{:S(2)}, u32[]{:S(2)}) %collective-permute-start.6) | collective-permute-done | bytes 196640 | tf_op jit(solution)/shard_map/ppermute | solution.py:1000
  88.9 2.8 %collective-permute-start.8 = (bf16[4,192,512]{2,1,0:T(8,128)(2,1)S(1)}, bf16[4,192,512]{2,1,0:T(8,128)(2,1)S(1)}, u32[]{:S(2)}, u32[]{:S(2)}) collective-permute-start(bf16[4,192,512]{2,1,0:T(8,128)(2,1)S(1)} %shard_map.414.own), channel_id=1, source_target_pairs={{0,1},{2,3},{1,0},{3,2},{4,5},{6,7},{5,4},{7,6},{8,9},{10,11},{9,8... | collective-permute-start | bytes 2359304 | tf_op jit(solution)/shard_map/ppermute | solution.py:1000
  94.6 9.1 %shard_map.415 = (bf16[12,256,384]{2,1,0:T(8,128)(2,1)}, bf16[384,256]{1,0:T(8,128)(2,1)}, f32[384,256]{1,0:T(8,128)}, f32[384,256]{1,0:T(8,128)}, f32[64,256]{1,0:T(8,128)}) custom-call(s32[6]{0:T(128)} %copy-done.38, s32[384,5]{1,0:T(8,128)} %bitcast.60, s32[384,5]{1,0:T(8,128)} %bitcast.45, f32[384,256]{1,0:T(8,128)} %get-tuple-element.114.hidden, ...), custom_call_target="tpu_custom_call" | custom-call | bytes 4194304 | tf_op jit(solution)/shard_map/pallas_call | solution.py:368
  103.8 9.4 %collective-permute-start.11 = (f32[64,256]{1,0:T(8,128)}, f32[64,256]{1,0:T(8,128)S(1)}, u32[]{:S(2)}, u32[]{:S(2)}) collective-permute-start(f32[64,256]{1,0:T(8,128)} %get-tuple-element.120), channel_id=1, source_target_pairs={{0,2},{1,3},{2,0},{3,1},{4,6},{5,7},{6,4},{7,5},{8,10},{9,11},{10,... | collective-permute-start | bytes 196616 | tf_op jit(solution)/shard_map/ppermute | solution.py:1013
  113.3 3.2 %collective-permute-done.11 = f32[64,256]{1,0:T(8,128)S(1)} collective-permute-done((f32[64,256]{1,0:T(8,128)}, f32[64,256]{1,0:T(8,128)S(1)}, u32[]{:S(2)}, u32[]{:S(2)}) %collective-permute-start.11) | collective-permute-done | bytes 65568 | tf_op jit(solution)/shard_map/ppermute | solution.py:1013
  117.4 3.5 %collective-permute-start.15 = (f32[64,256]{1,0:T(8,128)S(1)}, f32[64,256]{1,0:T(8,128)S(1)}, u32[]{:S(2)}, u32[]{:S(2)}) collective-permute-start(f32[64,256]{1,0:T(8,128)S(1)} %add_add_fusion.1), channel_id=1, source_target_pairs={{0,12},{4,8},{8,4},{12,0},{16,28},{20,24},{24,20},{28,16},{1,13},{... | collective-permute-start | bytes 196616 | tf_op jit(solution)/shard_map/ppermute | solution.py:1013
  131.4 12.8 %shard_map.416 = (f32[8,128]{1,0:T(8,128)}, f32[32,1024]{1,0:T(8,128)}, f32[1,1024]{1,0:T(1,128)}, f32[384,256]{1,0:T(8,128)}, bf16[4,1024,128]{2,1,0:T(8,128)(2...) custom-call(s32[6]{0:T(128)} %copy-done.38, ...), custom_call_target="tpu_custom_call" | custom-call | bytes 4194304 | tf_op jit(solution)/shard_map/pallas_call | solution.py:368
  145.1 3.9 %collective-permute-start.18 = (bf16[4,192,512]{2,1,0:T(8,128)(2,1)}, bf16[4,192,512]{2,1,0:T(8,128)(2,1)S(1)}, u32[]{:S(2)}, u32[]{:S(2)}) collective-permute-start(bf16[4,192,512]{2,1,0:T(8,128)(2,1)} %get-tuple-element.131), channel_id=1, source_target_pairs={{0,1},{2,3},{1,0},{3,2},{4,5},{6,7},{5,4},{7,6},{8,9},{10,11},{9,8... | collective-permute-start | bytes 2359304 | tf_op jit(solution)/shard_map/ppermute | solution.py:1000
  154.4 4.1 %collective-permute-done.19.drowa = bf16[4,48,512]{2,1,0:T(8,128)(2,1)S(1)} collective-permute-done((bf16[4,48,512]{2,1,0:T(8,128)(2,1)S(1)}, bf16[4,48,512]{2,1,0:T(8,128)(2,1)S(1)}, u32[]{:S(2)}, u32[]{:S(2)}) %collective-permute-start.19) | collective-permute-done | bytes 196640 | tf_op jit(solution)/shard_map/ppermute | solution.py:1000
  159.2 12.9 %shard_map.419 = (f32[384,256]{1,0:T(8,128)}, bf16[4,1280,128]{2,1,0:T(8,128)(2,1)}, f32[8,256]{1,0:T(8,128)}, f32[512,512]{1,0:T(8,128)}, bf16[384,256]{1,0:T(8...) custom-call(s32[6]{0:T(128)} %copy-done.38, ...), custom_call_target="tpu_custom_call" | custom-call | bytes 4194304 | tf_op jit(solution)/shard_map/pallas_call | solution.py:368
  172.2 4.7 %collective-permute-start.21 = (bf16[4,48,512]{2,1,0:T(8,128)(2,1)}, bf16[4,48,512]{2,1,0:T(8,128)(2,1)S(1)}, u32[]{:S(2)}, u32[]{:S(2)}) collective-permute-start(bf16[4,48,512]{2,1,0:T(8,128)(2,1)} %get-tuple-element.144), channel_id=1, source_target_pairs={{0,4},{8,12},{16,20},{24,28},{4,0},{12,8},{20,16},{28,24},{1,5},{9... | collective-permute-start | bytes 589832 | tf_op jit(solution)/shard_map/ppermute | solution.py:1000
  182.1 9.8 %collective-permute-start.24 = (bf16[192,512]{1,0:T(8,128)(2,1)S(1)}, bf16[192,512]{1,0:T(8,128)(2,1)S(1)}, u32[]{:S(2)}, u32[]{:S(2)}) collective-permute-start(bf16[192,512]{1,0:T(8,128)(2,1)S(1)} %get-tuple-element.150), channel_id=1, source_target_pairs={{0,1},{2,3},{1,0},{3,2},{4,5},{6,7},{5,4},{7,6},{8,9},{10,11},{9,8... | collective-permute-start | bytes 589832 | tf_op jit(solution)/shard_map/ppermute | solution.py:1000
  193.0 3.4 %shard_map.422 = (bf16[2,1088,128]{2,1,0:T(8,128)(2,1)S(1)}, bf16[2,1088,128]{2,1,0:T(8,128)(2,1)S(1)}) custom-call(s32[6]{0:T(128)S(1)} %copy-done.41, f32[384,256]{1,0:T(8,128)S(1)} %copy-done.19, bf16[384,256]{1,0:T(8,128)(2,1)S(1)} %copy-done.28, f32[2,192,512]{2,1,0:T(8,128)S(1)} %copy-done.12, ...), custom_call_target="tpu_custom_call" | custom-call | bytes 4194304 | tf_op jit(solution)/shard_map/pallas_call | solution.py:368
  203.9 9.3 %collective-permute-done.26.given = bf16[1,1088,128]{2,1,0:T(8,128)(2,1)S(1)} collective-permute-done((bf16[1,1088,128]{2,1,0:T(8,128)(2,1)S(1)}, bf16[1,1088,128]{2,1,0:T(8,128)(2,1)S(1)}, u32[]{:S(2)}, u32[]{:S(2)}) %collective-permute-start.26) | collective-permute-done | bytes 278560 | tf_op jit(solution)/shard_map/ppermute | solution.py:1203
  216.2 5.5 %all-to-all-start.2 = ((bf16[8,480,128]{2,1,0:T(8,128)(2,1)}), bf16[8,480,128]{2,1,0:T(8,128)(2,1)S(1)}, u32[]{:S(2)}, u32[]{:S(2)}) async-start(bf16[8,480,128]{2,1,0:T(8,128)(2,1)} %shard_map.424), calls=%async_computation.4 | async-start | bytes 1966080 | tf_op jit(solution)/shard_map/all_to_all | solution.py:1221
  225.1 21.0 %all-to-all-done.2.parts = bf16[8,480,128]{2,1,0:T(8,128)(2,1)S(1)} async-done(((bf16[8,480,128]{2,1,0:T(8,128)(2,1)}), bf16[8,480,128]{2,1,0:T(8,128)(2,1)S(1)}, u32[]{:S(2)}, u32[]{:S(2)}) %all-to-all-start.2) | async-done | bytes 983072 | tf_op jit(solution)/shard_map/all_to_all | solution.py:1221
  246.5 6.2 %all-gather.3 = bf16[1664,128]{1,0:T(8,128)(2,1)S(1)} all-gather(bf16[416,128]{1,0:T(8,128)(2,1)S(1)} %get-tuple-element.159), channel_id=5, replica_groups=mesh['row'=8,'col'=4] {'col'}, dimensions={0}, use_global_device_ids=true | all-gather | bytes 532480 | tf_op jit(solution)/shard_map/all_gather | solution.py:1225
  (233 shorter events, 72.4 us)
Async XLA Ops:
  9.6 16.7 %all-to-all-start = ((bf16[8,128,128]{2,1,0:T(8,128)(2,1)}), bf16[8,128,128]{2,1,0:T(8,128)(2,1)S(1)}, u32[]{:S(2)}, u32[]{:S(2)}) async-start(bf16[8,128,128]{2,1,0:T(8,128)(2,1)} %get-tuple-element.100), calls=%async_computation | async-start | bytes 524288 | tf_op jit(solution)/shard_map/all_to_all | solution.py:1048
  16.8 25.7 %all-gather.8.cloned.1.call-start = ((), (), s32[]{:S(2)}) async-start(), calls=%async_computation.7 | async-start | bytes 1310720 | tf_op jit(solution)/shard_map/all_gather | solution.py:1076
  17.6 8.7 %collective-permute-start = (bf16[1,32,128]{2,1,0:T(8,128)(2,1)S(1)}, bf16[1,32,128]{2,1,0:T(8,128)(2,1)S(1)}, u32[]{:S(2)}, u32[]{:S(2)}) collective-permute-start(bf16[1,32,128]{2,1,0:T(8,128)(2,1)S(1)} %slice.51), channel_id=1, source_target_pairs={{0,4},{4,8},{8,12},{12,16},{16,20},{20,24},{24,28},{28,0},{1,5},{5... | collective-permute-start | bytes 24584 | tf_op jit(solution)/shard_map/ppermute | solution.py:993
  27.0 21.5 %all-to-all-start.1 = ((bf16[8,352,128]{2,1,0:T(8,128)(2,1)}), bf16[8,352,128]{2,1,0:T(8,128)(2,1)S(1)}, u32[]{:S(2)}, u32[]{:S(2)}) async-start(bf16[8,352,128]{2,1,0:T(8,128)(2,1)} %get-tuple-element.112), calls=%async_computation.1 | async-start | bytes 1441792 | tf_op jit(solution)/shard_map/all_to_all | solution.py:1077
  30.6 36.1 %all-gather.10.cloned.1.call-start = ((), (), s32[]{:S(2)}) async-start(), calls=%async_computation.8 | async-start | bytes 1638400 | tf_op jit(solution)/shard_map/all_gather | solution.py:1086
  49.3 43.3 %all-gather.12.cloned.1.call-start = ((), (), s32[]{:S(2)}) async-start(), calls=%async_computation.9 | async-start | bytes 1966080 | tf_op jit(solution)/shard_map/all_gather | solution.py:1087
  50.1 153.7 %reduce-scatter.3.cloned.1.call-start = ((), (), s32[]{:S(2)}) async-start(), calls=%async_computation.5 | async-start | bytes 1310720 | tf_op jit(solution)/shard_map/reduce_scatter | solution.py:1167
  52.3 5.7 %collective-permute-start.4 = (bf16[4,48,512]{2,1,0:T(8,128)(2,1)S(1)}, bf16[4,48,512]{2,1,0:T(8,128)(2,1)S(1)}, u32[]{:S(2)}, u32[]{:S(2)}) collective-permute-start(bf16[4,48,512]{2,1,0:T(8,128)(2,1)S(1)} %get-tuple-element.108), channel_id=1, source_target_pairs={{0,4},{8,12},{16,20},{24,28},{4,0},{12,8},{20,16},{28,24},{1,5},{9... | collective-permute-start | bytes 589832 | tf_op jit(solution)/shard_map/ppermute | solution.py:1000
  75.8 10.6 %collective-permute-start.6 = (bf16[4,48,512]{2,1,0:T(8,128)(2,1)}, bf16[4,48,512]{2,1,0:T(8,128)(2,1)S(1)}, u32[]{:S(2)}, u32[]{:S(2)}) collective-permute-start(bf16[4,48,512]{2,1,0:T(8,128)(2,1)} %get-tuple-element.117), channel_id=1, source_target_pairs={{0,4},{8,12},{16,20},{24,28},{4,0},{12,8},{20,16},{28,24},{1,5},{9... | collective-permute-start | bytes 589832 | tf_op jit(solution)/shard_map/ppermute | solution.py:1000
  77.3 9.1 %collective-permute-start.7 = (bf16[4,48,512]{2,1,0:T(8,128)(2,1)}, bf16[4,48,512]{2,1,0:T(8,128)(2,1)S(1)}, u32[]{:S(2)}, u32[]{:S(2)}) collective-permute-start(bf16[4,48,512]{2,1,0:T(8,128)(2,1)} %get-tuple-element.118), channel_id=1, source_target_pairs={{4,8},{12,16},{20,24},{8,4},{16,12},{24,20},{5,9},{13,17},{21,25},... | collective-permute-start | bytes 589832 | tf_op jit(solution)/shard_map/ppermute | solution.py:1000
  103.7 9.6 %collective-permute-start.12 = (f32[64,256]{1,0:T(8,128)}, f32[64,256]{1,0:T(8,128)S(1)}, u32[]{:S(2)}, u32[]{:S(2)}) collective-permute-start(f32[64,256]{1,0:T(8,128)} %get-tuple-element.120), channel_id=1, source_target_pairs={{0,3},{1,2},{2,1},{3,0},{4,7},{5,6},{6,5},{7,4},{8,11},{9,10},{10,... | collective-permute-start | bytes 196616 | tf_op jit(solution)/shard_map/ppermute | solution.py:1013
  103.8 12.7 %collective-permute-start.11 = (f32[64,256]{1,0:T(8,128)}, f32[64,256]{1,0:T(8,128)S(1)}, u32[]{:S(2)}, u32[]{:S(2)}) collective-permute-start(f32[64,256]{1,0:T(8,128)} %get-tuple-element.120), channel_id=1, source_target_pairs={{0,2},{1,3},{2,0},{3,1},{4,6},{5,7},{6,4},{7,5},{8,10},{9,11},{10,... | collective-permute-start | bytes 196616 | tf_op jit(solution)/shard_map/ppermute | solution.py:1013
  117.4 6.4 %collective-permute-start.15 = (f32[64,256]{1,0:T(8,128)S(1)}, f32[64,256]{1,0:T(8,128)S(1)}, u32[]{:S(2)}, u32[]{:S(2)}) collective-permute-start(f32[64,256]{1,0:T(8,128)S(1)} %add_add_fusion.1), channel_id=1, source_target_pairs={{0,12},{4,8},{8,4},{12,0},{16,28},{20,24},{24,20},{28,16},{1,13},{... | collective-permute-start | bytes 196616 | tf_op jit(solution)/shard_map/ppermute | solution.py:1013
  125.6 5.2 %collective-permute-start.16 = (f32[64,256]{1,0:T(8,128)S(1)}, f32[64,256]{1,0:T(8,128)S(1)}, u32[]{:S(2)}, u32[]{:S(2)}) collective-permute-start(f32[64,256]{1,0:T(8,128)S(1)} %add_add_fusion.sums_a), channel_id=1, source_target_pairs={{0,16},{4,20},{8,24},{12,28},{16,0},{20,4},{24,8},{28,12},{1,17},{... | collective-permute-start | bytes 196616 | tf_op jit(solution)/shard_map/ppermute | solution.py:1013
  144.3 68.8 %reduce-scatter.5.cloned.1.call-start = ((), (), s32[]{:S(2)}) async-start(), calls=%async_computation.6 | async-start | bytes 1638400 | tf_op jit(solution)/shard_map/reduce_scatter | solution.py:1186
  144.4 7.6 %collective-permute-start.17 = (bf16[4,192,512]{2,1,0:T(8,128)(2,1)}, bf16[4,192,512]{2,1,0:T(8,128)(2,1)S(1)}, u32[]{:S(2)}, u32[]{:S(2)}) collective-permute-start(bf16[4,192,512]{2,1,0:T(8,128)(2,1)} %get-tuple-element.130), channel_id=1, source_target_pairs={{1,2},{2,1},{5,6},{6,5},{9,10},{10,9},{13,14},{14,13},{17,18},{18,... | collective-permute-start | bytes 2359304 | tf_op jit(solution)/shard_map/ppermute | solution.py:1000
  145.1 6.9 %collective-permute-start.18 = (bf16[4,192,512]{2,1,0:T(8,128)(2,1)}, bf16[4,192,512]{2,1,0:T(8,128)(2,1)S(1)}, u32[]{:S(2)}, u32[]{:S(2)}) collective-permute-start(bf16[4,192,512]{2,1,0:T(8,128)(2,1)} %get-tuple-element.131), channel_id=1, source_target_pairs={{0,1},{2,3},{1,0},{3,2},{4,5},{6,7},{5,4},{7,6},{8,9},{10,11},{9,8... | collective-permute-start | bytes 2359304 | tf_op jit(solution)/shard_map/ppermute | solution.py:1000
  152.7 5.7 %collective-permute-start.19 = (bf16[4,48,512]{2,1,0:T(8,128)(2,1)S(1)}, bf16[4,48,512]{2,1,0:T(8,128)(2,1)S(1)}, u32[]{:S(2)}, u32[]{:S(2)}) collective-permute-start(bf16[4,48,512]{2,1,0:T(8,128)(2,1)S(1)} %get-tuple-element.135), channel_id=1, source_target_pairs={{0,4},{8,12},{16,20},{24,28},{4,0},{12,8},{20,16},{28,24},{1,5},{9... | collective-permute-start | bytes 589832 | tf_op jit(solution)/shard_map/ppermute | solution.py:1000
  153.5 5.0 %collective-permute-start.20 = (bf16[4,48,512]{2,1,0:T(8,128)(2,1)S(1)}, bf16[4,48,512]{2,1,0:T(8,128)(2,1)S(1)}, u32[]{:S(2)}, u32[]{:S(2)}) collective-permute-start(bf16[4,48,512]{2,1,0:T(8,128)(2,1)S(1)} %get-tuple-element.136), channel_id=1, source_target_pairs={{4,8},{12,16},{20,24},{8,4},{16,12},{24,20},{5,9},{13,17},{21,25},... | collective-permute-start | bytes 589832 | tf_op jit(solution)/shard_map/ppermute | solution.py:1000
  172.2 8.6 %collective-permute-start.21 = (bf16[4,48,512]{2,1,0:T(8,128)(2,1)}, bf16[4,48,512]{2,1,0:T(8,128)(2,1)S(1)}, u32[]{:S(2)}, u32[]{:S(2)}) collective-permute-start(bf16[4,48,512]{2,1,0:T(8,128)(2,1)} %get-tuple-element.144), channel_id=1, source_target_pairs={{0,4},{8,12},{16,20},{24,28},{4,0},{12,8},{20,16},{28,24},{1,5},{9... | collective-permute-start | bytes 589832 | tf_op jit(solution)/shard_map/ppermute | solution.py:1000
  181.4 10.5 %collective-permute-start.23 = (bf16[192,512]{1,0:T(8,128)(2,1)S(1)}, bf16[192,512]{1,0:T(8,128)(2,1)S(1)}, u32[]{:S(2)}, u32[]{:S(2)}) collective-permute-start(bf16[192,512]{1,0:T(8,128)(2,1)S(1)} %get-tuple-element.149), channel_id=1, source_target_pairs={{1,2},{2,1},{5,6},{6,5},{9,10},{10,9},{13,14},{14,13},{17,18},{18,... | collective-permute-start | bytes 589832 | tf_op jit(solution)/shard_map/ppermute | solution.py:1000
  182.1 10.9 %collective-permute-start.24 = (bf16[192,512]{1,0:T(8,128)(2,1)S(1)}, bf16[192,512]{1,0:T(8,128)(2,1)S(1)}, u32[]{:S(2)}, u32[]{:S(2)}) collective-permute-start(bf16[192,512]{1,0:T(8,128)(2,1)S(1)} %get-tuple-element.150), channel_id=1, source_target_pairs={{0,1},{2,3},{1,0},{3,2},{4,5},{6,7},{5,4},{7,6},{8,9},{10,11},{9,8... | collective-permute-start | bytes 589832 | tf_op jit(solution)/shard_map/ppermute | solution.py:1000
  201.9 11.3 %collective-permute-start.26 = (bf16[1,1088,128]{2,1,0:T(8,128)(2,1)S(1)}, bf16[1,1088,128]{2,1,0:T(8,128)(2,1)S(1)}, u32[]{:S(2)}, u32[]{:S(2)}) collective-permute-start(bf16[1,1088,128]{2,1,0:T(8,128)(2,1)S(1)} %get-tuple-element.158), channel_id=1, source_target_pairs={{0,2},{1,3},{2,0},{3,1},{4,6},{5,7},{6,4},{7,5},{8,10},{9,11},{10,... | collective-permute-start | bytes 835592 | tf_op jit(solution)/shard_map/ppermute | solution.py:1203
  216.2 30.0 %all-to-all-start.2 = ((bf16[8,480,128]{2,1,0:T(8,128)(2,1)}), bf16[8,480,128]{2,1,0:T(8,128)(2,1)S(1)}, u32[]{:S(2)}, u32[]{:S(2)}) async-start(bf16[8,480,128]{2,1,0:T(8,128)(2,1)} %shard_map.424), calls=%async_computation.4 | async-start | bytes 1966080 | tf_op jit(solution)/shard_map/all_to_all | solution.py:1221
  (74 other events, 1069.9 us)
Sparse Core Ops, SparseCore 0:
  27.1 15.3 all-gather.7
  49.4 17.2 all-gather.9
  68.3 19.6 all-gather.11
  144.4 25.0 reduce-scatter.2
  172.3 38.2 reduce-scatter.4

commit v8 on v7

--- a/solution.py
+++ b/solution.py
@@ -569,6 +569,10 @@
     return copies.start(own, pieces.at[0]) + copies.start_received(
         place, EVEN_COL, first, second, pieces.at[1], pieces.at[2]
     )
+
+
+def bring_kernel(source, near):
+    near[...] = source[...]
 
 
 def extend_kernel(place, keyval, first, second, result):
@@ -920,7 +924,7 @@
     halve(place, stage, total, keep, give)
 
 
-def between_kernel(second, first, kept, given, result):
+def lay_out_kernel(second, first, result):
     rows = result.shape[0]
     sh = D // rows
     begin = 0
@@ -928,6 +932,13 @@
         for k in range(group.shape[0] // D):
             result[:, begin : begin + sh, :] = group[k * D : (k + 1) * D, :].reshape(rows, sh, 128)
             begin += sh
+
+
+def between_kernel(ready, kept, given, result):
+    rows = result.shape[0]
+    sh = D // rows
+    begin = ready.shape[1]
+    result[:, :begin, :] = ready[...]
     for k in range(kept.shape[1] // D):
         span = slice(k * D, (k + 1) * D)
         total = kept[0, span, :].astype(f32) + given[0, span, :].astype(f32)
@@ -1119,7 +1130,8 @@
         {0: hbm},
     )
     rows2 = swaps(*edges, "row")
-    own2 = run(extend_kernel, [ext], [place, keyval2, *rows2], specs={0: SMEM})[0]
+    near_keyval2 = run(bring_kernel, [out(keyval2.shape, bf16)], [keyval2])[0]
+    own2 = run(extend_kernel, [ext], [place, near_keyval2, *rows2], specs={0: SMEM})[0]
     near2 = [own2, *swaps(own2, own2, "col")]
     kept2, att2, middle2, last2, sums = run(
         second_block_kernel,
@@ -1212,11 +1224,11 @@
             [pltpu.VMEM((2 * count, part, 128), bf16)],
             {0: SMEM},
         )
+    ready = run(lay_out_kernel, [out((nr, (per[0] + per[1]) * sh, 128), bf16)], [grads2, grads1])[0]
     mine = run(
         between_kernel,
         [out((nr, sum(per) * sh + SMALL_ROWS, 128), bf16)],
-        [grads2, grads1, kept, given],
-        vmem=56,
+        [ready, kept, given],
     )[0]
     mine = lax.all_to_all(mine, "row", 0, 0, tiled=True)
     mine, small = run(

time: 264 us -> 263 us (level)
    ppermute x2, waiting for transfers between devices: 10.9 us -> 1.59 us  [on_device(): given = lax.ppermute(given, 'col', [(i, i ^ 1 << stage) for i in range(nc)])]
    reduce_scatter x1, waiting for transfers between devices: 0.01 us -> 8.04 us  [on_device(): grads1 = lax.psum_scatter(grads1, 'col', scatter_dimension=0, tiled=False)]
    pallas_call x19 -> x21, Pallas kernels: 64.7 us -> 63.5 us  [run(): pl.pallas_call(kernel, out_shape=outs, in_specs=in_specs, out_specs=resul...]
where the time goes in v8:
time: 263 us; the launch traced here: 262 us
  waiting for transfers between devices  80.6 us (31%)
  starting transfers between devices  71.8 us (27%)
  Pallas kernels  63.5 us (24%)
  local copies, waits for them, and re-layouts  20.4 us (8%)
  between operations  14.7 us (6%)
  blocking collectives  6.24 us (2%)
  other arithmetic  4.24 us (2%)
    pallas_call x21, Pallas kernels, run(): pl.pallas_call(kernel, out_shape=outs, in_specs=in_specs, out_specs=resul...  63.5 us
    ppermute x8, starting transfers between devices, swaps(): lax.ppermute(first, axis, both[0])  25.1 us
    all_to_all x1, waiting for transfers between devices, on_device(): mine = lax.all_to_all(mine, 'row', 0, 0, tiled=True)  20.7 us
    ppermute x7, starting transfers between devices, other(): lax.ppermute(value, axis, [(i, i ^ flip * first) for i in range(count)])  16.2 us
    ppermute x8, waiting for transfers between devices, swaps(): lax.ppermute(first, axis, both[0])  15 us
    unnamed x124, local copies, waits for them, and re-layouts  12.7 us
    ppermute x2, waiting for transfers between devices, onward(): lax.ppermute(value, axis, [(i, (i + 1) % count) for i in range(count)])  9.48 us
    all_gather x1, waiting for transfers between devices, on_device(): late1 = lax.all_gather(late[:, :parts[1]], 'col', axis=0)  8.65 us
  transfers between devices with their start and end apart: 35, of which 20 were waited for; matrix products, arithmetic and copies ran while one was open for 3% of the time, Pallas kernels for 14%

profile of v8, /device:TPU:0, one launch (start us, length us, event | category | flops | bytes accessed | tf_op | source)
XLA Modules:
  0.0 261.5 jit_solution(9879299398684747455)
XLA Ops:
  9.6 7.3 %all-to-all-start = ((bf16[8,128,128]{2,1,0:T(8,128)(2,1)}), bf16[8,128,128]{2,1,0:T(8,128)(2,1)S(1)}, u32[]{:S(2)}, u32[]{:S(2)}) async-start(bf16[8,128,128]{2,1,0:T(8,128)(2,1)} %get-tuple-element.100), calls=%async_computation | async-start | bytes 524288 | tf_op jit(solution)/shard_map/all_to_all | solution.py:1059
  19.6 6.7 %collective-permute-done = bf16[1,32,128]{2,1,0:T(8,128)(2,1)S(1)} collective-permute-done((bf16[1,32,128]{2,1,0:T(8,128)(2,1)S(1)}, bf16[1,32,128]{2,1,0:T(8,128)(2,1)S(1)}, u32[]{:S(2)}, u32[]{:S(2)}) %collective-permute-start) | collective-permute-done | bytes 8224 | tf_op jit(solution)/shard_map/ppermute | solution.py:1004
  27.0 3.6 %all-to-all-start.1 = ((bf16[8,352,128]{2,1,0:T(8,128)(2,1)}), bf16[8,352,128]{2,1,0:T(8,128)(2,1)S(1)}, u32[]{:S(2)}, u32[]{:S(2)}) async-start(bf16[8,352,128]{2,1,0:T(8,128)(2,1)} %get-tuple-element.112), calls=%async_computation.1 | async-start | bytes 1441792 | tf_op jit(solution)/shard_map/all_to_all | solution.py:1088
  31.2 2.8 %collective-permute-done.1 = bf16[49,1,128]{2,0,1:T(8,128)(2,1)S(1)} collective-permute-done((bf16[49,1,128]{2,0,1:T(8,128)(2,1)S(1)}, bf16[49,1,128]{2,0,1:T(8,128)(2,1)S(1)}, u32[]{:S(2)}, u32[]{:S(2)}) %collective-permute-start.1) | collective-permute-done | bytes 12576 | tf_op jit(solution)/shard_map/ppermute | solution.py:1004
  34.8 7.7 %all-gather.8.cloned.1.call-done = bf16[32,128,128]{2,1,0:T(8,128)(2,1)} async-done(((bf16[8,128,128]{2,1,0:T(8,128)(2,1)}), bf16[32,128,128]{2,1,0:T(8,128)(2,1)}) %all-gather.8.cloned.1.call-update) | async-done | bytes 1048592 | tf_op jit(solution)/shard_map/all_gather | solution.py:1087
  58.1 8.6 %all-gather.10.cloned.1.call-done = bf16[32,160,128]{2,1,0:T(8,128)(2,1)} async-done(((bf16[8,160,128]{2,1,0:T(8,128)(2,1)}), bf16[32,160,128]{2,1,0:T(8,128)(2,1)}) %all-gather.10.cloned.1.call-update) | async-done | bytes 1310736 | tf_op jit(solution)/shard_map/all_gather | solution.py:1097
  66.7 9.0 %shard_map.413 = (bf16[6,512,512]{2,1,0:T(8,128)(2,1)}, bf16[384,256]{1,0:T(8,128)(2,1)}, f32[384,256]{1,0:T(8,128)}, f32[384,256]{1,0:T(8,128)}, bf16[384,256]{...) custom-call(s32[6]{0:T(128)} %copy-done.39, ...), custom_call_target="tpu_custom_call" | custom-call | bytes 4194304 | tf_op jit(solution)/shard_map/pallas_call | solution.py:368
  79.0 7.4 %collective-permute-done.6.first = bf16[4,48,512]{2,1,0:T(8,128)(2,1)S(1)} collective-permute-done((bf16[4,48,512]{2,1,0:T(8,128)(2,1)}, bf16[4,48,512]{2,1,0:T(8,128)(2,1)S(1)}, u32[]{:S(2)}, u32[]{:S(2)}) %collective-permute-start.6) | collective-permute-done | bytes 196640 | tf_op jit(solution)/shard_map/ppermute | solution.py:1011
  87.9 2.8 %collective-permute-start.8 = (bf16[4,192,512]{2,1,0:T(8,128)(2,1)S(1)}, bf16[4,192,512]{2,1,0:T(8,128)(2,1)S(1)}, u32[]{:S(2)}, u32[]{:S(2)}) collective-permute-start(bf16[4,192,512]{2,1,0:T(8,128)(2,1)S(1)} %shard_map.415.own), channel_id=1, source_target_pairs={{0,1},{2,3},{1,0},{3,2},{4,5},{6,7},{5,4},{7,6},{8,9},{10,11},{9,8... | collective-permute-start | bytes 2359304 | tf_op jit(solution)/shard_map/ppermute | solution.py:1011
  93.6 9.1 %shard_map.416 = (bf16[12,256,384]{2,1,0:T(8,128)(2,1)}, bf16[384,256]{1,0:T(8,128)(2,1)}, f32[384,256]{1,0:T(8,128)}, f32[384,256]{1,0:T(8,128)}, f32[64,256]{1,0:T(8,128)}) custom-call(s32[6]{0:T(128)} %copy-done.39, s32[384,5]{1,0:T(8,128)} %bitcast.62, s32[384,5]{1,0:T(8,128)} %bitcast.45, f32[384,256]{1,0:T(8,128)} %get-tuple-element.114.hidden, ...), custom_call_target="tpu_custom_call" | custom-call | bytes 4194304 | tf_op jit(solution)/shard_map/pallas_call | solution.py:368
  102.8 9.4 %collective-permute-start.11 = (f32[64,256]{1,0:T(8,128)}, f32[64,256]{1,0:T(8,128)S(1)}, u32[]{:S(2)}, u32[]{:S(2)}) collective-permute-start(f32[64,256]{1,0:T(8,128)} %get-tuple-element.120), channel_id=1, source_target_pairs={{0,2},{1,3},{2,0},{3,1},{4,6},{5,7},{6,4},{7,5},{8,10},{9,11},{10,... | collective-permute-start | bytes 196616 | tf_op jit(solution)/shard_map/ppermute | solution.py:1024
  112.3 3.2 %collective-permute-done.11 = f32[64,256]{1,0:T(8,128)S(1)} collective-permute-done((f32[64,256]{1,0:T(8,128)}, f32[64,256]{1,0:T(8,128)S(1)}, u32[]{:S(2)}, u32[]{:S(2)}) %collective-permute-start.11) | collective-permute-done | bytes 65568 | tf_op jit(solution)/shard_map/ppermute | solution.py:1024
  116.4 3.5 %collective-permute-start.15 = (f32[64,256]{1,0:T(8,128)S(1)}, f32[64,256]{1,0:T(8,128)S(1)}, u32[]{:S(2)}, u32[]{:S(2)}) collective-permute-start(f32[64,256]{1,0:T(8,128)S(1)} %add_add_fusion.1), channel_id=1, source_target_pairs={{0,12},{4,8},{8,4},{12,0},{16,28},{20,24},{24,20},{28,16},{1,13},{... | collective-permute-start | bytes 196616 | tf_op jit(solution)/shard_map/ppermute | solution.py:1024
  130.5 12.8 %shard_map.417 = (f32[8,128]{1,0:T(8,128)}, f32[32,1024]{1,0:T(8,128)}, f32[1,1024]{1,0:T(1,128)}, f32[384,256]{1,0:T(8,128)}, bf16[4,1024,128]{2,1,0:T(8,128)(2...) custom-call(s32[6]{0:T(128)} %copy-done.39, ...), custom_call_target="tpu_custom_call" | custom-call | bytes 4194304 | tf_op jit(solution)/shard_map/pallas_call | solution.py:368
  144.1 3.9 %collective-permute-start.18 = (bf16[4,192,512]{2,1,0:T(8,128)(2,1)}, bf16[4,192,512]{2,1,0:T(8,128)(2,1)S(1)}, u32[]{:S(2)}, u32[]{:S(2)}) collective-permute-start(bf16[4,192,512]{2,1,0:T(8,128)(2,1)} %get-tuple-element.131), channel_id=1, source_target_pairs={{0,1},{2,3},{1,0},{3,2},{4,5},{6,7},{5,4},{7,6},{8,9},{10,11},{9,8... | collective-permute-start | bytes 2359304 | tf_op jit(solution)/shard_map/ppermute | solution.py:1011
  153.4 4.1 %collective-permute-done.19.drowa = bf16[4,48,512]{2,1,0:T(8,128)(2,1)S(1)} collective-permute-done((bf16[4,48,512]{2,1,0:T(8,128)(2,1)S(1)}, bf16[4,48,512]{2,1,0:T(8,128)(2,1)S(1)}, u32[]{:S(2)}, u32[]{:S(2)}) %collective-permute-start.19) | collective-permute-done | bytes 196640 | tf_op jit(solution)/shard_map/ppermute | solution.py:1011
  158.2 12.9 %shard_map.420 = (f32[384,256]{1,0:T(8,128)}, bf16[4,1280,128]{2,1,0:T(8,128)(2,1)}, f32[8,256]{1,0:T(8,128)}, f32[512,512]{1,0:T(8,128)}, bf16[384,256]{1,0:T(8...) custom-call(s32[6]{0:T(128)} %copy-done.39, ...), custom_call_target="tpu_custom_call" | custom-call | bytes 4194304 | tf_op jit(solution)/shard_map/pallas_call | solution.py:368
  171.2 4.7 %collective-permute-start.21 = (bf16[4,48,512]{2,1,0:T(8,128)(2,1)}, bf16[4,48,512]{2,1,0:T(8,128)(2,1)S(1)}, u32[]{:S(2)}, u32[]{:S(2)}) collective-permute-start(bf16[4,48,512]{2,1,0:T(8,128)(2,1)} %get-tuple-element.144), channel_id=1, source_target_pairs={{0,4},{8,12},{16,20},{24,28},{4,0},{12,8},{20,16},{28,24},{1,5},{9... | collective-permute-start | bytes 589832 | tf_op jit(solution)/shard_map/ppermute | solution.py:1011
  181.1 9.8 %collective-permute-start.24 = (bf16[192,512]{1,0:T(8,128)(2,1)S(1)}, bf16[192,512]{1,0:T(8,128)(2,1)S(1)}, u32[]{:S(2)}, u32[]{:S(2)}) collective-permute-start(bf16[192,512]{1,0:T(8,128)(2,1)S(1)} %get-tuple-element.150), channel_id=1, source_target_pairs={{0,1},{2,3},{1,0},{3,2},{4,5},{6,7},{5,4},{7,6},{8,9},{10,11},{9,8... | collective-permute-start | bytes 589832 | tf_op jit(solution)/shard_map/ppermute | solution.py:1011
  192.1 3.4 %shard_map.424 = (bf16[2,1088,128]{2,1,0:T(8,128)(2,1)S(1)}, bf16[2,1088,128]{2,1,0:T(8,128)(2,1)S(1)}) custom-call(s32[6]{0:T(128)S(1)} %copy-done.42, f32[384,256]{1,0:T(8,128)S(1)} %copy-done.19, bf16[384,256]{1,0:T(8,128)(2,1)S(1)} %copy-done.29, f32[2,192,512]{2,1,0:T(8,128)S(1)} %copy-done.12, ...), custom_call_target="tpu_custom_call" | custom-call | bytes 4194304 | tf_op jit(solution)/shard_map/pallas_call | solution.py:368
  202.2 8.0 %reduce-scatter.5.cloned.1.call-done = bf16[1,1280,128]{2,1,0:T(8,128)(2,1)} async-done(((bf16[4,1280,128]{2,1,0:T(8,128)(2,1)}), bf16[1,1280,128]{2,1,0:T(8,128)(2,1)}) %reduce-scatter.5.cloned.1.call-update) | async-done | bytes 327696 | tf_op jit(solution)/shard_map/reduce_scatter | solution.py:1198
  213.3 7.3 %all-to-all-start.2 = ((bf16[8,480,128]{2,1,0:T(8,128)(2,1)}), bf16[8,480,128]{2,1,0:T(8,128)(2,1)S(1)}, u32[]{:S(2)}, u32[]{:S(2)}) async-start(bf16[8,480,128]{2,1,0:T(8,128)(2,1)} %shard_map.426), calls=%async_computation.4 | async-start | bytes 1966080 | tf_op jit(solution)/shard_map/all_to_all | solution.py:1233
  224.1 20.7 %all-to-all-done.2.parts = bf16[8,480,128]{2,1,0:T(8,128)(2,1)S(1)} async-done(((bf16[8,480,128]{2,1,0:T(8,128)(2,1)}), bf16[8,480,128]{2,1,0:T(8,128)(2,1)S(1)}, u32[]{:S(2)}, u32[]{:S(2)}) %all-to-all-start.2) | async-done | bytes 983072 | tf_op jit(solution)/shard_map/all_to_all | solution.py:1233
  245.2 6.2 %all-gather.3 = bf16[1664,128]{1,0:T(8,128)(2,1)S(1)} all-gather(bf16[416,128]{1,0:T(8,128)(2,1)S(1)} %get-tuple-element.159), channel_id=5, replica_groups=mesh['row'=8,'col'=4] {'col'}, dimensions={0}, use_global_device_ids=true | all-gather | bytes 532480 | tf_op jit(solution)/shard_map/all_gather | solution.py:1237
  (235 shorter events, 71.8 us)
Async XLA Ops:
  9.6 16.7 %all-to-all-start = ((bf16[8,128,128]{2,1,0:T(8,128)(2,1)}), bf16[8,128,128]{2,1,0:T(8,128)(2,1)S(1)}, u32[]{:S(2)}, u32[]{:S(2)}) async-start(bf16[8,128,128]{2,1,0:T(8,128)(2,1)} %get-tuple-element.100), calls=%async_computation | async-start | bytes 524288 | tf_op jit(solution)/shard_map/all_to_all | solution.py:1059
  16.8 25.7 %all-gather.8.cloned.1.call-start = ((), (), s32[]{:S(2)}) async-start(), calls=%async_computation.7 | async-start | bytes 1310720 | tf_op jit(solution)/shard_map/all_gather | solution.py:1087
  17.6 8.7 %collective-permute-start = (bf16[1,32,128]{2,1,0:T(8,128)(2,1)S(1)}, bf16[1,32,128]{2,1,0:T(8,128)(2,1)S(1)}, u32[]{:S(2)}, u32[]{:S(2)}) collective-permute-start(bf16[1,32,128]{2,1,0:T(8,128)(2,1)S(1)} %slice.51), channel_id=1, source_target_pairs={{0,4},{4,8},{8,12},{12,16},{16,20},{20,24},{24,28},{28,0},{1,5},{5... | collective-permute-start | bytes 24584 | tf_op jit(solution)/shard_map/ppermute | solution.py:1004
  27.0 21.5 %all-to-all-start.1 = ((bf16[8,352,128]{2,1,0:T(8,128)(2,1)}), bf16[8,352,128]{2,1,0:T(8,128)(2,1)S(1)}, u32[]{:S(2)}, u32[]{:S(2)}) async-start(bf16[8,352,128]{2,1,0:T(8,128)(2,1)} %get-tuple-element.112), calls=%async_computation.1 | async-start | bytes 1441792 | tf_op jit(solution)/shard_map/all_to_all | solution.py:1088
  30.6 36.1 %all-gather.10.cloned.1.call-start = ((), (), s32[]{:S(2)}) async-start(), calls=%async_computation.8 | async-start | bytes 1638400 | tf_op jit(solution)/shard_map/all_gather | solution.py:1097
  49.3 42.4 %all-gather.12.cloned.1.call-start = ((), (), s32[]{:S(2)}) async-start(), calls=%async_computation.9 | async-start | bytes 1966080 | tf_op jit(solution)/shard_map/all_gather | solution.py:1098
  50.1 152.1 %reduce-scatter.3.cloned.1.call-start = ((), (), s32[]{:S(2)}) async-start(), calls=%async_computation.5 | async-start | bytes 1310720 | tf_op jit(solution)/shard_map/reduce_scatter | solution.py:1179
  52.3 5.7 %collective-permute-start.4 = (bf16[4,48,512]{2,1,0:T(8,128)(2,1)S(1)}, bf16[4,48,512]{2,1,0:T(8,128)(2,1)S(1)}, u32[]{:S(2)}, u32[]{:S(2)}) collective-permute-start(bf16[4,48,512]{2,1,0:T(8,128)(2,1)S(1)} %get-tuple-element.108), channel_id=1, source_target_pairs={{0,4},{8,12},{16,20},{24,28},{4,0},{12,8},{20,16},{28,24},{1,5},{9... | collective-permute-start | bytes 589832 | tf_op jit(solution)/shard_map/ppermute | solution.py:1011
  75.8 10.6 %collective-permute-start.6 = (bf16[4,48,512]{2,1,0:T(8,128)(2,1)}, bf16[4,48,512]{2,1,0:T(8,128)(2,1)S(1)}, u32[]{:S(2)}, u32[]{:S(2)}) collective-permute-start(bf16[4,48,512]{2,1,0:T(8,128)(2,1)} %get-tuple-element.117), channel_id=1, source_target_pairs={{0,4},{8,12},{16,20},{24,28},{4,0},{12,8},{20,16},{28,24},{1,5},{9... | collective-permute-start | bytes 589832 | tf_op jit(solution)/shard_map/ppermute | solution.py:1011
  77.3 9.1 %collective-permute-start.7 = (bf16[4,48,512]{2,1,0:T(8,128)(2,1)}, bf16[4,48,512]{2,1,0:T(8,128)(2,1)S(1)}, u32[]{:S(2)}, u32[]{:S(2)}) collective-permute-start(bf16[4,48,512]{2,1,0:T(8,128)(2,1)} %get-tuple-element.118), channel_id=1, source_target_pairs={{4,8},{12,16},{20,24},{8,4},{16,12},{24,20},{5,9},{13,17},{21,25},... | collective-permute-start | bytes 589832 | tf_op jit(solution)/shard_map/ppermute | solution.py:1011
  102.7 9.6 %collective-permute-start.12 = (f32[64,256]{1,0:T(8,128)}, f32[64,256]{1,0:T(8,128)S(1)}, u32[]{:S(2)}, u32[]{:S(2)}) collective-permute-start(f32[64,256]{1,0:T(8,128)} %get-tuple-element.120), channel_id=1, source_target_pairs={{0,3},{1,2},{2,1},{3,0},{4,7},{5,6},{6,5},{7,4},{8,11},{9,10},{10,... | collective-permute-start | bytes 196616 | tf_op jit(solution)/shard_map/ppermute | solution.py:1024
  102.8 12.7 %collective-permute-start.11 = (f32[64,256]{1,0:T(8,128)}, f32[64,256]{1,0:T(8,128)S(1)}, u32[]{:S(2)}, u32[]{:S(2)}) collective-permute-start(f32[64,256]{1,0:T(8,128)} %get-tuple-element.120), channel_id=1, source_target_pairs={{0,2},{1,3},{2,0},{3,1},{4,6},{5,7},{6,4},{7,5},{8,10},{9,11},{10,... | collective-permute-start | bytes 196616 | tf_op jit(solution)/shard_map/ppermute | solution.py:1024
  116.4 6.4 %collective-permute-start.15 = (f32[64,256]{1,0:T(8,128)S(1)}, f32[64,256]{1,0:T(8,128)S(1)}, u32[]{:S(2)}, u32[]{:S(2)}) collective-permute-start(f32[64,256]{1,0:T(8,128)S(1)} %add_add_fusion.1), channel_id=1, source_target_pairs={{0,12},{4,8},{8,4},{12,0},{16,28},{20,24},{24,20},{28,16},{1,13},{... | collective-permute-start | bytes 196616 | tf_op jit(solution)/shard_map/ppermute | solution.py:1024
  124.6 5.2 %collective-permute-start.16 = (f32[64,256]{1,0:T(8,128)S(1)}, f32[64,256]{1,0:T(8,128)S(1)}, u32[]{:S(2)}, u32[]{:S(2)}) collective-permute-start(f32[64,256]{1,0:T(8,128)S(1)} %add_add_fusion.sums_a), channel_id=1, source_target_pairs={{0,16},{4,20},{8,24},{12,28},{16,0},{20,4},{24,8},{28,12},{1,17},{... | collective-permute-start | bytes 196616 | tf_op jit(solution)/shard_map/ppermute | solution.py:1024
  143.3 66.9 %reduce-scatter.5.cloned.1.call-start = ((), (), s32[]{:S(2)}) async-start(), calls=%async_computation.6 | async-start | bytes 1638400 | tf_op jit(solution)/shard_map/reduce_scatter | solution.py:1198
  143.4 7.6 %collective-permute-start.17 = (bf16[4,192,512]{2,1,0:T(8,128)(2,1)}, bf16[4,192,512]{2,1,0:T(8,128)(2,1)S(1)}, u32[]{:S(2)}, u32[]{:S(2)}) collective-permute-start(bf16[4,192,512]{2,1,0:T(8,128)(2,1)} %get-tuple-element.130), channel_id=1, source_target_pairs={{1,2},{2,1},{5,6},{6,5},{9,10},{10,9},{13,14},{14,13},{17,18},{18,... | collective-permute-start | bytes 2359304 | tf_op jit(solution)/shard_map/ppermute | solution.py:1011
  144.1 6.9 %collective-permute-start.18 = (bf16[4,192,512]{2,1,0:T(8,128)(2,1)}, bf16[4,192,512]{2,1,0:T(8,128)(2,1)S(1)}, u32[]{:S(2)}, u32[]{:S(2)}) collective-permute-start(bf16[4,192,512]{2,1,0:T(8,128)(2,1)} %get-tuple-element.131), channel_id=1, source_target_pairs={{0,1},{2,3},{1,0},{3,2},{4,5},{6,7},{5,4},{7,6},{8,9},{10,11},{9,8... | collective-permute-start | bytes 2359304 | tf_op jit(solution)/shard_map/ppermute | solution.py:1011
  151.7 5.7 %collective-permute-start.19 = (bf16[4,48,512]{2,1,0:T(8,128)(2,1)S(1)}, bf16[4,48,512]{2,1,0:T(8,128)(2,1)S(1)}, u32[]{:S(2)}, u32[]{:S(2)}) collective-permute-start(bf16[4,48,512]{2,1,0:T(8,128)(2,1)S(1)} %get-tuple-element.135), channel_id=1, source_target_pairs={{0,4},{8,12},{16,20},{24,28},{4,0},{12,8},{20,16},{28,24},{1,5},{9... | collective-permute-start | bytes 589832 | tf_op jit(solution)/shard_map/ppermute | solution.py:1011
  152.5 5.0 %collective-permute-start.20 = (bf16[4,48,512]{2,1,0:T(8,128)(2,1)S(1)}, bf16[4,48,512]{2,1,0:T(8,128)(2,1)S(1)}, u32[]{:S(2)}, u32[]{:S(2)}) collective-permute-start(bf16[4,48,512]{2,1,0:T(8,128)(2,1)S(1)} %get-tuple-element.136), channel_id=1, source_target_pairs={{4,8},{12,16},{20,24},{8,4},{16,12},{24,20},{5,9},{13,17},{21,25},... | collective-permute-start | bytes 589832 | tf_op jit(solution)/shard_map/ppermute | solution.py:1011
  171.2 8.6 %collective-permute-start.21 = (bf16[4,48,512]{2,1,0:T(8,128)(2,1)}, bf16[4,48,512]{2,1,0:T(8,128)(2,1)S(1)}, u32[]{:S(2)}, u32[]{:S(2)}) collective-permute-start(bf16[4,48,512]{2,1,0:T(8,128)(2,1)} %get-tuple-element.144), channel_id=1, source_target_pairs={{0,4},{8,12},{16,20},{24,28},{4,0},{12,8},{20,16},{28,24},{1,5},{9... | collective-permute-start | bytes 589832 | tf_op jit(solution)/shard_map/ppermute | solution.py:1011
  180.5 10.5 %collective-permute-start.23 = (bf16[192,512]{1,0:T(8,128)(2,1)S(1)}, bf16[192,512]{1,0:T(8,128)(2,1)S(1)}, u32[]{:S(2)}, u32[]{:S(2)}) collective-permute-start(bf16[192,512]{1,0:T(8,128)(2,1)S(1)} %get-tuple-element.149), channel_id=1, source_target_pairs={{1,2},{2,1},{5,6},{6,5},{9,10},{10,9},{13,14},{14,13},{17,18},{18,... | collective-permute-start | bytes 589832 | tf_op jit(solution)/shard_map/ppermute | solution.py:1011
  181.1 10.9 %collective-permute-start.24 = (bf16[192,512]{1,0:T(8,128)(2,1)S(1)}, bf16[192,512]{1,0:T(8,128)(2,1)S(1)}, u32[]{:S(2)}, u32[]{:S(2)}) collective-permute-start(bf16[192,512]{1,0:T(8,128)(2,1)S(1)} %get-tuple-element.150), channel_id=1, source_target_pairs={{0,1},{2,3},{1,0},{3,2},{4,5},{6,7},{5,4},{7,6},{8,9},{10,11},{9,8... | collective-permute-start | bytes 589832 | tf_op jit(solution)/shard_map/ppermute | solution.py:1011
  200.2 12.1 %collective-permute-start.26 = (bf16[1,1088,128]{2,1,0:T(8,128)(2,1)S(1)}, bf16[1,1088,128]{2,1,0:T(8,128)(2,1)S(1)}, u32[]{:S(2)}, u32[]{:S(2)}) collective-permute-start(bf16[1,1088,128]{2,1,0:T(8,128)(2,1)S(1)} %get-tuple-element.158), channel_id=1, source_target_pairs={{0,2},{1,3},{2,0},{3,1},{4,6},{5,7},{6,4},{7,5},{8,10},{9,11},{10,... | collective-permute-start | bytes 835592 | tf_op jit(solution)/shard_map/ppermute | solution.py:1215
  213.3 31.5 %all-to-all-start.2 = ((bf16[8,480,128]{2,1,0:T(8,128)(2,1)}), bf16[8,480,128]{2,1,0:T(8,128)(2,1)S(1)}, u32[]{:S(2)}, u32[]{:S(2)}) async-start(bf16[8,480,128]{2,1,0:T(8,128)(2,1)} %shard_map.426), calls=%async_computation.4 | async-start | bytes 1966080 | tf_op jit(solution)/shard_map/all_to_all | solution.py:1233
  (74 other events, 1065.8 us)
Sparse Core Ops, SparseCore 0:
  27.1 15.3 all-gather.7
  49.4 17.2 all-gather.9
  68.3 19.6 all-gather.11
  143.5 25.0 reduce-scatter.2
  171.3 38.9 reduce-scatter.4
